TPU v7x, 32 devices: a whole 2x2x4 slice. The times are simulated.
32 devices in a mesh: row: 4 (over x, core), col: 4 (over z), depth: 2 (over y).
Axes of the slice: x: 2, y: 2, z: 4, core: 2. Of those that a mesh axis runs over, the one named last changes fastest.
Arguments:
- tokens: bfloat16 [768, 3072], P(('col', 'depth'), 'row'), may hold values from -6 to 6
- weight_in: bfloat16 [3072, 12288], P('row', 'col'), may hold values from -0.109375 to 0.109375
- weight_out: bfloat16 [12288, 3072], P('col', 'row'), may hold values from -0.0546875 to 0.0546875
- output_grad: bfloat16 [768, 3072], P(('col', 'depth'), 'row'), may hold values from -6 to 6
Outputs:
- output: bfloat16 [768, 3072], P(('col', 'depth'), 'row')
- input_grad: bfloat16 [768, 3072], P(('col', 'depth'), 'row')
- weight_in_grad: float32 [3072, 12288], P(('row', 'depth'), 'col')
- weight_out_grad: float32 [12288, 3072], P(('col', 'depth'), 'row')
All inputs are finite; a program needn't handle non-finite values.
Results may differ from a plain program's by a relative error of at most 0.018.
Values may be sent and summed in bfloat16 or wider, within the bound.
No kernel may reach another device: no remote copies, remote signals or barrier semaphores. Data moves between devices by JAX's collectives and lax.ppermute only.
A program may use at most 128 MiB of HBM per device.

v0:
```python
import jax
import jax.numpy as jnp
from jax import lax
from jax.sharding import PartitionSpec as P


def gelu_parts(hidden_pre):
    normal_cdf = 0.5 * (1.0 + lax.erf(hidden_pre * 0.7071067811865476))
    normal_pdf = jnp.exp(-0.5 * hidden_pre * hidden_pre) * 0.3989422804014327
    return (hidden_pre * normal_cdf, normal_cdf + hidden_pre * normal_pdf)


def product_rows(panel, weight, contract):
    return lax.dot_general(
        panel, weight, (((1,), (contract,)), ((), ())), preferred_element_type=jnp.float32
    )


def full_product(panel, weight, contract):
    return lax.dot_general(
        panel, weight, (((1,), (contract,)), ((), ())), preferred_element_type=jnp.float32
    )


def hidden_total(term):
    return lax.psum(term.astype(jnp.bfloat16), "row").astype(jnp.float32)


def model_summed(panel, weight, contract):
    return lax.psum_scatter(
        product_rows(panel, weight, contract).astype(jnp.bfloat16),
        "col",
        scatter_dimension=0,
        tiled=True,
    ).astype(jnp.float32)


def shards(tokens, weight_in, weight_out, output_grad):
    x_panel, dy_panel = (
        lax.all_gather(tokens, "col", axis=0, tiled=True),
        lax.all_gather(output_grad, "col", axis=0, tiled=True),
    )
    hidden_pre = hidden_total(full_product(x_panel, weight_in, 0))
    gelu_value, gelu_slope = gelu_parts(hidden_pre)
    act_panel = gelu_value.astype(jnp.bfloat16)
    output = model_summed(act_panel, weight_out, 0).astype(jnp.bfloat16)
    act_grad = hidden_total(full_product(dy_panel, weight_out, 1))
    grad_panel = (act_grad * gelu_slope).astype(jnp.bfloat16)
    input_grad = model_summed(grad_panel, weight_in, 1).astype(jnp.bfloat16)
    term_in = lax.dot_general(
        x_panel, grad_panel, (((0,), (0,)), ((), ())), preferred_element_type=jnp.float32
    )
    term_out = lax.dot_general(
        act_panel, dy_panel, (((0,), (0,)), ((), ())), preferred_element_type=jnp.float32
    )
    weight_in_grad, weight_out_grad = (
        lax.psum_scatter(
            term_in.astype(jnp.bfloat16), "depth", scatter_dimension=0, tiled=True
        ).astype(jnp.float32),
        lax.psum_scatter(
            term_out.astype(jnp.bfloat16), "depth", scatter_dimension=0, tiled=True
        ).astype(jnp.float32),
    )
    return (output, input_grad, weight_in_grad, weight_out_grad)


def solution(mesh):
    placed = (
        P(("col", "depth"), "row"),
        P("row", "col"),
        P("col", "row"),
        P(("col", "depth"), "row"),
    )
    return jax.shard_map(
        shards,
        mesh=mesh,
        in_specs=placed,
        out_specs=(
            P(("col", "depth"), "row"),
            P(("col", "depth"), "row"),
            P(("row", "depth"), "col"),
            P(("col", "depth"), "row"),
        ),
        check_vma=False,
    )
```

profile of v0, /device:TPU:0, one launch (start us, length us, event | category | flops | bytes accessed | tf_op | source)
XLA Modules:
  0.0 341.0 jit_solution(11481241054604734372)
XLA Ops:
  7.2 0.0 all-reduce.3.cloned.1.call-start
  7.2 18.4 %all_gather.6 = bf16[384,768]{1,0:T(8,128)(2,1)S(1)} all-gather(bf16[96,768]{1,0:T(8,128)(2,1)} %param.4), channel_id=1, replica_groups=mesh['row'=4,'col'=4,'depth'=2] {'col'}, dimensions={0}, use_global_device_ids=true | all-gather | bytes 737280 | tf_op jit(solution)/shard_map/all_gather | solution.py:40
  25.6 0.0 slice-start
  25.6 16.6 %all_gather.7 = bf16[384,768]{1,0:T(8,128)(2,1)S(1)} all-gather(bf16[96,768]{1,0:T(8,128)(2,1)} %param.7), channel_id=1, replica_groups=mesh['row'=4,'col'=4,'depth'=2] {'col'}, dimensions={0}, use_global_device_ids=true | all-gather | bytes 737280 | tf_op jit(solution)/shard_map/all_gather | solution.py:41
  42.2 0.0 slice-start.1
  42.2 5.8 %convolution_convert_fusion.2 = bf16[384,3072]{1,0:T(8,128)(2,1)} fusion(bf16[384,768]{1,0:T(8,128)(2,1)S(1)} %all_gather.7, bf16[3072,768]{1,0:T(8,128)(2,1)} %param.6), kind=kOutput, calls=%fused_computation.17 | convolution fusion | flops 1813118976 | bytes 7667712 | tf_op jit(solution)/shard_map/dot_general | solution.py:20
  48.1 0.0 slice-done
  48.1 0.0 slice-done.1
  48.1 3.4 %convolution_convert_fusion.3 = bf16[384,3072]{1,0:T(8,128)(2,1)} fusion(bf16[384,768]{1,0:T(8,128)(2,1)S(1)} %all_gather.6, bf16[768,3072]{1,0:T(8,128)(2,1)S(1)} %bitcast.14), kind=kOutput, calls=%fused_computation.18 | convolution fusion | flops 1813118976 | bytes 7667712 | tf_op jit(solution)/shard_map/dot_general | solution.py:20
  51.5 0.0 all-reduce.3.cloned.1.call-update
  51.6 0.0 reduce-scatter.13.cloned.1.call-start
  51.6 95.5 %all-reduce.3.cloned.1.call-done = (bf16[384,3072]{1,0:T(8,128)(2,1)}, bf16[384,3072]{1,0:T(8,128)(2,1)}) async-done(((bf16[384,3072]{1,0:T(8,128)(2,1)}, bf16[384,3072]{1,0:T(8,128)(2,1)}), (bf16[384,3072]{1,0:T(8,128)(2,1)}, bf16[384,3072]{1,0:T(8,128)(2,1)})) %all-reduce.3.cloned.1.call-update) | async-done | bytes 4718608 | tf_op jit(solution)/shard_map/psum | solution.py:26
  147.1 3.9 %fusion.8 = bf16[384,3072]{1,0:T(8,128)(2,1)S(1)} fusion(bf16[384,3072]{1,0:T(8,128)(2,1)} %get-tuple-element.12, bf16[384,3072]{1,0:T(8,128)(2,1)} %get-tuple-element.13), kind=kLoop, calls=%fused_computation.15 | loop fusion | flops 14155776 | bytes 7077888 | tf_op jit(solution)/shard_map/convert_element_type | solution.py:48
  151.0 0.0 copy-start.1
  151.0 1.4 copy-done.1
  152.4 4.3 %fusion.9 = bf16[768,3072]{0,1:T(8,128)(2,1)} fusion(bf16[384,3072]{1,0:T(8,128)(2,1)S(1)} %fusion.8, bf16[384,768]{1,0:T(8,128)(2,1)S(1)} %all_gather.6), kind=kOutput, calls=%fused_computation.16 | convolution fusion | flops 1814298624 | bytes 7667712 | tf_op jit(solution)/shard_map/dot_general | solution.py:50
  156.7 6.6 %copy.10 = bf16[768,3072]{1,0:T(8,128)(2,1)} copy(bf16[768,3072]{0,1:T(8,128)(2,1)} %fusion.9) | data formatting | bytes 9437184
  163.3 0.0 copy-start
  163.3 0.0 reduce-scatter.13.cloned.1.call-update
  163.4 0.0 reduce-scatter.11.cloned.1.call-start
  163.4 1.6 copy-done
  165.0 4.4 %convolution_convert_fusion = bf16[3072,768]{1,0:T(8,128)(2,1)} fusion(bf16[384,768]{1,0:T(8,128)(2,1)S(1)} %all_gather.7, bf16[384,3072]{1,0:T(8,128)(2,1)S(1)} %copy-done), kind=kOutput, calls=%fused_computation.5 | convolution fusion | flops 1821376512 | bytes 7667712 | tf_op jit(solution)/shard_map/dot_general | solution.py:53
  169.4 0.0 reduce-scatter.11.cloned.1.call-update
  169.4 0.0 reduce-scatter.9.cloned.1.call-start
  169.5 6.2 %convolution_convert_fusion.4 = bf16[384,768]{1,0:T(8,128)(2,1)} fusion(bf16[384,3072]{1,0:T(8,128)(2,1)} %copy-done.1, bf16[768,3072]{1,0:T(8,128)(2,1)} %param.5), kind=kOutput, calls=%fused_computation.19 | convolution fusion | flops 1812234240 | bytes 7667712 | tf_op jit(solution)/shard_map/dot_general | solution.py:14
  175.7 0.0 reduce-scatter.9.cloned.1.call-update
  175.7 0.2 reduce-scatter.7.cloned.1.call-start
  176.0 5.7 %convolution_convert_fusion.5 = bf16[384,768]{1,0:T(8,128)(2,1)} fusion(bf16[3072,768]{1,0:T(8,128)(2,1)} %param.6, bf16[384,3072]{1,0:T(8,128)(2,1)S(1)} %copy-done), kind=kOutput, calls=%fused_computation.20 | convolution fusion | flops 1819312128 | bytes 7667712 | tf_op jit(solution)/shard_map/dot_general | solution.py:14
  181.6 0.0 reduce-scatter.7.cloned.1.call-update
  181.7 42.0 %reduce-scatter.13.cloned.1.call-done = bf16[384,3072]{1,0:T(8,128)(2,1)} async-done(((bf16[768,3072]{1,0:T(8,128)(2,1)}), bf16[384,3072]{1,0:T(8,128)(2,1)}) %reduce-scatter.13.cloned.1.call-update) | async-done | bytes 2359312
  223.7 3.0 copy.11
  226.7 3.1 copy.9
  229.8 56.9 %reduce-scatter.11.cloned.1.call-done = bf16[1536,768]{1,0:T(8,128)(2,1)} async-done(((bf16[3072,768]{1,0:T(8,128)(2,1)}), bf16[1536,768]{1,0:T(8,128)(2,1)}) %reduce-scatter.11.cloned.1.call-update) | async-done | bytes 2359312 | tf_op jit(solution)/shard_map/reduce_scatter | solution.py:60
  286.7 4.2 %convert_element_type.55 = f32[1536,768]{1,0:T(8,128)} convert(bf16[1536,768]{1,0:T(8,128)(2,1)} %reduce-scatter.11.cloned.1.call-done) | non-fusion elementwise | flops 1179648 | bytes 7077888 | tf_op jit(solution)/shard_map/convert_element_type | solution.py:62
  290.9 20.5 %reduce-scatter.9.cloned.1.call-done = bf16[96,768]{1,0:T(8,128)(2,1)} async-done(((bf16[384,768]{1,0:T(8,128)(2,1)}), bf16[96,768]{1,0:T(8,128)(2,1)}) %reduce-scatter.9.cloned.1.call-update) | async-done | bytes 147472 | tf_op jit(solution)/shard_map/reduce_scatter | solution.py:30
  311.4 23.1 %reduce-scatter.7.cloned.1.call-done = bf16[96,768]{1,0:T(8,128)(2,1)} async-done(((bf16[384,768]{1,0:T(8,128)(2,1)}), bf16[96,768]{1,0:T(8,128)(2,1)}) %reduce-scatter.7.cloned.1.call-update) | async-done | bytes 147472 | tf_op jit(solution)/shard_map/reduce_scatter | solution.py:30
  (1 shorter events, 0.0 us)
Async XLA Ops:
  7.2 140.0 %all-reduce.3.cloned.1.call-start = ((), (), s32[]{:S(2)}) async-start(), calls=%async_computation.8 | async-start | bytes 9437184 | tf_op jit(solution)/shard_map/psum | solution.py:26
  25.6 22.5 %slice-start = ((s8[4718592]{0:T(1024)(128)(4,1)}), s8[4194304]{0:T(1024)(128)(4,1)S(1)}, s32[]{:S(2)}) async-start(s8[4718592]{0:T(1024)(128)(4,1)} %bitcast.13), calls=%async_computation.9 | async-start | bytes 8388608
  42.2 5.8 %slice-start.1 = ((s8[4718592]{0:T(1024)(128)(4,1)}), s8[524288]{0:T(1024)(128)(4,1)S(1)}, s32[]{:S(2)}) async-start(s8[4718592]{0:T(1024)(128)(4,1)} %bitcast.13), calls=%async_computation.10 | async-start | bytes 1048576
  51.6 172.1 %reduce-scatter.13.cloned.1.call-start = ((), (), s32[]{:S(2)}) async-start(), calls=%async_computation.7 | async-start | bytes 7077888
  151.0 1.4 copy-start.1
  163.3 1.7 copy-start
  163.4 123.3 %reduce-scatter.11.cloned.1.call-start = ((), (), s32[]{:S(2)}) async-start(), calls=%async_computation.6 | async-start | bytes 7077888 | tf_op jit(solution)/shard_map/reduce_scatter | solution.py:60
  169.4 141.9 %reduce-scatter.9.cloned.1.call-start = ((), (), s32[]{:S(2)}) async-start(), calls=%async_computation.5 | async-start | bytes 737280 | tf_op jit(solution)/shard_map/reduce_scatter | solution.py:30
  175.7 158.7 %reduce-scatter.7.cloned.1.call-start = ((), (), s32[]{:S(2)}) async-start(), calls=%async_computation.4 | async-start | bytes 737280 | tf_op jit(solution)/shard_map/reduce_scatter | solution.py:30
Sparse Core Ops, SparseCore 0:
  51.7 95.3 all-reduce.2
  163.5 60.1 reduce-scatter.12
  226.6 59.9 reduce-scatter.10
  289.4 21.9 reduce-scatter.8
  314.1 20.3 reduce-scatter.6
where the time goes:
time: 341 us
  waiting for transfers between devices  238 us (70%)
  blocking collectives  35 us (10%)
  matrix products  29.9 us (9%)
  local copies, waits for them, and re-layouts  15.8 us (5%)
  between operations  13.8 us (4%)
  other arithmetic  8.08 us (2%)
    psum x1, waiting for transfers between devices, hidden_total(): return lax.psum(term.astype(jnp.bfloat16), 'row').astype(jnp.float32)  95.5 us
    reduce_scatter x1, waiting for transfers between devices, shards(): lax.psum_scatter(term_out.astype(jnp.bfloat16), 'depth', scatter_dimensio...  56.9 us
    reduce_scatter x2, waiting for transfers between devices, model_summed(): lax.psum_scatter(product_rows(panel, weight, contract).astype(jnp.bfloat1...  43.6 us
    unnamed x6, waiting for transfers between devices  42.1 us
    all_gather x1, blocking collectives, shards(): lax.all_gather(tokens, 'col', axis=0, tiled=True)  18.4 us
    all_gather x1, blocking collectives, shards(): lax.all_gather(output_grad, 'col', axis=0, tiled=True)  16.6 us
    unnamed x11, local copies, waits for them, and re-layouts  15.8 us
    dot_general x2, matrix products, product_rows(): lax.dot_general(panel, weight, (((1,), (contract,)), ((), ())), preferred...  11.9 us
  transfers between devices with their start and end apart: 5, of which 5 were waited for; matrix products, arithmetic and copies ran while one was open for 8% of the time, Pallas kernels for 0%

commit v1 on v0

v1 whole, which is shorter than its diff:
```python
import functools

import jax
import jax.numpy as jnp
from jax import lax
from jax.experimental import pallas as pl
from jax.experimental.pallas import tpu as pltpu
from jax.sharding import PartitionSpec as P

BF16, F32 = jnp.bfloat16, jnp.float32
VMEM_LIMIT = 32 * 1024 * 1024


def gelu_parts(hidden_pre):
    normal_cdf = 0.5 * (1.0 + lax.erf(hidden_pre * 0.7071067811865476))
    normal_pdf = jnp.exp(-0.5 * hidden_pre * hidden_pre) * 0.3989422804014327
    return (hidden_pre * normal_cdf, normal_cdf + hidden_pre * normal_pdf)


def dot(left, right, left_dim, right_dim):
    return lax.dot_general(
        left, right, (((left_dim,), (right_dim,)), ((), ())), preferred_element_type=F32
    )


def call(kernel, grid, in_specs, out_specs, out_shape, scratch, flops, bytes_accessed):
    return pl.pallas_call(
        kernel,
        grid_spec=pltpu.PrefetchScalarGridSpec(
            num_scalar_prefetch=1,
            grid=grid,
            in_specs=in_specs,
            out_specs=out_specs,
            scratch_shapes=scratch,
        ),
        out_shape=out_shape,
        compiler_params=pltpu.CompilerParams(vmem_limit_bytes=VMEM_LIMIT),
        cost_estimate=pl.CostEstimate(
            flops=flops, bytes_accessed=bytes_accessed, transcendentals=0
        ),
    )


def hidden_kernel(blocks, where, tokens, cotangent, weight_in, weight_out, *outs):
    step = pl.program_id(0)
    other_hidden, other_grad, own_hidden, own_grad = outs
    hidden = dot(tokens[...], weight_in[...], 1, 0).astype(BF16)
    grad = dot(cotangent[...], weight_out[...], 1, 1).astype(BF16)

    @pl.when(step < blocks)
    def _():
        other_hidden[...] = hidden
        other_grad[...] = grad

    @pl.when(step >= blocks)
    def _():
        own_hidden[...] = hidden
        own_grad[...] = grad


def hidden_partials(where, tokens, cotangent, weight_in, weight_out):
    rows, features = tokens.shape
    half = weight_in.shape[1] // 2
    blocks = 2
    width = half // blocks

    def place(step, where):
        core = jnp.where(step < blocks, 1 - where[0], where[0])
        return core * blocks + step % blocks

    whole = pl.BlockSpec((rows, features), lambda step, where: (0, 0))
    other = pl.BlockSpec((rows, width), lambda step, where: (0, jnp.minimum(step, blocks - 1)))
    own = pl.BlockSpec((rows, width), lambda step, where: (0, jnp.maximum(step - blocks, 0)))
    return call(
        functools.partial(hidden_kernel, blocks),
        (2 * blocks,),
        [
            whole,
            whole,
            pl.BlockSpec((features, width), lambda step, where: (0, place(step, where))),
            pl.BlockSpec((width, features), lambda step, where: (place(step, where), 0)),
        ],
        [other, other, own, own],
        [jax.ShapeDtypeStruct((rows, half), BF16)] * 4,
        [],
        8 * rows * features * half,
        8 * features * half + 12 * rows * half,
    )(where, tokens, cotangent, weight_in, weight_out)


def model_kernel(ring, where, *refs):
    step = pl.program_id(0)
    own_act, own_pre, other_act, other_pre, out_a, in_a, out_b, in_b = refs[:8]
    arrived = refs[8:10] if ring else ()
    out, grad, out_sum, grad_sum = refs[-4:]
    new_out = dot(own_act[...], out_a[...], 1, 0) + dot(other_act[...], out_b[...], 1, 0)
    new_grad = dot(own_pre[...], in_a[...], 1, 1) + dot(other_pre[...], in_b[...], 1, 1)

    @pl.when(step == 0)
    def _():
        out_sum[...] = new_out
        grad_sum[...] = new_grad

    @pl.when(step > 0)
    def _():
        out_sum[...] += new_out
        grad_sum[...] += new_grad

    @pl.when(step == pl.num_programs(0) - 1)
    def _():
        if ring:
            out[...] = (out_sum[...] + arrived[0][...].astype(F32)).astype(BF16)
            grad[...] = (grad_sum[...] + arrived[1][...].astype(F32)).astype(BF16)
        else:
            out[...] = out_sum[...].astype(BF16)
            grad[...] = grad_sum[...].astype(BF16)


def model_partials(where, own, other, weight_in, weight_out, arrived):
    rows, half = own[0].shape
    features = weight_in.shape[0]
    blocks = 2
    width = half // blocks
    block = pl.BlockSpec((rows, width), lambda step, where: (0, step))
    whole = pl.BlockSpec((rows, features), lambda step, where: (0, 0))

    def weights(core):
        return [
            pl.BlockSpec((width, features), lambda step, where: (core(where) * blocks + step, 0)),
            pl.BlockSpec((features, width), lambda step, where: (0, core(where) * blocks + step)),
        ]

    return call(
        functools.partial(model_kernel, bool(arrived)),
        (blocks,),
        [block] * 4
        + weights(lambda where: where[0])
        + weights(lambda where: 1 - where[0])
        + [whole] * len(arrived),
        [whole, whole],
        [jax.ShapeDtypeStruct((rows, features), BF16)] * 2,
        [pltpu.VMEM((rows, features), F32)] * 2,
        8 * rows * features * half,
        8 * features * half + 8 * rows * half,
    )(where, *own, *other, weight_out, weight_in, weight_out, weight_in, *arrived)


def weight_kernel(chunks, blocks, pieces, before, where, *refs):
    step = pl.program_id(0)
    tokens, cotangents = refs[:chunks], refs[chunks : 2 * chunks]
    own_pre, other_pre = refs[2 * chunks : 3 * chunks], refs[3 * chunks : 4 * chunks]
    own_act, other_act = refs[4 * chunks : 5 * chunks], refs[5 * chunks : 6 * chunks]
    earlier = refs[6 * chunks : 6 * chunks + 2] if before else ()
    in_grad, out_grad, all_tokens, all_cotangents, all_pre, all_act = refs[-6:]
    rows = tokens[0].shape[0]

    def fill(target, sources):
        for index, source in enumerate(sources):
            target[index * rows : (index + 1) * rows, :] = source[...]

    @pl.when(step == 0)
    def _():
        fill(all_tokens, tokens)
        fill(all_cotangents, cotangents)

    @pl.when(step < blocks)
    def _():
        fill(all_pre, own_pre)

    @pl.when(step >= blocks)
    def _():
        fill(all_pre, other_pre)

    new_in = dot(all_tokens[...], all_pre[...], 0, 0)
    if before:
        new_in += earlier[0][...].astype(F32)
    in_grad[...] = new_in.astype(in_grad.dtype)

    @pl.when(step < pieces)
    def _():
        @pl.when(where[2] == 1)
        def _():
            fill(all_act, own_act)

        @pl.when(where[2] == 0)
        def _():
            fill(all_act, other_act)

        new_out = dot(all_act[...], all_cotangents[...], 0, 0)
        if before:
            new_out += earlier[1][...].astype(F32)
        out_grad[...] = new_out.astype(out_grad.dtype)


def weight_terms(where, tokens, cotangents, pre, act, before, kind):
    chunks = len(tokens)
    rows, part = tokens[0].shape
    features = cotangents[0].shape[1]
    half = pre[0][0].shape[1]
    share = act[0][0].shape[1]
    blocks = 2
    width = half // blocks
    pieces = 2 * blocks if share % (256 * blocks) == 0 else 1
    piece = share // pieces

    def column(step, where):
        core = jnp.where(step < blocks, where[0], 1 - where[0])
        return core * blocks + step % blocks

    in_block = pl.BlockSpec((part, width), lambda step, where: (0, column(step, where)))
    out_block = pl.BlockSpec(
        (piece, features), lambda step, where: (jnp.minimum(step, pieces - 1), 0)
    )
    act_block = pl.BlockSpec((rows, piece), lambda step, where: (0, jnp.minimum(step, pieces - 1)))
    own_block = pl.BlockSpec((rows, width), lambda step, where: (0, jnp.minimum(step, blocks - 1)))
    other_block = pl.BlockSpec(
        (rows, width), lambda step, where: (0, jnp.maximum(step - blocks, 0))
    )
    return call(
        functools.partial(weight_kernel, chunks, blocks, pieces, bool(before)),
        (2 * blocks,),
        [pl.BlockSpec((rows, part), lambda step, where: (0, 0))] * chunks
        + [pl.BlockSpec((rows, features), lambda step, where: (0, 0))] * chunks
        + [own_block] * chunks
        + [other_block] * chunks
        + [act_block] * (2 * chunks)
        + ([in_block, out_block] if before else []),
        [in_block, out_block],
        [
            jax.ShapeDtypeStruct((part, 2 * half), kind),
            jax.ShapeDtypeStruct((share, features), kind),
        ],
        [
            pltpu.VMEM((chunks * rows, part), BF16),
            pltpu.VMEM((chunks * rows, features), BF16),
            pltpu.VMEM((chunks * rows, width), BF16),
            pltpu.VMEM((chunks * rows, piece), BF16),
        ],
        2 * chunks * rows * (2 * part * half + share * features),
        2 * chunks * rows * (part + features + 2 * half + share) + 8 * part * half + 4 * share * features,
    )(
        where,
        *tokens,
        *cotangents,
        *[pair[0] for pair in pre],
        *[pair[1] for pair in pre],
        *[pair[0] for pair in act],
        *[pair[1] for pair in act],
        *before,
    )


def shards(n_row, n_col, n_depth, tokens, weight_in, weight_out, output_grad):
    core = lax.axis_index("row") % 2
    depth = lax.axis_index("depth")
    half = weight_in.shape[1] // 2
    share = weight_in.shape[1] // n_depth
    part = tokens.shape[1] // n_depth
    halves = max(n_depth // 2, 1)
    where = jnp.stack([core, depth, (core == depth // halves).astype(jnp.int32)]).astype(jnp.int32)

    def swap_cores(value):
        return lax.ppermute(value, "row", [(r, r ^ 1) for r in range(n_row)])

    def to_chip(value, k):
        return lax.ppermute(value, "row", [(r, (r + 2 * k) % n_row) for r in range(n_row)])

    def to_depth(value, k):
        return lax.ppermute(value, "depth", [(d, (d + k) % n_depth) for d in range(n_depth)])

    def to_next(value):
        return lax.ppermute(value, "col", [(c, (c + 1) % n_col) for c in range(n_col)])

    def hidden_share(value, owner):
        if share == half:
            return value
        return lax.dynamic_slice_in_dim(value, (owner % halves) * share, share, 1)

    def feature_part(value, owner):
        return lax.dynamic_slice_in_dim(value, owner * part, part, 1)

    ring = [(tokens, output_grad)]
    for _ in range(n_col - 1):
        ring.append(tuple(to_next(value) for value in ring[-1]))

    own_tokens, own_cotangents, own_pre, own_act = [], [], [], []
    far = {k: ([], [], [], []) for k in range(1, n_depth)}
    kept, arrived = None, ()
    for stage, (panel, cotangent) in enumerate(ring):
        other_hidden, other_grad, mine_hidden, mine_grad = hidden_partials(
            where, panel, cotangent, weight_in, weight_out
        )
        chip_hidden = (mine_hidden.astype(F32) + swap_cores(other_hidden).astype(F32)).astype(BF16)
        chip_grad = (mine_grad.astype(F32) + swap_cores(other_grad).astype(F32)).astype(BF16)
        hidden, grad = chip_hidden.astype(F32), chip_grad.astype(F32)
        for k in range(1, n_row // 2):
            hidden += to_chip(chip_hidden, k).astype(F32)
            grad += to_chip(chip_grad, k).astype(F32)
        value, slope = gelu_parts(hidden)
        act, pre = value.astype(BF16), (grad * slope).astype(BF16)
        other_act, other_pre = swap_cores(act), swap_cores(pre)

        own_tokens.append(feature_part(panel, depth))
        own_cotangents.append(cotangent)
        own_pre.append((pre, other_pre))
        own_act.append((hidden_share(act, depth), hidden_share(other_act, depth)))

        for k in range(1, n_depth):
            target = (depth + k) % n_depth
            far_tokens, far_cotangents, far_pre, far_act = far[k]
            far_tokens.append(to_depth(feature_part(panel, target), k))
            far_cotangents.append(to_depth(cotangent, k))
            came = to_depth(pre, k)
            far_pre.append((came, swap_cores(came)))
            pairs = [
                (r * n_depth + d, r * n_depth + (d + k) % n_depth)
                for r in range(n_row)
                for d in range(n_depth)
                if r % 2 == (d + k) % n_depth // halves
            ]
            came = lax.ppermute(hidden_share(act, target), ("row", "depth"), pairs)
            pairs = [
                (r * n_depth + d, (r ^ 1) * n_depth + d)
                for r in range(n_row)
                for d in range(n_depth)
                if r % 2 == d // halves
            ]
            far_act.append((came, lax.ppermute(came, ("row", "depth"), pairs)))

        sums = model_partials(
            where, (act, pre), (other_act, other_pre), weight_in, weight_out, arrived
        )
        if stage == 0:
            kept = sums
        else:
            arrived = tuple(to_next(value) for value in sums)

    output, input_grad = (
        (mine.astype(F32) + came.astype(F32)).astype(BF16) for mine, came in zip(kept, arrived)
    )
    last = n_depth - 1
    terms = weight_terms(
        where, own_tokens, own_cotangents, own_pre, own_act, (), BF16 if last else F32
    )
    for k in range(1, n_depth):
        terms = weight_terms(where, *far[k], terms, F32 if k == last else BF16)
    return (output, input_grad, *terms)


def solution(mesh):
    placed = (
        P(("col", "depth"), "row"),
        P("row", "col"),
        P("col", "row"),
        P(("col", "depth"), "row"),
    )
    sizes = (mesh.shape["row"], mesh.shape["col"], mesh.shape["depth"])
    return jax.shard_map(
        functools.partial(shards, *sizes),
        mesh=mesh,
        in_specs=placed,
        out_specs=(
            P(("col", "depth"), "row"),
            P(("col", "depth"), "row"),
            P(("row", "depth"), "col"),
            P(("col", "depth"), "row"),
        ),
        check_vma=False,
    )
```

time: 341 us -> 173 us (0.51)
  waiting for transfers between devices: 238 us -> 66.5 us
  starting transfers between devices: 0.39 us -> 45.2 us
  Pallas kernels: 0 us -> 43.8 us
  blocking collectives: 35 us -> 0 us
  matrix products: 29.9 us -> 0 us
  between operations: 13.8 us -> 1.21 us
  local copies, waits for them, and re-layouts: 15.8 us -> 11.3 us
  other arithmetic: 8.08 us -> 3.59 us
    reduce_scatter x3 -> x0, waiting for transfers between devices: 100 us -> none  [the longest x1 56.9 us: shards(): lax.psum_scatter(term_out.astype(jnp.bfloat16), 'depth', scatter_dimensio...]
    psum x1 -> x0, waiting for transfers between devices: 95.5 us -> none  [hidden_total(): return lax.psum(term.astype(jnp.bfloat16), 'row').astype(jnp.float32)]
    ppermute x0 -> x60, waiting for transfers between devices: none -> 66.5 us  [the longest x12 35.4 us: to_next(): lax.ppermute(value, 'col', [(c, (c + 1) % n_col) for c in range(n_col)])]
    ppermute x0 -> x60, starting transfers between devices: none -> 45.2 us  [the longest x12 11.9 us: to_depth(): lax.ppermute(value, 'depth', [(d, (d + k) % n_depth) for d in range(n_dep...]
    pallas_call x0 -> x10, Pallas kernels: none -> 43.8 us  [the longest x4 15.6 us: hidden_partials(): call(functools.partial(hidden_kernel, blocks), (2 * blocks,), [whole, who...]
    unnamed x6 -> x0, waiting for transfers between devices: 42.1 us -> none
    all_gather x2 -> x0, blocking collectives: 35 us -> none  [the longest x1 18.4 us: shards(): lax.all_gather(tokens, 'col', axis=0, tiled=True)]
    dot_general x6 -> x0, matrix products: 29.9 us -> none  [the longest x2 11.9 us: product_rows(): lax.dot_general(panel, weight, (((1,), (contract,)), ((), ())), preferred...]
  transfers between devices with their start and end apart: 5 -> 60, of which waited for: 5 -> 21; matrix products, arithmetic and copies ran while one was open for 8% -> 2% of each run, Pallas kernels for 0% -> 21%
where the time goes in v1:
time: 173 us; the launch traced here: 172 us
  waiting for transfers between devices  66.5 us (38%)
  starting transfers between devices  45.2 us (26%)
  Pallas kernels  43.8 us (25%)
  local copies, waits for them, and re-layouts  11.3 us (7%)
  other arithmetic  3.59 us (2%)
    ppermute x12, waiting for transfers between devices, to_next(): lax.ppermute(value, 'col', [(c, (c + 1) % n_col) for c in range(n_col)])  35.4 us
    ppermute x8, waiting for transfers between devices, to_chip(): lax.ppermute(value, 'row', [(r, (r + 2 * k) % n_row) for r in range(n_row)])  21 us
    pallas_call x4, Pallas kernels, hidden_partials(): call(functools.partial(hidden_kernel, blocks), (2 * blocks,), [whole, who...  15.6 us
    pallas_call x4, Pallas kernels, model_partials(): call(functools.partial(model_kernel, bool(arrived)), (blocks,), [block] *...  14.4 us
    pallas_call x2, Pallas kernels, weight_terms(): call(functools.partial(weight_kernel, chunks, blocks, pieces, bool(before...  13.7 us
    ppermute x12, starting transfers between devices, to_depth(): lax.ppermute(value, 'depth', [(d, (d + k) % n_depth) for d in range(n_dep...  11.9 us
    unnamed x20, local copies, waits for them, and re-layouts  11.2 us
    ppermute x4, starting transfers between devices, shards(): far_act.append((came, lax.ppermute(came, ('row', 'depth'), pairs)))  8.03 us
  transfers between devices with their start and end apart: 60, of which 21 were waited for; matrix products, arithmetic and copies ran while one was open for 2% of the time, Pallas kernels for 21%

profile of v1, /device:TPU:0, one launch (start us, length us, event | category | flops | bytes accessed | tf_op | source)
XLA Modules:
  0.0 171.5 jit_solution(11324456138348653167)
XLA Ops:
  0.6 3.1 %collective-permute-start.9 = (bf16[96,768]{1,0:T(8,128)(2,1)}, bf16[96,768]{1,0:T(8,128)(2,1)S(1)}, u32[]{:S(2)}, u32[]{:S(2)}) collective-permute-start(bf16[96,768]{1,0:T(8,128)(2,1)} %refs_4_.9), channel_id=1, source_target_pairs={{0,2},{2,4},{4,6},{6,0},{1,3},{3,5},{5,7},{7,1},{8,10},{10,12},{12... | collective-permute-start | bytes 442376 | tf_op jit(solution)/shard_map/ppermute | solution.py:272
  3.7 1.5 collective-permute-start.40
  5.2 1.6 collective-permute-start.6
  6.9 2.3 %copy-done = bf16[768,3072]{1,0:T(8,128)(2,1)S(1)} copy-done((bf16[768,3072]{1,0:T(8,128)(2,1)S(1)}, bf16[768,3072]{1,0:T(8,128)(2,1)}, u32[]{:S(2)}) %copy-start) | copy-done | bytes 4718616
  9.2 2.3 %copy-done.2 = bf16[3072,768]{1,0:T(8,128)(2,1)S(1)} copy-done((bf16[3072,768]{1,0:T(8,128)(2,1)S(1)}, bf16[3072,768]{1,0:T(8,128)(2,1)}, u32[]{:S(2)}) %copy-start.2) | copy-done | bytes 4718616
  13.4 3.9 %shard_map.75 = (bf16[96,1536]{1,0:T(8,128)(2,1)S(1)}, bf16[96,1536]{1,0:T(8,128)(2,1)S(1)}, bf16[96,1536]{1,0:T(8,128)(2,1)S(1)}, bf16[96,1536]{1,0:T(8,128)(2,1)S(1)}) custom-call(s32[3]{0:T(128)S(1)} %pad_add_fusion.where, bf16[96,768]{1,0:T(8,128)(2,1)S(1)} %copy-done.4, bf16[96,768]{1,0:T(8,128)(2,1)S(1)} %copy-done.6, bf16[768,3072]{1,0:T(8,128)(2,1)S(1)} %copy-done, ...), custom_call_target="tpu_custom_call" | custom-call | flops 905969664 | bytes 11206656 | tf_op jit(solution)/shard_map/pallas_call | solution.py:74
  17.9 2.3 %copy-done.1 = bf16[768,3072]{1,0:T(8,128)(2,1)S(1)} copy-done((bf16[768,3072]{1,0:T(8,128)(2,1)S(1)}, bf16[768,3072]{1,0:T(8,128)(2,1)}, u32[]{:S(2)}) %copy-start.1) | copy-done | bytes 4718616
  20.2 2.3 %copy-done.3 = bf16[3072,768]{1,0:T(8,128)(2,1)S(1)} copy-done((bf16[3072,768]{1,0:T(8,128)(2,1)S(1)}, bf16[3072,768]{1,0:T(8,128)(2,1)}, u32[]{:S(2)}) %copy-start.3) | copy-done | bytes 4718616
  22.6 3.9 %shard_map.79 = (bf16[96,1536]{1,0:T(8,128)(2,1)S(1)}, bf16[96,1536]{1,0:T(8,128)(2,1)S(1)}, bf16[96,1536]{1,0:T(8,128)(2,1)S(1)}, bf16[96,1536]{1,0:T(8,128)(2,1)S(1)}) custom-call(s32[3]{0:T(128)S(1)} %pad_add_fusion.where, bf16[96,768]{1,0:T(8,128)(2,1)S(1)} %collective-permute-done.6.tokens, ...), custom_call_target="tpu_custom_call" | custom-call | flops 905969664 | bytes 11206656 | tf_op jit(solution)/shard_map/pallas_call | solution.py:74
  27.1 1.6 collective-permute-start.7
  29.2 6.5 %collective-permute-done.7.tokens = bf16[96,768]{1,0:T(8,128)(2,1)S(1)} collective-permute-done((bf16[96,768]{1,0:T(8,128)(2,1)S(1)}, bf16[96,768]{1,0:T(8,128)(2,1)S(1)}, u32[]{:S(2)}, u32[]{:S(2)}) %collective-permute-start.7) | collective-permute-done | bytes 147488 | tf_op jit(solution)/shard_map/ppermute | solution.py:272
  35.7 1.5 collective-permute-start.3
  37.9 1.5 collective-permute-start.1
  39.4 3.9 %shard_map.78 = (bf16[96,1536]{1,0:T(8,128)(2,1)S(1)}, bf16[96,1536]{1,0:T(8,128)(2,1)S(1)}, bf16[96,1536]{1,0:T(8,128)(2,1)S(1)}, bf16[96,1536]{1,0:T(8,128)(2,1)S(1)}) custom-call(s32[3]{0:T(128)S(1)} %pad_add_fusion.where, bf16[96,768]{1,0:T(8,128)(2,1)S(1)} %collective-permute-done.7.tokens, ...), custom_call_target="tpu_custom_call" | custom-call | flops 905969664 | bytes 11206656 | tf_op jit(solution)/shard_map/pallas_call | solution.py:74
  43.7 7.8 %collective-permute-done.8.tokens = bf16[96,768]{1,0:T(8,128)(2,1)S(1)} collective-permute-done((bf16[96,768]{1,0:T(8,128)(2,1)S(1)}, bf16[96,768]{1,0:T(8,128)(2,1)S(1)}, u32[]{:S(2)}, u32[]{:S(2)}) %collective-permute-start.8) | collective-permute-done | bytes 147488 | tf_op jit(solution)/shard_map/ppermute | solution.py:272
  53.6 3.9 %shard_map.77 = (bf16[96,1536]{1,0:T(8,128)(2,1)S(1)}, bf16[96,1536]{1,0:T(8,128)(2,1)S(1)}, bf16[96,1536]{1,0:T(8,128)(2,1)S(1)}, bf16[96,1536]{1,0:T(8,128)(2,1)S(1)}) custom-call(s32[3]{0:T(128)S(1)} %pad_add_fusion.where, bf16[96,768]{1,0:T(8,128)(2,1)S(1)} %collective-permute-done.8.tokens, ...), custom_call_target="tpu_custom_call" | custom-call | flops 905969664 | bytes 11206656 | tf_op jit(solution)/shard_map/pallas_call | solution.py:74
  59.9 1.6 collective-permute-start.25
  61.5 7.6 %collective-permute-done.27 = bf16[96,1536]{1,0:T(8,128)(2,1)S(1)} collective-permute-done((bf16[96,1536]{1,0:T(8,128)(2,1)S(1)}, bf16[96,1536]{1,0:T(8,128)(2,1)S(1)}, u32[]{:S(2)}, u32[]{:S(2)}) %collective-permute-start.27) | collective-permute-done | bytes 294944 | tf_op jit(solution)/shard_map/ppermute | solution.py:266
  69.1 1.5 collective-permute-start.41
  70.6 4.0 %collective-permute-done.25 = bf16[96,1536]{1,0:T(8,128)(2,1)S(1)} collective-permute-done((bf16[96,1536]{1,0:T(8,128)(2,1)S(1)}, bf16[96,1536]{1,0:T(8,128)(2,1)S(1)}, u32[]{:S(2)}, u32[]{:S(2)}) %collective-permute-start.25) | collective-permute-done | bytes 294944 | tf_op jit(solution)/shard_map/ppermute | solution.py:266
  75.0 1.6 collective-permute-start.38
  77.2 1.6 collective-permute-start.39
  80.7 2.6 %collective-permute-done.42.refs_6_ = bf16[96,768]{1,0:T(8,128)(2,1)S(1)} collective-permute-done((bf16[96,768]{1,0:T(8,128)(2,1)S(1)}, bf16[96,768]{1,0:T(8,128)(2,1)S(1)}, u32[]{:S(2)}, u32[]{:S(2)}) %collective-permute-start.42) | collective-permute-done | bytes 147488 | tf_op jit(solution)/shard_map/ppermute | solution.py:269
  84.9 2.8 %collective-permute-done.43.refs_7_ = bf16[96,768]{1,0:T(8,128)(2,1)S(1)} collective-permute-done((bf16[96,768]{1,0:T(8,128)(2,1)S(1)}, bf16[96,768]{1,0:T(8,128)(2,1)S(1)}, u32[]{:S(2)}, u32[]{:S(2)}) %collective-permute-start.43) | collective-permute-done | bytes 147488 | tf_op jit(solution)/shard_map/ppermute | solution.py:269
  87.7 1.5 collective-permute-start.44
  90.1 1.3 collective-permute-start.52
  91.4 3.4 %collective-permute-done.19 = bf16[96,1536]{1,0:T(8,128)(2,1)S(1)} collective-permute-done((bf16[96,1536]{1,0:T(8,128)(2,1)S(1)}, bf16[96,1536]{1,0:T(8,128)(2,1)S(1)}, u32[]{:S(2)}, u32[]{:S(2)}) %collective-permute-start.19) | collective-permute-done | bytes 294944 | tf_op jit(solution)/shard_map/ppermute | solution.py:266
  97.7 1.8 %collective-permute-done.52.refs_16_ = bf16[96,1536]{1,0:T(8,128)(2,1)S(1)} collective-permute-done((bf16[96,1536]{1,0:T(8,128)(2,1)S(1)}, bf16[96,1536]{1,0:T(8,128)(2,1)S(1)}, u32[]{:S(2)}, u32[]{:S(2)}) %collective-permute-start.52) | collective-permute-done | bytes 294944 | tf_op jit(solution)/shard_map/ppermute | solution.py:321
  100.9 3.6 %shard_map.80 = (bf16[96,768]{1,0:T(8,128)(2,1)S(1)}, bf16[96,768]{1,0:T(8,128)(2,1)S(1)}) custom-call(s32[3]{0:T(128)S(1)} %pad_add_fusion.where, bf16[96,1536]{1,0:T(8,128)(2,1)S(1)} %get-tuple-element.63.refs_0_.refs_17_, bf16[96,1536]{1,0:T(8,128)(2,1)S(1)} %get-tuple-element.62.refs_1_.refs_9_, ...), custom_call_target="tpu_custom_call" | custom-call | flops 905969664 | bytes 10616832 | tf_op jit(solution)/shard_map/pallas_call | solution.py:133
  105.6 1.3 collective-permute-start.53
  106.9 4.1 %collective-permute-done.13 = bf16[96,1536]{1,0:T(8,128)(2,1)S(1)} collective-permute-done((bf16[96,1536]{1,0:T(8,128)(2,1)S(1)}, bf16[96,1536]{1,0:T(8,128)(2,1)S(1)}, u32[]{:S(2)}, u32[]{:S(2)}) %collective-permute-start.13) | collective-permute-done | bytes 294944 | tf_op jit(solution)/shard_map/ppermute | solution.py:266
  110.9 1.5 collective-permute-start.46
  113.0 8.0 %collective-permute-done.30.refs_8_ = bf16[96,768]{1,0:T(8,128)(2,1)S(1)} collective-permute-done((bf16[96,768]{1,0:T(8,128)(2,1)S(1)}, bf16[96,768]{1,0:T(8,128)(2,1)S(1)}, u32[]{:S(2)}, u32[]{:S(2)}) %collective-permute-start.30) | collective-permute-done | bytes 147488 | tf_op jit(solution)/shard_map/ppermute | solution.py:272
  121.0 2.7 %collective-permute-done.31.refs_9_ = bf16[96,768]{1,0:T(8,128)(2,1)S(1)} collective-permute-done((bf16[96,768]{1,0:T(8,128)(2,1)S(1)}, bf16[96,768]{1,0:T(8,128)(2,1)S(1)}, u32[]{:S(2)}, u32[]{:S(2)}) %collective-permute-start.31) | collective-permute-done | bytes 147488 | tf_op jit(solution)/shard_map/ppermute | solution.py:272
  123.7 3.6 %shard_map.81 = (bf16[96,768]{1,0:T(8,128)(2,1)S(1)}, bf16[96,768]{1,0:T(8,128)(2,1)S(1)}) custom-call(s32[3]{0:T(128)S(1)} %pad_add_fusion.where, bf16[96,1536]{1,0:T(8,128)(2,1)S(1)} %get-tuple-element.65.refs_0_.refs_18_, bf16[96,1536]{1,0:T(8,128)(2,1)S(1)} %get-tuple-element.64.refs_1_.refs_10_, ...), custom_call_target="tpu_custom_call" | custom-call | flops 905969664 | bytes 10616832 | tf_op jit(solution)/shard_map/pallas_call | solution.py:133
  127.5 1.3 collective-permute-start.54
  128.8 7.0 %collective-permute-done.32.refs_8_ = bf16[96,768]{1,0:T(8,128)(2,1)S(1)} collective-permute-done((bf16[96,768]{1,0:T(8,128)(2,1)S(1)}, bf16[96,768]{1,0:T(8,128)(2,1)S(1)}, u32[]{:S(2)}, u32[]{:S(2)}) %collective-permute-start.32) | collective-permute-done | bytes 147488 | tf_op jit(solution)/shard_map/ppermute | solution.py:272
  135.8 1.3 collective-permute-start.56
  137.1 1.5 collective-permute-done.33.refs_9_
  139.1 1.5 collective-permute-start.55
  140.6 1.4 collective-permute-start.49
  142.0 3.6 %shard_map.76 = (bf16[96,768]{1,0:T(8,128)(2,1)S(1)}, bf16[96,768]{1,0:T(8,128)(2,1)S(1)}) custom-call(s32[3]{0:T(128)S(1)} %pad_add_fusion.where, bf16[96,1536]{1,0:T(8,128)(2,1)S(1)} %get-tuple-element.61.refs_0_.refs_16_, bf16[96,1536]{1,0:T(8,128)(2,1)S(1)} %get-tuple-element.60.refs_1_.refs_8_, ...), custom_call_target="tpu_custom_call" | custom-call | flops 905969664 | bytes 10616832 | tf_op jit(solution)/shard_map/pallas_call | solution.py:133
  145.6 3.6 %shard_map.82 = (bf16[96,768]{1,0:T(8,128)(2,1)S(1)}, bf16[96,768]{1,0:T(8,128)(2,1)S(1)}) custom-call(s32[3]{0:T(128)S(1)} %pad_add_fusion.where, bf16[96,1536]{1,0:T(8,128)(2,1)S(1)} %get-tuple-element.67.refs_0_.refs_19_, bf16[96,1536]{1,0:T(8,128)(2,1)S(1)} %get-tuple-element.66.refs_1_.refs_11_, ...), custom_call_target="tpu_custom_call" | custom-call | flops 905969664 | bytes 10616832 | tf_op jit(solution)/shard_map/pallas_call | solution.py:133
  149.4 6.1 %shard_map.83 = (bf16[384,3072]{1,0:T(8,128)(2,1)S(1)}, bf16[1536,768]{1,0:T(8,128)(2,1)S(1)}) custom-call(s32[3]{0:T(128)S(1)} %pad_add_fusion.where, bf16[96,384]{1,0:T(8,128)(2,1)S(1)} %get-tuple-element.74.refs_0_, bf16[96,384]{1,0:T(8,128)(2,1)S(1)} %get-tuple-element.72.refs_1_, bf16[96,384]{1,0:T(8,128)(2,1)S(1)} %get-tuple-element.70.refs_2_, ...), custom_call_target="tpu_custom_call" | custom-call | flops 1811939328 | bytes 13860864 | tf_op jit(solution)/shard_map/pallas_call | solution.py:219
  155.6 1.9 %collective-permute-start.57 = (bf16[96,1536]{1,0:T(8,128)(2,1)S(1)}, bf16[96,1536]{1,0:T(8,128)(2,1)S(1)}, u32[]{:S(2)}, u32[]{:S(2)}) collective-permute-start(bf16[96,1536]{1,0:T(8,128)(2,1)S(1)} %collective-permute-done.53.refs_17_), channel_id=1, source_target_pairs={{0,8},{9,1},{16,24},{25,17},{2,10},{11,3},{18,26},{27,19},{4,12},{... | collective-permute-start | bytes 884744 | tf_op jit(solution)/shard_map/ppermute | solution.py:328
  157.6 2.4 %collective-permute-start.58 = (bf16[96,1536]{1,0:T(8,128)(2,1)S(1)}, bf16[96,1536]{1,0:T(8,128)(2,1)S(1)}, u32[]{:S(2)}, u32[]{:S(2)}) collective-permute-start(bf16[96,1536]{1,0:T(8,128)(2,1)S(1)} %collective-permute-done.54.refs_18_), channel_id=1, source_target_pairs={{0,8},{9,1},{16,24},{25,17},{2,10},{11,3},{18,26},{27,19},{4,12},{... | collective-permute-start | bytes 884744 | tf_op jit(solution)/shard_map/ppermute | solution.py:328
  160.1 2.4 %collective-permute-start.59 = (bf16[96,1536]{1,0:T(8,128)(2,1)S(1)}, bf16[96,1536]{1,0:T(8,128)(2,1)S(1)}, u32[]{:S(2)}, u32[]{:S(2)}) collective-permute-start(bf16[96,1536]{1,0:T(8,128)(2,1)S(1)} %collective-permute-done.55.refs_19_), channel_id=1, source_target_pairs={{0,8},{9,1},{16,24},{25,17},{2,10},{11,3},{18,26},{27,19},{4,12},{... | collective-permute-start | bytes 884744 | tf_op jit(solution)/shard_map/ppermute | solution.py:328
  164.0 7.6 %shard_map.84 = (f32[384,3072]{1,0:T(8,128)}, f32[1536,768]{1,0:T(8,128)}) custom-call(s32[3]{0:T(128)S(1)} %pad_add_fusion.where, bf16[96,384]{1,0:T(8,128)(2,1)S(1)} %collective-permute-done.36.refs_0_, bf16[96,384]{1,0:T(8,128)(2,1)S(1)} %collective-permute-done.37.refs_1_, bf16[96,384]{1,0:T(8,128)(2,1)S(1)} %collective-permute-done.38.refs_2_, ...), custom_call_target="tpu_custom_call" | custom-call | flops 1811939328 | bytes 13860864 | tf_op jit(solution)/shard_map/pallas_call | solution.py:219
  (122 shorter events, 22.8 us)
Async XLA Ops:
  0.6 17.3 %collective-permute-start.9 = (bf16[96,768]{1,0:T(8,128)(2,1)}, bf16[96,768]{1,0:T(8,128)(2,1)S(1)}, u32[]{:S(2)}, u32[]{:S(2)}) collective-permute-start(bf16[96,768]{1,0:T(8,128)(2,1)} %refs_4_.9), channel_id=1, source_target_pairs={{0,2},{2,4},{4,6},{6,0},{1,3},{3,5},{5,7},{7,1},{8,10},{10,12},{12... | collective-permute-start | bytes 442376 | tf_op jit(solution)/shard_map/ppermute | solution.py:272
  3.7 72.9 %collective-permute-start.40 = (bf16[96,768]{1,0:T(8,128)(2,1)}, bf16[96,768]{1,0:T(8,128)(2,1)S(1)}, u32[]{:S(2)}, u32[]{:S(2)}) collective-permute-start(bf16[96,768]{1,0:T(8,128)(2,1)} %refs_4_.9), channel_id=1, source_target_pairs={{0,1},{1,0},{2,3},{3,2},{4,5},{5,4},{6,7},{7,6},{8,9},{9,8},{10,11... | collective-permute-start | bytes 442376 | tf_op jit(solution)/shard_map/ppermute | solution.py:269
  5.2 12.7 %collective-permute-start.6 = (bf16[96,768]{1,0:T(8,128)(2,1)}, bf16[96,768]{1,0:T(8,128)(2,1)S(1)}, u32[]{:S(2)}, u32[]{:S(2)}) collective-permute-start(bf16[96,768]{1,0:T(8,128)(2,1)} %tokens.1), channel_id=1, source_target_pairs={{0,2},{2,4},{4,6},{6,0},{1,3},{3,5},{5,7},{7,1},{8,10},{10,12},{12... | collective-permute-start | bytes 442376 | tf_op jit(solution)/shard_map/ppermute | solution.py:272
  17.3 9.8 %collective-permute-start.2 = (bf16[96,1536]{1,0:T(8,128)(2,1)S(1)}, bf16[96,1536]{1,0:T(8,128)(2,1)S(1)}, u32[]{:S(2)}, u32[]{:S(2)}) collective-permute-start(bf16[96,1536]{1,0:T(8,128)(2,1)S(1)} %get-tuple-element.35), channel_id=1, source_target_pairs={{0,8},{8,0},{16,24},{24,16},{1,9},{9,1},{17,25},{25,17},{2,10},{10... | collective-permute-start | bytes 884744 | tf_op jit(solution)/shard_map/ppermute | solution.py:263
  17.4 11.4 %collective-permute-start = (bf16[96,1536]{1,0:T(8,128)(2,1)S(1)}, bf16[96,1536]{1,0:T(8,128)(2,1)S(1)}, u32[]{:S(2)}, u32[]{:S(2)}) collective-permute-start(bf16[96,1536]{1,0:T(8,128)(2,1)S(1)} %get-tuple-element.33), channel_id=1, source_target_pairs={{0,8},{8,0},{16,24},{24,16},{1,9},{9,1},{17,25},{25,17},{2,10},{10... | collective-permute-start | bytes 884744 | tf_op jit(solution)/shard_map/ppermute | solution.py:263
  26.5 16.9 %collective-permute-start.26 = (bf16[96,1536]{1,0:T(8,128)(2,1)S(1)}, bf16[96,1536]{1,0:T(8,128)(2,1)S(1)}, u32[]{:S(2)}, u32[]{:S(2)}) collective-permute-start(bf16[96,1536]{1,0:T(8,128)(2,1)S(1)} %get-tuple-element.48), channel_id=1, source_target_pairs={{0,8},{8,0},{16,24},{24,16},{1,9},{9,1},{17,25},{25,17},{2,10},{10... | collective-permute-start | bytes 884744 | tf_op jit(solution)/shard_map/ppermute | solution.py:263
  26.6 16.9 %collective-permute-start.24 = (bf16[96,1536]{1,0:T(8,128)(2,1)S(1)}, bf16[96,1536]{1,0:T(8,128)(2,1)S(1)}, u32[]{:S(2)}, u32[]{:S(2)}) collective-permute-start(bf16[96,1536]{1,0:T(8,128)(2,1)S(1)} %get-tuple-element.46), channel_id=1, source_target_pairs={{0,8},{8,0},{16,24},{24,16},{1,9},{9,1},{17,25},{25,17},{2,10},{10... | collective-permute-start | bytes 884744 | tf_op jit(solution)/shard_map/ppermute | solution.py:263
  27.1 8.6 %collective-permute-start.7 = (bf16[96,768]{1,0:T(8,128)(2,1)S(1)}, bf16[96,768]{1,0:T(8,128)(2,1)S(1)}, u32[]{:S(2)}, u32[]{:S(2)}) collective-permute-start(bf16[96,768]{1,0:T(8,128)(2,1)S(1)} %collective-permute-done.6.tokens), channel_id=1, source_target_pairs={{0,2},{2,4},{4,6},{6,0},{1,3},{3,5},{5,7},{7,1},{8,10},{10,12},{12... | collective-permute-start | bytes 442376 | tf_op jit(solution)/shard_map/ppermute | solution.py:272
  28.8 9.1 %collective-permute-start.10 = (bf16[96,768]{1,0:T(8,128)(2,1)S(1)}, bf16[96,768]{1,0:T(8,128)(2,1)S(1)}, u32[]{:S(2)}, u32[]{:S(2)}) collective-permute-start(bf16[96,768]{1,0:T(8,128)(2,1)S(1)} %collective-permute-done.9.cotangent.refs_5_), channel_id=1, source_target_pairs={{0,2},{2,4},{4,6},{6,0},{1,3},{3,5},{5,7},{7,1},{8,10},{10,12},{12... | collective-permute-start | bytes 442376 | tf_op jit(solution)/shard_map/ppermute | solution.py:272
  35.7 21.9 %collective-permute-start.3 = (bf16[96,1536]{1,0:T(8,128)(2,1)S(1)}, bf16[96,1536]{1,0:T(8,128)(2,1)S(1)}, u32[]{:S(2)}, u32[]{:S(2)}) collective-permute-start(bf16[96,1536]{1,0:T(8,128)(2,1)S(1)} %add_convert_fusion.6), channel_id=1, source_target_pairs={{0,16},{8,24},{16,0},{24,8},{1,17},{9,25},{17,1},{25,9},{2,18},{10... | collective-permute-start | bytes 884744 | tf_op jit(solution)/shard_map/ppermute | solution.py:266
  37.9 19.7 %collective-permute-start.1 = (bf16[96,1536]{1,0:T(8,128)(2,1)S(1)}, bf16[96,1536]{1,0:T(8,128)(2,1)S(1)}, u32[]{:S(2)}, u32[]{:S(2)}) collective-permute-start(bf16[96,1536]{1,0:T(8,128)(2,1)S(1)} %add_convert_fusion.7), channel_id=1, source_target_pairs={{0,16},{8,24},{16,0},{24,8},{1,17},{9,25},{17,1},{25,9},{2,18},{10... | collective-permute-start | bytes 884744 | tf_op jit(solution)/shard_map/ppermute | solution.py:266
  43.4 8.1 %collective-permute-start.8 = (bf16[96,768]{1,0:T(8,128)(2,1)S(1)}, bf16[96,768]{1,0:T(8,128)(2,1)S(1)}, u32[]{:S(2)}, u32[]{:S(2)}) collective-permute-start(bf16[96,768]{1,0:T(8,128)(2,1)S(1)} %collective-permute-done.7.tokens), channel_id=1, source_target_pairs={{0,2},{2,4},{4,6},{6,0},{1,3},{3,5},{5,7},{7,1},{8,10},{10,12},{12... | collective-permute-start | bytes 442376 | tf_op jit(solution)/shard_map/ppermute | solution.py:272
  43.5 9.6 %collective-permute-start.11 = (bf16[96,768]{1,0:T(8,128)(2,1)S(1)}, bf16[96,768]{1,0:T(8,128)(2,1)S(1)}, u32[]{:S(2)}, u32[]{:S(2)}) collective-permute-start(bf16[96,768]{1,0:T(8,128)(2,1)S(1)} %collective-permute-done.10.cotangent.refs_6_), channel_id=1, source_target_pairs={{0,2},{2,4},{4,6},{6,0},{1,3},{3,5},{5,7},{7,1},{8,10},{10,12},{12... | collective-permute-start | bytes 442376 | tf_op jit(solution)/shard_map/ppermute | solution.py:272
  51.5 23.5 %collective-permute-start.36 = (bf16[96,384]{1,0:T(8,128)(2,1)S(1)}, bf16[96,384]{1,0:T(8,128)(2,1)S(1)}, u32[]{:S(2)}, u32[]{:S(2)}) collective-permute-start(bf16[96,384]{1,0:T(8,128)(2,1)S(1)} %get-tuple-element.75), channel_id=1, source_target_pairs={{0,1},{1,0},{2,3},{3,2},{4,5},{5,4},{6,7},{7,6},{8,9},{9,8},{10,11... | collective-permute-start | bytes 221192 | tf_op jit(solution)/shard_map/ppermute | solution.py:269
  53.1 24.1 %collective-permute-start.37 = (bf16[96,384]{1,0:T(8,128)(2,1)S(1)}, bf16[96,384]{1,0:T(8,128)(2,1)S(1)}, u32[]{:S(2)}, u32[]{:S(2)}) collective-permute-start(bf16[96,384]{1,0:T(8,128)(2,1)S(1)} %get-tuple-element.73), channel_id=1, source_target_pairs={{0,1},{1,0},{2,3},{3,2},{4,5},{5,4},{6,7},{7,6},{8,9},{9,8},{10,11... | collective-permute-start | bytes 221192 | tf_op jit(solution)/shard_map/ppermute | solution.py:269
  59.2 9.9 %collective-permute-start.27 = (bf16[96,1536]{1,0:T(8,128)(2,1)S(1)}, bf16[96,1536]{1,0:T(8,128)(2,1)S(1)}, u32[]{:S(2)}, u32[]{:S(2)}) collective-permute-start(bf16[96,1536]{1,0:T(8,128)(2,1)S(1)} %add_convert_fusion), channel_id=1, source_target_pairs={{0,16},{8,24},{16,0},{24,8},{1,17},{9,25},{17,1},{25,9},{2,18},{10... | collective-permute-start | bytes 884744 | tf_op jit(solution)/shard_map/ppermute | solution.py:266
  59.9 14.8 %collective-permute-start.25 = (bf16[96,1536]{1,0:T(8,128)(2,1)S(1)}, bf16[96,1536]{1,0:T(8,128)(2,1)S(1)}, u32[]{:S(2)}, u32[]{:S(2)}) collective-permute-start(bf16[96,1536]{1,0:T(8,128)(2,1)S(1)} %add_convert_fusion.1), channel_id=1, source_target_pairs={{0,16},{8,24},{16,0},{24,8},{1,17},{9,25},{17,1},{25,9},{2,18},{10... | collective-permute-start | bytes 884744 | tf_op jit(solution)/shard_map/ppermute | solution.py:266
  69.1 9.7 %collective-permute-start.41 = (bf16[96,768]{1,0:T(8,128)(2,1)S(1)}, bf16[96,768]{1,0:T(8,128)(2,1)S(1)}, u32[]{:S(2)}, u32[]{:S(2)}) collective-permute-start(bf16[96,768]{1,0:T(8,128)(2,1)S(1)} %collective-permute-done.9.cotangent.refs_5_), channel_id=1, source_target_pairs={{0,1},{1,0},{2,3},{3,2},{4,5},{5,4},{6,7},{7,6},{8,9},{9,8},{10,11... | collective-permute-start | bytes 442376 | tf_op jit(solution)/shard_map/ppermute | solution.py:269
  77.2 7.7 %collective-permute-start.39 = (bf16[96,384]{1,0:T(8,128)(2,1)S(1)}, bf16[96,384]{1,0:T(8,128)(2,1)S(1)}, u32[]{:S(2)}, u32[]{:S(2)}) collective-permute-start(bf16[96,384]{1,0:T(8,128)(2,1)S(1)} %get-tuple-element.69), channel_id=1, source_target_pairs={{0,1},{1,0},{2,3},{3,2},{4,5},{5,4},{6,7},{7,6},{8,9},{9,8},{10,11... | collective-permute-start | bytes 221192 | tf_op jit(solution)/shard_map/ppermute | solution.py:269
  78.8 8.9 %collective-permute-start.43 = (bf16[96,768]{1,0:T(8,128)(2,1)S(1)}, bf16[96,768]{1,0:T(8,128)(2,1)S(1)}, u32[]{:S(2)}, u32[]{:S(2)}) collective-permute-start(bf16[96,768]{1,0:T(8,128)(2,1)S(1)} %collective-permute-done.11.cotangent.refs_7_), channel_id=1, source_target_pairs={{0,1},{1,0},{2,3},{3,2},{4,5},{5,4},{6,7},{7,6},{8,9},{9,8},{10,11... | collective-permute-start | bytes 442376 | tf_op jit(solution)/shard_map/ppermute | solution.py:269
  80.1 9.9 %collective-permute-start.21 = (bf16[96,1536]{1,0:T(8,128)(2,1)S(1)}, bf16[96,1536]{1,0:T(8,128)(2,1)S(1)}, u32[]{:S(2)}, u32[]{:S(2)}) collective-permute-start(bf16[96,1536]{1,0:T(8,128)(2,1)S(1)} %add_convert_fusion.2), channel_id=1, source_target_pairs={{0,16},{8,24},{16,0},{24,8},{1,17},{9,25},{17,1},{25,9},{2,18},{10... | collective-permute-start | bytes 884744 | tf_op jit(solution)/shard_map/ppermute | solution.py:266
  83.3 11.4 %collective-permute-start.19 = (bf16[96,1536]{1,0:T(8,128)(2,1)S(1)}, bf16[96,1536]{1,0:T(8,128)(2,1)S(1)}, u32[]{:S(2)}, u32[]{:S(2)}) collective-permute-start(bf16[96,1536]{1,0:T(8,128)(2,1)S(1)} %add_convert_fusion.3), channel_id=1, source_target_pairs={{0,16},{8,24},{16,0},{24,8},{1,17},{9,25},{17,1},{25,9},{2,18},{10... | collective-permute-start | bytes 884744 | tf_op jit(solution)/shard_map/ppermute | solution.py:266
  83.8 10.9 %collective-permute-start.4 = (bf16[96,1536]{1,0:T(8,128)(2,1)S(1)}, bf16[96,1536]{1,0:T(8,128)(2,1)S(1)}, u32[]{:S(2)}, u32[]{:S(2)}) collective-permute-start(bf16[96,1536]{1,0:T(8,128)(2,1)S(1)} %get-tuple-element.61.refs_0_.refs_16_), channel_id=1, source_target_pairs={{0,8},{8,0},{16,24},{24,16},{1,9},{9,1},{17,25},{25,17},{2,10},{10... | collective-permute-start | bytes 884744 | tf_op jit(solution)/shard_map/ppermute | solution.py:263
  84.9 10.8 %collective-permute-start.5 = (bf16[96,1536]{1,0:T(8,128)(2,1)S(1)}, bf16[96,1536]{1,0:T(8,128)(2,1)S(1)}, u32[]{:S(2)}, u32[]{:S(2)}) collective-permute-start(bf16[96,1536]{1,0:T(8,128)(2,1)S(1)} %get-tuple-element.60.refs_1_.refs_8_), channel_id=1, source_target_pairs={{0,8},{8,0},{16,24},{24,16},{1,9},{9,1},{17,25},{25,17},{2,10},{10... | collective-permute-start | bytes 884744 | tf_op jit(solution)/shard_map/ppermute | solution.py:263
  87.7 8.9 %collective-permute-start.44 = (bf16[96,1536]{1,0:T(8,128)(2,1)S(1)}, bf16[96,1536]{1,0:T(8,128)(2,1)S(1)}, u32[]{:S(2)}, u32[]{:S(2)}) collective-permute-start(bf16[96,1536]{1,0:T(8,128)(2,1)S(1)} %get-tuple-element.60.refs_1_.refs_8_), channel_id=1, source_target_pairs={{0,1},{1,0},{2,3},{3,2},{4,5},{5,4},{6,7},{7,6},{8,9},{9,8},{10,11... | collective-permute-start | bytes 884744 | tf_op jit(solution)/shard_map/ppermute | solution.py:269
  90.1 9.4 %collective-permute-start.52 = (bf16[96,1536]{1,0:T(8,128)(2,1)S(1)}, bf16[96,1536]{1,0:T(8,128)(2,1)S(1)}, u32[]{:S(2)}, u32[]{:S(2)}) collective-permute-start(bf16[96,1536]{1,0:T(8,128)(2,1)S(1)} %get-tuple-element.61.refs_0_.refs_16_), channel_id=1, source_target_pairs={{1,0},{8,9},{17,16},{24,25},{3,2},{10,11},{19,18},{26,27},{5,4},{1... | collective-permute-start | bytes 884744 | tf_op jit(solution)/shard_map/ppermute | solution.py:321
  95.6 9.9 %collective-permute-start.15 = (bf16[96,1536]{1,0:T(8,128)(2,1)S(1)}, bf16[96,1536]{1,0:T(8,128)(2,1)S(1)}, u32[]{:S(2)}, u32[]{:S(2)}) collective-permute-start(bf16[96,1536]{1,0:T(8,128)(2,1)S(1)} %add_convert_fusion.4), channel_id=1, source_target_pairs={{0,16},{8,24},{16,0},{24,8},{1,17},{9,25},{17,1},{25,9},{2,18},{10... | collective-permute-start | bytes 884744 | tf_op jit(solution)/shard_map/ppermute | solution.py:266
  96.6 14.3 %collective-permute-start.13 = (bf16[96,1536]{1,0:T(8,128)(2,1)S(1)}, bf16[96,1536]{1,0:T(8,128)(2,1)S(1)}, u32[]{:S(2)}, u32[]{:S(2)}) collective-permute-start(bf16[96,1536]{1,0:T(8,128)(2,1)S(1)} %add_convert_fusion.5), channel_id=1, source_target_pairs={{0,16},{8,24},{16,0},{24,8},{1,17},{9,25},{17,1},{25,9},{2,18},{10... | collective-permute-start | bytes 884744 | tf_op jit(solution)/shard_map/ppermute | solution.py:266
  99.5 13.0 %collective-permute-start.45 = (bf16[96,1536]{1,0:T(8,128)(2,1)S(1)}, bf16[96,1536]{1,0:T(8,128)(2,1)S(1)}, u32[]{:S(2)}, u32[]{:S(2)}) collective-permute-start(bf16[96,1536]{1,0:T(8,128)(2,1)S(1)} %get-tuple-element.62.refs_1_.refs_9_), channel_id=1, source_target_pairs={{0,1},{1,0},{2,3},{3,2},{4,5},{5,4},{6,7},{7,6},{8,9},{9,8},{10,11... | collective-permute-start | bytes 884744 | tf_op jit(solution)/shard_map/ppermute | solution.py:269
  99.6 12.8 %collective-permute-start.22 = (bf16[96,1536]{1,0:T(8,128)(2,1)S(1)}, bf16[96,1536]{1,0:T(8,128)(2,1)S(1)}, u32[]{:S(2)}, u32[]{:S(2)}) collective-permute-start(bf16[96,1536]{1,0:T(8,128)(2,1)S(1)} %get-tuple-element.65.refs_0_.refs_18_), channel_id=1, source_target_pairs={{0,8},{8,0},{16,24},{24,16},{1,9},{9,1},{17,25},{25,17},{2,10},{10... | collective-permute-start | bytes 884744 | tf_op jit(solution)/shard_map/ppermute | solution.py:263
  100.8 11.7 %collective-permute-start.23 = (bf16[96,1536]{1,0:T(8,128)(2,1)S(1)}, bf16[96,1536]{1,0:T(8,128)(2,1)S(1)}, u32[]{:S(2)}, u32[]{:S(2)}) collective-permute-start(bf16[96,1536]{1,0:T(8,128)(2,1)S(1)} %get-tuple-element.64.refs_1_.refs_10_), channel_id=1, source_target_pairs={{0,8},{8,0},{16,24},{24,16},{1,9},{9,1},{17,25},{25,17},{2,10},{10... | collective-permute-start | bytes 884744 | tf_op jit(solution)/shard_map/ppermute | solution.py:263
  105.6 21.7 %collective-permute-start.53 = (bf16[96,1536]{1,0:T(8,128)(2,1)S(1)}, bf16[96,1536]{1,0:T(8,128)(2,1)S(1)}, u32[]{:S(2)}, u32[]{:S(2)}) collective-permute-start(bf16[96,1536]{1,0:T(8,128)(2,1)S(1)} %get-tuple-element.63.refs_0_.refs_17_), channel_id=1, source_target_pairs={{1,0},{8,9},{17,16},{24,25},{3,2},{10,11},{19,18},{26,27},{5,4},{1... | collective-permute-start | bytes 884744 | tf_op jit(solution)/shard_map/ppermute | solution.py:321
  110.9 16.5 %collective-permute-start.46 = (bf16[96,1536]{1,0:T(8,128)(2,1)S(1)}, bf16[96,1536]{1,0:T(8,128)(2,1)S(1)}, u32[]{:S(2)}, u32[]{:S(2)}) collective-permute-start(bf16[96,1536]{1,0:T(8,128)(2,1)S(1)} %get-tuple-element.64.refs_1_.refs_10_), channel_id=1, source_target_pairs={{0,1},{1,0},{2,3},{3,2},{4,5},{5,4},{6,7},{7,6},{8,9},{9,8},{10,11... | collective-permute-start | bytes 884744 | tf_op jit(solution)/shard_map/ppermute | solution.py:269
  112.5 15.0 %collective-permute-start.48 = (bf16[96,1536]{1,0:T(8,128)(2,1)S(1)}, bf16[96,1536]{1,0:T(8,128)(2,1)S(1)}, u32[]{:S(2)}, u32[]{:S(2)}) collective-permute-start(bf16[96,1536]{1,0:T(8,128)(2,1)S(1)} %collective-permute-done.44.refs_8_), channel_id=1, source_target_pairs={{0,8},{8,0},{16,24},{24,16},{1,9},{9,1},{17,25},{25,17},{2,10},{10... | collective-permute-start | bytes 884744 | tf_op jit(solution)/shard_map/ppermute | solution.py:263
  112.5 8.5 %collective-permute-start.30 = (bf16[96,768]{1,0:T(8,128)(2,1)S(1)}, bf16[96,768]{1,0:T(8,128)(2,1)S(1)}, u32[]{:S(2)}, u32[]{:S(2)}) collective-permute-start(bf16[96,768]{1,0:T(8,128)(2,1)S(1)} %get-tuple-element.49), channel_id=1, source_target_pairs={{0,2},{2,4},{4,6},{6,0},{1,3},{3,5},{5,7},{7,1},{8,10},{10,12},{12... | collective-permute-start | bytes 442376 | tf_op jit(solution)/shard_map/ppermute | solution.py:272
  112.5 11.1 %collective-permute-start.31 = (bf16[96,768]{1,0:T(8,128)(2,1)S(1)}, bf16[96,768]{1,0:T(8,128)(2,1)S(1)}, u32[]{:S(2)}, u32[]{:S(2)}) collective-permute-start(bf16[96,768]{1,0:T(8,128)(2,1)S(1)} %get-tuple-element.50), channel_id=1, source_target_pairs={{0,2},{2,4},{4,6},{6,0},{1,3},{3,5},{5,7},{7,1},{8,10},{10,12},{12... | collective-permute-start | bytes 442376 | tf_op jit(solution)/shard_map/ppermute | solution.py:272
  121.0 18.2 %collective-permute-start.16 = (bf16[96,1536]{1,0:T(8,128)(2,1)S(1)}, bf16[96,1536]{1,0:T(8,128)(2,1)S(1)}, u32[]{:S(2)}, u32[]{:S(2)}) collective-permute-start(bf16[96,1536]{1,0:T(8,128)(2,1)S(1)} %get-tuple-element.67.refs_0_.refs_19_), channel_id=1, source_target_pairs={{0,8},{8,0},{16,24},{24,16},{1,9},{9,1},{17,25},{25,17},{2,10},{10... | collective-permute-start | bytes 884744 | tf_op jit(solution)/shard_map/ppermute | solution.py:263
  123.7 16.9 %collective-permute-start.17 = (bf16[96,1536]{1,0:T(8,128)(2,1)S(1)}, bf16[96,1536]{1,0:T(8,128)(2,1)S(1)}, u32[]{:S(2)}, u32[]{:S(2)}) collective-permute-start(bf16[96,1536]{1,0:T(8,128)(2,1)S(1)} %get-tuple-element.66.refs_1_.refs_11_), channel_id=1, source_target_pairs={{0,8},{8,0},{16,24},{24,16},{1,9},{9,1},{17,25},{25,17},{2,10},{10... | collective-permute-start | bytes 884744 | tf_op jit(solution)/shard_map/ppermute | solution.py:263
  127.3 8.5 %collective-permute-start.32 = (bf16[96,768]{1,0:T(8,128)(2,1)S(1)}, bf16[96,768]{1,0:T(8,128)(2,1)S(1)}, u32[]{:S(2)}, u32[]{:S(2)}) collective-permute-start(bf16[96,768]{1,0:T(8,128)(2,1)S(1)} %get-tuple-element.51), channel_id=1, source_target_pairs={{0,2},{2,4},{4,6},{6,0},{1,3},{3,5},{5,7},{7,1},{8,10},{10,12},{12... | collective-permute-start | bytes 442376 | tf_op jit(solution)/shard_map/ppermute | solution.py:272
  127.4 11.2 %collective-permute-start.33 = (bf16[96,768]{1,0:T(8,128)(2,1)S(1)}, bf16[96,768]{1,0:T(8,128)(2,1)S(1)}, u32[]{:S(2)}, u32[]{:S(2)}) collective-permute-start(bf16[96,768]{1,0:T(8,128)(2,1)S(1)} %get-tuple-element.52), channel_id=1, source_target_pairs={{0,2},{2,4},{4,6},{6,0},{1,3},{3,5},{5,7},{7,1},{8,10},{10,12},{12... | collective-permute-start | bytes 442376 | tf_op jit(solution)/shard_map/ppermute | solution.py:272
  127.5 21.8 %collective-permute-start.54 = (bf16[96,1536]{1,0:T(8,128)(2,1)S(1)}, bf16[96,1536]{1,0:T(8,128)(2,1)S(1)}, u32[]{:S(2)}, u32[]{:S(2)}) collective-permute-start(bf16[96,1536]{1,0:T(8,128)(2,1)S(1)} %get-tuple-element.65.refs_0_.refs_18_), channel_id=1, source_target_pairs={{1,0},{8,9},{17,16},{24,25},{3,2},{10,11},{19,18},{26,27},{5,4},{1... | collective-permute-start | bytes 884744 | tf_op jit(solution)/shard_map/ppermute | solution.py:321
  135.8 13.5 %collective-permute-start.56 = (bf16[96,1536]{1,0:T(8,128)(2,1)S(1)}, bf16[96,1536]{1,0:T(8,128)(2,1)S(1)}, u32[]{:S(2)}, u32[]{:S(2)}) collective-permute-start(bf16[96,1536]{1,0:T(8,128)(2,1)S(1)} %collective-permute-done.52.refs_16_), channel_id=1, source_target_pairs={{0,8},{9,1},{16,24},{25,17},{2,10},{11,3},{18,26},{27,19},{4,12},{... | collective-permute-start | bytes 884744 | tf_op jit(solution)/shard_map/ppermute | solution.py:328
  138.6 17.0 %collective-permute-start.47 = (bf16[96,1536]{1,0:T(8,128)(2,1)S(1)}, bf16[96,1536]{1,0:T(8,128)(2,1)S(1)}, u32[]{:S(2)}, u32[]{:S(2)}) collective-permute-start(bf16[96,1536]{1,0:T(8,128)(2,1)S(1)} %get-tuple-element.66.refs_1_.refs_11_), channel_id=1, source_target_pairs={{0,1},{1,0},{2,3},{3,2},{4,5},{5,4},{6,7},{7,6},{8,9},{9,8},{10,11... | collective-permute-start | bytes 884744 | tf_op jit(solution)/shard_map/ppermute | solution.py:269
  139.1 18.5 %collective-permute-start.55 = (bf16[96,1536]{1,0:T(8,128)(2,1)S(1)}, bf16[96,1536]{1,0:T(8,128)(2,1)S(1)}, u32[]{:S(2)}, u32[]{:S(2)}) collective-permute-start(bf16[96,1536]{1,0:T(8,128)(2,1)S(1)} %get-tuple-element.67.refs_0_.refs_19_), channel_id=1, source_target_pairs={{1,0},{8,9},{17,16},{24,25},{3,2},{10,11},{19,18},{26,27},{5,4},{1... | collective-permute-start | bytes 884744 | tf_op jit(solution)/shard_map/ppermute | solution.py:321
  140.6 16.9 %collective-permute-start.49 = (bf16[96,1536]{1,0:T(8,128)(2,1)S(1)}, bf16[96,1536]{1,0:T(8,128)(2,1)S(1)}, u32[]{:S(2)}, u32[]{:S(2)}) collective-permute-start(bf16[96,1536]{1,0:T(8,128)(2,1)S(1)} %collective-permute-done.45.refs_9_), channel_id=1, source_target_pairs={{0,8},{8,0},{16,24},{24,16},{1,9},{9,1},{17,25},{25,17},{2,10},{10... | collective-permute-start | bytes 884744 | tf_op jit(solution)/shard_map/ppermute | solution.py:263
  149.3 10.8 %collective-permute-start.34 = (bf16[96,768]{1,0:T(8,128)(2,1)S(1)}, bf16[96,768]{1,0:T(8,128)(2,1)S(1)}, u32[]{:S(2)}, u32[]{:S(2)}) collective-permute-start(bf16[96,768]{1,0:T(8,128)(2,1)S(1)} %get-tuple-element.53), channel_id=1, source_target_pairs={{0,2},{2,4},{4,6},{6,0},{1,3},{3,5},{5,7},{7,1},{8,10},{10,12},{12... | collective-permute-start | bytes 442376 | tf_op jit(solution)/shard_map/ppermute | solution.py:272
  149.3 10.8 %collective-permute-start.35 = (bf16[96,768]{1,0:T(8,128)(2,1)S(1)}, bf16[96,768]{1,0:T(8,128)(2,1)S(1)}, u32[]{:S(2)}, u32[]{:S(2)}) collective-permute-start(bf16[96,768]{1,0:T(8,128)(2,1)S(1)} %get-tuple-element.55), channel_id=1, source_target_pairs={{0,2},{2,4},{4,6},{6,0},{1,3},{3,5},{5,7},{7,1},{8,10},{10,12},{12... | collective-permute-start | bytes 442376 | tf_op jit(solution)/shard_map/ppermute | solution.py:272
  155.6 8.4 %collective-permute-start.57 = (bf16[96,1536]{1,0:T(8,128)(2,1)S(1)}, bf16[96,1536]{1,0:T(8,128)(2,1)S(1)}, u32[]{:S(2)}, u32[]{:S(2)}) collective-permute-start(bf16[96,1536]{1,0:T(8,128)(2,1)S(1)} %collective-permute-done.53.refs_17_), channel_id=1, source_target_pairs={{0,8},{9,1},{16,24},{25,17},{2,10},{11,3},{18,26},{27,19},{4,12},{... | collective-permute-start | bytes 884744 | tf_op jit(solution)/shard_map/ppermute | solution.py:328
  (22 other events, 124.8 us)

commit v2 on v0

v2 whole, which is shorter than its diff:
```python
import functools

import jax
import jax.numpy as jnp
from jax import lax
from jax.experimental import pallas as pl
from jax.experimental.pallas import tpu as pltpu
from jax.sharding import PartitionSpec as P

BF16, F32 = jnp.bfloat16, jnp.float32
MIB = 1024 * 1024
IN_VMEM = pl.BlockSpec(memory_space=pltpu.VMEM)
IN_SMEM = pl.BlockSpec(memory_space=pltpu.SMEM)
IN_HBM = pl.BlockSpec(memory_space=pltpu.HBM)
ANYWHERE = pl.BlockSpec(memory_space=pl.ANY)
TOKEN = jax.ShapeDtypeStruct((8, 128), F32)


def gelu_parts(hidden_pre):
    normal_cdf = 0.5 * (1.0 + lax.erf(hidden_pre * 0.7071067811865476))
    normal_pdf = jnp.exp(-0.5 * hidden_pre * hidden_pre) * 0.3989422804014327
    return (hidden_pre * normal_cdf, normal_cdf + hidden_pre * normal_pdf)


def dot(left, right, left_dim, right_dim):
    return lax.dot_general(
        left, right, (((left_dim,), (right_dim,)), ((), ())), preferred_element_type=F32
    )


def shape(*sizes, kind=BF16):
    return jax.ShapeDtypeStruct(sizes, kind)


class Chain:
    def __init__(self, where):
        self.where = where
        self.token = jnp.zeros(TOKEN.shape, TOKEN.dtype)

    def __call__(self, kernel, inputs, out_shapes, after=(), scratch=(), limit=16, specs=None, to=IN_VMEM):
        n_in, n_after, n_out = len(inputs), len(after) + 1, len(out_shapes)

        def body(where, *refs):
            ins = refs[:n_in]
            outs = refs[n_in + n_after : n_in + n_after + n_out]
            token = refs[n_in + n_after + n_out]
            kernel(where, ins, outs, refs[n_in + n_after + n_out + 1 :])
            token[...] = jnp.zeros(token.shape, token.dtype)

        *results, self.token = pl.pallas_call(
            body,
            in_specs=[IN_SMEM] + (specs or [IN_VMEM] * n_in) + [ANYWHERE] * n_after,
            out_specs=[to] * n_out + [IN_VMEM],
            out_shape=list(out_shapes) + [TOKEN],
            scratch_shapes=list(scratch),
            compiler_params=pltpu.CompilerParams(vmem_limit_bytes=limit * MIB),
            cost_estimate=pl.CostEstimate(flops=1000, bytes_accessed=1000, transcendentals=0),
        )(self.where, *inputs, *after, self.token)
        return results


def block_of(where, rel, index, width):
    core = where[0] if rel == 0 else 1 - where[0]
    return pl.ds(pl.multiple_of((2 * index + core) * width, 128), width)


def cut_parts(where, chunks, own_part, messages):
    (rows, part), n_depth = own_part.shape, len(messages) + 1
    own_part[...] = chunks[-1][0, :, pl.ds(pl.multiple_of(where[1] * part, 128), part)]
    for k, message in enumerate(messages, 1):
        owner = lax.rem(where[1] + k, n_depth)
        for index, both in enumerate(chunks):
            at = slice(index * rows, (index + 1) * rows)
            message[at, :part] = both[0, :, pl.ds(pl.multiple_of(owner * part, 128), part)]
            message[at, part:] = both[1]


def hidden_kernel(where, ins, outs, scratch):
    both, weight_in, weight_out = ins[:3]
    other_hidden, other_grad, own = outs[:3]
    blocks, _, width = other_hidden.shape
    for rel in (1, 0):
        targets = (own.at[0], own.at[1]) if rel == 0 else (other_hidden, other_grad)
        for index in range(blocks):
            cut = block_of(where, rel, index, width)
            targets[0][index] = dot(both[0], weight_in[:, cut], 1, 0).astype(BF16)
            targets[1][index] = dot(both[1], weight_out[cut, :], 1, 1).astype(BF16)
    cut_parts(where, list(ins[3:]) + [both], outs[3], outs[4:])


def first_kernel(where, ins, outs, scratch):
    both, from_in, from_out = ins
    own, weight_in, weight_out, own_part = outs[:4]
    _, blocks, _, width = own.shape
    n_others = 2 * blocks
    others, messages = outs[-n_others:], outs[4:-n_others]
    steps = []
    for rel in (1, 0):
        for index in range(blocks):
            cut = block_of(where, rel, index, width)
            for which, source, target in ((0, from_in, weight_in), (1, from_out, weight_out)):
                at = (slice(None), cut) if which == 0 else (cut, slice(None))
                copy = pltpu.make_async_copy(source.at[at], target.at[at], scratch[0].at[len(steps)])
                copy.start()
                spot = others[which * blocks + index] if rel else own.at[which].at[index]
                steps.append((copy, which, at, spot))
    cut_parts(where, [both], own_part, messages)
    for copy, which, at, spot in steps:
        copy.wait()
        weight = weight_out if which else weight_in
        spot[...] = dot(both[which], weight[at], 1, which).astype(BF16)


def chip_kernel(where, ins, outs, scratch):
    blocks = ins[0].shape[1]
    for which in range(2):
        for index in range(blocks):
            came = ins[1 + which][index] if len(ins) == 3 else ins[1 + which * blocks + index][...]
            total = ins[0][which, index].astype(F32) + came.astype(F32)
            outs[0][which, index] = total.astype(BF16)


def gelu_kernel(where, ins, outs, scratch):
    blocks = ins[0].shape[1]
    depth, n_depth = where[1], len(outs)
    for index in range(blocks):
        hidden, grad = ins[0][0, index].astype(F32), ins[0][1, index].astype(F32)
        for other in ins[1:]:
            hidden += other[0, index].astype(F32)
            grad += other[1, index].astype(F32)
        value, slope = gelu_parts(hidden)
        act, pre = value.astype(BF16), (grad * slope).astype(BF16)
        outs[0][0, index] = act
        outs[0][1, index] = pre
        for message in outs[1:]:
            message[index] = pre
    for k in range(1, n_depth):
        outs[k][blocks] = outs[0][0, lax.rem(depth + k, n_depth)]


def model_kernel(where, ins, outs, scratch):
    weight_in, weight_out = ins[2:4]
    _, blocks, _, width = ins[0].shape
    out = grad = 0.0
    for rel in range(2):
        for index in range(blocks):
            cut = block_of(where, rel, index, width)
            out += dot(ins[rel][0, index], weight_out[cut, :], 1, 0)
            grad += dot(ins[rel][1, index], weight_in[:, cut], 1, 1)
    if len(ins) > 4:
        out += ins[4][0].astype(F32)
        grad += ins[4][1].astype(F32)
    outs[0][0] = out.astype(BF16)
    outs[0][1] = grad.astype(BF16)


def relay_kernel(where, ins, outs, scratch):
    for index, target in enumerate(outs):
        target[...] = ins[0][index]


def final_kernel(where, ins, outs, scratch):
    for index in range(2):
        total = ins[0][index].astype(F32) + ins[1][index].astype(F32)
        outs[index][...] = total.astype(BF16)


def weight_kernel(own, far, before, send, where, ins, outs, scratch):
    all_tokens, all_cotangents, all_values = scratch[:3]
    width, part = all_values.shape[1], all_tokens.shape[1]
    blocks = outs[0].shape[1] // (2 * width)
    ins = list(ins)
    tokens, cotangents = [], []
    acts, pres = ([], []), ([], [])
    for _ in range(own):
        share, both, *values = (ins.pop(0) for _ in range(4))
        rows = share.shape[0]
        tokens.append(share)
        cotangents.append(both.at[1])
        for rel, value in enumerate(values):
            acts[rel].append(value.at[0].at[where[1]])
            pres[rel].append([value.at[1].at[index] for index in range(blocks)])
    for start in far:
        sent, mine = ins.pop(0), ins.pop(0)
        rows = mine.shape[1]
        tokens.append(sent.at[start : start + rows, :part])
        cotangents.append(sent.at[start : start + rows, part:])
        pieces = [mine.at[index] for index in range(blocks + 1)]
        if send:
            swapped = [ins.pop(0) for _ in range(blocks + 1)]
        else:
            swapped = ins.pop(0)
            swapped = [swapped.at[index] for index in range(blocks + 1)]
        for rel, value in enumerate((pieces, swapped)):
            acts[rel].append(value[blocks])
            pres[rel].append(value[:blocks])

    def fill(target, sources):
        for index, source in enumerate(sources):
            target[index * rows : (index + 1) * rows, :] = source[...]

    copies = []

    def put(which, at, term):
        if before:
            term += ins[which][at]
        if not send:
            outs[which][at] = term
            return
        held, semaphore = scratch[3 + which], scratch[5].at[len(copies)]
        held[at] = term
        copies.append(pltpu.make_async_copy(held.at[at], outs[which].at[at], semaphore))
        copies[-1].start()

    fill(all_tokens, tokens)
    fill(all_cotangents, cotangents)
    for rel in range(2):
        core = where[0] if rel == 0 else 1 - where[0]
        for index in range(blocks):
            fill(all_values, [value[index] for value in pres[rel]])
            at = (slice(None), block_of(where, rel, index, width))
            put(0, at, dot(all_tokens[...], all_values[...], 0, 0))
        fill(all_values, acts[rel])
        at = (pl.ds(pl.multiple_of(core * width, 128), width), slice(None))
        put(1, at, dot(all_values[...], all_cotangents[...], 0, 0))
    for copy in copies:
        copy.wait()


class Plain:
    def __init__(self, core, depth, n_depth):
        self.core, self.depth, self.n_depth = core, depth, n_depth

    def split(self, value, axis):
        size = value.shape[axis] // (2 * self.n_depth)
        lead = value.shape[:axis] + (self.n_depth, 2, size) + value.shape[axis + 1 :]
        value = value.reshape(lead)
        take = lambda c: lax.dynamic_index_in_dim(value, c, axis + 1, False)
        return take(self.core), take(1 - self.core)

    def join(self, own, other):
        first = jnp.where(self.core == 0, own, other)
        second = jnp.where(self.core == 0, other, own)
        return jnp.stack([first, second], axis=-3)

    def hidden(self, both, weight_in, weight_out):
        hidden = dot(both[0], weight_in, 1, 0).astype(BF16)
        grad = dot(both[1], weight_out, 1, 1).astype(BF16)
        pairs = zip(self.split(hidden, 1), self.split(grad, 1))
        own, other = (jnp.stack([h, g]).transpose(0, 2, 1, 3) for h, g in pairs)
        return other, own

    def parts(self, both, size):
        cuts = [
            lax.dynamic_slice_in_dim(both[0], (self.depth + k) % self.n_depth * size, size, 1)
            for k in range(self.n_depth)
        ]
        return cuts[:1] + [jnp.concatenate([cut, both[1]], axis=1) for cut in cuts[1:]]

    def gelu(self, parts):
        total = sum(part.astype(F32) for part in parts)
        value, slope = gelu_parts(total[0])
        act, pre = value.astype(BF16), (total[1] * slope).astype(BF16)
        messages = []
        for k in range(1, self.n_depth):
            share = lax.dynamic_index_in_dim(act, (self.depth + k) % self.n_depth, 0)
            messages.append(jnp.concatenate([pre, share]))
        return [jnp.stack([act, pre])] + messages

    def flat(self, own, other):
        joined = self.join(own, other)
        blocks, cores, rows, width = joined.shape
        return joined.transpose(2, 0, 1, 3).reshape(rows, blocks * cores * width)

    def model(self, own, other, weight_in, weight_out, arrived):
        out = dot(self.flat(own[0], other[0]), weight_out, 1, 0)
        grad = dot(self.flat(own[1], other[1]), weight_in, 1, 1)
        sums = jnp.stack([out, grad])
        return (sums + sum(value.astype(F32) for value in arrived)).astype(BF16)

    def weights(self, own_rows, far_rows):
        in_grad = out_grad = 0.0
        for part, both, own, other in own_rows:
            act = [lax.dynamic_index_in_dim(v[0], self.depth, 0) for v in (own, other)]
            in_grad += dot(part, self.flat(own[1], other[1]), 0, 0)
            out_grad += dot(self.flat(*act), both[1], 0, 0)
        for (sent, own, other), start in far_rows:
            sent = sent[start : start + own.shape[1]]
            size = sent.shape[1] - own_rows[0][1].shape[2]
            part, cotangent = sent[:, :size], sent[:, size:]
            in_grad += dot(part, self.flat(own[:-1], other[:-1]), 0, 0)
            out_grad += dot(self.flat(own[-1:], other[-1:]), cotangent, 0, 0)
        return in_grad, out_grad


def shards(n_row, n_col, n_depth, tokens, weight_in, weight_out, output_grad):
    core = lax.axis_index("row") % 2
    depth = lax.axis_index("depth")
    rows, features = tokens.shape
    part = features // n_depth
    blocks, width = n_depth, weight_in.shape[1] // (2 * n_depth)
    aligned = width % 128 == 0 and part % 128 == 0
    chain = Chain(jnp.stack([core, depth]).astype(jnp.int32))
    plain = Plain(core, depth, n_depth)

    def swap_cores(value):
        return lax.ppermute(value, "row", [(r, r ^ 1) for r in range(n_row)])

    def to_chip(value, k):
        return lax.ppermute(value, "row", [(r, (r + 2 * k) % n_row) for r in range(n_row)])

    def to_depth(value, k):
        return lax.ppermute(value, "depth", [(d, (d + k) % n_depth) for d in range(n_depth)])

    def to_next(value):
        return lax.ppermute(value, "col", [(c, (c + 1) % n_col) for c in range(n_col)])

    far = range(1, n_depth)
    pair_shape = shape(2, blocks, rows, width)
    both = [jnp.stack([tokens, output_grad])]
    chips, crossed, parts, far_parts = {}, {}, {}, {}

    weights = [weight_in, weight_out]
    pairs, swaps = {}, {}
    late = []
    n_single = min(2, n_col - 1)

    def place(stage):
        return max(stage - n_single, 0) * rows

    def hidden_step(stage):
        single = shape(blocks, rows, width)
        if stage < n_single:
            waiting = []
        else:
            waiting = both[n_single:stage] if stage == n_col - 1 else None
        cuts = [shape(rows, part)]
        if waiting is not None:
            cuts += [shape(rows * (len(waiting) + 1), part + features)] * (n_depth - 1)
        if not aligned:
            others, own = plain.hidden(both[stage], *weights)
            parts[stage], *sent = plain.parts(both[stage], part)
            if stage >= n_single:
                late.append(sent)
                sent = [jnp.concatenate(values) for values in zip(*late)]
        elif stage == 0:
            results = chain(
                first_kernel,
                [both[stage]] + weights,
                [pair_shape, shape(*weight_in.shape), shape(*weight_out.shape)]
                + cuts
                + [shape(rows, width)] * (2 * blocks),
                scratch=[pltpu.SemaphoreType.DMA((4 * blocks,))],
                specs=[IN_VMEM, IN_HBM, IN_HBM],
                limit=42,
            )
            own, weights[0], weights[1], parts[stage] = results[:4]
            sent, others = results[4 : -2 * blocks], results[-2 * blocks :]
        else:
            results = chain(
                hidden_kernel,
                [both[stage]] + weights + (waiting or []),
                [single, single, pair_shape] + cuts,
                after=far_parts[0] if stage == 1 else [],
            )
            *others, own, parts[stage] = results[:4]
            sent = results[4:]
        if stage + 1 < n_col:
            both.append(to_next(both[stage]))
        came = [swap_cores(other) for other in others]
        if aligned:
            (chips[stage],) = chain(chip_kernel, [own] + came, [pair_shape])
        else:
            chips[stage] = (own.astype(F32) + jnp.stack(came).astype(F32)).astype(BF16)
        crossed[stage] = [to_chip(chips[stage], k) for k in range(1, n_row // 2)]
        if waiting is not None:
            far_parts[stage] = [to_depth(sent[k - 1], k) for k in far]

    own_rows, far_came = [], []

    def gelu_step(stage):
        if aligned:
            after = {0: far_parts.get(1, []), n_col - 2: far_parts.get(n_col - 1, [])}.get(stage, [])
            after = list(after)
            if stage > 0:
                after += far_came[stage - 1]
            pairs[stage], *messages = chain(
                gelu_kernel,
                [chips[stage]] + crossed[stage],
                [pair_shape] + [shape(blocks + 1, rows, width)] * (n_depth - 1),
                after=after,
            )
        else:
            pairs[stage], *messages = plain.gelu([chips[stage]] + crossed[stage])
        swaps[stage] = swap_cores(pairs[stage])
        own_rows.append([parts[stage], both[stage], pairs[stage], swaps[stage]])
        group = []
        for k in far:
            group.append(to_depth(messages[k - 1], k))
        far_came.append(group)

    kept, arrived = None, []

    def model_step(stage):
        nonlocal kept, arrived
        if aligned:
            (sums,) = chain(
                model_kernel,
                [pairs[stage], swaps[stage]] + weights + arrived,
                [shape(2, rows, features)],
            )
        else:
            sums = plain.model(pairs[stage], swaps[stage], *weights, arrived)
        if stage == 0:
            kept = sums
        else:
            arrived = [to_next(sums)]

    for stage in range(n_col):
        hidden_step(stage)
        if stage > 1:
            model_step(stage - 2)
        if stage > 0:
            gelu_step(stage - 1)
    model_step(n_col - 2)
    gelu_step(n_col - 1)
    model_step(n_col - 1)

    far_rows = [
        [
            [far_parts[stage if stage < n_single else n_col - 1][k - 1], far_came[stage][k - 1]]
            for k in far
        ]
        for stage in range(n_col)
    ]
    groups = [(row, stage) for stage, group in enumerate(far_rows[:-1]) for row in group]
    early_rows = [(row + [swap_cores(row[1])], place(stage)) for row, stage in groups]
    if aligned:
        grads = [
            shape(part, 2 * blocks * width, kind=F32),
            shape(2 * width, features, kind=F32),
        ]

        def weight_call(own, away, before, send):
            count = rows * (len(own) + len(away))
            starts = [start for _, start in away]
            scratch = [
                pltpu.VMEM((count, part), BF16),
                pltpu.VMEM((count, features), BF16),
                pltpu.VMEM((count, width), BF16),
            ]
            if send:
                scratch += [pltpu.VMEM(grad.shape, F32) for grad in grads]
                scratch += [pltpu.SemaphoreType.DMA((2 * blocks + 2,))]
            values = [value for row in own for value in row]
            values += [value for row, _ in away for value in row]
            return chain(
                functools.partial(weight_kernel, len(own), starts, bool(before), send),
                values + list(before),
                grads,
                scratch=scratch,
                limit=24,
                to=IN_HBM if send else IN_VMEM,
            )

        terms = weight_call(own_rows, early_rows, (), not far)
        if far:
            last_rows = []
            for sent, came in far_rows[-1]:
                pieces = chain(relay_kernel, [came], [shape(rows, width)] * (blocks + 1))
                swapped = [swap_cores(piece) for piece in pieces]
                last_rows.append(([sent, came] + swapped, place(n_col - 1)))
            terms = weight_call((), last_rows, terms, True)
        output, input_grad = chain(
            final_kernel, [kept] + arrived, [shape(rows, features)] * 2
        )
    else:
        last_rows = [(row + [swap_cores(row[1])], place(n_col - 1)) for row in far_rows[-1]]
        terms = plain.weights(own_rows, early_rows + last_rows)
        output, input_grad = (kept.astype(F32) + arrived[0].astype(F32)).astype(BF16)
    return (output, input_grad, *terms)


def solution(mesh):
    placed = (
        P(("col", "depth"), "row"),
        P("row", "col"),
        P("col", "row"),
        P(("col", "depth"), "row"),
    )
    sizes = (mesh.shape["row"], mesh.shape["col"], mesh.shape["depth"])
    return jax.shard_map(
        functools.partial(shards, *sizes),
        mesh=mesh,
        in_specs=placed,
        out_specs=(
            P(("col", "depth"), "row"),
            P(("col", "depth"), "row"),
            P(("row", "depth"), "col"),
            P(("col", "depth"), "row"),
        ),
        check_vma=False,
    )
```

time: 341 us -> 123 us (0.36)
  waiting for transfers between devices: 238 us -> 53 us
  Pallas kernels: 0 us -> 43.8 us
  blocking collectives: 35 us -> 0 us
  matrix products: 29.9 us -> 0 us
  starting transfers between devices: 0.39 us -> 24.4 us
  local copies, waits for them, and re-layouts: 15.8 us -> 0.01 us
  between operations: 13.8 us -> 0.94 us
  other arithmetic: 8.08 us -> 1.09 us
    reduce_scatter x3 -> x0, waiting for transfers between devices: 100 us -> none  [the longest x1 56.9 us: shards(): lax.psum_scatter(term_out.astype(jnp.bfloat16), 'depth', scatter_dimensio...]
    psum x1 -> x0, waiting for transfers between devices: 95.5 us -> none  [hidden_total(): return lax.psum(term.astype(jnp.bfloat16), 'row').astype(jnp.float32)]
    ppermute x0 -> x37, waiting for transfers between devices: none -> 53 us  [the longest x7 25.6 us: to_depth(): lax.ppermute(value, 'depth', [(d, (d + k) % n_depth) for d in range(n_dep...]
    pallas_call x0 -> x20, Pallas kernels: none -> 43.8 us  [__call__(): pl.pallas_call(body, in_specs=[IN_SMEM] + (specs or [IN_VMEM] * n_in) + [...]
    unnamed x6 -> x0, waiting for transfers between devices: 42.1 us -> none
    all_gather x2 -> x0, blocking collectives: 35 us -> none  [the longest x1 18.4 us: shards(): lax.all_gather(tokens, 'col', axis=0, tiled=True)]
    dot_general x6 -> x0, matrix products: 29.9 us -> none  [the longest x2 11.9 us: product_rows(): lax.dot_general(panel, weight, (((1,), (contract,)), ((), ())), preferred...]
    ppermute x0 -> x37, starting transfers between devices: none -> 24.4 us  [the longest x7 8.68 us: to_depth(): lax.ppermute(value, 'depth', [(d, (d + k) % n_depth) for d in range(n_dep...]
  transfers between devices with their start and end apart: 5 -> 37, of which waited for: 5 -> 16; matrix products, arithmetic and copies ran while one was open for 8% -> 0% of each run, Pallas kernels for 0% -> 27%
where the time goes in v2:
time: 123 us
  waiting for transfers between devices  53 us (43%)
  Pallas kernels  43.8 us (36%)
  starting transfers between devices  24.4 us (20%)
    pallas_call x20, Pallas kernels, __call__(): pl.pallas_call(body, in_specs=[IN_SMEM] + (specs or [IN_VMEM] * n_in) + [...  43.8 us
    ppermute x7, waiting for transfers between devices, to_depth(): lax.ppermute(value, 'depth', [(d, (d + k) % n_depth) for d in range(n_dep...  25.6 us
    ppermute x6, waiting for transfers between devices, to_next(): lax.ppermute(value, 'col', [(c, (c + 1) % n_col) for c in range(n_col)])  17.3 us
    ppermute x7, starting transfers between devices, to_depth(): lax.ppermute(value, 'depth', [(d, (d + k) % n_depth) for d in range(n_dep...  8.68 us
    ppermute x6, starting transfers between devices, to_next(): lax.ppermute(value, 'col', [(c, (c + 1) % n_col) for c in range(n_col)])  7.09 us
    ppermute x4, waiting for transfers between devices, to_chip(): lax.ppermute(value, 'row', [(r, (r + 2 * k) % n_row) for r in range(n_row)])  6.83 us
    ppermute x20, starting transfers between devices, swap_cores(): return lax.ppermute(value, 'row', [(r, r ^ 1) for r in range(n_row)])  4.34 us
    ppermute x4, starting transfers between devices, to_chip(): lax.ppermute(value, 'row', [(r, (r + 2 * k) % n_row) for r in range(n_row)])  4.25 us
  transfers between devices with their start and end apart: 37, of which 16 were waited for; matrix products, arithmetic and copies ran while one was open for 0% of the time, Pallas kernels for 27%

profile of v2, /device:TPU:0, one launch (start us, length us, event | category | flops | bytes accessed | tf_op | source)
XLA Modules:
  0.0 123.2 jit_solution(13941558870483507333)
XLA Ops:
  0.7 1.0 pad_maximum_fusion.refs_0_.refs_1_
  1.7 5.8 %shard_map.75 = (bf16[2,2,96,768]{3,2,1,0:T(8,128)(2,1)S(1)}, bf16[768,3072]{1,0:T(8,128)(2,1)S(1)}, bf16[3072,768]{1,0:T(8,128)(2,1)S(1)}, bf16[96,384]{1,0:T(8...) custom-call(s32[2]{0:T(128)S(1)} %pad_add_fusion.where, ...), custom_call_target="tpu_custom_call" | custom-call | flops 1000 | bytes 1000 | tf_op jit(solution)/shard_map/pallas_call | solution.py:50
  7.5 0.5 collective-permute-start
  8.6 3.0 %collective-permute-start.5 = (bf16[2,96,768]{2,1,0:T(8,128)(2,1)S(1)}, bf16[2,96,768]{2,1,0:T(8,128)(2,1)S(1)}, u32[]{:S(2)}, u32[]{:S(2)}) collective-permute-start(bf16[2,96,768]{2,1,0:T(8,128)(2,1)S(1)} %pad_maximum_fusion.refs_0_.refs_1_), channel_id=1, source_target_pairs={{0,2},{2,4},{4,6},{6,0},{1,3},{3,5},{5,7},{7,1},{8,10},{10,12},{12... | collective-permute-start | bytes 884744 | tf_op jit(solution)/shard_map/ppermute | solution.py:316
  11.7 0.7 shard_map.76
  12.3 1.6 %collective-permute-start.4 = (bf16[2,2,96,768]{3,2,1,0:T(8,128)(2,1)S(1)}, bf16[2,2,96,768]{3,2,1,0:T(8,128)(2,1)S(1)}, u32[]{:S(2)}, u32[]{:S(2)}) collective-permute-start(bf16[2,2,96,768]{3,2,1,0:T(8,128)(2,1)S(1)} %get-tuple-element.77.refs_0_), channel_id=1, source_target_pairs={{0,16},{8,24},{16,0},{24,8},{1,17},{9,25},{17,1},{25,9},{2,18},{10... | collective-permute-start | bytes 1769480 | tf_op jit(solution)/shard_map/ppermute | solution.py:310
  13.9 1.5 %collective-permute-start.6 = (bf16[96,1152]{1,0:T(8,128)(2,1)S(1)}, bf16[96,1152]{1,0:T(8,128)(2,1)S(1)}, u32[]{:S(2)}, u32[]{:S(2)}) collective-permute-start(bf16[96,1152]{1,0:T(8,128)(2,1)S(1)} %get-tuple-element.80), channel_id=1, source_target_pairs={{0,1},{1,0},{2,3},{3,2},{4,5},{5,4},{6,7},{7,6},{8,9},{9,8},{10,11... | collective-permute-start | bytes 663560 | tf_op jit(solution)/shard_map/ppermute | solution.py:313
  15.4 5.3 %collective-permute-done.6.refs_3_.refs_16_ = bf16[96,1152]{1,0:T(8,128)(2,1)S(1)} collective-permute-done((bf16[96,1152]{1,0:T(8,128)(2,1)S(1)}, bf16[96,1152]{1,0:T(8,128)(2,1)S(1)}, u32[]{:S(2)}, u32[]{:S(2)}) %collective-permute-start.6) | collective-permute-done | bytes 221216 | tf_op jit(solution)/shard_map/ppermute | solution.py:313
  20.9 2.8 %shard_map.77 = (bf16[2,96,768]{2,1,0:T(8,128)(2,1)S(1)}, bf16[2,96,768]{2,1,0:T(8,128)(2,1)S(1)}, bf16[2,2,96,768]{3,2,1,0:T(8,128)(2,1)S(1)}, bf16[96,384]{1,0...) custom-call(s32[2]{0:T(128)S(1)} %pad_add_fusion.where, ...), custom_call_target="tpu_custom_call" | custom-call | flops 1000 | bytes 1000 | tf_op jit(solution)/shard_map/pallas_call | solution.py:50
  23.8 0.5 collective-permute-start.9
  24.3 1.4 %collective-permute-start.11 = (bf16[2,96,768]{2,1,0:T(8,128)(2,1)S(1)}, bf16[2,96,768]{2,1,0:T(8,128)(2,1)S(1)}, u32[]{:S(2)}, u32[]{:S(2)}) collective-permute-start(bf16[2,96,768]{2,1,0:T(8,128)(2,1)S(1)} %collective-permute-done.5.refs_0_.refs_5_), channel_id=1, source_target_pairs={{0,2},{2,4},{4,6},{6,0},{1,3},{3,5},{5,7},{7,1},{8,10},{10,12},{12... | collective-permute-start | bytes 884744 | tf_op jit(solution)/shard_map/ppermute | solution.py:316
  25.7 1.5 %collective-permute-start.7 = (bf16[96,1152]{1,0:T(8,128)(2,1)S(1)}, bf16[96,1152]{1,0:T(8,128)(2,1)S(1)}, u32[]{:S(2)}, u32[]{:S(2)}) collective-permute-start(bf16[96,1152]{1,0:T(8,128)(2,1)S(1)} %get-tuple-element.82), channel_id=1, source_target_pairs={{0,1},{1,0},{2,3},{3,2},{4,5},{5,4},{6,7},{7,6},{8,9},{9,8},{10,11... | collective-permute-start | bytes 663560 | tf_op jit(solution)/shard_map/ppermute | solution.py:313
  27.2 0.7 shard_map.78
  27.9 4.9 %collective-permute-done.7.refs_2_.refs_19_ = bf16[96,1152]{1,0:T(8,128)(2,1)S(1)} collective-permute-done((bf16[96,1152]{1,0:T(8,128)(2,1)S(1)}, bf16[96,1152]{1,0:T(8,128)(2,1)S(1)}, u32[]{:S(2)}, u32[]{:S(2)}) %collective-permute-start.7) | collective-permute-done | bytes 221216 | tf_op jit(solution)/shard_map/ppermute | solution.py:313
  32.9 1.1 shard_map.79
  34.1 0.6 collective-permute-start.15
  35.1 2.8 %shard_map.80 = (bf16[2,96,768]{2,1,0:T(8,128)(2,1)S(1)}, bf16[2,96,768]{2,1,0:T(8,128)(2,1)S(1)}, bf16[2,2,96,768]{3,2,1,0:T(8,128)(2,1)S(1)}, bf16[96,384]{1,0:T(8,128)(2,1)S(1)}, f32[8,128]{1,0:T(8,128)S(1)}) custom-call(s32[2]{0:T(128)S(1)} %pad_add_fusion.where, bf16[2,96,768]{2,1,0:T(8,128)(2,1)S(1)} %collective-permute-done.11.refs_0_.refs_3_.refs_9_, ...), custom_call_target="tpu_custom_call" | custom-call | flops 1000 | bytes 1000 | tf_op jit(solution)/shard_map/pallas_call | solution.py:50
  38.0 1.6 %collective-permute-start.16 = (bf16[3,96,768]{2,1,0:T(8,128)(2,1)S(1)}, bf16[3,96,768]{2,1,0:T(8,128)(2,1)S(1)}, u32[]{:S(2)}, u32[]{:S(2)}) collective-permute-start(bf16[3,96,768]{2,1,0:T(8,128)(2,1)S(1)} %get-tuple-element.97), channel_id=1, source_target_pairs={{0,1},{1,0},{2,3},{3,2},{4,5},{5,4},{6,7},{7,6},{8,9},{9,8},{10,11... | collective-permute-start | bytes 1327112 | tf_op jit(solution)/shard_map/ppermute | solution.py:313
  39.7 1.2 collective-permute-start.14
  41.1 0.7 shard_map.81
  41.8 2.8 %shard_map.82 = (bf16[2,96,768]{2,1,0:T(8,128)(2,1)S(1)}, f32[8,128]{1,0:T(8,128)S(1)}) custom-call(s32[2]{0:T(128)S(1)} %pad_add_fusion.where, bf16[2,2,96,768]{3,2,1,0:T(8,128)(2,1)S(1)} %get-tuple-element.88.refs_0_.refs_2_, bf16[2,2,96,768]{3,2,1,0:T(8,128)(2,1)S(1)} %collective-permute-done.10.refs_1_.refs_3_, ...), custom_call_target="tpu_custom_call" | custom-call | flops 1000 | bytes 1000 | tf_op jit(solution)/shard_map/pallas_call | solution.py:50
  44.6 5.9 %collective-permute-done.16.refs_2_.refs_17_ = bf16[3,96,768]{2,1,0:T(8,128)(2,1)S(1)} collective-permute-done((bf16[3,96,768]{2,1,0:T(8,128)(2,1)S(1)}, bf16[3,96,768]{2,1,0:T(8,128)(2,1)S(1)}, u32[]{:S(2)}, u32[]{:S(2)}) %collective-permute-start.16) | collective-permute-done | bytes 442400 | tf_op jit(solution)/shard_map/ppermute | solution.py:313
  50.6 1.1 shard_map.83
  51.7 2.8 %shard_map.84 = (bf16[2,96,768]{2,1,0:T(8,128)(2,1)S(1)}, bf16[2,96,768]{2,1,0:T(8,128)(2,1)S(1)}, bf16[2,2,96,768]{3,2,1,0:T(8,128)(2,1)S(1)}, bf16[96,384]{1,0...) custom-call(s32[2]{0:T(128)S(1)} %pad_add_fusion.where, ...), custom_call_target="tpu_custom_call" | custom-call | flops 1000 | bytes 1000 | tf_op jit(solution)/shard_map/pallas_call | solution.py:50
  54.6 0.5 collective-permute-start.23
  55.1 1.5 %collective-permute-start.20 = (bf16[2,2,96,768]{3,2,1,0:T(8,128)(2,1)S(1)}, bf16[2,2,96,768]{3,2,1,0:T(8,128)(2,1)S(1)}, u32[]{:S(2)}, u32[]{:S(2)}) collective-permute-start(bf16[2,2,96,768]{3,2,1,0:T(8,128)(2,1)S(1)} %get-tuple-element.105.refs_0_), channel_id=1, source_target_pairs={{0,16},{8,24},{16,0},{24,8},{1,17},{9,25},{17,1},{25,9},{2,18},{10... | collective-permute-start | bytes 1769480 | tf_op jit(solution)/shard_map/ppermute | solution.py:310
  56.6 1.5 %collective-permute-start.22 = (bf16[3,96,768]{2,1,0:T(8,128)(2,1)S(1)}, bf16[3,96,768]{2,1,0:T(8,128)(2,1)S(1)}, u32[]{:S(2)}, u32[]{:S(2)}) collective-permute-start(bf16[3,96,768]{2,1,0:T(8,128)(2,1)S(1)} %get-tuple-element.107), channel_id=1, source_target_pairs={{0,1},{1,0},{2,3},{3,2},{4,5},{5,4},{6,7},{7,6},{8,9},{9,8},{10,11... | collective-permute-start | bytes 1327112 | tf_op jit(solution)/shard_map/ppermute | solution.py:313
  58.6 1.6 %collective-permute-done.18.refs_2_ = bf16[2,96,768]{2,1,0:T(8,128)(2,1)S(1)} collective-permute-done((bf16[2,96,768]{2,1,0:T(8,128)(2,1)S(1)}, bf16[2,96,768]{2,1,0:T(8,128)(2,1)S(1)}, u32[]{:S(2)}, u32[]{:S(2)}) %collective-permute-start.18) | collective-permute-done | bytes 294944 | tf_op jit(solution)/shard_map/ppermute | solution.py:307
  60.2 0.7 shard_map.85
  60.9 2.8 %shard_map.86 = (bf16[2,96,768]{2,1,0:T(8,128)(2,1)S(1)}, f32[8,128]{1,0:T(8,128)S(1)}) custom-call(s32[2]{0:T(128)S(1)} %pad_add_fusion.where, bf16[2,2,96,768]{3,2,1,0:T(8,128)(2,1)S(1)} %get-tuple-element.108.refs_0_.refs_6_, bf16[2,2,96,768]{3,2,1,0:T(8,128)(2,1)S(1)} %collective-permute-done.23.refs_1_.refs_7_, ...), custom_call_target="tpu_custom_call" | custom-call | flops 1000 | bytes 1000 | tf_op jit(solution)/shard_map/pallas_call | solution.py:50
  63.7 6.7 %collective-permute-done.20.refs_1_ = bf16[2,2,96,768]{3,2,1,0:T(8,128)(2,1)S(1)} collective-permute-done((bf16[2,2,96,768]{3,2,1,0:T(8,128)(2,1)S(1)}, bf16[2,2,96,768]{3,2,1,0:T(8,128)(2,1)S(1)}, u32[]{:S(2)}, u32[]{:S(2)}) %collective-permute-start.20) | collective-permute-done | bytes 589856 | tf_op jit(solution)/shard_map/ppermute | solution.py:310
  70.4 7.5 %collective-permute-done.21.refs_2_.refs_22_.refs_0_ = bf16[192,1152]{1,0:T(8,128)(2,1)S(1)} collective-permute-done((bf16[192,1152]{1,0:T(8,128)(2,1)S(1)}, bf16[192,1152]{1,0:T(8,128)(2,1)S(1)}, u32[]{:S(2)}, u32[]{:S(2)}) %collective-permute-start.21) | collective-permute-done | bytes 442400 | tf_op jit(solution)/shard_map/ppermute | solution.py:313
  77.9 1.1 shard_map.87
  79.2 0.6 collective-permute-start.19
  79.8 1.5 %collective-permute-start.24 = (bf16[3,96,768]{2,1,0:T(8,128)(2,1)S(1)}, bf16[3,96,768]{2,1,0:T(8,128)(2,1)S(1)}, u32[]{:S(2)}, u32[]{:S(2)}) collective-permute-start(bf16[3,96,768]{2,1,0:T(8,128)(2,1)S(1)} %get-tuple-element.111), channel_id=1, source_target_pairs={{0,1},{1,0},{2,3},{3,2},{4,5},{5,4},{6,7},{7,6},{8,9},{9,8},{10,11... | collective-permute-start | bytes 1327112 | tf_op jit(solution)/shard_map/ppermute | solution.py:313
  81.3 1.2 collective-permute-start.26
  82.5 9.4 %collective-permute-done.26.refs_4_ = bf16[2,96,768]{2,1,0:T(8,128)(2,1)S(1)} collective-permute-done((bf16[2,96,768]{2,1,0:T(8,128)(2,1)S(1)}, bf16[2,96,768]{2,1,0:T(8,128)(2,1)S(1)}, u32[]{:S(2)}, u32[]{:S(2)}) %collective-permute-start.26) | collective-permute-done | bytes 294944 | tf_op jit(solution)/shard_map/ppermute | solution.py:316
  91.9 2.8 %shard_map.88 = (bf16[2,96,768]{2,1,0:T(8,128)(2,1)S(1)}, f32[8,128]{1,0:T(8,128)S(1)}) custom-call(s32[2]{0:T(128)S(1)} %pad_add_fusion.where, bf16[2,2,96,768]{3,2,1,0:T(8,128)(2,1)S(1)} %get-tuple-element.112.refs_0_.refs_10_, bf16[2,2,96,768]{3,2,1,0:T(8,128)(2,1)S(1)} %collective-permute-done.25.refs_1_.refs_11_, ...), custom_call_target="tpu_custom_call" | custom-call | flops 1000 | bytes 1000 | tf_op jit(solution)/shard_map/pallas_call | solution.py:50
  94.9 1.1 shard_map.89
  96.2 0.5 collective-permute-start.31
  97.2 7.3 %collective-permute-done.28.refs_4_ = bf16[2,96,768]{2,1,0:T(8,128)(2,1)S(1)} collective-permute-done((bf16[2,96,768]{2,1,0:T(8,128)(2,1)S(1)}, bf16[2,96,768]{2,1,0:T(8,128)(2,1)S(1)}, u32[]{:S(2)}, u32[]{:S(2)}) %collective-permute-start.28) | collective-permute-done | bytes 294944 | tf_op jit(solution)/shard_map/ppermute | solution.py:316
  105.0 2.8 %shard_map.90 = (bf16[2,96,768]{2,1,0:T(8,128)(2,1)S(1)}, f32[8,128]{1,0:T(8,128)S(1)}) custom-call(s32[2]{0:T(128)S(1)} %pad_add_fusion.where, bf16[2,2,96,768]{3,2,1,0:T(8,128)(2,1)S(1)} %get-tuple-element.116.refs_0_.refs_14_, bf16[2,2,96,768]{3,2,1,0:T(8,128)(2,1)S(1)} %collective-permute-done.27.refs_1_.refs_15_, ...), custom_call_target="tpu_custom_call" | custom-call | flops 1000 | bytes 1000 | tf_op jit(solution)/shard_map/pallas_call | solution.py:50
  108.1 4.6 %shard_map.91 = (f32[384,3072]{1,0:T(8,128)S(1)}, f32[1536,768]{1,0:T(8,128)S(1)}, f32[8,128]{1,0:T(8,128)S(1)}) custom-call(s32[2]{0:T(128)S(1)} %pad_add_fusion.where, bf16[96,384]{1,0:T(8,128)(2,1)S(1)} %get-tuple-element.121.refs_0_, bf16[2,96,768]{2,1,0:T(8,128)(2,1)S(1)} %pad_maximum_fusion.refs_0_.refs_1_, ...), custom_call_target="tpu_custom_call" | custom-call | flops 1000 | bytes 1000 | tf_op jit(solution)/shard_map/pallas_call | solution.py:50
  112.7 2.0 %collective-permute-done.30.refs_0_.refs_1_ = bf16[3,96,768]{2,1,0:T(8,128)(2,1)S(1)} collective-permute-done((bf16[3,96,768]{2,1,0:T(8,128)(2,1)S(1)}, bf16[3,96,768]{2,1,0:T(8,128)(2,1)S(1)}, u32[]{:S(2)}, u32[]{:S(2)}) %collective-permute-start.30) | collective-permute-done | bytes 442400 | tf_op jit(solution)/shard_map/ppermute | solution.py:313
  114.7 0.6 shard_map.92
  115.9 0.8 collective-permute-done.34.refs_2_
  117.2 4.7 %shard_map.93 = (f32[384,3072]{1,0:T(8,128)}, f32[1536,768]{1,0:T(8,128)}, f32[8,128]{1,0:T(8,128)S(1)}) custom-call(s32[2]{0:T(128)S(1)} %pad_add_fusion.where, bf16[192,1152]{1,0:T(8,128)(2,1)S(1)} %collective-permute-done.21.refs_2_.refs_22_.refs_0_, bf16[3,96,768]{2,1,0:T(8,128)(2,1)S(1)} %collective-permute-done.30.refs_0_.refs_1_, ...), custom_call_target="tpu_custom_call" | custom-call | flops 1000 | bytes 1000 | tf_op jit(solution)/shard_map/pallas_call | solution.py:50
  121.9 1.3 %shard_map.94 = (bf16[96,768]{1,0:T(8,128)(2,1)}, bf16[96,768]{1,0:T(8,128)(2,1)}, f32[8,128]{1,0:T(8,128)}) custom-call(s32[2]{0:T(128)S(1)} %pad_add_fusion.where, bf16[2,96,768]{2,1,0:T(8,128)(2,1)S(1)} %get-tuple-element.95.refs_0_, bf16[2,96,768]{2,1,0:T(8,128)(2,1)S(1)} %collective-permute-done.29.refs_1_, f32[8,128]{1,0:T(8,128)S(1)} %get-tuple-element.133.refs_2_), custom_call_target="tpu_custom_call" | custom-call | flops 1000 | bytes 1000 | tf_op jit(solution)/shard_map/pallas_call | solution.py:50
  (49 shorter events, 5.2 us)
Async XLA Ops:
  7.5 4.1 %collective-permute-start = (bf16[96,768]{1,0:T(8,128)(2,1)S(1)}, bf16[96,768]{1,0:T(8,128)(2,1)S(1)}, u32[]{:S(2)}, u32[]{:S(2)}) collective-permute-start(bf16[96,768]{1,0:T(8,128)(2,1)S(1)} %get-tuple-element.72), channel_id=1, source_target_pairs={{0,8},{8,0},{16,24},{24,16},{1,9},{9,1},{17,25},{25,17},{2,10},{10... | collective-permute-start | bytes 442376 | tf_op jit(solution)/shard_map/ppermute | solution.py:307
  8.0 3.6 %collective-permute-start.1 = (bf16[96,768]{1,0:T(8,128)(2,1)S(1)}, bf16[96,768]{1,0:T(8,128)(2,1)S(1)}, u32[]{:S(2)}, u32[]{:S(2)}) collective-permute-start(bf16[96,768]{1,0:T(8,128)(2,1)S(1)} %get-tuple-element.73), channel_id=1, source_target_pairs={{0,8},{8,0},{16,24},{24,16},{1,9},{9,1},{17,25},{25,17},{2,10},{10... | collective-permute-start | bytes 442376 | tf_op jit(solution)/shard_map/ppermute | solution.py:307
  8.1 3.5 %collective-permute-start.2 = (bf16[96,768]{1,0:T(8,128)(2,1)S(1)}, bf16[96,768]{1,0:T(8,128)(2,1)S(1)}, u32[]{:S(2)}, u32[]{:S(2)}) collective-permute-start(bf16[96,768]{1,0:T(8,128)(2,1)S(1)} %get-tuple-element.74), channel_id=1, source_target_pairs={{0,8},{8,0},{16,24},{24,16},{1,9},{9,1},{17,25},{25,17},{2,10},{10... | collective-permute-start | bytes 442376 | tf_op jit(solution)/shard_map/ppermute | solution.py:307
  8.5 3.1 %collective-permute-start.3 = (bf16[96,768]{1,0:T(8,128)(2,1)S(1)}, bf16[96,768]{1,0:T(8,128)(2,1)S(1)}, u32[]{:S(2)}, u32[]{:S(2)}) collective-permute-start(bf16[96,768]{1,0:T(8,128)(2,1)S(1)} %get-tuple-element.75), channel_id=1, source_target_pairs={{0,8},{8,0},{16,24},{24,16},{1,9},{9,1},{17,25},{25,17},{2,10},{10... | collective-permute-start | bytes 442376 | tf_op jit(solution)/shard_map/ppermute | solution.py:307
  8.6 12.3 %collective-permute-start.5 = (bf16[2,96,768]{2,1,0:T(8,128)(2,1)S(1)}, bf16[2,96,768]{2,1,0:T(8,128)(2,1)S(1)}, u32[]{:S(2)}, u32[]{:S(2)}) collective-permute-start(bf16[2,96,768]{2,1,0:T(8,128)(2,1)S(1)} %pad_maximum_fusion.refs_0_.refs_1_), channel_id=1, source_target_pairs={{0,2},{2,4},{4,6},{6,0},{1,3},{3,5},{5,7},{7,1},{8,10},{10,12},{12... | collective-permute-start | bytes 884744 | tf_op jit(solution)/shard_map/ppermute | solution.py:316
  12.3 20.5 %collective-permute-start.4 = (bf16[2,2,96,768]{3,2,1,0:T(8,128)(2,1)S(1)}, bf16[2,2,96,768]{3,2,1,0:T(8,128)(2,1)S(1)}, u32[]{:S(2)}, u32[]{:S(2)}) collective-permute-start(bf16[2,2,96,768]{3,2,1,0:T(8,128)(2,1)S(1)} %get-tuple-element.77.refs_0_), channel_id=1, source_target_pairs={{0,16},{8,24},{16,0},{24,8},{1,17},{9,25},{17,1},{25,9},{2,18},{10... | collective-permute-start | bytes 1769480 | tf_op jit(solution)/shard_map/ppermute | solution.py:310
  13.9 6.9 %collective-permute-start.6 = (bf16[96,1152]{1,0:T(8,128)(2,1)S(1)}, bf16[96,1152]{1,0:T(8,128)(2,1)S(1)}, u32[]{:S(2)}, u32[]{:S(2)}) collective-permute-start(bf16[96,1152]{1,0:T(8,128)(2,1)S(1)} %get-tuple-element.80), channel_id=1, source_target_pairs={{0,1},{1,0},{2,3},{3,2},{4,5},{5,4},{6,7},{7,6},{8,9},{9,8},{10,11... | collective-permute-start | bytes 663560 | tf_op jit(solution)/shard_map/ppermute | solution.py:313
  23.7 3.5 %collective-permute-start.8 = (bf16[2,96,768]{2,1,0:T(8,128)(2,1)S(1)}, bf16[2,96,768]{2,1,0:T(8,128)(2,1)S(1)}, u32[]{:S(2)}, u32[]{:S(2)}) collective-permute-start(bf16[2,96,768]{2,1,0:T(8,128)(2,1)S(1)} %get-tuple-element.84), channel_id=1, source_target_pairs={{0,8},{8,0},{16,24},{24,16},{1,9},{9,1},{17,25},{25,17},{2,10},{10... | collective-permute-start | bytes 884744 | tf_op jit(solution)/shard_map/ppermute | solution.py:307
  23.8 3.4 %collective-permute-start.9 = (bf16[2,96,768]{2,1,0:T(8,128)(2,1)S(1)}, bf16[2,96,768]{2,1,0:T(8,128)(2,1)S(1)}, u32[]{:S(2)}, u32[]{:S(2)}) collective-permute-start(bf16[2,96,768]{2,1,0:T(8,128)(2,1)S(1)} %get-tuple-element.85), channel_id=1, source_target_pairs={{0,8},{8,0},{16,24},{24,16},{1,9},{9,1},{17,25},{25,17},{2,10},{10... | collective-permute-start | bytes 884744 | tf_op jit(solution)/shard_map/ppermute | solution.py:307
  24.3 10.8 %collective-permute-start.11 = (bf16[2,96,768]{2,1,0:T(8,128)(2,1)S(1)}, bf16[2,96,768]{2,1,0:T(8,128)(2,1)S(1)}, u32[]{:S(2)}, u32[]{:S(2)}) collective-permute-start(bf16[2,96,768]{2,1,0:T(8,128)(2,1)S(1)} %collective-permute-done.5.refs_0_.refs_5_), channel_id=1, source_target_pairs={{0,2},{2,4},{4,6},{6,0},{1,3},{3,5},{5,7},{7,1},{8,10},{10,12},{12... | collective-permute-start | bytes 884744 | tf_op jit(solution)/shard_map/ppermute | solution.py:316
  25.7 7.1 %collective-permute-start.7 = (bf16[96,1152]{1,0:T(8,128)(2,1)S(1)}, bf16[96,1152]{1,0:T(8,128)(2,1)S(1)}, u32[]{:S(2)}, u32[]{:S(2)}) collective-permute-start(bf16[96,1152]{1,0:T(8,128)(2,1)S(1)} %get-tuple-element.82), channel_id=1, source_target_pairs={{0,1},{1,0},{2,3},{3,2},{4,5},{5,4},{6,7},{7,6},{8,9},{9,8},{10,11... | collective-permute-start | bytes 663560 | tf_op jit(solution)/shard_map/ppermute | solution.py:313
  34.0 7.8 %collective-permute-start.10 = (bf16[2,2,96,768]{3,2,1,0:T(8,128)(2,1)S(1)}, bf16[2,2,96,768]{3,2,1,0:T(8,128)(2,1)S(1)}, u32[]{:S(2)}, u32[]{:S(2)}) collective-permute-start(bf16[2,2,96,768]{3,2,1,0:T(8,128)(2,1)S(1)} %get-tuple-element.88.refs_0_.refs_2_), channel_id=1, source_target_pairs={{0,8},{8,0},{16,24},{24,16},{1,9},{9,1},{17,25},{25,17},{2,10},{10... | collective-permute-start | bytes 1769480 | tf_op jit(solution)/shard_map/ppermute | solution.py:307
  34.1 16.5 %collective-permute-start.15 = (bf16[2,2,96,768]{3,2,1,0:T(8,128)(2,1)S(1)}, bf16[2,2,96,768]{3,2,1,0:T(8,128)(2,1)S(1)}, u32[]{:S(2)}, u32[]{:S(2)}) collective-permute-start(bf16[2,2,96,768]{3,2,1,0:T(8,128)(2,1)S(1)} %get-tuple-element.96.refs_0_), channel_id=1, source_target_pairs={{0,16},{8,24},{16,0},{24,8},{1,17},{9,25},{17,1},{25,9},{2,18},{10... | collective-permute-start | bytes 1769480 | tf_op jit(solution)/shard_map/ppermute | solution.py:310
  37.9 1.8 %collective-permute-start.12 = (bf16[2,96,768]{2,1,0:T(8,128)(2,1)S(1)}, bf16[2,96,768]{2,1,0:T(8,128)(2,1)S(1)}, u32[]{:S(2)}, u32[]{:S(2)}) collective-permute-start(bf16[2,96,768]{2,1,0:T(8,128)(2,1)S(1)} %get-tuple-element.91), channel_id=1, source_target_pairs={{0,8},{8,0},{16,24},{24,16},{1,9},{9,1},{17,25},{25,17},{2,10},{10... | collective-permute-start | bytes 884744 | tf_op jit(solution)/shard_map/ppermute | solution.py:307
  38.0 12.6 %collective-permute-start.16 = (bf16[3,96,768]{2,1,0:T(8,128)(2,1)S(1)}, bf16[3,96,768]{2,1,0:T(8,128)(2,1)S(1)}, u32[]{:S(2)}, u32[]{:S(2)}) collective-permute-start(bf16[3,96,768]{2,1,0:T(8,128)(2,1)S(1)} %get-tuple-element.97), channel_id=1, source_target_pairs={{0,1},{1,0},{2,3},{3,2},{4,5},{5,4},{6,7},{7,6},{8,9},{9,8},{10,11... | collective-permute-start | bytes 1327112 | tf_op jit(solution)/shard_map/ppermute | solution.py:313
  39.6 1.6 %collective-permute-start.13 = (bf16[2,96,768]{2,1,0:T(8,128)(2,1)S(1)}, bf16[2,96,768]{2,1,0:T(8,128)(2,1)S(1)}, u32[]{:S(2)}, u32[]{:S(2)}) collective-permute-start(bf16[2,96,768]{2,1,0:T(8,128)(2,1)S(1)} %get-tuple-element.92), channel_id=1, source_target_pairs={{0,8},{8,0},{16,24},{24,16},{1,9},{9,1},{17,25},{25,17},{2,10},{10... | collective-permute-start | bytes 884744 | tf_op jit(solution)/shard_map/ppermute | solution.py:307
  39.7 12.0 %collective-permute-start.14 = (bf16[2,96,768]{2,1,0:T(8,128)(2,1)S(1)}, bf16[2,96,768]{2,1,0:T(8,128)(2,1)S(1)}, u32[]{:S(2)}, u32[]{:S(2)}) collective-permute-start(bf16[2,96,768]{2,1,0:T(8,128)(2,1)S(1)} %collective-permute-done.11.refs_0_.refs_3_.refs_9_), channel_id=1, source_target_pairs={{0,2},{2,4},{4,6},{6,0},{1,3},{3,5},{5,7},{7,1},{8,10},{10,12},{12... | collective-permute-start | bytes 884744 | tf_op jit(solution)/shard_map/ppermute | solution.py:316
  54.5 4.1 %collective-permute-start.17 = (bf16[2,96,768]{2,1,0:T(8,128)(2,1)S(1)}, bf16[2,96,768]{2,1,0:T(8,128)(2,1)S(1)}, u32[]{:S(2)}, u32[]{:S(2)}) collective-permute-start(bf16[2,96,768]{2,1,0:T(8,128)(2,1)S(1)} %get-tuple-element.101), channel_id=1, source_target_pairs={{0,8},{8,0},{16,24},{24,16},{1,9},{9,1},{17,25},{25,17},{2,10},{10... | collective-permute-start | bytes 884744 | tf_op jit(solution)/shard_map/ppermute | solution.py:307
  54.6 6.3 %collective-permute-start.23 = (bf16[2,2,96,768]{3,2,1,0:T(8,128)(2,1)S(1)}, bf16[2,2,96,768]{3,2,1,0:T(8,128)(2,1)S(1)}, u32[]{:S(2)}, u32[]{:S(2)}) collective-permute-start(bf16[2,2,96,768]{3,2,1,0:T(8,128)(2,1)S(1)} %get-tuple-element.108.refs_0_.refs_6_), channel_id=1, source_target_pairs={{0,8},{8,0},{16,24},{24,16},{1,9},{9,1},{17,25},{25,17},{2,10},{10... | collective-permute-start | bytes 1769480 | tf_op jit(solution)/shard_map/ppermute | solution.py:307
  55.1 15.3 %collective-permute-start.20 = (bf16[2,2,96,768]{3,2,1,0:T(8,128)(2,1)S(1)}, bf16[2,2,96,768]{3,2,1,0:T(8,128)(2,1)S(1)}, u32[]{:S(2)}, u32[]{:S(2)}) collective-permute-start(bf16[2,2,96,768]{3,2,1,0:T(8,128)(2,1)S(1)} %get-tuple-element.105.refs_0_), channel_id=1, source_target_pairs={{0,16},{8,24},{16,0},{24,8},{1,17},{9,25},{17,1},{25,9},{2,18},{10... | collective-permute-start | bytes 1769480 | tf_op jit(solution)/shard_map/ppermute | solution.py:310
  56.6 13.8 %collective-permute-start.22 = (bf16[3,96,768]{2,1,0:T(8,128)(2,1)S(1)}, bf16[3,96,768]{2,1,0:T(8,128)(2,1)S(1)}, u32[]{:S(2)}, u32[]{:S(2)}) collective-permute-start(bf16[3,96,768]{2,1,0:T(8,128)(2,1)S(1)} %get-tuple-element.107), channel_id=1, source_target_pairs={{0,1},{1,0},{2,3},{3,2},{4,5},{5,4},{6,7},{7,6},{8,9},{9,8},{10,11... | collective-permute-start | bytes 1327112 | tf_op jit(solution)/shard_map/ppermute | solution.py:313
  58.1 19.8 %collective-permute-start.21 = (bf16[192,1152]{1,0:T(8,128)(2,1)S(1)}, bf16[192,1152]{1,0:T(8,128)(2,1)S(1)}, u32[]{:S(2)}, u32[]{:S(2)}) collective-permute-start(bf16[192,1152]{1,0:T(8,128)(2,1)S(1)} %get-tuple-element.106), channel_id=1, source_target_pairs={{0,1},{1,0},{2,3},{3,2},{4,5},{5,4},{6,7},{7,6},{8,9},{9,8},{10,11... | collective-permute-start | bytes 1327112 | tf_op jit(solution)/shard_map/ppermute | solution.py:313
  58.6 1.6 %collective-permute-start.18 = (bf16[2,96,768]{2,1,0:T(8,128)(2,1)S(1)}, bf16[2,96,768]{2,1,0:T(8,128)(2,1)S(1)}, u32[]{:S(2)}, u32[]{:S(2)}) collective-permute-start(bf16[2,96,768]{2,1,0:T(8,128)(2,1)S(1)} %get-tuple-element.102), channel_id=1, source_target_pairs={{0,8},{8,0},{16,24},{24,16},{1,9},{9,1},{17,25},{25,17},{2,10},{10... | collective-permute-start | bytes 884744 | tf_op jit(solution)/shard_map/ppermute | solution.py:307
  79.1 12.8 %collective-permute-start.25 = (bf16[2,2,96,768]{3,2,1,0:T(8,128)(2,1)S(1)}, bf16[2,2,96,768]{3,2,1,0:T(8,128)(2,1)S(1)}, u32[]{:S(2)}, u32[]{:S(2)}) collective-permute-start(bf16[2,2,96,768]{3,2,1,0:T(8,128)(2,1)S(1)} %get-tuple-element.112.refs_0_.refs_10_), channel_id=1, source_target_pairs={{0,8},{8,0},{16,24},{24,16},{1,9},{9,1},{17,25},{25,17},{2,10},{10... | collective-permute-start | bytes 1769480 | tf_op jit(solution)/shard_map/ppermute | solution.py:307
  79.2 15.7 %collective-permute-start.19 = (bf16[2,2,96,768]{3,2,1,0:T(8,128)(2,1)S(1)}, bf16[2,2,96,768]{3,2,1,0:T(8,128)(2,1)S(1)}, u32[]{:S(2)}, u32[]{:S(2)}) collective-permute-start(bf16[2,2,96,768]{3,2,1,0:T(8,128)(2,1)S(1)} %get-tuple-element.104.refs_0_), channel_id=1, source_target_pairs={{0,16},{8,24},{16,0},{24,8},{1,17},{9,25},{17,1},{25,9},{2,18},{10... | collective-permute-start | bytes 1769480 | tf_op jit(solution)/shard_map/ppermute | solution.py:310
  79.8 15.2 %collective-permute-start.24 = (bf16[3,96,768]{2,1,0:T(8,128)(2,1)S(1)}, bf16[3,96,768]{2,1,0:T(8,128)(2,1)S(1)}, u32[]{:S(2)}, u32[]{:S(2)}) collective-permute-start(bf16[3,96,768]{2,1,0:T(8,128)(2,1)S(1)} %get-tuple-element.111), channel_id=1, source_target_pairs={{0,1},{1,0},{2,3},{3,2},{4,5},{5,4},{6,7},{7,6},{8,9},{9,8},{10,11... | collective-permute-start | bytes 1327112 | tf_op jit(solution)/shard_map/ppermute | solution.py:313
  81.3 10.6 %collective-permute-start.26 = (bf16[2,96,768]{2,1,0:T(8,128)(2,1)S(1)}, bf16[2,96,768]{2,1,0:T(8,128)(2,1)S(1)}, u32[]{:S(2)}, u32[]{:S(2)}) collective-permute-start(bf16[2,96,768]{2,1,0:T(8,128)(2,1)S(1)} %get-tuple-element.113), channel_id=1, source_target_pairs={{0,2},{2,4},{4,6},{6,0},{1,3},{3,5},{5,7},{7,1},{8,10},{10,12},{12... | collective-permute-start | bytes 884744 | tf_op jit(solution)/shard_map/ppermute | solution.py:316
  94.7 9.8 %collective-permute-start.28 = (bf16[2,96,768]{2,1,0:T(8,128)(2,1)S(1)}, bf16[2,96,768]{2,1,0:T(8,128)(2,1)S(1)}, u32[]{:S(2)}, u32[]{:S(2)}) collective-permute-start(bf16[2,96,768]{2,1,0:T(8,128)(2,1)S(1)} %get-tuple-element.117), channel_id=1, source_target_pairs={{0,2},{2,4},{4,6},{6,0},{1,3},{3,5},{5,7},{7,1},{8,10},{10,12},{12... | collective-permute-start | bytes 884744 | tf_op jit(solution)/shard_map/ppermute | solution.py:316
  96.1 8.9 %collective-permute-start.27 = (bf16[2,2,96,768]{3,2,1,0:T(8,128)(2,1)S(1)}, bf16[2,2,96,768]{3,2,1,0:T(8,128)(2,1)S(1)}, u32[]{:S(2)}, u32[]{:S(2)}) collective-permute-start(bf16[2,2,96,768]{3,2,1,0:T(8,128)(2,1)S(1)} %get-tuple-element.116.refs_0_.refs_14_), channel_id=1, source_target_pairs={{0,8},{8,0},{16,24},{24,16},{1,9},{9,1},{17,25},{25,17},{2,10},{10... | collective-permute-start | bytes 1769480 | tf_op jit(solution)/shard_map/ppermute | solution.py:307
  96.2 11.9 %collective-permute-start.31 = (bf16[3,96,768]{2,1,0:T(8,128)(2,1)S(1)}, bf16[3,96,768]{2,1,0:T(8,128)(2,1)S(1)}, u32[]{:S(2)}, u32[]{:S(2)}) collective-permute-start(bf16[3,96,768]{2,1,0:T(8,128)(2,1)S(1)} %collective-permute-done.16.refs_2_.refs_17_), channel_id=1, source_target_pairs={{0,8},{8,0},{16,24},{24,16},{1,9},{9,1},{17,25},{25,17},{2,10},{10... | collective-permute-start | bytes 1327112 | tf_op jit(solution)/shard_map/ppermute | solution.py:307
  96.7 11.5 %collective-permute-start.32 = (bf16[3,96,768]{2,1,0:T(8,128)(2,1)S(1)}, bf16[3,96,768]{2,1,0:T(8,128)(2,1)S(1)}, u32[]{:S(2)}, u32[]{:S(2)}) collective-permute-start(bf16[3,96,768]{2,1,0:T(8,128)(2,1)S(1)} %collective-permute-done.22.refs_3_.refs_20_), channel_id=1, source_target_pairs={{0,8},{8,0},{16,24},{24,16},{1,9},{9,1},{17,25},{25,17},{2,10},{10... | collective-permute-start | bytes 1327112 | tf_op jit(solution)/shard_map/ppermute | solution.py:307
  96.7 11.4 %collective-permute-start.33 = (bf16[3,96,768]{2,1,0:T(8,128)(2,1)S(1)}, bf16[3,96,768]{2,1,0:T(8,128)(2,1)S(1)}, u32[]{:S(2)}, u32[]{:S(2)}) collective-permute-start(bf16[3,96,768]{2,1,0:T(8,128)(2,1)S(1)} %collective-permute-done.24.refs_2_.refs_23_), channel_id=1, source_target_pairs={{0,8},{8,0},{16,24},{24,16},{1,9},{9,1},{17,25},{25,17},{2,10},{10... | collective-permute-start | bytes 1327112 | tf_op jit(solution)/shard_map/ppermute | solution.py:307
  104.5 10.2 %collective-permute-start.30 = (bf16[3,96,768]{2,1,0:T(8,128)(2,1)S(1)}, bf16[3,96,768]{2,1,0:T(8,128)(2,1)S(1)}, u32[]{:S(2)}, u32[]{:S(2)}) collective-permute-start(bf16[3,96,768]{2,1,0:T(8,128)(2,1)S(1)} %get-tuple-element.120), channel_id=1, source_target_pairs={{0,1},{1,0},{2,3},{3,2},{4,5},{5,4},{6,7},{7,6},{8,9},{9,8},{10,11... | collective-permute-start | bytes 1327112 | tf_op jit(solution)/shard_map/ppermute | solution.py:313
  107.8 14.1 %collective-permute-start.29 = (bf16[2,96,768]{2,1,0:T(8,128)(2,1)S(1)}, bf16[2,96,768]{2,1,0:T(8,128)(2,1)S(1)}, u32[]{:S(2)}, u32[]{:S(2)}) collective-permute-start(bf16[2,96,768]{2,1,0:T(8,128)(2,1)S(1)} %get-tuple-element.119), channel_id=1, source_target_pairs={{0,2},{2,4},{4,6},{6,0},{1,3},{3,5},{5,7},{7,1},{8,10},{10,12},{12... | collective-permute-start | bytes 884744 | tf_op jit(solution)/shard_map/ppermute | solution.py:316
  115.3 1.4 %collective-permute-start.34 = (bf16[96,768]{1,0:T(8,128)(2,1)S(1)}, bf16[96,768]{1,0:T(8,128)(2,1)S(1)}, u32[]{:S(2)}, u32[]{:S(2)}) collective-permute-start(bf16[96,768]{1,0:T(8,128)(2,1)S(1)} %get-tuple-element.127), channel_id=1, source_target_pairs={{0,8},{8,0},{16,24},{24,16},{1,9},{9,1},{17,25},{25,17},{2,10},{10... | collective-permute-start | bytes 442376 | tf_op jit(solution)/shard_map/ppermute | solution.py:307
  115.3 1.6 %collective-permute-start.35 = (bf16[96,768]{1,0:T(8,128)(2,1)S(1)}, bf16[96,768]{1,0:T(8,128)(2,1)S(1)}, u32[]{:S(2)}, u32[]{:S(2)}) collective-permute-start(bf16[96,768]{1,0:T(8,128)(2,1)S(1)} %get-tuple-element.128), channel_id=1, source_target_pairs={{0,8},{8,0},{16,24},{24,16},{1,9},{9,1},{17,25},{25,17},{2,10},{10... | collective-permute-start | bytes 442376 | tf_op jit(solution)/shard_map/ppermute | solution.py:307
  115.8 1.4 %collective-permute-start.36 = (bf16[96,768]{1,0:T(8,128)(2,1)S(1)}, bf16[96,768]{1,0:T(8,128)(2,1)S(1)}, u32[]{:S(2)}, u32[]{:S(2)}) collective-permute-start(bf16[96,768]{1,0:T(8,128)(2,1)S(1)} %get-tuple-element.129), channel_id=1, source_target_pairs={{0,8},{8,0},{16,24},{24,16},{1,9},{9,1},{17,25},{25,17},{2,10},{10... | collective-permute-start | bytes 442376 | tf_op jit(solution)/shard_map/ppermute | solution.py:307

commit v3 on v0

v3 whole, which is shorter than its diff:
```python
import functools

import jax
import jax.numpy as jnp
from jax import lax
from jax.experimental import pallas as pl
from jax.experimental.pallas import tpu as pltpu
from jax.sharding import PartitionSpec as P

BF16, F32 = jnp.bfloat16, jnp.float32
MIB = 1024 * 1024
IN_VMEM = pl.BlockSpec(memory_space=pltpu.VMEM)
IN_SMEM = pl.BlockSpec(memory_space=pltpu.SMEM)
IN_HBM = pl.BlockSpec(memory_space=pltpu.HBM)
ANYWHERE = pl.BlockSpec(memory_space=pl.ANY)
TOKEN = jax.ShapeDtypeStruct((8, 128), F32)


def gelu_parts(hidden_pre):
    normal_cdf = 0.5 * (1.0 + lax.erf(hidden_pre * 0.7071067811865476))
    normal_pdf = jnp.exp(-0.5 * hidden_pre * hidden_pre) * 0.3989422804014327
    return (hidden_pre * normal_cdf, normal_cdf + hidden_pre * normal_pdf)


def dot(left, right, left_dim, right_dim):
    return lax.dot_general(
        left, right, (((left_dim,), (right_dim,)), ((), ())), preferred_element_type=F32
    )


def shape(*sizes, kind=BF16):
    return jax.ShapeDtypeStruct(sizes, kind)


class Chain:
    def __init__(self, where):
        self.where = where
        self.token = jnp.zeros(TOKEN.shape, TOKEN.dtype)

    def __call__(
        self, kernel, inputs, out_shapes, after=(), scratch=(), limit=16, specs=None, to=IN_VMEM
    ):
        n_in, n_after, n_out = len(inputs), len(after) + 1, len(out_shapes)

        def body(where, *refs):
            ins = refs[:n_in]
            outs = refs[n_in + n_after : n_in + n_after + n_out]
            token = refs[n_in + n_after + n_out]
            kernel(where, ins, outs, refs[n_in + n_after + n_out + 1 :])
            token[...] = jnp.zeros(token.shape, token.dtype)

        *results, self.token = pl.pallas_call(
            body,
            in_specs=[IN_SMEM] + (specs or [IN_VMEM] * n_in) + [ANYWHERE] * n_after,
            out_specs=[to] * n_out + [IN_VMEM],
            out_shape=list(out_shapes) + [TOKEN],
            scratch_shapes=list(scratch),
            compiler_params=pltpu.CompilerParams(vmem_limit_bytes=limit * MIB),
            cost_estimate=pl.CostEstimate(flops=1000, bytes_accessed=1000, transcendentals=0),
        )(self.where, *inputs, *after, self.token)
        return results


def block_of(where, rel, index, width):
    core = where[0] if rel == 0 else 1 - where[0]
    return pl.ds(pl.multiple_of((2 * index + core) * width, 128), width)


def part_of(where, owner, part):
    return pl.ds(pl.multiple_of(owner * part, 128), part)


def cut_shares(where, both, features, messages):
    for k, message in enumerate(messages, 1):
        part = message.shape[1] - features
        owner = lax.rem(where[1] + k, len(messages) + 1)
        message[:, :part] = both[:, part_of(where, owner, part)]
        message[:, part:] = both[:, features : 2 * features]


def fetch(where, rel, sources, targets, semaphores):
    from_in, from_out = sources
    weight_in, weight_out = targets
    copies = []
    for index in range(weight_in.shape[0]):
        cut = block_of(where, rel, index, weight_in.shape[2])
        for source, target in (
            (from_in.at[:, cut], weight_in.at[index]),
            (from_out.at[cut, :], weight_out.at[index]),
        ):
            copies.append(pltpu.make_async_copy(source, target, semaphores.at[len(copies)]))
            copies[-1].start()
    return copies


def fetch_kernel(where, ins, outs, scratch):
    copies = fetch(where, 1, ins[2:], outs[1:3], scratch[0])
    features = ins[0].shape[1]
    outs[0][:, :features] = ins[0][...]
    outs[0][:, features:] = ins[1][...]
    cut_shares(where, outs[0], features, outs[3:])
    for copy in copies:
        copy.wait()


def other_kernel(where, ins, outs, scratch):
    both, weight_in, weight_out = ins
    features = weight_in.shape[1]
    for index in range(weight_in.shape[0]):
        outs[0][index] = dot(both[:, :features], weight_in[index], 1, 0).astype(BF16)
        outs[1][index] = dot(both[:, features:], weight_out[index], 1, 1).astype(BF16)


def own_kernel(where, ins, outs, scratch):
    both, *sources = ins
    weight_in, weight_out, hidden, grad = outs
    copies = fetch(where, 0, sources, outs[:2], scratch[0])
    features = weight_in.shape[1]
    for index in range(weight_in.shape[0]):
        copies[2 * index].wait()
        hidden[index] = dot(both[:, :features], weight_in[index], 1, 0).astype(BF16)
        copies[2 * index + 1].wait()
        grad[index] = dot(both[:, features:], weight_out[index], 1, 1).astype(BF16)


def arrive_kernel(where, ins, outs, scratch):
    outs[0][...] = ins[0][...]
    for number, value in enumerate(ins[1:]):
        rows = value.shape[0]
        outs[1][number * rows : (number + 1) * rows, :] = value[...]


def join_kernel(where, ins, outs, scratch):
    for which in range(2):
        total = ins[which][...].astype(F32) + ins[2 + which][...].astype(F32)
        outs[0][which] = total.astype(BF16)


def hidden_kernel(keep, where, ins, outs, scratch):
    own, other, own_in, own_out, other_in, other_out = ins
    if keep:
        outs[-2][...] = other_in[...]
        outs[-1][...] = other_out[...]
    cut_shares(where, own, own_in.shape[1], outs[1 : len(outs) - 2 * keep])
    features = own_in.shape[1]
    tokens, cotangents = slice(0, features), slice(features, 2 * features)
    for index in range(own_in.shape[0]):
        hidden = dot(own[:, tokens], own_in[index], 1, 0)
        hidden += dot(other[:, tokens], other_in[index], 1, 0)
        outs[0][0, index] = hidden.astype(BF16)
        grad = dot(own[:, cotangents], own_out[index], 1, 1)
        grad += dot(other[:, cotangents], other_out[index], 1, 1)
        outs[0][1, index] = grad.astype(BF16)


def gelu_kernel(n_depth, where, ins, outs, scratch):
    blocks = ins[0].shape[1]
    depth = where[1]
    n_late = (n_depth - 1) * (len(outs) - n_depth)
    ins, late = ins[: len(ins) - n_late], ins[len(ins) - n_late :]
    for index in range(blocks):
        hidden, grad = ins[0][0, index].astype(F32), ins[0][1, index].astype(F32)
        for other in ins[1:]:
            hidden += other[0, index].astype(F32)
            grad += other[1, index].astype(F32)
        value, slope = gelu_parts(hidden)
        act, pre = value.astype(BF16), (grad * slope).astype(BF16)
        outs[0][0, index] = act
        outs[0][1, index] = pre
        for message in outs[1:]:
            message[index] = pre
    for k in range(1, n_depth):
        outs[k][blocks] = outs[0][0, lax.rem(depth + k, n_depth)]
    for message in outs[n_depth:]:
        message[blocks] = outs[0][0, depth]
        for number, value in enumerate(late, 1):
            message[number * (blocks + 1) : (number + 1) * (blocks + 1)] = value[...]


def model_kernel(where, ins, outs, scratch):
    pair, *weights = ins
    for rel, target in enumerate(outs):
        weight_in, weight_out = weights[2 * rel : 2 * rel + 2]
        out = grad = 0.0
        for index in range(pair.shape[1]):
            out += dot(pair[0, index], weight_out[index], 1, 0)
            grad += dot(pair[1, index], weight_in[index], 1, 1)
        target[0] = out.astype(BF16)
        target[1] = grad.astype(BF16)


def sum_kernel(where, ins, outs, scratch):
    for index in range(2):
        total = sum(value[index].astype(F32) for value in ins)
        if len(outs) == 1:
            outs[0][index] = total.astype(BF16)
        else:
            outs[index][...] = total.astype(BF16)


def early_kernel(near, where, ins, outs, scratch):
    all_tokens, all_cotangents, all_values = scratch
    own_in, own_out, other_in, other_out = outs
    blocks, part, width = own_in.shape
    features = own_out.shape[1]
    pairs, shares, came = ins[2 * near : 3 * near], ins[3 * near : 3 * near + 2], ins[3 * near + 2 :]
    rows = ins[0].shape[0]
    for rel in range(2):
        here = slice(rel * part, (rel + 1) * part)
        there = slice(rel * features, (rel + 1) * features)
        for number in range(near):
            at, source = slice(number * rows, (number + 1) * rows), ins[rel * near + number]
            all_tokens[at, here] = source[:, part_of(where, where[1], part)]
            all_cotangents[at, there] = source[:, features : 2 * features]
        for number in range(len(came)):
            at, source = slice(number * rows, (number + 1) * rows), shares[rel]
            start = (near + number) * rows
            all_tokens[start : start + rows, here] = source[at, :part]
            all_cotangents[start : start + rows, there] = source[at, part:]
    acts = [pair.at[0].at[where[1]] for pair in pairs] + [value.at[blocks] for value in came]
    pres = [[pair.at[1].at[index] for index in range(blocks)] for pair in pairs]
    pres += [[value.at[index] for index in range(blocks)] for value in came]

    def fill(sources):
        for number, source in enumerate(sources):
            all_values[number * rows : (number + 1) * rows, :] = source[...]

    for index in range(blocks):
        fill([value[index] for value in pres])
        term = dot(all_tokens[...], all_values[...], 0, 0)
        own_in[index] = term[:part]
        other_in[index] = term[part:].astype(BF16)
    fill(acts)
    term = dot(all_values[...], all_cotangents[...], 0, 0)
    own_out[...] = term[:, :features]
    other_out[...] = term[:, features:].astype(BF16)


def relay_kernel(where, ins, outs, scratch):
    outs[0][...] = ins[0][...]


def last_kernel(groups, where, ins, outs, scratch):
    all_tokens, all_cotangents, all_values, held_in, held_out, semaphores = scratch
    own, pair, late, *ins = ins
    early = ins[-4:]
    shares, ins = ins[: 2 * groups], ins[2 * groups :]
    _, blocks, rows, width = pair.shape
    part, features = all_tokens.shape[1], all_cotangents.shape[1]
    before, came, swapped = ins[:groups], ins[groups : 2 * groups], ins[2 * groups : 3 * groups]
    values = ([[pair.at[1].at[index] for index in range(blocks)]], [])
    values[0][0].append(pair.at[0].at[where[1]])
    for number in range(groups + 1):
        start = number * (blocks + 1)
        values[1].append([late.at[start + index] for index in range(blocks + 1)])
    for value in list(before) + list(came):
        values[0].append([value.at[index] for index in range(blocks + 1)])
    for value in swapped:
        values[1].append([value.at[index] for index in range(blocks + 1)])
    all_tokens[:rows, :] = own[:, part_of(where, where[1], part)]
    all_cotangents[:rows, :] = own[:, features : 2 * features]
    for number in range(2 * groups):
        start = (number + 1) * rows
        all_tokens[start : start + rows, :] = shares[number][:, :part]
        all_cotangents[start : start + rows, :] = shares[number][:, part:]
    copies = []

    def fill(sources):
        for number, source in enumerate(sources):
            all_values[number * rows : (number + 1) * rows, :] = source[...]

    def put(held, target, at, term):
        held[at] = term
        copies.append(pltpu.make_async_copy(held.at[at], target.at[at], semaphores.at[len(copies)]))
        copies[-1].start()

    for rel in range(2):
        early_in, early_out = early[2 * rel : 2 * rel + 2]
        core = where[0] if rel == 0 else 1 - where[0]
        for index in range(blocks):
            fill([value[index] for value in values[rel]])
            term = dot(all_tokens[...], all_values[...], 0, 0) + early_in[index].astype(F32)
            put(held_in, outs[0], (slice(None), block_of(where, rel, index, width)), term)
        fill([value[blocks] for value in values[rel]])
        term = dot(all_values[...], all_cotangents[...], 0, 0) + early_out[...].astype(F32)
        at = (pl.ds(pl.multiple_of(core * width, 128), width), slice(None))
        put(held_out, outs[1], at, term)
    for copy in copies:
        copy.wait()


def shards(n_row, n_col, n_depth, tokens, weight_in, weight_out, output_grad):
    rows, features = tokens.shape
    part = features // n_depth
    blocks, width = n_depth, weight_in.shape[1] // (2 * n_depth)
    core = lax.axis_index("row") % 2
    depth = lax.axis_index("depth")
    chain = Chain(jnp.stack([core, depth]).astype(jnp.int32))

    def swap_cores(value):
        return lax.ppermute(value, "row", [(r, r ^ 1) for r in range(n_row)])

    def to_chip(value, k):
        return lax.ppermute(value, "row", [(r, (r + 2 * k) % n_row) for r in range(n_row)])

    def to_depth(value, k):
        return lax.ppermute(value, "depth", [(d, (d + k) % n_depth) for d in range(n_depth)])

    def to_col(value, k):
        return lax.ppermute(value, "col", [(c, (c + k) % n_col) for c in range(n_col)])

    single, pair_shape = shape(blocks, rows, width), shape(2, blocks, rows, width)
    model_shape = shape(2, rows, features)
    message_shape = shape(blocks + 1, rows, width)
    weight_shapes = [shape(blocks, features, width), shape(blocks, width, features)]
    groups = n_depth - 1
    last = n_col - 1
    own, other, shares = {}, {}, {}
    chip, crossed, pairs, came, model = {}, {}, {}, {}, {}

    def cross(stage):
        crossed[stage] = [to_chip(chip[stage], k) for k in range(1, n_row // 2)]

    share_shapes = [shape(rows, part + features)] * groups
    semaphores = [pltpu.SemaphoreType.DMA((2 * blocks,))]

    def send_shares(stage, values):
        shares[stage] = [to_depth(value, k) for k, value in enumerate(values, 1)]

    own[0], sent_in, sent_out, *results = chain(
        fetch_kernel,
        [tokens, output_grad, weight_in, weight_out],
        [shape(rows, 2 * features)] + weight_shapes + share_shapes,
        scratch=semaphores,
        specs=[IN_VMEM, IN_VMEM, IN_HBM, IN_HBM],
        limit=48,
    )
    send_shares(0, results)
    other_weights = [swap_cores(sent_in), swap_cores(sent_out)]
    results = chain(other_kernel, [own[0], sent_in, sent_out], [single, single])
    swapped = [swap_cores(value) for value in results]
    *own_weights, hidden, grad = chain(
        own_kernel,
        [own[0], weight_in, weight_out],
        weight_shapes + [single, single],
        scratch=semaphores,
        specs=[IN_VMEM, IN_HBM, IN_HBM],
        limit=44,
    )
    (chip[0],) = chain(join_kernel, [hidden, grad] + swapped, [pair_shape])
    cross(0)
    other[0] = swap_cores(own[0])
    own[1] = to_col(own[0], 1)
    raw, early_shares = {1: own[1]}, []

    def arrive_step(stage, after=()):
        raw[stage] = to_col(raw[stage - 1], 1)
        near, stacked = [raw[stage]], []
        if stage == last - 1:
            near += [value for earlier in range(stage) for value in shares[earlier]]
            stacked = [shape(stage * groups * rows, part + features)]
        own[stage], *results = chain(
            arrive_kernel, near, [shape(rows, 2 * features)] + stacked, after=after
        )
        if results:
            early_shares.extend(results + [swap_cores(results[0])])

    def hidden_step(stage, after=()):
        other[stage] = swap_cores(own[stage])
        chip[stage], *results = chain(
            functools.partial(hidden_kernel, stage == 1),
            [own[stage], other[stage]] + own_weights + other_weights,
            [pair_shape] + share_shapes + (weight_shapes if stage == 1 else []),
            after=after,
        )
        send_shares(stage, results[:groups])
        other_weights[:] = results[groups:] or other_weights
        cross(stage)

    def gelu_step(stage, after=()):
        inputs, outputs = [chip[stage]] + crossed[stage], [pair_shape] + [message_shape] * groups
        if stage == last:
            inputs += came[stage - 1]
            outputs += [shape(n_depth * (blocks + 1), rows, width)]
        pairs[stage], *messages = chain(
            functools.partial(gelu_kernel, n_depth), inputs, outputs, after=after
        )
        came[stage] = [to_depth(value, k) for k, value in enumerate(messages[:groups], 1)]
        return messages[groups:]

    def model_step(stage, after=()):
        mine, theirs = chain(
            model_kernel, [pairs[stage]] + own_weights + other_weights, [model_shape] * 2, after=after
        )
        model[stage] = [mine, swap_cores(theirs)]

    def sum_step(stage):
        arrived = ring[stage - 1] if stage > 1 else []
        (total,) = chain(sum_kernel, model[stage] + arrived, [model_shape])
        ring[stage] = [to_col(total, 1)]

    ring = {}
    hidden_step(1, shares[0])
    gelu_step(0, [other[0]])
    for stage in range(2, n_col):
        arrive_step(stage, shares[stage - 1])
        model_step(stage - 2)
        hidden_step(stage)
        after = came[stage - 2] + (model[0] if stage == 2 else [])
        gelu_step(stage - 1, after)
        if stage > 2:
            sum_step(stage - 2)
    model_step(last - 1)
    near = list(range(last))
    early_values = [values[stage] for values in (own, other, pairs) for stage in near]
    early_values += early_shares
    early_values += [value for stage in range(last - 1) for value in came[stage]]
    count = rows * (last + (last - 1) * groups)
    term_sizes = [(blocks, part, width), (width, features)]
    *own_early, sent_in, sent_out = chain(
        functools.partial(early_kernel, last),
        early_values,
        [shape(*share, kind=kind) for kind in (F32, BF16) for share in term_sizes],
        scratch=[
            pltpu.VMEM((count, 2 * part), BF16),
            pltpu.VMEM((count, 2 * features), BF16),
            pltpu.VMEM((count, width), BF16),
        ],
        limit=24,
    )
    other_early = [swap_cores(sent_in), swap_cores(sent_out)]
    (late,) = gelu_step(last, shares[last])
    late = swap_cores(late)
    model_step(last)
    sum_step(last - 1)
    sum_step(last)
    relayed = [
        value
        for source in came[last]
        for value in chain(relay_kernel, [source], [message_shape])
    ]
    last_values = [own[last], pairs[last], late] + shares[last - 1] + shares[last]
    last_values += came[last - 1] + came[last]
    last_values += [swap_cores(value) for value in relayed]
    count = rows * (1 + 2 * groups)
    grads = [shape(part, 2 * blocks * width, kind=F32), shape(2 * width, features, kind=F32)]
    in_grad, out_grad = chain(
        functools.partial(last_kernel, groups),
        last_values + own_early + other_early,
        grads,
        scratch=[
            pltpu.VMEM((count, part), BF16),
            pltpu.VMEM((count, features), BF16),
            pltpu.VMEM((count, width), BF16),
            pltpu.VMEM(grads[0].shape, F32),
            pltpu.VMEM(grads[1].shape, F32),
            pltpu.SemaphoreType.DMA((2 * blocks + 2,)),
        ],
        limit=20,
        to=IN_HBM,
    )
    output, input_grad = chain(
        sum_kernel,
        model[0] + ring[last],
        [shape(rows, features)] * 2,
    )
    return output, input_grad, in_grad, out_grad


def plain_shards(tokens, weight_in, weight_out, output_grad):
    x_panel = lax.all_gather(tokens, "col", axis=0, tiled=True)
    dy_panel = lax.all_gather(output_grad, "col", axis=0, tiled=True)

    def hidden_total(term):
        return lax.psum(term.astype(BF16), "row").astype(F32)

    def scattered(term, axis):
        return lax.psum_scatter(term.astype(BF16), axis, scatter_dimension=0, tiled=True)

    value, slope = gelu_parts(hidden_total(dot(x_panel, weight_in, 1, 0)))
    act = value.astype(BF16)
    pre = (hidden_total(dot(dy_panel, weight_out, 1, 1)) * slope).astype(BF16)
    return (
        scattered(dot(act, weight_out, 1, 0), "col"),
        scattered(dot(pre, weight_in, 1, 1), "col"),
        scattered(dot(x_panel, pre, 0, 0), "depth").astype(F32),
        scattered(dot(act, dy_panel, 0, 0), "depth").astype(F32),
    )


def solution(mesh):
    placed = (
        P(("col", "depth"), "row"),
        P("row", "col"),
        P("col", "row"),
        P(("col", "depth"), "row"),
    )
    sizes = (mesh.shape["row"], mesh.shape["col"], mesh.shape["depth"])

    def local(tokens, weight_in, weight_out, output_grad):
        arrays = (tokens, weight_in, weight_out, output_grad)
        n_row, n_col, n_depth = sizes
        width, part = weight_in.shape[1] // (2 * n_depth), tokens.shape[1] // n_depth
        fits = width % 128 == 0 and part % 128 == 0 and tokens.shape[0] % 16 == 0
        if fits and n_row % 2 == 0 and n_col > 2 and n_depth > 1:
            return shards(*sizes, *arrays)
        return plain_shards(*arrays)

    return jax.shard_map(
        local,
        mesh=mesh,
        in_specs=placed,
        out_specs=(
            P(("col", "depth"), "row"),
            P(("col", "depth"), "row"),
            P(("row", "depth"), "col"),
            P(("col", "depth"), "row"),
        ),
        check_vma=False,
    )
```

time: 341 us -> 113 us (0.33)
  waiting for transfers between devices: 238 us -> 37.2 us
  Pallas kernels: 0 us -> 47.4 us
  blocking collectives: 35 us -> 0 us
  matrix products: 29.9 us -> 0 us
  starting transfers between devices: 0.39 us -> 25.9 us
  local copies, waits for them, and re-layouts: 15.8 us -> 1.82 us
  between operations: 13.8 us -> 0.89 us
  other arithmetic: 8.08 us -> 0.08 us
    reduce_scatter x3 -> x0, waiting for transfers between devices: 100 us -> none  [the longest x1 56.9 us: shards(): lax.psum_scatter(term_out.astype(jnp.bfloat16), 'depth', scatter_dimensio...]
    psum x1 -> x0, waiting for transfers between devices: 95.5 us -> none  [hidden_total(): return lax.psum(term.astype(jnp.bfloat16), 'row').astype(jnp.float32)]
    pallas_call x0 -> x24, Pallas kernels: none -> 47.4 us  [__call__(): pl.pallas_call(body, in_specs=[IN_SMEM] + (specs or [IN_VMEM] * n_in) + [...]
    unnamed x6 -> x0, waiting for transfers between devices: 42.1 us -> none
    ppermute x0 -> x35, waiting for transfers between devices: none -> 37.2 us  [the longest x6 19.6 us: to_col(): lax.ppermute(value, 'col', [(c, (c + k) % n_col) for c in range(n_col)])]
    all_gather x2 -> x0, blocking collectives: 35 us -> none  [the longest x1 18.4 us: shards(): lax.all_gather(tokens, 'col', axis=0, tiled=True)]
    dot_general x6 -> x0, matrix products: 29.9 us -> none  [the longest x2 11.9 us: product_rows(): lax.dot_general(panel, weight, (((1,), (contract,)), ((), ())), preferred...]
    ppermute x0 -> x35, starting transfers between devices: none -> 25.9 us  [the longest x8 10.2 us: to_depth(): lax.ppermute(value, 'depth', [(d, (d + k) % n_depth) for d in range(n_dep...]
  transfers between devices with their start and end apart: 5 -> 35, of which waited for: 5 -> 11; matrix products, arithmetic and copies ran while one was open for 8% -> 0% of each run, Pallas kernels for 0% -> 38%
where the time goes in v3:
time: 113 us
  Pallas kernels  47.4 us (42%)
  waiting for transfers between devices  37.2 us (33%)
  starting transfers between devices  25.9 us (23%)
  local copies, waits for them, and re-layouts  1.82 us (2%)
    pallas_call x24, Pallas kernels, __call__(): pl.pallas_call(body, in_specs=[IN_SMEM] + (specs or [IN_VMEM] * n_in) + [...  47.4 us
    ppermute x6, waiting for transfers between devices, to_col(): lax.ppermute(value, 'col', [(c, (c + k) % n_col) for c in range(n_col)])  19.6 us
    ppermute x8, waiting for transfers between devices, to_depth(): lax.ppermute(value, 'depth', [(d, (d + k) % n_depth) for d in range(n_dep...  14.8 us
    ppermute x8, starting transfers between devices, to_depth(): lax.ppermute(value, 'depth', [(d, (d + k) % n_depth) for d in range(n_dep...  10.2 us
    ppermute x6, starting transfers between devices, to_col(): lax.ppermute(value, 'col', [(c, (c + k) % n_col) for c in range(n_col)])  8.15 us
    ppermute x4, starting transfers between devices, to_chip(): lax.ppermute(value, 'row', [(r, (r + 2 * k) % n_row) for r in range(n_row)])  4.25 us
    ppermute x17, starting transfers between devices, swap_cores(): return lax.ppermute(value, 'row', [(r, r ^ 1) for r in range(n_row)])  3.24 us
    ppermute x17, waiting for transfers between devices, swap_cores(): return lax.ppermute(value, 'row', [(r, r ^ 1) for r in range(n_row)])  2.71 us
  transfers between devices with their start and end apart: 35, of which 11 were waited for; matrix products, arithmetic and copies ran while one was open for 0% of the time, Pallas kernels for 38%

profile of v3, /device:TPU:0, one launch (start us, length us, event | category | flops | bytes accessed | tf_op | source)
XLA Modules:
  0.0 113.2 jit_solution(13673767835147652049)
XLA Ops:
  0.7 0.9 copy-done.1
  1.6 0.9 copy-done.2
  2.5 2.9 %shard_map.75 = (bf16[96,1536]{1,0:T(8,128)(2,1)S(1)}, bf16[2,768,768]{2,1,0:T(8,128)(2,1)S(1)}, bf16[2,768,768]{2,1,0:T(8,128)(2,1)S(1)}, bf16[96,1152]{1,0:T(8,128)(2,1)S(1)}, f32[8,128]{1,0:T(8,128)S(1)}) custom-call(s32[2]{0:T(128)S(1)} %pad_add_fusion.where, bf16[96,768]{1,0:T(8,128)(2,1)S(1)} %copy-done.1, bf16[96,768]{1,0:T(8,128)(2,1)S(1)} %copy-done.2, ...), custom_call_target="tpu_custom_call" | custom-call | flops 1000 | bytes 1000 | tf_op jit(solution)/shard_map/pallas_call | solution.py:52
  6.1 2.4 %shard_map.76 = (bf16[2,96,768]{2,1,0:T(8,128)(2,1)}, bf16[2,96,768]{2,1,0:T(8,128)(2,1)}, f32[8,128]{1,0:T(8,128)S(1)}) custom-call(s32[2]{0:T(128)S(1)} %pad_add_fusion.where, bf16[96,1536]{1,0:T(8,128)(2,1)S(1)} %get-tuple-element.78.refs_0_, bf16[2,768,768]{2,1,0:T(8,128)(2,1)S(1)} %get-tuple-element.79.refs_1_, ...), custom_call_target="tpu_custom_call" | custom-call | flops 1000 | bytes 1000 | tf_op jit(solution)/shard_map/pallas_call | solution.py:52
  9.0 3.0 %collective-permute-start.4 = (bf16[96,1536]{1,0:T(8,128)(2,1)S(1)}, bf16[96,1536]{1,0:T(8,128)(2,1)S(1)}, u32[]{:S(2)}, u32[]{:S(2)}) collective-permute-start(bf16[96,1536]{1,0:T(8,128)(2,1)S(1)} %get-tuple-element.78.refs_0_), channel_id=1, source_target_pairs={{0,2},{2,4},{4,6},{6,0},{1,3},{3,5},{5,7},{7,1},{8,10},{10,12},{12... | collective-permute-start | bytes 884744 | tf_op jit(solution)/shard_map/ppermute | solution.py:310
  12.0 3.6 %shard_map.77 = (bf16[2,768,768]{2,1,0:T(8,128)(2,1)S(1)}, bf16[2,768,768]{2,1,0:T(8,128)(2,1)S(1)}, bf16[2,96,768]{2,1,0:T(8,128)(2,1)S(1)}, bf16[2,96,768]{2,1,0:T(8,128)(2,1)S(1)}, f32[8,128]{1,0:T(8,128)S(1)}) custom-call(s32[2]{0:T(128)S(1)} %pad_add_fusion.where, bf16[96,1536]{1,0:T(8,128)(2,1)S(1)} %get-tuple-element.78.refs_0_, ...), custom_call_target="tpu_custom_call" | custom-call | flops 1000 | bytes 1000 | tf_op jit(solution)/shard_map/pallas_call | solution.py:52
  15.6 0.7 shard_map.78
  16.3 1.6 %collective-permute-start.2 = (bf16[2,2,96,768]{3,2,1,0:T(8,128)(2,1)S(1)}, bf16[2,2,96,768]{3,2,1,0:T(8,128)(2,1)S(1)}, u32[]{:S(2)}, u32[]{:S(2)}) collective-permute-start(bf16[2,2,96,768]{3,2,1,0:T(8,128)(2,1)S(1)} %get-tuple-element.88.refs_0_), channel_id=1, source_target_pairs={{0,16},{8,24},{16,0},{24,8},{1,17},{9,25},{17,1},{25,9},{2,18},{10... | collective-permute-start | bytes 1769480 | tf_op jit(solution)/shard_map/ppermute | solution.py:304
  17.9 1.5 %collective-permute-start.8 = (bf16[96,1152]{1,0:T(8,128)(2,1)S(1)}, bf16[96,1152]{1,0:T(8,128)(2,1)S(1)}, u32[]{:S(2)}, u32[]{:S(2)}) collective-permute-start(bf16[96,1152]{1,0:T(8,128)(2,1)S(1)} %get-tuple-element.91), channel_id=1, source_target_pairs={{0,1},{1,0},{2,3},{3,2},{4,5},{5,4},{6,7},{7,6},{8,9},{9,8},{10,11... | collective-permute-start | bytes 663560 | tf_op jit(solution)/shard_map/ppermute | solution.py:307
  19.4 1.9 %collective-permute-done.4.refs_0_.refs_1_ = bf16[96,1536]{1,0:T(8,128)(2,1)S(1)} collective-permute-done((bf16[96,1536]{1,0:T(8,128)(2,1)S(1)}, bf16[96,1536]{1,0:T(8,128)(2,1)S(1)}, u32[]{:S(2)}, u32[]{:S(2)}) %collective-permute-start.4) | collective-permute-done | bytes 294944 | tf_op jit(solution)/shard_map/ppermute | solution.py:310
  21.3 3.4 %collective-permute-done.8.refs_6_.refs_1_ = bf16[96,1152]{1,0:T(8,128)(2,1)S(1)} collective-permute-done((bf16[96,1152]{1,0:T(8,128)(2,1)S(1)}, bf16[96,1152]{1,0:T(8,128)(2,1)S(1)}, u32[]{:S(2)}, u32[]{:S(2)}) %collective-permute-start.8) | collective-permute-done | bytes 221216 | tf_op jit(solution)/shard_map/ppermute | solution.py:307
  24.7 1.6 %collective-permute-start.9 = (bf16[96,1536]{1,0:T(8,128)(2,1)S(1)}, bf16[96,1536]{1,0:T(8,128)(2,1)S(1)}, u32[]{:S(2)}, u32[]{:S(2)}) collective-permute-start(bf16[96,1536]{1,0:T(8,128)(2,1)S(1)} %collective-permute-done.4.refs_0_.refs_1_), channel_id=1, source_target_pairs={{0,2},{2,4},{4,6},{6,0},{1,3},{3,5},{5,7},{7,1},{8,10},{10,12},{12... | collective-permute-start | bytes 884744 | tf_op jit(solution)/shard_map/ppermute | solution.py:310
  26.3 3.1 %shard_map.79 = (bf16[2,2,96,768]{3,2,1,0:T(8,128)(2,1)S(1)}, bf16[96,1152]{1,0:T(8,128)(2,1)S(1)}, bf16[2,768,768]{2,1,0:T(8,128)(2,1)S(1)}, bf16[2,768,768]{2,1,0:T(8,128)(2,1)S(1)}, f32[8,128]{1,0:T(8,128)S(1)}) custom-call(s32[2]{0:T(128)S(1)} %pad_add_fusion.where, bf16[96,1536]{1,0:T(8,128)(2,1)S(1)} %collective-permute-done.4.refs_0_.refs_1_, ...), custom_call_target="tpu_custom_call" | custom-call | flops 1000 | bytes 1000 | tf_op jit(solution)/shard_map/pallas_call | solution.py:52
  29.4 1.6 %collective-permute-start.10 = (bf16[96,1152]{1,0:T(8,128)(2,1)S(1)}, bf16[96,1152]{1,0:T(8,128)(2,1)S(1)}, u32[]{:S(2)}, u32[]{:S(2)}) collective-permute-start(bf16[96,1152]{1,0:T(8,128)(2,1)S(1)} %get-tuple-element.97), channel_id=1, source_target_pairs={{0,1},{1,0},{2,3},{3,2},{4,5},{5,4},{6,7},{7,6},{8,9},{9,8},{10,11... | collective-permute-start | bytes 663560 | tf_op jit(solution)/shard_map/ppermute | solution.py:307
  31.6 1.1 %shard_map.80 = (bf16[2,2,96,768]{3,2,1,0:T(8,128)(2,1)S(1)}, bf16[3,96,768]{2,1,0:T(8,128)(2,1)S(1)}, f32[8,128]{1,0:T(8,128)S(1)}) custom-call(s32[2]{0:T(128)S(1)} %pad_add_fusion.where, bf16[2,2,96,768]{3,2,1,0:T(8,128)(2,1)S(1)} %get-tuple-element.88.refs_0_, bf16[2,2,96,768]{3,2,1,0:T(8,128)(2,1)S(1)} %collective-permute-done.2.refs_1_, ...), custom_call_target="tpu_custom_call" | custom-call | flops 1000 | bytes 1000 | tf_op jit(solution)/shard_map/pallas_call | solution.py:52
  32.7 1.4 %collective-permute-start.16 = (bf16[3,96,768]{2,1,0:T(8,128)(2,1)S(1)}, bf16[3,96,768]{2,1,0:T(8,128)(2,1)S(1)}, u32[]{:S(2)}, u32[]{:S(2)}) collective-permute-start(bf16[3,96,768]{2,1,0:T(8,128)(2,1)S(1)} %get-tuple-element.106), channel_id=1, source_target_pairs={{0,1},{1,0},{2,3},{3,2},{4,5},{5,4},{6,7},{7,6},{8,9},{9,8},{10,11... | collective-permute-start | bytes 1327112 | tf_op jit(solution)/shard_map/ppermute | solution.py:307
  34.2 1.8 %collective-permute-done.9.refs_0_ = bf16[96,1536]{1,0:T(8,128)(2,1)S(1)} collective-permute-done((bf16[96,1536]{1,0:T(8,128)(2,1)S(1)}, bf16[96,1536]{1,0:T(8,128)(2,1)S(1)}, u32[]{:S(2)}, u32[]{:S(2)}) %collective-permute-start.9) | collective-permute-done | bytes 294944 | tf_op jit(solution)/shard_map/ppermute | solution.py:310
  36.0 1.8 %collective-permute-done.10.refs_2_.refs_3_ = bf16[96,1152]{1,0:T(8,128)(2,1)S(1)} collective-permute-done((bf16[96,1152]{1,0:T(8,128)(2,1)S(1)}, bf16[96,1152]{1,0:T(8,128)(2,1)S(1)}, u32[]{:S(2)}, u32[]{:S(2)}) %collective-permute-start.10) | collective-permute-done | bytes 221216 | tf_op jit(solution)/shard_map/ppermute | solution.py:307
  37.8 0.6 shard_map.81
  38.5 2.8 %shard_map.82 = (bf16[2,96,768]{2,1,0:T(8,128)(2,1)S(1)}, bf16[2,96,768]{2,1,0:T(8,128)(2,1)S(1)}, f32[8,128]{1,0:T(8,128)S(1)}) custom-call(s32[2]{0:T(128)S(1)} %pad_add_fusion.where, bf16[2,2,96,768]{3,2,1,0:T(8,128)(2,1)S(1)} %get-tuple-element.94.refs_0_.refs_6_, bf16[2,768,768]{2,1,0:T(8,128)(2,1)S(1)} %get-tuple-element.89.refs_2_.refs_1_, ...), custom_call_target="tpu_custom_call" | custom-call | flops 1000 | bytes 1000 | tf_op jit(solution)/shard_map/pallas_call | solution.py:52
  41.8 1.6 %collective-permute-start.12 = (bf16[96,1536]{1,0:T(8,128)(2,1)S(1)}, bf16[96,1536]{1,0:T(8,128)(2,1)S(1)}, u32[]{:S(2)}, u32[]{:S(2)}) collective-permute-start(bf16[96,1536]{1,0:T(8,128)(2,1)S(1)} %collective-permute-done.9.refs_0_), channel_id=1, source_target_pairs={{0,2},{2,4},{4,6},{6,0},{1,3},{3,5},{5,7},{7,1},{8,10},{10,12},{12... | collective-permute-start | bytes 884744 | tf_op jit(solution)/shard_map/ppermute | solution.py:310
  43.4 2.8 %shard_map.83 = (bf16[2,2,96,768]{3,2,1,0:T(8,128)(2,1)S(1)}, bf16[96,1152]{1,0:T(8,128)(2,1)S(1)}, f32[8,128]{1,0:T(8,128)S(1)}) custom-call(s32[2]{0:T(128)S(1)} %pad_add_fusion.where, bf16[96,1536]{1,0:T(8,128)(2,1)S(1)} %get-tuple-element.102.refs_0_.refs_2_, bf16[96,1536]{1,0:T(8,128)(2,1)S(1)} %collective-permute-done.13.refs_1_.refs_5_, ...), custom_call_target="tpu_custom_call" | custom-call | flops 1000 | bytes 1000 | tf_op jit(solution)/shard_map/pallas_call | solution.py:52
  46.2 0.6 collective-permute-start.19
  46.8 1.5 %collective-permute-start.14 = (bf16[96,1152]{1,0:T(8,128)(2,1)S(1)}, bf16[96,1152]{1,0:T(8,128)(2,1)S(1)}, u32[]{:S(2)}, u32[]{:S(2)}) collective-permute-start(bf16[96,1152]{1,0:T(8,128)(2,1)S(1)} %get-tuple-element.104), channel_id=1, source_target_pairs={{0,1},{1,0},{2,3},{3,2},{4,5},{5,4},{6,7},{7,6},{8,9},{9,8},{10,11... | collective-permute-start | bytes 663560 | tf_op jit(solution)/shard_map/ppermute | solution.py:307
  48.3 1.1 %shard_map.84 = (bf16[2,2,96,768]{3,2,1,0:T(8,128)(2,1)S(1)}, bf16[3,96,768]{2,1,0:T(8,128)(2,1)S(1)}, f32[8,128]{1,0:T(8,128)S(1)}) custom-call(s32[2]{0:T(128)S(1)} %pad_add_fusion.where, bf16[2,2,96,768]{3,2,1,0:T(8,128)(2,1)S(1)} %get-tuple-element.105.refs_0_, bf16[2,2,96,768]{3,2,1,0:T(8,128)(2,1)S(1)} %collective-permute-done.15.refs_1_, ...), custom_call_target="tpu_custom_call" | custom-call | flops 1000 | bytes 1000 | tf_op jit(solution)/shard_map/pallas_call | solution.py:52
  50.1 2.7 %collective-permute-done.12.refs_0_ = bf16[96,1536]{1,0:T(8,128)(2,1)S(1)} collective-permute-done((bf16[96,1536]{1,0:T(8,128)(2,1)S(1)}, bf16[96,1536]{1,0:T(8,128)(2,1)S(1)}, u32[]{:S(2)}, u32[]{:S(2)}) %collective-permute-start.12) | collective-permute-done | bytes 294944 | tf_op jit(solution)/shard_map/ppermute | solution.py:310
  52.8 2.4 %collective-permute-done.14.refs_1_.refs_3_ = bf16[96,1152]{1,0:T(8,128)(2,1)S(1)} collective-permute-done((bf16[96,1152]{1,0:T(8,128)(2,1)S(1)}, bf16[96,1152]{1,0:T(8,128)(2,1)S(1)}, u32[]{:S(2)}, u32[]{:S(2)}) %collective-permute-start.14) | collective-permute-done | bytes 221216 | tf_op jit(solution)/shard_map/ppermute | solution.py:307
  56.3 2.8 %shard_map.86 = (bf16[2,96,768]{2,1,0:T(8,128)(2,1)S(1)}, bf16[2,96,768]{2,1,0:T(8,128)(2,1)S(1)}, f32[8,128]{1,0:T(8,128)S(1)}) custom-call(s32[2]{0:T(128)S(1)} %pad_add_fusion.where, bf16[2,2,96,768]{3,2,1,0:T(8,128)(2,1)S(1)} %get-tuple-element.110.refs_0_.refs_7_, bf16[2,768,768]{2,1,0:T(8,128)(2,1)S(1)} %get-tuple-element.89.refs_2_.refs_1_, ...), custom_call_target="tpu_custom_call" | custom-call | flops 1000 | bytes 1000 | tf_op jit(solution)/shard_map/pallas_call | solution.py:52
  59.2 2.8 %shard_map.87 = (bf16[2,2,96,768]{3,2,1,0:T(8,128)(2,1)S(1)}, bf16[96,1152]{1,0:T(8,128)(2,1)S(1)}, f32[8,128]{1,0:T(8,128)S(1)}) custom-call(s32[2]{0:T(128)S(1)} %pad_add_fusion.where, bf16[96,1536]{1,0:T(8,128)(2,1)S(1)} %get-tuple-element.109.refs_0_, bf16[96,1536]{1,0:T(8,128)(2,1)S(1)} %collective-permute-done.17.refs_1_, ...), custom_call_target="tpu_custom_call" | custom-call | flops 1000 | bytes 1000 | tf_op jit(solution)/shard_map/pallas_call | solution.py:52
  62.1 1.6 %collective-permute-start.18 = (bf16[2,2,96,768]{3,2,1,0:T(8,128)(2,1)S(1)}, bf16[2,2,96,768]{3,2,1,0:T(8,128)(2,1)S(1)}, u32[]{:S(2)}, u32[]{:S(2)}) collective-permute-start(bf16[2,2,96,768]{3,2,1,0:T(8,128)(2,1)S(1)} %get-tuple-element.113.refs_0_), channel_id=1, source_target_pairs={{0,16},{8,24},{16,0},{24,8},{1,17},{9,25},{17,1},{25,9},{2,18},{10... | collective-permute-start | bytes 1769480 | tf_op jit(solution)/shard_map/ppermute | solution.py:304
  63.6 1.1 %shard_map.88 = (bf16[2,2,96,768]{3,2,1,0:T(8,128)(2,1)S(1)}, bf16[3,96,768]{2,1,0:T(8,128)(2,1)S(1)}, f32[8,128]{1,0:T(8,128)S(1)}) custom-call(s32[2]{0:T(128)S(1)} %pad_add_fusion.where, bf16[2,2,96,768]{3,2,1,0:T(8,128)(2,1)S(1)} %get-tuple-element.114.refs_0_, bf16[2,2,96,768]{3,2,1,0:T(8,128)(2,1)S(1)} %collective-permute-done.19.refs_1_, ...), custom_call_target="tpu_custom_call" | custom-call | flops 1000 | bytes 1000 | tf_op jit(solution)/shard_map/pallas_call | solution.py:52
  64.8 1.6 %collective-permute-start.21 = (bf16[3,96,768]{2,1,0:T(8,128)(2,1)S(1)}, bf16[3,96,768]{2,1,0:T(8,128)(2,1)S(1)}, u32[]{:S(2)}, u32[]{:S(2)}) collective-permute-start(bf16[3,96,768]{2,1,0:T(8,128)(2,1)S(1)} %get-tuple-element.117), channel_id=1, source_target_pairs={{0,1},{1,0},{2,3},{3,2},{4,5},{5,4},{6,7},{7,6},{8,9},{9,8},{10,11... | collective-permute-start | bytes 1327112 | tf_op jit(solution)/shard_map/ppermute | solution.py:307
  66.9 0.6 shard_map.89
  67.5 2.8 %shard_map.90 = (bf16[2,96,768]{2,1,0:T(8,128)(2,1)S(1)}, bf16[2,96,768]{2,1,0:T(8,128)(2,1)S(1)}, f32[8,128]{1,0:T(8,128)S(1)}) custom-call(s32[2]{0:T(128)S(1)} %pad_add_fusion.where, bf16[2,2,96,768]{3,2,1,0:T(8,128)(2,1)S(1)} %get-tuple-element.119.refs_0_.refs_8_, bf16[2,768,768]{2,1,0:T(8,128)(2,1)S(1)} %get-tuple-element.89.refs_2_.refs_1_, ...), custom_call_target="tpu_custom_call" | custom-call | flops 1000 | bytes 1000 | tf_op jit(solution)/shard_map/pallas_call | solution.py:52
  70.4 1.0 collective-permute-start.27
  71.4 3.2 %shard_map.91 = (f32[2,384,768]{2,1,0:T(8,128)S(1)}, f32[768,768]{1,0:T(8,128)S(1)}, bf16[2,384,768]{2,1,0:T(8,128)(2,1)S(1)}, bf16[768,768]{1,0:T(8,128)(2,1)S(1)}, f32[8,128]{1,0:T(8,128)S(1)}) custom-call(s32[2]{0:T(128)S(1)} %pad_add_fusion.where, bf16[96,1536]{1,0:T(8,128)(2,1)S(1)} %get-tuple-element.78.refs_0_, ...), custom_call_target="tpu_custom_call" | custom-call | flops 1000 | bytes 1000 | tf_op jit(solution)/shard_map/pallas_call | solution.py:52
  74.6 7.2 %collective-permute-done.22.refs_3_.refs_4_ = bf16[96,1152]{1,0:T(8,128)(2,1)S(1)} collective-permute-done((bf16[96,1152]{1,0:T(8,128)(2,1)S(1)}, bf16[96,1152]{1,0:T(8,128)(2,1)S(1)}, u32[]{:S(2)}, u32[]{:S(2)}) %collective-permute-start.22) | collective-permute-done | bytes 221216 | tf_op jit(solution)/shard_map/ppermute | solution.py:307
  82.3 1.2 %shard_map.92 = (bf16[2,2,96,768]{3,2,1,0:T(8,128)(2,1)S(1)}, bf16[3,96,768]{2,1,0:T(8,128)(2,1)S(1)}, bf16[6,96,768]{2,1,0:T(8,128)(2,1)S(1)}, f32[8,128]{1,0:T(8,128)S(1)}) custom-call(s32[2]{0:T(128)S(1)} %pad_add_fusion.where, bf16[2,2,96,768]{3,2,1,0:T(8,128)(2,1)S(1)} %get-tuple-element.113.refs_0_, ...), custom_call_target="tpu_custom_call" | custom-call | flops 1000 | bytes 1000 | tf_op jit(solution)/shard_map/pallas_call | solution.py:52
  83.5 2.8 %shard_map.93 = (bf16[2,96,768]{2,1,0:T(8,128)(2,1)S(1)}, bf16[2,96,768]{2,1,0:T(8,128)(2,1)S(1)}, f32[8,128]{1,0:T(8,128)S(1)}) custom-call(s32[2]{0:T(128)S(1)} %pad_add_fusion.where, bf16[2,2,96,768]{3,2,1,0:T(8,128)(2,1)S(1)} %get-tuple-element.127.refs_0_.refs_1_, bf16[2,768,768]{2,1,0:T(8,128)(2,1)S(1)} %get-tuple-element.89.refs_2_.refs_1_, ...), custom_call_target="tpu_custom_call" | custom-call | flops 1000 | bytes 1000 | tf_op jit(solution)/shard_map/pallas_call | solution.py:52
  86.4 0.7 shard_map.94
  87.4 1.5 %collective-permute-start.31 = (bf16[3,96,768]{2,1,0:T(8,128)(2,1)S(1)}, bf16[3,96,768]{2,1,0:T(8,128)(2,1)S(1)}, u32[]{:S(2)}, u32[]{:S(2)}) collective-permute-start(bf16[3,96,768]{2,1,0:T(8,128)(2,1)S(1)} %get-tuple-element.139), channel_id=1, source_target_pairs={{0,1},{1,0},{2,3},{3,2},{4,5},{5,4},{6,7},{7,6},{8,9},{9,8},{10,11... | collective-permute-start | bytes 1327112 | tf_op jit(solution)/shard_map/ppermute | solution.py:307
  89.0 8.8 %collective-permute-done.28.refs_2_ = bf16[2,96,768]{2,1,0:T(8,128)(2,1)S(1)} collective-permute-done((bf16[2,96,768]{2,1,0:T(8,128)(2,1)S(1)}, bf16[2,96,768]{2,1,0:T(8,128)(2,1)S(1)}, u32[]{:S(2)}, u32[]{:S(2)}) %collective-permute-start.28) | collective-permute-done | bytes 294944 | tf_op jit(solution)/shard_map/ppermute | solution.py:310
  97.8 1.6 %collective-permute-done.25.refs_1_ = bf16[2,96,768]{2,1,0:T(8,128)(2,1)S(1)} collective-permute-done((bf16[2,96,768]{2,1,0:T(8,128)(2,1)S(1)}, bf16[2,96,768]{2,1,0:T(8,128)(2,1)S(1)}, u32[]{:S(2)}, u32[]{:S(2)}) %collective-permute-start.25) | collective-permute-done | bytes 294944 | tf_op jit(solution)/shard_map/ppermute | solution.py:301
  99.4 0.7 shard_map.95
  101.4 1.1 collective-permute-done.32.refs_7_
  102.5 5.0 %shard_map.97 = (f32[384,3072]{1,0:T(8,128)}, f32[1536,768]{1,0:T(8,128)}, f32[8,128]{1,0:T(8,128)S(1)}) custom-call(s32[2]{0:T(128)S(1)} %pad_add_fusion.where, bf16[96,1536]{1,0:T(8,128)(2,1)S(1)} %get-tuple-element.109.refs_0_, bf16[2,2,96,768]{3,2,1,0:T(8,128)(2,1)S(1)} %get-tuple-element.127.refs_0_.refs_1_, ...), custom_call_target="tpu_custom_call" | custom-call | flops 1000 | bytes 1000 | tf_op jit(solution)/shard_map/pallas_call | solution.py:52
  107.5 4.4 %collective-permute-done.29.refs_2_ = bf16[2,96,768]{2,1,0:T(8,128)(2,1)S(1)} collective-permute-done((bf16[2,96,768]{2,1,0:T(8,128)(2,1)S(1)}, bf16[2,96,768]{2,1,0:T(8,128)(2,1)S(1)}, u32[]{:S(2)}, u32[]{:S(2)}) %collective-permute-start.29) | collective-permute-done | bytes 294944 | tf_op jit(solution)/shard_map/ppermute | solution.py:310
  111.9 1.3 %shard_map.98 = (bf16[96,768]{1,0:T(8,128)(2,1)}, bf16[96,768]{1,0:T(8,128)(2,1)}, f32[8,128]{1,0:T(8,128)}) custom-call(s32[2]{0:T(128)S(1)} %pad_add_fusion.where, bf16[2,96,768]{2,1,0:T(8,128)(2,1)S(1)} %get-tuple-element.100.refs_3_.refs_0_, bf16[2,96,768]{2,1,0:T(8,128)(2,1)S(1)} %collective-permute-done.11.refs_4_.refs_1_, ...), custom_call_target="tpu_custom_call" | custom-call | flops 1000 | bytes 1000 | tf_op jit(solution)/shard_map/pallas_call | solution.py:52
  (54 shorter events, 7.1 us)
Async XLA Ops:
  0.7 0.9 copy-start.1
  1.6 0.9 copy-start.2
  5.5 20.8 %collective-permute-start.6 = (bf16[2,768,768]{2,1,0:T(8,128)(2,1)S(1)}, bf16[2,768,768]{2,1,0:T(8,128)(2,1)S(1)}, u32[]{:S(2)}, u32[]{:S(2)}) collective-permute-start(bf16[2,768,768]{2,1,0:T(8,128)(2,1)S(1)} %get-tuple-element.79.refs_1_), channel_id=1, source_target_pairs={{0,8},{8,0},{16,24},{24,16},{1,9},{9,1},{17,25},{25,17},{2,10},{10... | collective-permute-start | bytes 7077896 | tf_op jit(solution)/shard_map/ppermute | solution.py:301
  6.0 20.3 %collective-permute-start.7 = (bf16[2,768,768]{2,1,0:T(8,128)(2,1)S(1)}, bf16[2,768,768]{2,1,0:T(8,128)(2,1)S(1)}, u32[]{:S(2)}, u32[]{:S(2)}) collective-permute-start(bf16[2,768,768]{2,1,0:T(8,128)(2,1)S(1)} %get-tuple-element.80.refs_2_), channel_id=1, source_target_pairs={{0,8},{8,0},{16,24},{24,16},{1,9},{9,1},{17,25},{25,17},{2,10},{10... | collective-permute-start | bytes 7077896 | tf_op jit(solution)/shard_map/ppermute | solution.py:301
  6.1 5.9 %copy-start = (bf16[768,3072]{1,0:T(8,128)(2,1)S(1)}, bf16[768,3072]{1,0:T(8,128)(2,1)}, u32[]{:S(2)}) copy-start(bf16[768,3072]{1,0:T(8,128)(2,1)} %refs_1_.3) | copy-start | bytes 14155780
  8.5 7.1 %collective-permute-start = (bf16[2,96,768]{2,1,0:T(8,128)(2,1)}, bf16[2,96,768]{2,1,0:T(8,128)(2,1)S(1)}, u32[]{:S(2)}, u32[]{:S(2)}) collective-permute-start(bf16[2,96,768]{2,1,0:T(8,128)(2,1)} %get-tuple-element.85), channel_id=1, source_target_pairs={{0,8},{8,0},{16,24},{24,16},{1,9},{9,1},{17,25},{25,17},{2,10},{10... | collective-permute-start | bytes 884744 | tf_op jit(solution)/shard_map/ppermute | solution.py:301
  8.9 6.7 %collective-permute-start.1 = (bf16[2,96,768]{2,1,0:T(8,128)(2,1)}, bf16[2,96,768]{2,1,0:T(8,128)(2,1)S(1)}, u32[]{:S(2)}, u32[]{:S(2)}) collective-permute-start(bf16[2,96,768]{2,1,0:T(8,128)(2,1)} %get-tuple-element.86), channel_id=1, source_target_pairs={{0,8},{8,0},{16,24},{24,16},{1,9},{9,1},{17,25},{25,17},{2,10},{10... | collective-permute-start | bytes 884744 | tf_op jit(solution)/shard_map/ppermute | solution.py:301
  9.0 12.3 %collective-permute-start.4 = (bf16[96,1536]{1,0:T(8,128)(2,1)S(1)}, bf16[96,1536]{1,0:T(8,128)(2,1)S(1)}, u32[]{:S(2)}, u32[]{:S(2)}) collective-permute-start(bf16[96,1536]{1,0:T(8,128)(2,1)S(1)} %get-tuple-element.78.refs_0_), channel_id=1, source_target_pairs={{0,2},{2,4},{4,6},{6,0},{1,3},{3,5},{5,7},{7,1},{8,10},{10,12},{12... | collective-permute-start | bytes 884744 | tf_op jit(solution)/shard_map/ppermute | solution.py:310
  16.3 15.2 %collective-permute-start.2 = (bf16[2,2,96,768]{3,2,1,0:T(8,128)(2,1)S(1)}, bf16[2,2,96,768]{3,2,1,0:T(8,128)(2,1)S(1)}, u32[]{:S(2)}, u32[]{:S(2)}) collective-permute-start(bf16[2,2,96,768]{3,2,1,0:T(8,128)(2,1)S(1)} %get-tuple-element.88.refs_0_), channel_id=1, source_target_pairs={{0,16},{8,24},{16,0},{24,8},{1,17},{9,25},{17,1},{25,9},{2,18},{10... | collective-permute-start | bytes 1769480 | tf_op jit(solution)/shard_map/ppermute | solution.py:304
  17.9 6.8 %collective-permute-start.8 = (bf16[96,1152]{1,0:T(8,128)(2,1)S(1)}, bf16[96,1152]{1,0:T(8,128)(2,1)S(1)}, u32[]{:S(2)}, u32[]{:S(2)}) collective-permute-start(bf16[96,1152]{1,0:T(8,128)(2,1)S(1)} %get-tuple-element.91), channel_id=1, source_target_pairs={{0,1},{1,0},{2,3},{3,2},{4,5},{5,4},{6,7},{7,6},{8,9},{9,8},{10,11... | collective-permute-start | bytes 663560 | tf_op jit(solution)/shard_map/ppermute | solution.py:307
  21.3 3.4 %collective-permute-start.5 = (bf16[96,1536]{1,0:T(8,128)(2,1)S(1)}, bf16[96,1536]{1,0:T(8,128)(2,1)S(1)}, u32[]{:S(2)}, u32[]{:S(2)}) collective-permute-start(bf16[96,1536]{1,0:T(8,128)(2,1)S(1)} %collective-permute-done.4.refs_0_.refs_1_), channel_id=1, source_target_pairs={{0,8},{8,0},{16,24},{24,16},{1,9},{9,1},{17,25},{25,17},{2,10},{10... | collective-permute-start | bytes 884744 | tf_op jit(solution)/shard_map/ppermute | solution.py:301
  24.7 6.8 %collective-permute-start.3 = (bf16[96,1536]{1,0:T(8,128)(2,1)S(1)}, bf16[96,1536]{1,0:T(8,128)(2,1)S(1)}, u32[]{:S(2)}, u32[]{:S(2)}) collective-permute-start(bf16[96,1536]{1,0:T(8,128)(2,1)S(1)} %get-tuple-element.78.refs_0_), channel_id=1, source_target_pairs={{0,8},{8,0},{16,24},{24,16},{1,9},{9,1},{17,25},{25,17},{2,10},{10... | collective-permute-start | bytes 884744 | tf_op jit(solution)/shard_map/ppermute | solution.py:301
  24.7 11.2 %collective-permute-start.9 = (bf16[96,1536]{1,0:T(8,128)(2,1)S(1)}, bf16[96,1536]{1,0:T(8,128)(2,1)S(1)}, u32[]{:S(2)}, u32[]{:S(2)}) collective-permute-start(bf16[96,1536]{1,0:T(8,128)(2,1)S(1)} %collective-permute-done.4.refs_0_.refs_1_), channel_id=1, source_target_pairs={{0,2},{2,4},{4,6},{6,0},{1,3},{3,5},{5,7},{7,1},{8,10},{10,12},{12... | collective-permute-start | bytes 884744 | tf_op jit(solution)/shard_map/ppermute | solution.py:310
  29.4 8.3 %collective-permute-start.10 = (bf16[96,1152]{1,0:T(8,128)(2,1)S(1)}, bf16[96,1152]{1,0:T(8,128)(2,1)S(1)}, u32[]{:S(2)}, u32[]{:S(2)}) collective-permute-start(bf16[96,1152]{1,0:T(8,128)(2,1)S(1)} %get-tuple-element.97), channel_id=1, source_target_pairs={{0,1},{1,0},{2,3},{3,2},{4,5},{5,4},{6,7},{7,6},{8,9},{9,8},{10,11... | collective-permute-start | bytes 663560 | tf_op jit(solution)/shard_map/ppermute | solution.py:307
  31.0 17.3 %collective-permute-start.15 = (bf16[2,2,96,768]{3,2,1,0:T(8,128)(2,1)S(1)}, bf16[2,2,96,768]{3,2,1,0:T(8,128)(2,1)S(1)}, u32[]{:S(2)}, u32[]{:S(2)}) collective-permute-start(bf16[2,2,96,768]{3,2,1,0:T(8,128)(2,1)S(1)} %get-tuple-element.105.refs_0_), channel_id=1, source_target_pairs={{0,16},{8,24},{16,0},{24,8},{1,17},{9,25},{17,1},{25,9},{2,18},{10... | collective-permute-start | bytes 1769480 | tf_op jit(solution)/shard_map/ppermute | solution.py:304
  32.7 14.1 %collective-permute-start.16 = (bf16[3,96,768]{2,1,0:T(8,128)(2,1)S(1)}, bf16[3,96,768]{2,1,0:T(8,128)(2,1)S(1)}, u32[]{:S(2)}, u32[]{:S(2)}) collective-permute-start(bf16[3,96,768]{2,1,0:T(8,128)(2,1)S(1)} %get-tuple-element.106), channel_id=1, source_target_pairs={{0,1},{1,0},{2,3},{3,2},{4,5},{5,4},{6,7},{7,6},{8,9},{9,8},{10,11... | collective-permute-start | bytes 1327112 | tf_op jit(solution)/shard_map/ppermute | solution.py:307
  38.4 5.0 %collective-permute-start.13 = (bf16[96,1536]{1,0:T(8,128)(2,1)S(1)}, bf16[96,1536]{1,0:T(8,128)(2,1)S(1)}, u32[]{:S(2)}, u32[]{:S(2)}) collective-permute-start(bf16[96,1536]{1,0:T(8,128)(2,1)S(1)} %get-tuple-element.102.refs_0_.refs_2_), channel_id=1, source_target_pairs={{0,8},{8,0},{16,24},{24,16},{1,9},{9,1},{17,25},{25,17},{2,10},{10... | collective-permute-start | bytes 884744 | tf_op jit(solution)/shard_map/ppermute | solution.py:301
  41.3 7.1 %collective-permute-start.11 = (bf16[2,96,768]{2,1,0:T(8,128)(2,1)S(1)}, bf16[2,96,768]{2,1,0:T(8,128)(2,1)S(1)}, u32[]{:S(2)}, u32[]{:S(2)}) collective-permute-start(bf16[2,96,768]{2,1,0:T(8,128)(2,1)S(1)} %get-tuple-element.101), channel_id=1, source_target_pairs={{0,8},{8,0},{16,24},{24,16},{1,9},{9,1},{17,25},{25,17},{2,10},{10... | collective-permute-start | bytes 884744 | tf_op jit(solution)/shard_map/ppermute | solution.py:301
  41.8 11.0 %collective-permute-start.12 = (bf16[96,1536]{1,0:T(8,128)(2,1)S(1)}, bf16[96,1536]{1,0:T(8,128)(2,1)S(1)}, u32[]{:S(2)}, u32[]{:S(2)}) collective-permute-start(bf16[96,1536]{1,0:T(8,128)(2,1)S(1)} %collective-permute-done.9.refs_0_), channel_id=1, source_target_pairs={{0,2},{2,4},{4,6},{6,0},{1,3},{3,5},{5,7},{7,1},{8,10},{10,12},{12... | collective-permute-start | bytes 884744 | tf_op jit(solution)/shard_map/ppermute | solution.py:310
  46.2 17.4 %collective-permute-start.19 = (bf16[2,2,96,768]{3,2,1,0:T(8,128)(2,1)S(1)}, bf16[2,2,96,768]{3,2,1,0:T(8,128)(2,1)S(1)}, u32[]{:S(2)}, u32[]{:S(2)}) collective-permute-start(bf16[2,2,96,768]{3,2,1,0:T(8,128)(2,1)S(1)} %get-tuple-element.114.refs_0_), channel_id=1, source_target_pairs={{0,16},{8,24},{16,0},{24,8},{1,17},{9,25},{17,1},{25,9},{2,18},{10... | collective-permute-start | bytes 1769480 | tf_op jit(solution)/shard_map/ppermute | solution.py:304
  46.8 8.3 %collective-permute-start.14 = (bf16[96,1152]{1,0:T(8,128)(2,1)S(1)}, bf16[96,1152]{1,0:T(8,128)(2,1)S(1)}, u32[]{:S(2)}, u32[]{:S(2)}) collective-permute-start(bf16[96,1152]{1,0:T(8,128)(2,1)S(1)} %get-tuple-element.104), channel_id=1, source_target_pairs={{0,1},{1,0},{2,3},{3,2},{4,5},{5,4},{6,7},{7,6},{8,9},{9,8},{10,11... | collective-permute-start | bytes 663560 | tf_op jit(solution)/shard_map/ppermute | solution.py:307
  49.5 14.1 %collective-permute-start.20 = (bf16[3,96,768]{2,1,0:T(8,128)(2,1)S(1)}, bf16[3,96,768]{2,1,0:T(8,128)(2,1)S(1)}, u32[]{:S(2)}, u32[]{:S(2)}) collective-permute-start(bf16[3,96,768]{2,1,0:T(8,128)(2,1)S(1)} %get-tuple-element.115), channel_id=1, source_target_pairs={{0,1},{1,0},{2,3},{3,2},{4,5},{5,4},{6,7},{7,6},{8,9},{9,8},{10,11... | collective-permute-start | bytes 1327112 | tf_op jit(solution)/shard_map/ppermute | solution.py:307
  55.7 3.5 %collective-permute-start.17 = (bf16[96,1536]{1,0:T(8,128)(2,1)S(1)}, bf16[96,1536]{1,0:T(8,128)(2,1)S(1)}, u32[]{:S(2)}, u32[]{:S(2)}) collective-permute-start(bf16[96,1536]{1,0:T(8,128)(2,1)S(1)} %get-tuple-element.109.refs_0_), channel_id=1, source_target_pairs={{0,8},{8,0},{16,24},{24,16},{1,9},{9,1},{17,25},{25,17},{2,10},{10... | collective-permute-start | bytes 884744 | tf_op jit(solution)/shard_map/ppermute | solution.py:301
  55.8 14.6 %collective-permute-start.23 = (bf16[192,1152]{1,0:T(8,128)(2,1)S(1)}, bf16[192,1152]{1,0:T(8,128)(2,1)S(1)}, u32[]{:S(2)}, u32[]{:S(2)}) collective-permute-start(bf16[192,1152]{1,0:T(8,128)(2,1)S(1)} %get-tuple-element.120.refs_9_), channel_id=1, source_target_pairs={{0,8},{8,0},{16,24},{24,16},{1,9},{9,1},{17,25},{25,17},{2,10},{10... | collective-permute-start | bytes 1327112 | tf_op jit(solution)/shard_map/ppermute | solution.py:301
  59.1 7.8 %collective-permute-start.24 = (bf16[2,96,768]{2,1,0:T(8,128)(2,1)S(1)}, bf16[2,96,768]{2,1,0:T(8,128)(2,1)S(1)}, u32[]{:S(2)}, u32[]{:S(2)}) collective-permute-start(bf16[2,96,768]{2,1,0:T(8,128)(2,1)S(1)} %get-tuple-element.122), channel_id=1, source_target_pairs={{0,8},{8,0},{16,24},{24,16},{1,9},{9,1},{17,25},{25,17},{2,10},{10... | collective-permute-start | bytes 884744 | tf_op jit(solution)/shard_map/ppermute | solution.py:301
  62.1 20.3 %collective-permute-start.18 = (bf16[2,2,96,768]{3,2,1,0:T(8,128)(2,1)S(1)}, bf16[2,2,96,768]{3,2,1,0:T(8,128)(2,1)S(1)}, u32[]{:S(2)}, u32[]{:S(2)}) collective-permute-start(bf16[2,2,96,768]{3,2,1,0:T(8,128)(2,1)S(1)} %get-tuple-element.113.refs_0_), channel_id=1, source_target_pairs={{0,16},{8,24},{16,0},{24,8},{1,17},{9,25},{17,1},{25,9},{2,18},{10... | collective-permute-start | bytes 1769480 | tf_op jit(solution)/shard_map/ppermute | solution.py:304
  64.8 17.0 %collective-permute-start.21 = (bf16[3,96,768]{2,1,0:T(8,128)(2,1)S(1)}, bf16[3,96,768]{2,1,0:T(8,128)(2,1)S(1)}, u32[]{:S(2)}, u32[]{:S(2)}) collective-permute-start(bf16[3,96,768]{2,1,0:T(8,128)(2,1)S(1)} %get-tuple-element.117), channel_id=1, source_target_pairs={{0,1},{1,0},{2,3},{3,2},{4,5},{5,4},{6,7},{7,6},{8,9},{9,8},{10,11... | collective-permute-start | bytes 1327112 | tf_op jit(solution)/shard_map/ppermute | solution.py:307
  66.4 15.4 %collective-permute-start.22 = (bf16[96,1152]{1,0:T(8,128)(2,1)S(1)}, bf16[96,1152]{1,0:T(8,128)(2,1)S(1)}, u32[]{:S(2)}, u32[]{:S(2)}) collective-permute-start(bf16[96,1152]{1,0:T(8,128)(2,1)S(1)} %get-tuple-element.118), channel_id=1, source_target_pairs={{0,1},{1,0},{2,3},{3,2},{4,5},{5,4},{6,7},{7,6},{8,9},{9,8},{10,11... | collective-permute-start | bytes 663560 | tf_op jit(solution)/shard_map/ppermute | solution.py:307
  70.3 16.1 %collective-permute-start.26 = (bf16[2,96,768]{2,1,0:T(8,128)(2,1)S(1)}, bf16[2,96,768]{2,1,0:T(8,128)(2,1)S(1)}, u32[]{:S(2)}, u32[]{:S(2)}) collective-permute-start(bf16[2,96,768]{2,1,0:T(8,128)(2,1)S(1)} %get-tuple-element.132), channel_id=1, source_target_pairs={{0,8},{8,0},{16,24},{24,16},{1,9},{9,1},{17,25},{25,17},{2,10},{10... | collective-permute-start | bytes 884744 | tf_op jit(solution)/shard_map/ppermute | solution.py:301
  70.4 16.0 %collective-permute-start.27 = (bf16[2,96,768]{2,1,0:T(8,128)(2,1)S(1)}, bf16[2,96,768]{2,1,0:T(8,128)(2,1)S(1)}, u32[]{:S(2)}, u32[]{:S(2)}) collective-permute-start(bf16[2,96,768]{2,1,0:T(8,128)(2,1)S(1)} %get-tuple-element.133), channel_id=1, source_target_pairs={{0,2},{2,4},{4,6},{6,0},{1,3},{3,5},{5,7},{7,1},{8,10},{10,12},{12... | collective-permute-start | bytes 884744 | tf_op jit(solution)/shard_map/ppermute | solution.py:310
  81.8 19.6 %collective-permute-start.33 = (bf16[2,384,768]{2,1,0:T(8,128)(2,1)S(1)}, bf16[2,384,768]{2,1,0:T(8,128)(2,1)S(1)}, u32[]{:S(2)}, u32[]{:S(2)}) collective-permute-start(bf16[2,384,768]{2,1,0:T(8,128)(2,1)S(1)} %get-tuple-element.144), channel_id=1, source_target_pairs={{0,8},{8,0},{16,24},{24,16},{1,9},{9,1},{17,25},{25,17},{2,10},{10... | collective-permute-start | bytes 3538952 | tf_op jit(solution)/shard_map/ppermute | solution.py:301
  81.8 19.6 %collective-permute-start.34 = (bf16[768,768]{1,0:T(8,128)(2,1)S(1)}, bf16[768,768]{1,0:T(8,128)(2,1)S(1)}, u32[]{:S(2)}, u32[]{:S(2)}) collective-permute-start(bf16[768,768]{1,0:T(8,128)(2,1)S(1)} %get-tuple-element.145), channel_id=1, source_target_pairs={{0,8},{8,0},{16,24},{24,16},{1,9},{9,1},{17,25},{25,17},{2,10},{10... | collective-permute-start | bytes 3538952 | tf_op jit(solution)/shard_map/ppermute | solution.py:301
  87.0 10.8 %collective-permute-start.28 = (bf16[2,96,768]{2,1,0:T(8,128)(2,1)S(1)}, bf16[2,96,768]{2,1,0:T(8,128)(2,1)S(1)}, u32[]{:S(2)}, u32[]{:S(2)}) collective-permute-start(bf16[2,96,768]{2,1,0:T(8,128)(2,1)S(1)} %get-tuple-element.135), channel_id=1, source_target_pairs={{0,2},{2,4},{4,6},{6,0},{1,3},{3,5},{5,7},{7,1},{8,10},{10,12},{12... | collective-permute-start | bytes 884744 | tf_op jit(solution)/shard_map/ppermute | solution.py:310
  87.4 12.6 %collective-permute-start.31 = (bf16[3,96,768]{2,1,0:T(8,128)(2,1)S(1)}, bf16[3,96,768]{2,1,0:T(8,128)(2,1)S(1)}, u32[]{:S(2)}, u32[]{:S(2)}) collective-permute-start(bf16[3,96,768]{2,1,0:T(8,128)(2,1)S(1)} %get-tuple-element.139), channel_id=1, source_target_pairs={{0,1},{1,0},{2,3},{3,2},{4,5},{5,4},{6,7},{7,6},{8,9},{9,8},{10,11... | collective-permute-start | bytes 1327112 | tf_op jit(solution)/shard_map/ppermute | solution.py:307
  89.0 13.5 %collective-permute-start.30 = (bf16[6,96,768]{2,1,0:T(8,128)(2,1)S(1)}, bf16[6,96,768]{2,1,0:T(8,128)(2,1)S(1)}, u32[]{:S(2)}, u32[]{:S(2)}) collective-permute-start(bf16[6,96,768]{2,1,0:T(8,128)(2,1)S(1)} %get-tuple-element.138), channel_id=1, source_target_pairs={{0,8},{8,0},{16,24},{24,16},{1,9},{9,1},{17,25},{25,17},{2,10},{10... | collective-permute-start | bytes 2654216 | tf_op jit(solution)/shard_map/ppermute | solution.py:301
  97.8 1.6 %collective-permute-start.25 = (bf16[2,96,768]{2,1,0:T(8,128)(2,1)S(1)}, bf16[2,96,768]{2,1,0:T(8,128)(2,1)S(1)}, u32[]{:S(2)}, u32[]{:S(2)}) collective-permute-start(bf16[2,96,768]{2,1,0:T(8,128)(2,1)S(1)} %get-tuple-element.130), channel_id=1, source_target_pairs={{0,8},{8,0},{16,24},{24,16},{1,9},{9,1},{17,25},{25,17},{2,10},{10... | collective-permute-start | bytes 884744 | tf_op jit(solution)/shard_map/ppermute | solution.py:301
  100.6 1.9 %collective-permute-start.32 = (bf16[3,96,768]{2,1,0:T(8,128)(2,1)S(1)}, bf16[3,96,768]{2,1,0:T(8,128)(2,1)S(1)}, u32[]{:S(2)}, u32[]{:S(2)}) collective-permute-start(bf16[3,96,768]{2,1,0:T(8,128)(2,1)S(1)} %get-tuple-element.141), channel_id=1, source_target_pairs={{0,8},{8,0},{16,24},{24,16},{1,9},{9,1},{17,25},{25,17},{2,10},{10... | collective-permute-start | bytes 1327112 | tf_op jit(solution)/shard_map/ppermute | solution.py:301
  100.8 11.1 %collective-permute-start.29 = (bf16[2,96,768]{2,1,0:T(8,128)(2,1)S(1)}, bf16[2,96,768]{2,1,0:T(8,128)(2,1)S(1)}, u32[]{:S(2)}, u32[]{:S(2)}) collective-permute-start(bf16[2,96,768]{2,1,0:T(8,128)(2,1)S(1)} %get-tuple-element.137), channel_id=1, source_target_pairs={{0,2},{2,4},{4,6},{6,0},{1,3},{3,5},{5,7},{7,1},{8,10},{10,12},{12... | collective-permute-start | bytes 884744 | tf_op jit(solution)/shard_map/ppermute | solution.py:310

commit v4 on v3

v4 whole, which is shorter than its diff:
```python
import functools

import jax
import jax.numpy as jnp
from jax import lax
from jax.experimental import pallas as pl
from jax.experimental.pallas import tpu as pltpu
from jax.sharding import PartitionSpec as P

BF16, F32 = jnp.bfloat16, jnp.float32
MIB = 1024 * 1024
IN_VMEM = pl.BlockSpec(memory_space=pltpu.VMEM)
IN_SMEM = pl.BlockSpec(memory_space=pltpu.SMEM)
IN_HBM = pl.BlockSpec(memory_space=pltpu.HBM)
ANYWHERE = pl.BlockSpec(memory_space=pl.ANY)
TOKEN = jax.ShapeDtypeStruct((8, 128), F32)


RING = True
HOPS = 0
HALVES = 2
COSTS = {}
PLANS = {
    3: (
        (
            ("H", 1), ("G", 0), ("U", 2), ("M", 0), ("H", 2), ("G", 1),
            ("U", 3), ("M", 1), ("H", 3), ("G", 2), ("S", 1), ("M", 2),
            ("E", 0), ("G", 3), ("G", 4), ("C", 0), ("M", 3), ("S", 2),
            ("S", 3), ("L", 0), ("L", 1), ("F", 0),
        ),
        {
            ("H", 1): (("T", 0),),
            ("G", 0): (("O", 0),),
            ("U", 2): (("T", 1),),
            ("U", 3): (("T", 2),),
            ("G", 1): (("Y", 0), ("M", 0),),
            ("G", 2): (("Y", 1),),
            ("G", 3): (("T", 3),),
        },
    ),
}


def default_plan(last):
    order = [("H", 1), ("G", 0)]
    for stage in range(2, last + 1):
        order += [("U", stage), ("M", stage - 2), ("H", stage), ("G", stage - 1)]
        order += [("S", stage - 2)] if stage > 2 else []
    order += [("M", last - 1), ("E", 0), ("C", 0)]
    order += [("G", last + half) for half in range(HALVES)]
    order += [("M", last), ("S", last - 1), ("S", last)]
    return order + [("L", 0), ("L", 1), ("F", 0)], {}


def gelu_parts(hidden_pre):
    normal_cdf = 0.5 * (1.0 + lax.erf(hidden_pre * 0.7071067811865476))
    normal_pdf = jnp.exp(-0.5 * hidden_pre * hidden_pre) * 0.3989422804014327
    return (hidden_pre * normal_cdf, normal_cdf + hidden_pre * normal_pdf)


def dot(left, right, left_dim, right_dim):
    return lax.dot_general(
        left, right, (((left_dim,), (right_dim,)), ((), ())), preferred_element_type=F32
    )


def shape(*sizes, kind=BF16):
    return jax.ShapeDtypeStruct(sizes, kind)


class Chain:
    def __init__(self, where):
        self.where = where
        self.token = jnp.zeros(TOKEN.shape, TOKEN.dtype)
        self.flops = 1000

    def __call__(
        self,
        kernel,
        inputs,
        out_shapes,
        after=(),
        scratch=(),
        limit=16,
        specs=None,
        to=IN_VMEM,
        filled=0,
    ):
        n_in, n_after, n_out = len(inputs), len(after) + 1, len(out_shapes)

        def body(where, *refs):
            ins = refs[:n_in]
            outs = refs[n_in + n_after : n_in + n_after + n_out]
            token = refs[n_in + n_after + n_out]
            kernel(where, ins, outs, refs[n_in + n_after + n_out + 1 :])
            token[...] = jnp.zeros(token.shape, token.dtype)

        *results, self.token = pl.pallas_call(
            body,
            in_specs=[IN_SMEM] + (specs or [IN_VMEM] * n_in) + [ANYWHERE] * n_after,
            out_specs=[to] * n_out + [IN_VMEM],
            out_shape=list(out_shapes) + [TOKEN],
            scratch_shapes=list(scratch),
            input_output_aliases={1 + n_in - filled + k: k for k in range(filled)},
            compiler_params=pltpu.CompilerParams(vmem_limit_bytes=limit * MIB),
            cost_estimate=pl.CostEstimate(
                flops=self.flops, bytes_accessed=1000, transcendentals=0
            ),
        )(self.where, *inputs, *after, self.token)
        return results


def block_of(where, rel, index, width):
    core = where[0] if rel == 0 else 1 - where[0]
    return pl.ds(pl.multiple_of((2 * index + core) * width, 128), width)


def part_of(where, owner, part):
    return pl.ds(pl.multiple_of(owner * part, 128), part)


def cut_shares(where, both, features, messages):
    for k, message in enumerate(messages, 1):
        part = message.shape[1] - features
        owner = lax.rem(where[1] + k, len(messages) + 1)
        message[:, :part] = both[:, part_of(where, owner, part)]
        message[:, part:] = both[:, features : 2 * features]


def fetch(where, rel, sources, targets, semaphores):
    from_in, from_out = sources
    weight_in, weight_out = targets
    copies = []
    for index in range(weight_in.shape[0]):
        cut = block_of(where, rel, index, weight_in.shape[2])
        for source, target in (
            (from_in.at[:, cut], weight_in.at[index]),
            (from_out.at[cut, :], weight_out.at[index]),
        ):
            copies.append(pltpu.make_async_copy(source, target, semaphores.at[len(copies)]))
            copies[-1].start()
    return copies


def fetch_kernel(where, ins, outs, scratch):
    for copy in fetch(where, 1, ins, outs, scratch[0]):
        copy.wait()


def other_kernel(where, ins, outs, scratch):
    *chunk, weight_in, weight_out = ins
    hidden, grad, both, *messages = outs
    features = weight_in.shape[1]
    both[:, :features] = chunk[0][...]
    both[:, features:] = chunk[1][...]
    cut_shares(where, both, features, messages)
    for index in range(weight_in.shape[0]):
        hidden[index] = dot(chunk[0][...], weight_in[index], 1, 0).astype(BF16)
        grad[index] = dot(chunk[1][...], weight_out[index], 1, 1).astype(BF16)


def own_kernel(where, ins, outs, scratch):
    both, *sources = ins
    copies = fetch(where, 0, sources, outs[:2], scratch[0])
    features = outs[0].shape[1]
    for index in range(outs[0].shape[0]):
        for which in range(2):
            copies[2 * index + which].wait()
            left = both[:, which * features : (which + 1) * features]
            outs[2 + which][index] = dot(left, outs[which][index], 1, which).astype(BF16)


def join_kernel(where, ins, outs, scratch):
    for which in range(2):
        total = ins[which][...].astype(F32) + ins[2 + which][...].astype(F32)
        outs[0][which] = total.astype(BF16)


def arrive_kernel(where, ins, outs, scratch):
    outs[0][...] = ins[0][...]
    for number, value in enumerate(ins[1:]):
        rows = value.shape[0]
        outs[1][number * rows : (number + 1) * rows, :] = value[...]


def lay(targets, which, index, value):
    rows = targets[0].shape[2]
    for number, target in enumerate(targets):
        target[which, index] = value[number * rows : (number + 1) * rows]


def hidden_kernel(keep, pieces, where, ins, outs, scratch):
    own, other, own_in, own_out, other_in, other_out = ins
    if keep:
        outs[-2][...] = other_in[...]
        outs[-1][...] = other_out[...]
    cut_shares(where, own, own_in.shape[1], outs[pieces : len(outs) - 2 * keep])
    features = own_in.shape[1]
    tokens, cotangents = slice(0, features), slice(features, 2 * features)
    for index in range(own_in.shape[0]):
        hidden = dot(own[:, tokens], own_in[index], 1, 0)
        hidden += dot(other[:, tokens], other_in[index], 1, 0)
        lay(outs[:pieces], 0, index, hidden.astype(BF16))
        grad = dot(own[:, cotangents], own_out[index], 1, 1)
        grad += dot(other[:, cotangents], other_out[index], 1, 1)
        lay(outs[:pieces], 1, index, grad.astype(BF16))


def gelu_kernel(n_depth, where, ins, outs, scratch):
    blocks = ins[0].shape[1]
    depth = where[1]
    for index in range(blocks):
        hidden, grad = ins[0][0, index].astype(F32), ins[0][1, index].astype(F32)
        for other in ins[1:]:
            hidden += other[0, index].astype(F32)
            grad += other[1, index].astype(F32)
        value, slope = gelu_parts(hidden)
        act, pre = value.astype(BF16), (grad * slope).astype(BF16)
        outs[0][0, index] = act
        outs[0][1, index] = pre
        for message in outs[1:]:
            message[index] = pre
    for k in range(1, len(outs)):
        owner = lax.rem(depth + k, n_depth) if k < n_depth else depth
        outs[k][blocks] = outs[0][0, owner]


def copy_kernel(where, ins, outs, scratch):
    outs[0][...] = ins[0][...]


def model_kernel(pieces, where, ins, outs, scratch):
    pairs, weights = ins[:pieces], ins[pieces:]
    pair = pairs[0]
    if pieces > 1:
        (pair,) = scratch
        rows = pairs[0].shape[2]
        for number, value in enumerate(pairs):
            pair[:, :, number * rows : (number + 1) * rows, :] = value[...]
    for rel, target in enumerate(outs):
        weight_in, weight_out = weights[2 * rel : 2 * rel + 2]
        out = grad = 0.0
        for index in range(pair.shape[1]):
            out += dot(pair[0, index], weight_out[index], 1, 0)
            grad += dot(pair[1, index], weight_in[index], 1, 1)
        target[0] = out.astype(BF16)
        target[1] = grad.astype(BF16)


def sum_kernel(where, ins, outs, scratch):
    for index in range(2):
        total = sum(value[index].astype(F32) for value in ins)
        if len(outs) == 1:
            outs[0][index] = total.astype(BF16)
        else:
            outs[index][...] = total.astype(BF16)


def early_kernel(near, where, ins, outs, scratch):
    all_tokens, all_cotangents, all_values = scratch
    own_in, own_out, other_in, other_out = outs
    blocks, part, width = own_in.shape
    features = own_out.shape[1]
    pairs, shares, came = ins[2 * near : 3 * near], ins[3 * near : 3 * near + 2], ins[3 * near + 2 :]
    rows = ins[0].shape[0]
    for rel in range(2):
        here = slice(rel * part, (rel + 1) * part)
        there = slice(rel * features, (rel + 1) * features)
        for number in range(near):
            at, source = slice(number * rows, (number + 1) * rows), ins[rel * near + number]
            all_tokens[at, here] = source[:, part_of(where, where[1], part)]
            all_cotangents[at, there] = source[:, features : 2 * features]
        for number in range(len(came)):
            at, source = slice(number * rows, (number + 1) * rows), shares[rel]
            start = (near + number) * rows
            all_tokens[start : start + rows, here] = source[at, :part]
            all_cotangents[start : start + rows, there] = source[at, part:]
    acts = [pair.at[0].at[where[1]] for pair in pairs] + [value.at[blocks] for value in came]
    pres = [[pair.at[1].at[index] for index in range(blocks)] for pair in pairs]
    pres += [[value.at[index] for index in range(blocks)] for value in came]

    def fill(sources):
        for number, source in enumerate(sources):
            all_values[number * rows : (number + 1) * rows, :] = source[...]

    for index in range(blocks):
        fill([value[index] for value in pres])
        term = dot(all_tokens[...], all_values[...], 0, 0)
        own_in[index] = term[:part]
        other_in[index] = term[part:].astype(BF16)
    fill(acts)
    term = dot(all_values[...], all_cotangents[...], 0, 0)
    own_out[...] = term[:, :features]
    other_out[...] = term[:, features:].astype(BF16)


def last_kernel(rel, groups, where, ins, outs, scratch):
    all_tokens, all_cotangents, all_values, held_in, held_out, semaphores = scratch
    own, *ins = ins
    shares, values, early = ins[: 2 * groups], ins[2 * groups : -2], ins[-2:]
    if rel:
        values, early = ins[2 * groups : -4], ins[-4:-2]
    rows, part = own.shape[0], all_tokens.shape[1]
    features, width = all_cotangents.shape[1], all_values.shape[1]
    blocks = held_in.shape[0]
    all_tokens[:rows, :] = own[:, part_of(where, where[1], part)]
    all_cotangents[:rows, :] = own[:, features : 2 * features]
    for number, share in enumerate(shares, 1):
        at = slice(number * rows, (number + 1) * rows)
        all_tokens[at, :] = share[:, :part]
        all_cotangents[at, :] = share[:, part:]
    copies = []

    def fill(index):
        row = 0
        for source in values:
            if len(source.shape) == 3:
                value = source[index]
            elif index < blocks:
                value = source[1, index]
            else:
                value = source[0, where[1]]
            all_values[row : row + value.shape[0], :] = value
            row += value.shape[0]

    def put(held, target, term):
        held[...] = term
        copies.append(pltpu.make_async_copy(held, target, semaphores.at[len(copies)]))
        copies[-1].start()

    core = where[0] if rel == 0 else 1 - where[0]
    for index in range(blocks):
        fill(index)
        before = early[0][index].astype(F32)
        term = dot(all_tokens[...], all_values[...], 0, 0) + before
        put(held_in.at[index], outs[0].at[:, block_of(where, rel, index, width)], term)
    fill(blocks)
    term = dot(all_values[...], all_cotangents[...], 0, 0) + early[1][...].astype(F32)
    at = pl.ds(pl.multiple_of(core * width, 128), width)
    put(held_out, outs[1].at[at, :], term)
    for copy in copies:
        copy.wait()


def shards(n_row, n_col, n_depth, tokens, weight_in, weight_out, output_grad):
    rows, features = tokens.shape
    part = features // n_depth
    blocks, width = n_depth, weight_in.shape[1] // (2 * n_depth)
    core = lax.axis_index("row") % 2
    depth = lax.axis_index("depth")
    chain = Chain(jnp.stack([core, depth]).astype(jnp.int32))

    def swap_cores(value):
        return lax.ppermute(value, "row", [(r, r ^ 1) for r in range(n_row)])

    def to_chip(value, k):
        return lax.ppermute(value, "row", [(r, (r + 2 * k) % n_row) for r in range(n_row)])

    def to_depth(value, k):
        return lax.ppermute(value, "depth", [(d, (d + k) % n_depth) for d in range(n_depth)])

    def to_col(value, k):
        return lax.ppermute(value, "col", [(c, (c + k) % n_col) for c in range(n_col)])

    single, pair_shape = shape(blocks, rows, width), shape(2, blocks, rows, width)
    model_shape = shape(2, rows, features)
    message_shape = shape(blocks + 1, rows, width)
    weight_shapes = [shape(blocks, features, width), shape(blocks, width, features)]
    groups = n_depth - 1
    last = n_col - 1
    own, other, shares = {}, {}, {}
    chip, crossed, pairs, came, model = {}, {}, {}, {}, {}

    def cross(stage):
        crossed[stage] = [
            [to_chip(value, k) for k in range(1, n_row // 2)] for value in chip[stage]
        ]

    ready = {}
    share_shapes = [shape(rows, part + features)] * groups
    semaphores = [pltpu.SemaphoreType.DMA((2 * blocks,))]

    def send_shares(stage, values):
        shares[stage] = [to_depth(value, k) for k, value in enumerate(values, 1)]
        ready["T", stage] = shares[stage]

    kept_weights = chain(
        fetch_kernel,
        [weight_in, weight_out],
        weight_shapes,
        scratch=semaphores,
        specs=[IN_HBM] * 2,
        limit=49,
    )
    other_weights = [swap_cores(value) for value in kept_weights]
    hidden, grad, own[0], *results = chain(
        other_kernel,
        [tokens, output_grad] + kept_weights,
        [single, single, shape(rows, 2 * features)] + share_shapes,
    )
    send_shares(0, results)
    swapped = [swap_cores(value) for value in (hidden, grad)]
    *own_weights, hidden, grad = chain(
        own_kernel,
        [own[0], weight_in, weight_out],
        weight_shapes + [single, single],
        scratch=semaphores,
        specs=[IN_VMEM] + [IN_HBM] * 2,
        limit=46,
    )
    chip[0] = chain(join_kernel, [hidden, grad] + swapped, [pair_shape])
    cross(0)
    other[0] = swap_cores(own[0])
    ready["O", 0] = [other[0]]
    own[1] = to_col(own[0], 1)
    raw, early_shares = {1: own[1]}, []

    def arrive_step(stage, after):
        raw[stage] = to_col(raw[stage - 1], 1)
        near, stacked = [raw[stage]], []
        if stage == last - 1:
            near += [value for earlier in range(stage) for value in shares[earlier]]
            stacked = [shape(stage * groups * rows, part + features)]
        own[stage], *results = chain(
            arrive_kernel, near, [shape(rows, 2 * features)] + stacked, after=after
        )
        if results:
            early_shares.extend(results + [swap_cores(results[0])])

    def hidden_step(stage, after):
        other[stage] = swap_cores(own[stage])
        sends = stage <= last - HOPS
        pieces = HALVES if stage == last else 1
        results = chain(
            functools.partial(hidden_kernel, stage == 1, pieces),
            [own[stage], other[stage]] + own_weights + other_weights,
            [shape(2, blocks, rows // pieces, width)] * pieces
            + (share_shapes if sends else [])
            + (weight_shapes if stage == 1 else []),
            after=after,
        )
        chip[stage], results = results[:pieces], results[pieces:]
        if sends:
            send_shares(stage, results[:groups])
        else:
            shares[stage] = [to_col(value, 1) for value in shares[stage - 1]]
            ready["T", stage] = shares[stage]
        if stage == 1:
            other_weights[:] = results[groups * sends :]
        cross(stage)

    def gelu_step(step, after):
        stage = min(step, last)
        piece = step - stage
        size = chip[stage][piece].shape[2]
        inputs = [chip[stage][piece]] + crossed[stage][piece]
        outputs = [shape(2, blocks, size, width)] + [shape(blocks + 1, size, width)] * groups
        if stage == last:
            outputs += [shape(blocks + 1, size, width)]
        pair, *messages = chain(
            functools.partial(gelu_kernel, n_depth), inputs, outputs, after=after
        )
        pairs.setdefault(stage, []).append(pair)
        arrived = [to_depth(value, k) for k, value in enumerate(messages[:groups], 1)]
        came.setdefault(stage, []).append(arrived)
        ready["Y", step] = arrived
        if stage == last:
            late.append(swap_cores(messages[groups]))

    def pass_step(stage, after):
        for value in came[last - 1][0]:
            (copied,) = chain(copy_kernel, [value], [message_shape], after=after)
            late_far.append(swap_cores(copied))
        ready["C", 0] = late_far[:]

    def model_step(stage, after):
        pieces = len(pairs[stage])
        mine, theirs = chain(
            functools.partial(model_kernel, pieces),
            pairs[stage] + own_weights + other_weights,
            [model_shape] * 2,
            after=after,
            scratch=[pltpu.VMEM(pair_shape.shape, BF16)] if pieces > 1 else [],
        )
        model[stage] = [mine, swap_cores(theirs)]
        ready["M", stage] = model[stage][1:]

    def sum_step(stage, after):
        brought = ring.get(stage - 1, []) if RING else []
        (total,) = chain(sum_kernel, model[stage] + brought, [model_shape], after=after)
        if RING:
            ring[stage] = [to_col(total, 1)]
        else:
            ring[stage] = [to_col(total, n_col - stage)]
        ready["S", stage] = ring[stage]

    def early_step(stage, after):
        count = rows * (last + (last - 1) * groups)
        term_sizes = [(blocks, part, width), (width, features)]
        near = list(range(last))
        values = [source[number] for source in (own, other) for number in near]
        values += [pairs[number][0] for number in near] + early_shares
        values += [value for number in range(last - 1) for value in came[number][0]]
        first_in, first_out, sent_in, sent_out = chain(
            functools.partial(early_kernel, last),
            values,
            [shape(*size, kind=kind) for kind in (F32, BF16) for size in term_sizes],
            after=after,
            scratch=[
                pltpu.VMEM((count, 2 * part), BF16),
                pltpu.VMEM((count, 2 * features), BF16),
                pltpu.VMEM((count, width), BF16),
            ],
            limit=24,
        )
        early.extend([first_in, first_out, swap_cores(sent_in), swap_cores(sent_out)])
        ready["E", 0] = early[2:]

    def last_step(rel, after):
        chunk = [own[last]] + shares[last - 1] + shares[last]
        arrived = [half[k] for k in range(groups) for half in came[last]]
        if rel == 0:
            values = pairs[last] + came[last - 1][0] + arrived
            swapped.extend(swap_cores(value) for value in arrived)
        else:
            values = late + late_far + swapped
        inputs = chunk + values + early[2 * rel : 2 * rel + 2] + results[2:]
        count = rows * (1 + 2 * groups)
        grads = [shape(part, 2 * blocks * width, kind=F32), shape(2 * width, features, kind=F32)]
        results[2:] = chain(
            functools.partial(last_kernel, rel, groups),
            inputs,
            grads,
            after=after,
            scratch=[
                pltpu.VMEM((count, part), BF16),
                pltpu.VMEM((count, features), BF16),
                pltpu.VMEM((count, width), BF16),
                pltpu.VMEM((blocks, part, width), F32),
                pltpu.VMEM((width, features), F32),
                pltpu.SemaphoreType.DMA((blocks + 1,)),
            ],
            specs=[IN_VMEM] * (len(inputs) - 2 * rel) + [IN_HBM] * (2 * rel),
            limit=20,
            to=IN_HBM,
            filled=2 * rel,
        )

    def final_step(stage, after):
        values = model[0] + (ring[last] if RING else [v for s in range(1, n_col) for v in ring[s]])
        results[:2] = chain(sum_kernel, values, [shape(rows, features)] * 2, after=after)

    ring, early, results = {}, [], [None, None]
    late, late_far, swapped = [], [], []
    steps = {
        "U": arrive_step,
        "H": hidden_step,
        "G": gelu_step,
        "C": pass_step,
        "M": model_step,
        "S": sum_step,
        "E": early_step,
        "L": last_step,
        "F": final_step,
    }
    order, waits = PLANS.get(last) or default_plan(last)
    for name, stage in order:
        chain.flops = COSTS.get((name, stage), 1000)
        steps[name](stage, [v for key in waits.get((name, stage), ()) for v in ready[key]])
    return tuple(results)


def plain_shards(tokens, weight_in, weight_out, output_grad):
    x_panel = lax.all_gather(tokens, "col", axis=0, tiled=True)
    dy_panel = lax.all_gather(output_grad, "col", axis=0, tiled=True)

    def hidden_total(term):
        return lax.psum(term.astype(BF16), "row").astype(F32)

    def scattered(term, axis):
        return lax.psum_scatter(term.astype(BF16), axis, scatter_dimension=0, tiled=True)

    value, slope = gelu_parts(hidden_total(dot(x_panel, weight_in, 1, 0)))
    act = value.astype(BF16)
    pre = (hidden_total(dot(dy_panel, weight_out, 1, 1)) * slope).astype(BF16)
    return (
        scattered(dot(act, weight_out, 1, 0), "col"),
        scattered(dot(pre, weight_in, 1, 1), "col"),
        scattered(dot(x_panel, pre, 0, 0), "depth").astype(F32),
        scattered(dot(act, dy_panel, 0, 0), "depth").astype(F32),
    )


def solution(mesh):
    placed = (
        P(("col", "depth"), "row"),
        P("row", "col"),
        P("col", "row"),
        P(("col", "depth"), "row"),
    )
    sizes = (mesh.shape["row"], mesh.shape["col"], mesh.shape["depth"])

    def local(tokens, weight_in, weight_out, output_grad):
        arrays = (tokens, weight_in, weight_out, output_grad)
        n_row, n_col, n_depth = sizes
        width, part = weight_in.shape[1] // (2 * n_depth), tokens.shape[1] // n_depth
        fits = width % 128 == 0 and part % 128 == 0 and tokens.shape[0] % (16 * HALVES) == 0
        if fits and n_row % 2 == 0 and n_col > 2 and n_depth > 1:
            return shards(*sizes, *arrays)
        return plain_shards(*arrays)

    return jax.shard_map(
        local,
        mesh=mesh,
        in_specs=placed,
        out_specs=(
            P(("col", "depth"), "row"),
            P(("col", "depth"), "row"),
            P(("row", "depth"), "col"),
            P(("col", "depth"), "row"),
        ),
        check_vma=False,
    )
```

time: 113 us -> 110 us (0.973)
  waiting for transfers between devices: 37.2 us -> 32.3 us
  Pallas kernels: 47.4 us -> 49.3 us
  local copies, waits for them, and re-layouts: 1.82 us -> 0.01 us
  starting transfers between devices: 25.9 us -> 27.1 us
    ppermute x6, waiting for transfers between devices: 19.6 us -> 14.9 us  [to_col(): lax.ppermute(value, 'col', [(c, (c + k) % n_col) for c in range(n_col)])]
    ppermute x4 -> x5, waiting for transfers between devices: 0.01 us -> 2.97 us  [to_chip(): lax.ppermute(value, 'row', [(r, (r + 2 * k) % n_row) for r in range(n_row)])]
    ppermute x8 -> x9, waiting for transfers between devices: 14.8 us -> 12.7 us  [to_depth(): lax.ppermute(value, 'depth', [(d, (d + k) % n_depth) for d in range(n_dep...]
    pallas_call x24 -> x26, Pallas kernels: 47.4 us -> 49.3 us  [__call__(): pl.pallas_call(body, in_specs=[IN_SMEM] + (specs or [IN_VMEM] * n_in) + [...]
    unnamed x6 -> x4, local copies, waits for them, and re-layouts: 1.82 us -> 0.01 us
    ppermute x17 -> x20, waiting for transfers between devices: 2.71 us -> 1.75 us  [swap_cores(): return lax.ppermute(value, 'row', [(r, r ^ 1) for r in range(n_row)])]
    ppermute x17 -> x20, starting transfers between devices: 3.24 us -> 4.01 us  [swap_cores(): return lax.ppermute(value, 'row', [(r, r ^ 1) for r in range(n_row)])]
    ppermute x8 -> x9, starting transfers between devices: 10.2 us -> 10.9 us  [to_depth(): lax.ppermute(value, 'depth', [(d, (d + k) % n_depth) for d in range(n_dep...]
  transfers between devices with their start and end apart: 35 -> 40, of which waited for: 11 -> 15; matrix products, arithmetic and copies ran while one was open for 0% -> 0% of each run, Pallas kernels for 38% -> 41%
where the time goes in v4:
time: 110 us
  Pallas kernels  49.3 us (45%)
  waiting for transfers between devices  32.3 us (29%)
  starting transfers between devices  27.1 us (25%)
    pallas_call x26, Pallas kernels, __call__(): pl.pallas_call(body, in_specs=[IN_SMEM] + (specs or [IN_VMEM] * n_in) + [...  49.3 us
    ppermute x6, waiting for transfers between devices, to_col(): lax.ppermute(value, 'col', [(c, (c + k) % n_col) for c in range(n_col)])  14.9 us
    ppermute x9, waiting for transfers between devices, to_depth(): lax.ppermute(value, 'depth', [(d, (d + k) % n_depth) for d in range(n_dep...  12.7 us
    ppermute x9, starting transfers between devices, to_depth(): lax.ppermute(value, 'depth', [(d, (d + k) % n_depth) for d in range(n_dep...  10.9 us
    ppermute x6, starting transfers between devices, to_col(): lax.ppermute(value, 'col', [(c, (c + k) % n_col) for c in range(n_col)])  7.84 us
    ppermute x5, starting transfers between devices, to_chip(): lax.ppermute(value, 'row', [(r, (r + 2 * k) % n_row) for r in range(n_row)])  4.31 us
    ppermute x20, starting transfers between devices, swap_cores(): return lax.ppermute(value, 'row', [(r, r ^ 1) for r in range(n_row)])  4.01 us
    ppermute x5, waiting for transfers between devices, to_chip(): lax.ppermute(value, 'row', [(r, (r + 2 * k) % n_row) for r in range(n_row)])  2.97 us
  transfers between devices with their start and end apart: 40, of which 15 were waited for; matrix products, arithmetic and copies ran while one was open for 0% of the time, Pallas kernels for 41%

profile of v4, /device:TPU:0, one launch (start us, length us, event | category | flops | bytes accessed | tf_op | source)
XLA Modules:
  0.0 109.7 jit_solution(12305006076900968593)
XLA Ops:
  0.7 2.9 %shard_map.75 = (bf16[2,768,768]{2,1,0:T(8,128)(2,1)S(1)}, bf16[2,768,768]{2,1,0:T(8,128)(2,1)S(1)}, f32[8,128]{1,0:T(8,128)S(1)}) custom-call(s32[2]{0:T(128)S(1)} %pad_add_fusion.where, bf16[768,3072]{1,0:T(8,128)(2,1)} %refs_1_.5, bf16[3072,768]{1,0:T(8,128)(2,1)} %refs_2_.1, f32[8,128]{1,0:T(8,128)S(1)} %broadcast_in_dim.3.refs_2_), custom_call_target="tpu_custom_call" | custom-call | flops 1000 | bytes 1000 | tf_op jit(solution)/shard_map/pallas_call | solution.py:98
  4.3 1.7 %shard_map.76 = (bf16[2,96,768]{2,1,0:T(8,128)(2,1)S(1)}, bf16[2,96,768]{2,1,0:T(8,128)(2,1)S(1)}, bf16[96,1536]{1,0:T(8,128)(2,1)S(1)}, bf16[96,1152]{1,0:T(8,128)(2,1)S(1)}, f32[8,128]{1,0:T(8,128)S(1)}) custom-call(s32[2]{0:T(128)S(1)} %pad_add_fusion.where, bf16[96,768]{1,0:T(8,128)(2,1)S(1)} %copy-done, bf16[96,768]{1,0:T(8,128)(2,1)S(1)} %copy-done.1, ...), custom_call_target="tpu_custom_call" | custom-call | flops 1000 | bytes 1000 | tf_op jit(solution)/shard_map/pallas_call | solution.py:98
  6.6 3.0 %collective-permute-start.4 = (bf16[96,1536]{1,0:T(8,128)(2,1)S(1)}, bf16[96,1536]{1,0:T(8,128)(2,1)S(1)}, u32[]{:S(2)}, u32[]{:S(2)}) collective-permute-start(bf16[96,1536]{1,0:T(8,128)(2,1)S(1)} %get-tuple-element.89.refs_0_), channel_id=1, source_target_pairs={{0,2},{2,4},{4,6},{6,0},{1,3},{3,5},{5,7},{7,1},{8,10},{10,12},{12... | collective-permute-start | bytes 884744 | tf_op jit(solution)/shard_map/ppermute | solution.py:363
  9.6 3.8 %shard_map.77 = (bf16[2,768,768]{2,1,0:T(8,128)(2,1)S(1)}, bf16[2,768,768]{2,1,0:T(8,128)(2,1)S(1)}, bf16[2,96,768]{2,1,0:T(8,128)(2,1)S(1)}, bf16[2,96,768]{2,1,0:T(8,128)(2,1)S(1)}, f32[8,128]{1,0:T(8,128)S(1)}) custom-call(s32[2]{0:T(128)S(1)} %pad_add_fusion.where, bf16[96,1536]{1,0:T(8,128)(2,1)S(1)} %get-tuple-element.89.refs_0_, ...), custom_call_target="tpu_custom_call" | custom-call | flops 1000 | bytes 1000 | tf_op jit(solution)/shard_map/pallas_call | solution.py:98
  13.4 0.7 shard_map.78
  14.1 2.1 %collective-permute-start.2 = (bf16[2,2,96,768]{3,2,1,0:T(8,128)(2,1)S(1)}, bf16[2,2,96,768]{3,2,1,0:T(8,128)(2,1)S(1)}, u32[]{:S(2)}, u32[]{:S(2)}) collective-permute-start(bf16[2,2,96,768]{3,2,1,0:T(8,128)(2,1)S(1)} %get-tuple-element.96.refs_0_), channel_id=1, source_target_pairs={{0,16},{8,24},{16,0},{24,8},{1,17},{9,25},{17,1},{25,9},{2,18},{10... | collective-permute-start | bytes 1769480 | tf_op jit(solution)/shard_map/ppermute | solution.py:357
  16.2 1.5 %collective-permute-start.8 = (bf16[96,1152]{1,0:T(8,128)(2,1)S(1)}, bf16[96,1152]{1,0:T(8,128)(2,1)S(1)}, u32[]{:S(2)}, u32[]{:S(2)}) collective-permute-start(bf16[96,1152]{1,0:T(8,128)(2,1)S(1)} %get-tuple-element.99), channel_id=1, source_target_pairs={{0,1},{1,0},{2,3},{3,2},{4,5},{5,4},{6,7},{7,6},{8,9},{9,8},{10,11... | collective-permute-start | bytes 663560 | tf_op jit(solution)/shard_map/ppermute | solution.py:360
  17.7 1.2 %collective-permute-done.4.refs_0_.refs_1_ = bf16[96,1536]{1,0:T(8,128)(2,1)S(1)} collective-permute-done((bf16[96,1536]{1,0:T(8,128)(2,1)S(1)}, bf16[96,1536]{1,0:T(8,128)(2,1)S(1)}, u32[]{:S(2)}, u32[]{:S(2)}) %collective-permute-start.4) | collective-permute-done | bytes 294944 | tf_op jit(solution)/shard_map/ppermute | solution.py:363
  18.9 4.5 %collective-permute-done.8.refs_6_.refs_1_ = bf16[96,1152]{1,0:T(8,128)(2,1)S(1)} collective-permute-done((bf16[96,1152]{1,0:T(8,128)(2,1)S(1)}, bf16[96,1152]{1,0:T(8,128)(2,1)S(1)}, u32[]{:S(2)}, u32[]{:S(2)}) %collective-permute-start.8) | collective-permute-done | bytes 221216 | tf_op jit(solution)/shard_map/ppermute | solution.py:360
  23.4 1.6 %collective-permute-start.9 = (bf16[96,1536]{1,0:T(8,128)(2,1)S(1)}, bf16[96,1536]{1,0:T(8,128)(2,1)S(1)}, u32[]{:S(2)}, u32[]{:S(2)}) collective-permute-start(bf16[96,1536]{1,0:T(8,128)(2,1)S(1)} %collective-permute-done.4.refs_0_.refs_1_), channel_id=1, source_target_pairs={{0,2},{2,4},{4,6},{6,0},{1,3},{3,5},{5,7},{7,1},{8,10},{10,12},{12... | collective-permute-start | bytes 884744 | tf_op jit(solution)/shard_map/ppermute | solution.py:363
  24.9 3.1 %shard_map.79 = (bf16[2,2,96,768]{3,2,1,0:T(8,128)(2,1)S(1)}, bf16[96,1152]{1,0:T(8,128)(2,1)S(1)}, bf16[2,768,768]{2,1,0:T(8,128)(2,1)S(1)}, bf16[2,768,768]{2,1,0:T(8,128)(2,1)S(1)}, f32[8,128]{1,0:T(8,128)S(1)}) custom-call(s32[2]{0:T(128)S(1)} %pad_add_fusion.where, bf16[96,1536]{1,0:T(8,128)(2,1)S(1)} %collective-permute-done.4.refs_0_.refs_1_, ...), custom_call_target="tpu_custom_call" | custom-call | flops 1000 | bytes 1000 | tf_op jit(solution)/shard_map/pallas_call | solution.py:98
  28.1 1.6 %collective-permute-start.10 = (bf16[96,1152]{1,0:T(8,128)(2,1)S(1)}, bf16[96,1152]{1,0:T(8,128)(2,1)S(1)}, u32[]{:S(2)}, u32[]{:S(2)}) collective-permute-start(bf16[96,1152]{1,0:T(8,128)(2,1)S(1)} %get-tuple-element.105), channel_id=1, source_target_pairs={{0,1},{1,0},{2,3},{3,2},{4,5},{5,4},{6,7},{7,6},{8,9},{9,8},{10,11... | collective-permute-start | bytes 663560 | tf_op jit(solution)/shard_map/ppermute | solution.py:360
  30.2 1.1 %shard_map.80 = (bf16[2,2,96,768]{3,2,1,0:T(8,128)(2,1)S(1)}, bf16[3,96,768]{2,1,0:T(8,128)(2,1)S(1)}, f32[8,128]{1,0:T(8,128)S(1)}) custom-call(s32[2]{0:T(128)S(1)} %pad_add_fusion.where, bf16[2,2,96,768]{3,2,1,0:T(8,128)(2,1)S(1)} %get-tuple-element.96.refs_0_, bf16[2,2,96,768]{3,2,1,0:T(8,128)(2,1)S(1)} %collective-permute-done.2.refs_1_, ...), custom_call_target="tpu_custom_call" | custom-call | flops 1000 | bytes 1000 | tf_op jit(solution)/shard_map/pallas_call | solution.py:98
  31.3 1.4 %collective-permute-start.16 = (bf16[3,96,768]{2,1,0:T(8,128)(2,1)S(1)}, bf16[3,96,768]{2,1,0:T(8,128)(2,1)S(1)}, u32[]{:S(2)}, u32[]{:S(2)}) collective-permute-start(bf16[3,96,768]{2,1,0:T(8,128)(2,1)S(1)} %get-tuple-element.114), channel_id=1, source_target_pairs={{0,1},{1,0},{2,3},{3,2},{4,5},{5,4},{6,7},{7,6},{8,9},{9,8},{10,11... | collective-permute-start | bytes 1327112 | tf_op jit(solution)/shard_map/ppermute | solution.py:360
  32.8 1.9 %collective-permute-done.9.refs_0_ = bf16[96,1536]{1,0:T(8,128)(2,1)S(1)} collective-permute-done((bf16[96,1536]{1,0:T(8,128)(2,1)S(1)}, bf16[96,1536]{1,0:T(8,128)(2,1)S(1)}, u32[]{:S(2)}, u32[]{:S(2)}) %collective-permute-start.9) | collective-permute-done | bytes 294944 | tf_op jit(solution)/shard_map/ppermute | solution.py:363
  34.6 1.8 %collective-permute-done.10.refs_2_.refs_3_ = bf16[96,1152]{1,0:T(8,128)(2,1)S(1)} collective-permute-done((bf16[96,1152]{1,0:T(8,128)(2,1)S(1)}, bf16[96,1152]{1,0:T(8,128)(2,1)S(1)}, u32[]{:S(2)}, u32[]{:S(2)}) %collective-permute-start.10) | collective-permute-done | bytes 221216 | tf_op jit(solution)/shard_map/ppermute | solution.py:360
  37.1 2.8 %shard_map.82 = (bf16[2,96,768]{2,1,0:T(8,128)(2,1)S(1)}, bf16[2,96,768]{2,1,0:T(8,128)(2,1)S(1)}, f32[8,128]{1,0:T(8,128)S(1)}) custom-call(s32[2]{0:T(128)S(1)} %pad_add_fusion.where, bf16[2,2,96,768]{3,2,1,0:T(8,128)(2,1)S(1)} %get-tuple-element.102.refs_0_.refs_6_, bf16[2,768,768]{2,1,0:T(8,128)(2,1)S(1)} %get-tuple-element.97.refs_2_.refs_1_, ...), custom_call_target="tpu_custom_call" | custom-call | flops 1000 | bytes 1000 | tf_op jit(solution)/shard_map/pallas_call | solution.py:98
  40.4 1.6 %collective-permute-start.12 = (bf16[96,1536]{1,0:T(8,128)(2,1)S(1)}, bf16[96,1536]{1,0:T(8,128)(2,1)S(1)}, u32[]{:S(2)}, u32[]{:S(2)}) collective-permute-start(bf16[96,1536]{1,0:T(8,128)(2,1)S(1)} %collective-permute-done.9.refs_0_), channel_id=1, source_target_pairs={{0,2},{2,4},{4,6},{6,0},{1,3},{3,5},{5,7},{7,1},{8,10},{10,12},{12... | collective-permute-start | bytes 884744 | tf_op jit(solution)/shard_map/ppermute | solution.py:363
  42.0 2.8 %shard_map.83 = (bf16[2,2,96,768]{3,2,1,0:T(8,128)(2,1)S(1)}, bf16[96,1152]{1,0:T(8,128)(2,1)S(1)}, f32[8,128]{1,0:T(8,128)S(1)}) custom-call(s32[2]{0:T(128)S(1)} %pad_add_fusion.where, bf16[96,1536]{1,0:T(8,128)(2,1)S(1)} %get-tuple-element.110.refs_0_.refs_2_, bf16[96,1536]{1,0:T(8,128)(2,1)S(1)} %collective-permute-done.13.refs_1_.refs_5_, ...), custom_call_target="tpu_custom_call" | custom-call | flops 1000 | bytes 1000 | tf_op jit(solution)/shard_map/pallas_call | solution.py:98
  44.8 1.6 %collective-permute-start.14 = (bf16[96,1152]{1,0:T(8,128)(2,1)S(1)}, bf16[96,1152]{1,0:T(8,128)(2,1)S(1)}, u32[]{:S(2)}, u32[]{:S(2)}) collective-permute-start(bf16[96,1152]{1,0:T(8,128)(2,1)S(1)} %get-tuple-element.112), channel_id=1, source_target_pairs={{0,1},{1,0},{2,3},{3,2},{4,5},{5,4},{6,7},{7,6},{8,9},{9,8},{10,11... | collective-permute-start | bytes 663560 | tf_op jit(solution)/shard_map/ppermute | solution.py:360
  47.0 1.1 %shard_map.84 = (bf16[2,2,96,768]{3,2,1,0:T(8,128)(2,1)S(1)}, bf16[3,96,768]{2,1,0:T(8,128)(2,1)S(1)}, f32[8,128]{1,0:T(8,128)S(1)}) custom-call(s32[2]{0:T(128)S(1)} %pad_add_fusion.where, bf16[2,2,96,768]{3,2,1,0:T(8,128)(2,1)S(1)} %get-tuple-element.113.refs_0_, bf16[2,2,96,768]{3,2,1,0:T(8,128)(2,1)S(1)} %collective-permute-done.15.refs_1_, ...), custom_call_target="tpu_custom_call" | custom-call | flops 1000 | bytes 1000 | tf_op jit(solution)/shard_map/pallas_call | solution.py:98
  48.7 2.7 %collective-permute-done.12.refs_0_ = bf16[96,1536]{1,0:T(8,128)(2,1)S(1)} collective-permute-done((bf16[96,1536]{1,0:T(8,128)(2,1)S(1)}, bf16[96,1536]{1,0:T(8,128)(2,1)S(1)}, u32[]{:S(2)}, u32[]{:S(2)}) %collective-permute-start.12) | collective-permute-done | bytes 294944 | tf_op jit(solution)/shard_map/ppermute | solution.py:363
  51.4 1.8 %collective-permute-done.14.refs_1_ = bf16[96,1152]{1,0:T(8,128)(2,1)S(1)} collective-permute-done((bf16[96,1152]{1,0:T(8,128)(2,1)S(1)}, bf16[96,1152]{1,0:T(8,128)(2,1)S(1)}, u32[]{:S(2)}, u32[]{:S(2)}) %collective-permute-start.14) | collective-permute-done | bytes 221216 | tf_op jit(solution)/shard_map/ppermute | solution.py:360
  54.3 2.8 %shard_map.86 = (bf16[2,96,768]{2,1,0:T(8,128)(2,1)S(1)}, bf16[2,96,768]{2,1,0:T(8,128)(2,1)S(1)}, f32[8,128]{1,0:T(8,128)S(1)}) custom-call(s32[2]{0:T(128)S(1)} %pad_add_fusion.where, bf16[2,2,96,768]{3,2,1,0:T(8,128)(2,1)S(1)} %get-tuple-element.118.refs_0_.refs_7_, bf16[2,768,768]{2,1,0:T(8,128)(2,1)S(1)} %get-tuple-element.97.refs_2_.refs_1_, ...), custom_call_target="tpu_custom_call" | custom-call | flops 1000 | bytes 1000 | tf_op jit(solution)/shard_map/pallas_call | solution.py:98
  57.3 2.8 %shard_map.87 = (bf16[2,2,48,768]{3,2,1,0:T(8,128)(2,1)S(1)}, bf16[2,2,48,768]{3,2,1,0:T(8,128)(2,1)S(1)}, bf16[96,1152]{1,0:T(8,128)(2,1)S(1)}, f32[8,128]{1,0:T(8,128)S(1)}) custom-call(s32[2]{0:T(128)S(1)} %pad_add_fusion.where, bf16[96,1536]{1,0:T(8,128)(2,1)S(1)} %get-tuple-element.117.refs_0_, bf16[96,1536]{1,0:T(8,128)(2,1)S(1)} %collective-permute-done.17.refs_1_, ...), custom_call_target="tpu_custom_call" | custom-call | flops 1000 | bytes 1000 | tf_op jit(solution)/shard_map/pallas_call | solution.py:98
  60.1 0.6 collective-permute-start.18
  60.7 1.0 collective-permute-done.21.refs_2_.refs_12_
  61.7 1.5 %collective-permute-start.19 = (bf16[96,1152]{1,0:T(8,128)(2,1)S(1)}, bf16[96,1152]{1,0:T(8,128)(2,1)S(1)}, u32[]{:S(2)}, u32[]{:S(2)}) collective-permute-start(bf16[96,1152]{1,0:T(8,128)(2,1)S(1)} %get-tuple-element.122), channel_id=1, source_target_pairs={{0,1},{1,0},{2,3},{3,2},{4,5},{5,4},{6,7},{7,6},{8,9},{9,8},{10,11... | collective-permute-start | bytes 663560 | tf_op jit(solution)/shard_map/ppermute | solution.py:360
  63.2 1.1 %shard_map.88 = (bf16[2,2,96,768]{3,2,1,0:T(8,128)(2,1)S(1)}, bf16[3,96,768]{2,1,0:T(8,128)(2,1)S(1)}, f32[8,128]{1,0:T(8,128)S(1)}) custom-call(s32[2]{0:T(128)S(1)} %pad_add_fusion.where, bf16[2,2,96,768]{3,2,1,0:T(8,128)(2,1)S(1)} %get-tuple-element.123.refs_0_, bf16[2,2,96,768]{3,2,1,0:T(8,128)(2,1)S(1)} %collective-permute-done.20.refs_1_, ...), custom_call_target="tpu_custom_call" | custom-call | flops 1000 | bytes 1000 | tf_op jit(solution)/shard_map/pallas_call | solution.py:98
  65.5 0.6 shard_map.89
  66.1 2.8 %shard_map.90 = (bf16[2,96,768]{2,1,0:T(8,128)(2,1)S(1)}, bf16[2,96,768]{2,1,0:T(8,128)(2,1)S(1)}, f32[8,128]{1,0:T(8,128)S(1)}) custom-call(s32[2]{0:T(128)S(1)} %pad_add_fusion.where, bf16[2,2,96,768]{3,2,1,0:T(8,128)(2,1)S(1)} %get-tuple-element.126.refs_0_.refs_8_, bf16[2,768,768]{2,1,0:T(8,128)(2,1)S(1)} %get-tuple-element.97.refs_2_.refs_1_, ...), custom_call_target="tpu_custom_call" | custom-call | flops 1000 | bytes 1000 | tf_op jit(solution)/shard_map/pallas_call | solution.py:98
  69.0 3.2 %shard_map.91 = (f32[2,384,768]{2,1,0:T(8,128)S(1)}, f32[768,768]{1,0:T(8,128)S(1)}, bf16[2,384,768]{2,1,0:T(8,128)(2,1)S(1)}, bf16[768,768]{1,0:T(8,128)(2,1)S(1)}, f32[8,128]{1,0:T(8,128)S(1)}) custom-call(s32[2]{0:T(128)S(1)} %pad_add_fusion.where, bf16[96,1536]{1,0:T(8,128)(2,1)S(1)} %get-tuple-element.89.refs_0_, ...), custom_call_target="tpu_custom_call" | custom-call | flops 1000 | bytes 1000 | tf_op jit(solution)/shard_map/pallas_call | solution.py:98
  72.9 3.0 %collective-permute-done.24.refs_1_ = bf16[2,2,48,768]{3,2,1,0:T(8,128)(2,1)S(1)} collective-permute-done((bf16[2,2,48,768]{3,2,1,0:T(8,128)(2,1)S(1)}, bf16[2,2,48,768]{3,2,1,0:T(8,128)(2,1)S(1)}, u32[]{:S(2)}, u32[]{:S(2)}) %collective-permute-start.24) | collective-permute-done | bytes 294944 | tf_op jit(solution)/shard_map/ppermute | solution.py:357
  75.8 1.6 %collective-permute-start.28 = (bf16[2,96,768]{2,1,0:T(8,128)(2,1)S(1)}, bf16[2,96,768]{2,1,0:T(8,128)(2,1)S(1)}, u32[]{:S(2)}, u32[]{:S(2)}) collective-permute-start(bf16[2,96,768]{2,1,0:T(8,128)(2,1)S(1)} %get-tuple-element.145), channel_id=1, source_target_pairs={{0,2},{2,4},{4,6},{6,0},{1,3},{3,5},{5,7},{7,1},{8,10},{10,12},{12... | collective-permute-start | bytes 884744 | tf_op jit(solution)/shard_map/ppermute | solution.py:363
  77.4 0.8 shard_map.92
  78.2 0.8 shard_map.93
  79.1 1.6 %collective-permute-start.36 = (bf16[3,48,768]{2,1,0:T(8,128)(2,1)S(1)}, bf16[3,48,768]{2,1,0:T(8,128)(2,1)S(1)}, u32[]{:S(2)}, u32[]{:S(2)}) collective-permute-start(bf16[3,48,768]{2,1,0:T(8,128)(2,1)S(1)} %get-tuple-element.154), channel_id=1, source_target_pairs={{0,1},{1,0},{2,3},{3,2},{4,5},{5,4},{6,7},{7,6},{8,9},{9,8},{10,11... | collective-permute-start | bytes 663560 | tf_op jit(solution)/shard_map/ppermute | solution.py:360
  81.7 2.8 %shard_map.95 = (bf16[2,96,768]{2,1,0:T(8,128)(2,1)S(1)}, bf16[2,96,768]{2,1,0:T(8,128)(2,1)S(1)}, f32[8,128]{1,0:T(8,128)S(1)}) custom-call(s32[2]{0:T(128)S(1)} %pad_add_fusion.where, bf16[2,2,48,768]{3,2,1,0:T(8,128)(2,1)S(1)} %get-tuple-element.134.refs_0_.refs_3_, bf16[2,2,48,768]{3,2,1,0:T(8,128)(2,1)S(1)} %get-tuple-element.137.refs_1_.refs_4_, ...), custom_call_target="tpu_custom_call" | custom-call | flops 1000 | bytes 1000 | tf_op jit(solution)/shard_map/pallas_call | solution.py:98
  84.5 1.7 %collective-permute-done.28.refs_2_ = bf16[2,96,768]{2,1,0:T(8,128)(2,1)S(1)} collective-permute-done((bf16[2,96,768]{2,1,0:T(8,128)(2,1)S(1)}, bf16[2,96,768]{2,1,0:T(8,128)(2,1)S(1)}, u32[]{:S(2)}, u32[]{:S(2)}) %collective-permute-start.28) | collective-permute-done | bytes 294944 | tf_op jit(solution)/shard_map/ppermute | solution.py:363
  86.2 0.7 shard_map.96
  87.5 3.1 %collective-permute-done.34.refs_6_ = bf16[3,48,768]{2,1,0:T(8,128)(2,1)S(1)} collective-permute-done((bf16[3,48,768]{2,1,0:T(8,128)(2,1)S(1)}, bf16[3,48,768]{2,1,0:T(8,128)(2,1)S(1)}, u32[]{:S(2)}, u32[]{:S(2)}) %collective-permute-start.34) | collective-permute-done | bytes 221216 | tf_op jit(solution)/shard_map/ppermute | solution.py:360
  90.6 1.5 %collective-permute-done.32.refs_4_ = bf16[3,48,768]{2,1,0:T(8,128)(2,1)S(1)} collective-permute-done((bf16[3,48,768]{2,1,0:T(8,128)(2,1)S(1)}, bf16[3,48,768]{2,1,0:T(8,128)(2,1)S(1)}, u32[]{:S(2)}, u32[]{:S(2)}) %collective-permute-start.32) | collective-permute-done | bytes 221216 | tf_op jit(solution)/shard_map/ppermute | solution.py:354
  92.2 4.2 %collective-permute-done.29.refs_2_ = bf16[2,96,768]{2,1,0:T(8,128)(2,1)S(1)} collective-permute-done((bf16[2,96,768]{2,1,0:T(8,128)(2,1)S(1)}, bf16[2,96,768]{2,1,0:T(8,128)(2,1)S(1)}, u32[]{:S(2)}, u32[]{:S(2)}) %collective-permute-start.29) | collective-permute-done | bytes 294944 | tf_op jit(solution)/shard_map/ppermute | solution.py:363
  96.9 0.6 shard_map.97
  98.0 3.5 %shard_map.98 = (f32[384,3072]{1,0:T(8,128)}, f32[1536,768]{1,0:T(8,128)}, f32[8,128]{1,0:T(8,128)S(1)}) custom-call(s32[2]{0:T(128)S(1)} %pad_add_fusion.where, bf16[96,1536]{1,0:T(8,128)(2,1)S(1)} %get-tuple-element.117.refs_0_, bf16[96,1152]{1,0:T(8,128)(2,1)S(1)} %collective-permute-done.14.refs_1_, ...), custom_call_target="tpu_custom_call" | custom-call | flops 1000 | bytes 1000 | tf_op jit(solution)/shard_map/pallas_call | solution.py:98
  101.6 3.5 %shard_map.99 = (f32[384,3072]{1,0:T(8,128)}, f32[1536,768]{1,0:T(8,128)}, f32[8,128]{1,0:T(8,128)S(1)}) custom-call(s32[2]{0:T(128)S(1)} %pad_add_fusion.where, bf16[96,1536]{1,0:T(8,128)(2,1)S(1)} %get-tuple-element.117.refs_0_, bf16[96,1152]{1,0:T(8,128)(2,1)S(1)} %collective-permute-done.14.refs_1_, ...), custom_call_target="tpu_custom_call", output_to_operand_aliasing={{0}: (11, {}), {1}: (12, {})} | custom-call | flops 1000 | bytes 1000 | tf_op jit(solution)/shard_map/pallas_call | solution.py:98
  105.1 3.3 %collective-permute-done.30.refs_2_ = bf16[2,96,768]{2,1,0:T(8,128)(2,1)S(1)} collective-permute-done((bf16[2,96,768]{2,1,0:T(8,128)(2,1)S(1)}, bf16[2,96,768]{2,1,0:T(8,128)(2,1)S(1)}, u32[]{:S(2)}, u32[]{:S(2)}) %collective-permute-start.30) | collective-permute-done | bytes 294944 | tf_op jit(solution)/shard_map/ppermute | solution.py:363
  108.3 1.3 %shard_map.100 = (bf16[96,768]{1,0:T(8,128)(2,1)}, bf16[96,768]{1,0:T(8,128)(2,1)}, f32[8,128]{1,0:T(8,128)}) custom-call(s32[2]{0:T(128)S(1)} %pad_add_fusion.where, bf16[2,96,768]{2,1,0:T(8,128)(2,1)S(1)} %get-tuple-element.108.refs_0_, bf16[2,96,768]{2,1,0:T(8,128)(2,1)S(1)} %collective-permute-done.11.refs_3_.refs_1_, ...), custom_call_target="tpu_custom_call" | custom-call | flops 1000 | bytes 1000 | tf_op jit(solution)/shard_map/pallas_call | solution.py:98
  (64 shorter events, 10.0 us)
Async XLA Ops:
  0.7 3.5 %copy-start = (bf16[96,768]{1,0:T(8,128)(2,1)S(1)}, bf16[96,768]{1,0:T(8,128)(2,1)}, u32[]{:S(2)}) copy-start(bf16[96,768]{1,0:T(8,128)(2,1)} %refs_0_.3) | copy-start | bytes 442372
  0.7 3.5 %copy-start.1 = (bf16[96,768]{1,0:T(8,128)(2,1)S(1)}, bf16[96,768]{1,0:T(8,128)(2,1)}, u32[]{:S(2)}) copy-start(bf16[96,768]{1,0:T(8,128)(2,1)} %refs_1_.4) | copy-start | bytes 442372
  3.7 21.3 %collective-permute-start.6 = (bf16[2,768,768]{2,1,0:T(8,128)(2,1)S(1)}, bf16[2,768,768]{2,1,0:T(8,128)(2,1)S(1)}, u32[]{:S(2)}, u32[]{:S(2)}) collective-permute-start(bf16[2,768,768]{2,1,0:T(8,128)(2,1)S(1)} %get-tuple-element.86.refs_2_), channel_id=1, source_target_pairs={{0,8},{8,0},{16,24},{24,16},{1,9},{9,1},{17,25},{25,17},{2,10},{10... | collective-permute-start | bytes 7077896 | tf_op jit(solution)/shard_map/ppermute | solution.py:354
  4.2 20.8 %collective-permute-start.7 = (bf16[2,768,768]{2,1,0:T(8,128)(2,1)S(1)}, bf16[2,768,768]{2,1,0:T(8,128)(2,1)S(1)}, u32[]{:S(2)}, u32[]{:S(2)}) collective-permute-start(bf16[2,768,768]{2,1,0:T(8,128)(2,1)S(1)} %get-tuple-element.87.refs_3_), channel_id=1, source_target_pairs={{0,8},{8,0},{16,24},{24,16},{1,9},{9,1},{17,25},{25,17},{2,10},{10... | collective-permute-start | bytes 7077896 | tf_op jit(solution)/shard_map/ppermute | solution.py:354
  6.0 7.4 %collective-permute-start = (bf16[2,96,768]{2,1,0:T(8,128)(2,1)S(1)}, bf16[2,96,768]{2,1,0:T(8,128)(2,1)S(1)}, u32[]{:S(2)}, u32[]{:S(2)}) collective-permute-start(bf16[2,96,768]{2,1,0:T(8,128)(2,1)S(1)} %get-tuple-element.93), channel_id=1, source_target_pairs={{0,8},{8,0},{16,24},{24,16},{1,9},{9,1},{17,25},{25,17},{2,10},{10... | collective-permute-start | bytes 884744 | tf_op jit(solution)/shard_map/ppermute | solution.py:354
  6.5 6.9 %collective-permute-start.1 = (bf16[2,96,768]{2,1,0:T(8,128)(2,1)S(1)}, bf16[2,96,768]{2,1,0:T(8,128)(2,1)S(1)}, u32[]{:S(2)}, u32[]{:S(2)}) collective-permute-start(bf16[2,96,768]{2,1,0:T(8,128)(2,1)S(1)} %get-tuple-element.94), channel_id=1, source_target_pairs={{0,8},{8,0},{16,24},{24,16},{1,9},{9,1},{17,25},{25,17},{2,10},{10... | collective-permute-start | bytes 884744 | tf_op jit(solution)/shard_map/ppermute | solution.py:354
  6.6 12.3 %collective-permute-start.4 = (bf16[96,1536]{1,0:T(8,128)(2,1)S(1)}, bf16[96,1536]{1,0:T(8,128)(2,1)S(1)}, u32[]{:S(2)}, u32[]{:S(2)}) collective-permute-start(bf16[96,1536]{1,0:T(8,128)(2,1)S(1)} %get-tuple-element.89.refs_0_), channel_id=1, source_target_pairs={{0,2},{2,4},{4,6},{6,0},{1,3},{3,5},{5,7},{7,1},{8,10},{10,12},{12... | collective-permute-start | bytes 884744 | tf_op jit(solution)/shard_map/ppermute | solution.py:363
  14.1 16.1 %collective-permute-start.2 = (bf16[2,2,96,768]{3,2,1,0:T(8,128)(2,1)S(1)}, bf16[2,2,96,768]{3,2,1,0:T(8,128)(2,1)S(1)}, u32[]{:S(2)}, u32[]{:S(2)}) collective-permute-start(bf16[2,2,96,768]{3,2,1,0:T(8,128)(2,1)S(1)} %get-tuple-element.96.refs_0_), channel_id=1, source_target_pairs={{0,16},{8,24},{16,0},{24,8},{1,17},{9,25},{17,1},{25,9},{2,18},{10... | collective-permute-start | bytes 1769480 | tf_op jit(solution)/shard_map/ppermute | solution.py:357
  16.2 7.2 %collective-permute-start.8 = (bf16[96,1152]{1,0:T(8,128)(2,1)S(1)}, bf16[96,1152]{1,0:T(8,128)(2,1)S(1)}, u32[]{:S(2)}, u32[]{:S(2)}) collective-permute-start(bf16[96,1152]{1,0:T(8,128)(2,1)S(1)} %get-tuple-element.99), channel_id=1, source_target_pairs={{0,1},{1,0},{2,3},{3,2},{4,5},{5,4},{6,7},{7,6},{8,9},{9,8},{10,11... | collective-permute-start | bytes 663560 | tf_op jit(solution)/shard_map/ppermute | solution.py:360
  18.8 4.5 %collective-permute-start.5 = (bf16[96,1536]{1,0:T(8,128)(2,1)S(1)}, bf16[96,1536]{1,0:T(8,128)(2,1)S(1)}, u32[]{:S(2)}, u32[]{:S(2)}) collective-permute-start(bf16[96,1536]{1,0:T(8,128)(2,1)S(1)} %collective-permute-done.4.refs_0_.refs_1_), channel_id=1, source_target_pairs={{0,8},{8,0},{16,24},{24,16},{1,9},{9,1},{17,25},{25,17},{2,10},{10... | collective-permute-start | bytes 884744 | tf_op jit(solution)/shard_map/ppermute | solution.py:354
  23.4 6.8 %collective-permute-start.3 = (bf16[96,1536]{1,0:T(8,128)(2,1)S(1)}, bf16[96,1536]{1,0:T(8,128)(2,1)S(1)}, u32[]{:S(2)}, u32[]{:S(2)}) collective-permute-start(bf16[96,1536]{1,0:T(8,128)(2,1)S(1)} %get-tuple-element.89.refs_0_), channel_id=1, source_target_pairs={{0,8},{8,0},{16,24},{24,16},{1,9},{9,1},{17,25},{25,17},{2,10},{10... | collective-permute-start | bytes 884744 | tf_op jit(solution)/shard_map/ppermute | solution.py:354
  23.4 11.3 %collective-permute-start.9 = (bf16[96,1536]{1,0:T(8,128)(2,1)S(1)}, bf16[96,1536]{1,0:T(8,128)(2,1)S(1)}, u32[]{:S(2)}, u32[]{:S(2)}) collective-permute-start(bf16[96,1536]{1,0:T(8,128)(2,1)S(1)} %collective-permute-done.4.refs_0_.refs_1_), channel_id=1, source_target_pairs={{0,2},{2,4},{4,6},{6,0},{1,3},{3,5},{5,7},{7,1},{8,10},{10,12},{12... | collective-permute-start | bytes 884744 | tf_op jit(solution)/shard_map/ppermute | solution.py:363
  28.1 8.3 %collective-permute-start.10 = (bf16[96,1152]{1,0:T(8,128)(2,1)S(1)}, bf16[96,1152]{1,0:T(8,128)(2,1)S(1)}, u32[]{:S(2)}, u32[]{:S(2)}) collective-permute-start(bf16[96,1152]{1,0:T(8,128)(2,1)S(1)} %get-tuple-element.105), channel_id=1, source_target_pairs={{0,1},{1,0},{2,3},{3,2},{4,5},{5,4},{6,7},{7,6},{8,9},{9,8},{10,11... | collective-permute-start | bytes 663560 | tf_op jit(solution)/shard_map/ppermute | solution.py:360
  29.7 17.3 %collective-permute-start.15 = (bf16[2,2,96,768]{3,2,1,0:T(8,128)(2,1)S(1)}, bf16[2,2,96,768]{3,2,1,0:T(8,128)(2,1)S(1)}, u32[]{:S(2)}, u32[]{:S(2)}) collective-permute-start(bf16[2,2,96,768]{3,2,1,0:T(8,128)(2,1)S(1)} %get-tuple-element.113.refs_0_), channel_id=1, source_target_pairs={{0,16},{8,24},{16,0},{24,8},{1,17},{9,25},{17,1},{25,9},{2,18},{10... | collective-permute-start | bytes 1769480 | tf_op jit(solution)/shard_map/ppermute | solution.py:357
  31.3 15.1 %collective-permute-start.16 = (bf16[3,96,768]{2,1,0:T(8,128)(2,1)S(1)}, bf16[3,96,768]{2,1,0:T(8,128)(2,1)S(1)}, u32[]{:S(2)}, u32[]{:S(2)}) collective-permute-start(bf16[3,96,768]{2,1,0:T(8,128)(2,1)S(1)} %get-tuple-element.114), channel_id=1, source_target_pairs={{0,1},{1,0},{2,3},{3,2},{4,5},{5,4},{6,7},{7,6},{8,9},{9,8},{10,11... | collective-permute-start | bytes 1327112 | tf_op jit(solution)/shard_map/ppermute | solution.py:360
  37.0 5.0 %collective-permute-start.13 = (bf16[96,1536]{1,0:T(8,128)(2,1)S(1)}, bf16[96,1536]{1,0:T(8,128)(2,1)S(1)}, u32[]{:S(2)}, u32[]{:S(2)}) collective-permute-start(bf16[96,1536]{1,0:T(8,128)(2,1)S(1)} %get-tuple-element.110.refs_0_.refs_2_), channel_id=1, source_target_pairs={{0,8},{8,0},{16,24},{24,16},{1,9},{9,1},{17,25},{25,17},{2,10},{10... | collective-permute-start | bytes 884744 | tf_op jit(solution)/shard_map/ppermute | solution.py:354
  39.9 7.1 %collective-permute-start.11 = (bf16[2,96,768]{2,1,0:T(8,128)(2,1)S(1)}, bf16[2,96,768]{2,1,0:T(8,128)(2,1)S(1)}, u32[]{:S(2)}, u32[]{:S(2)}) collective-permute-start(bf16[2,96,768]{2,1,0:T(8,128)(2,1)S(1)} %get-tuple-element.109), channel_id=1, source_target_pairs={{0,8},{8,0},{16,24},{24,16},{1,9},{9,1},{17,25},{25,17},{2,10},{10... | collective-permute-start | bytes 884744 | tf_op jit(solution)/shard_map/ppermute | solution.py:354
  40.4 11.0 %collective-permute-start.12 = (bf16[96,1536]{1,0:T(8,128)(2,1)S(1)}, bf16[96,1536]{1,0:T(8,128)(2,1)S(1)}, u32[]{:S(2)}, u32[]{:S(2)}) collective-permute-start(bf16[96,1536]{1,0:T(8,128)(2,1)S(1)} %collective-permute-done.9.refs_0_), channel_id=1, source_target_pairs={{0,2},{2,4},{4,6},{6,0},{1,3},{3,5},{5,7},{7,1},{8,10},{10,12},{12... | collective-permute-start | bytes 884744 | tf_op jit(solution)/shard_map/ppermute | solution.py:363
  44.8 8.4 %collective-permute-start.14 = (bf16[96,1152]{1,0:T(8,128)(2,1)S(1)}, bf16[96,1152]{1,0:T(8,128)(2,1)S(1)}, u32[]{:S(2)}, u32[]{:S(2)}) collective-permute-start(bf16[96,1152]{1,0:T(8,128)(2,1)S(1)} %get-tuple-element.112), channel_id=1, source_target_pairs={{0,1},{1,0},{2,3},{3,2},{4,5},{5,4},{6,7},{7,6},{8,9},{9,8},{10,11... | collective-permute-start | bytes 663560 | tf_op jit(solution)/shard_map/ppermute | solution.py:360
  46.4 16.8 %collective-permute-start.20 = (bf16[2,2,96,768]{3,2,1,0:T(8,128)(2,1)S(1)}, bf16[2,2,96,768]{3,2,1,0:T(8,128)(2,1)S(1)}, u32[]{:S(2)}, u32[]{:S(2)}) collective-permute-start(bf16[2,2,96,768]{3,2,1,0:T(8,128)(2,1)S(1)} %get-tuple-element.123.refs_0_), channel_id=1, source_target_pairs={{0,16},{8,24},{16,0},{24,8},{1,17},{9,25},{17,1},{25,9},{2,18},{10... | collective-permute-start | bytes 1769480 | tf_op jit(solution)/shard_map/ppermute | solution.py:357
  48.1 13.6 %collective-permute-start.21 = (bf16[3,96,768]{2,1,0:T(8,128)(2,1)S(1)}, bf16[3,96,768]{2,1,0:T(8,128)(2,1)S(1)}, u32[]{:S(2)}, u32[]{:S(2)}) collective-permute-start(bf16[3,96,768]{2,1,0:T(8,128)(2,1)S(1)} %get-tuple-element.124), channel_id=1, source_target_pairs={{0,1},{1,0},{2,3},{3,2},{4,5},{5,4},{6,7},{7,6},{8,9},{9,8},{10,11... | collective-permute-start | bytes 1327112 | tf_op jit(solution)/shard_map/ppermute | solution.py:360
  53.8 3.5 %collective-permute-start.17 = (bf16[96,1536]{1,0:T(8,128)(2,1)S(1)}, bf16[96,1536]{1,0:T(8,128)(2,1)S(1)}, u32[]{:S(2)}, u32[]{:S(2)}) collective-permute-start(bf16[96,1536]{1,0:T(8,128)(2,1)S(1)} %get-tuple-element.117.refs_0_), channel_id=1, source_target_pairs={{0,8},{8,0},{16,24},{24,16},{1,9},{9,1},{17,25},{25,17},{2,10},{10... | collective-permute-start | bytes 884744 | tf_op jit(solution)/shard_map/ppermute | solution.py:354
  53.8 15.1 %collective-permute-start.22 = (bf16[192,1152]{1,0:T(8,128)(2,1)S(1)}, bf16[192,1152]{1,0:T(8,128)(2,1)S(1)}, u32[]{:S(2)}, u32[]{:S(2)}) collective-permute-start(bf16[192,1152]{1,0:T(8,128)(2,1)S(1)} %get-tuple-element.127.refs_9_), channel_id=1, source_target_pairs={{0,8},{8,0},{16,24},{24,16},{1,9},{9,1},{17,25},{25,17},{2,10},{10... | collective-permute-start | bytes 1327112 | tf_op jit(solution)/shard_map/ppermute | solution.py:354
  57.1 7.8 %collective-permute-start.23 = (bf16[2,96,768]{2,1,0:T(8,128)(2,1)S(1)}, bf16[2,96,768]{2,1,0:T(8,128)(2,1)S(1)}, u32[]{:S(2)}, u32[]{:S(2)}) collective-permute-start(bf16[2,96,768]{2,1,0:T(8,128)(2,1)S(1)} %get-tuple-element.129), channel_id=1, source_target_pairs={{0,8},{8,0},{16,24},{24,16},{1,9},{9,1},{17,25},{25,17},{2,10},{10... | collective-permute-start | bytes 884744 | tf_op jit(solution)/shard_map/ppermute | solution.py:354
  60.1 12.7 %collective-permute-start.18 = (bf16[2,2,48,768]{3,2,1,0:T(8,128)(2,1)S(1)}, bf16[2,2,48,768]{3,2,1,0:T(8,128)(2,1)S(1)}, u32[]{:S(2)}, u32[]{:S(2)}) collective-permute-start(bf16[2,2,48,768]{3,2,1,0:T(8,128)(2,1)S(1)} %get-tuple-element.121.refs_0_), channel_id=1, source_target_pairs={{0,16},{8,24},{16,0},{24,8},{1,17},{9,25},{17,1},{25,9},{2,18},{10... | collective-permute-start | bytes 884744 | tf_op jit(solution)/shard_map/ppermute | solution.py:357
  61.7 10.6 %collective-permute-start.19 = (bf16[96,1152]{1,0:T(8,128)(2,1)S(1)}, bf16[96,1152]{1,0:T(8,128)(2,1)S(1)}, u32[]{:S(2)}, u32[]{:S(2)}) collective-permute-start(bf16[96,1152]{1,0:T(8,128)(2,1)S(1)} %get-tuple-element.122), channel_id=1, source_target_pairs={{0,1},{1,0},{2,3},{3,2},{4,5},{5,4},{6,7},{7,6},{8,9},{9,8},{10,11... | collective-permute-start | bytes 663560 | tf_op jit(solution)/shard_map/ppermute | solution.py:360
  64.3 16.3 %collective-permute-start.25 = (bf16[3,96,768]{2,1,0:T(8,128)(2,1)S(1)}, bf16[3,96,768]{2,1,0:T(8,128)(2,1)S(1)}, u32[]{:S(2)}, u32[]{:S(2)}) collective-permute-start(bf16[3,96,768]{2,1,0:T(8,128)(2,1)S(1)} %get-tuple-element.138), channel_id=1, source_target_pairs={{0,1},{1,0},{2,3},{3,2},{4,5},{5,4},{6,7},{7,6},{8,9},{9,8},{10,11... | collective-permute-start | bytes 1327112 | tf_op jit(solution)/shard_map/ppermute | solution.py:360
  64.9 10.9 %collective-permute-start.24 = (bf16[2,2,48,768]{3,2,1,0:T(8,128)(2,1)S(1)}, bf16[2,2,48,768]{3,2,1,0:T(8,128)(2,1)S(1)}, u32[]{:S(2)}, u32[]{:S(2)}) collective-permute-start(bf16[2,2,48,768]{3,2,1,0:T(8,128)(2,1)S(1)} %get-tuple-element.135.refs_0_), channel_id=1, source_target_pairs={{0,16},{8,24},{16,0},{24,8},{1,17},{9,25},{17,1},{25,9},{2,18},{10... | collective-permute-start | bytes 884744 | tf_op jit(solution)/shard_map/ppermute | solution.py:357
  68.9 10.1 %collective-permute-start.27 = (bf16[2,96,768]{2,1,0:T(8,128)(2,1)S(1)}, bf16[2,96,768]{2,1,0:T(8,128)(2,1)S(1)}, u32[]{:S(2)}, u32[]{:S(2)}) collective-permute-start(bf16[2,96,768]{2,1,0:T(8,128)(2,1)S(1)} %get-tuple-element.144), channel_id=1, source_target_pairs={{0,8},{8,0},{16,24},{24,16},{1,9},{9,1},{17,25},{25,17},{2,10},{10... | collective-permute-start | bytes 884744 | tf_op jit(solution)/shard_map/ppermute | solution.py:354
  72.2 29.3 %collective-permute-start.38 = (bf16[2,384,768]{2,1,0:T(8,128)(2,1)S(1)}, bf16[2,384,768]{2,1,0:T(8,128)(2,1)S(1)}, u32[]{:S(2)}, u32[]{:S(2)}) collective-permute-start(bf16[2,384,768]{2,1,0:T(8,128)(2,1)S(1)} %get-tuple-element.155), channel_id=1, source_target_pairs={{0,8},{8,0},{16,24},{24,16},{1,9},{9,1},{17,25},{25,17},{2,10},{10... | collective-permute-start | bytes 3538952 | tf_op jit(solution)/shard_map/ppermute | solution.py:354
  72.8 28.8 %collective-permute-start.39 = (bf16[768,768]{1,0:T(8,128)(2,1)S(1)}, bf16[768,768]{1,0:T(8,128)(2,1)S(1)}, u32[]{:S(2)}, u32[]{:S(2)}) collective-permute-start(bf16[768,768]{1,0:T(8,128)(2,1)S(1)} %get-tuple-element.156), channel_id=1, source_target_pairs={{0,8},{8,0},{16,24},{24,16},{1,9},{9,1},{17,25},{25,17},{2,10},{10... | collective-permute-start | bytes 3538952 | tf_op jit(solution)/shard_map/ppermute | solution.py:354
  75.8 10.4 %collective-permute-start.28 = (bf16[2,96,768]{2,1,0:T(8,128)(2,1)S(1)}, bf16[2,96,768]{2,1,0:T(8,128)(2,1)S(1)}, u32[]{:S(2)}, u32[]{:S(2)}) collective-permute-start(bf16[2,96,768]{2,1,0:T(8,128)(2,1)S(1)} %get-tuple-element.145), channel_id=1, source_target_pairs={{0,2},{2,4},{4,6},{6,0},{1,3},{3,5},{5,7},{7,1},{8,10},{10,12},{12... | collective-permute-start | bytes 884744 | tf_op jit(solution)/shard_map/ppermute | solution.py:363
  79.1 8.4 %collective-permute-start.36 = (bf16[3,48,768]{2,1,0:T(8,128)(2,1)S(1)}, bf16[3,48,768]{2,1,0:T(8,128)(2,1)S(1)}, u32[]{:S(2)}, u32[]{:S(2)}) collective-permute-start(bf16[3,48,768]{2,1,0:T(8,128)(2,1)S(1)} %get-tuple-element.154), channel_id=1, source_target_pairs={{0,1},{1,0},{2,3},{3,2},{4,5},{5,4},{6,7},{7,6},{8,9},{9,8},{10,11... | collective-permute-start | bytes 663560 | tf_op jit(solution)/shard_map/ppermute | solution.py:360
  80.6 9.9 %collective-permute-start.34 = (bf16[3,48,768]{2,1,0:T(8,128)(2,1)S(1)}, bf16[3,48,768]{2,1,0:T(8,128)(2,1)S(1)}, u32[]{:S(2)}, u32[]{:S(2)}) collective-permute-start(bf16[3,48,768]{2,1,0:T(8,128)(2,1)S(1)} %get-tuple-element.153), channel_id=1, source_target_pairs={{0,1},{1,0},{2,3},{3,2},{4,5},{5,4},{6,7},{7,6},{8,9},{9,8},{10,11... | collective-permute-start | bytes 663560 | tf_op jit(solution)/shard_map/ppermute | solution.py:360
  86.9 9.5 %collective-permute-start.29 = (bf16[2,96,768]{2,1,0:T(8,128)(2,1)S(1)}, bf16[2,96,768]{2,1,0:T(8,128)(2,1)S(1)}, u32[]{:S(2)}, u32[]{:S(2)}) collective-permute-start(bf16[2,96,768]{2,1,0:T(8,128)(2,1)S(1)} %get-tuple-element.147), channel_id=1, source_target_pairs={{0,2},{2,4},{4,6},{6,0},{1,3},{3,5},{5,7},{7,1},{8,10},{10,12},{12... | collective-permute-start | bytes 884744 | tf_op jit(solution)/shard_map/ppermute | solution.py:363
  87.5 8.9 %collective-permute-start.26 = (bf16[2,96,768]{2,1,0:T(8,128)(2,1)S(1)}, bf16[2,96,768]{2,1,0:T(8,128)(2,1)S(1)}, u32[]{:S(2)}, u32[]{:S(2)}) collective-permute-start(bf16[2,96,768]{2,1,0:T(8,128)(2,1)S(1)} %get-tuple-element.142), channel_id=1, source_target_pairs={{0,8},{8,0},{16,24},{24,16},{1,9},{9,1},{17,25},{25,17},{2,10},{10... | collective-permute-start | bytes 884744 | tf_op jit(solution)/shard_map/ppermute | solution.py:354
  90.6 1.5 %collective-permute-start.32 = (bf16[3,48,768]{2,1,0:T(8,128)(2,1)S(1)}, bf16[3,48,768]{2,1,0:T(8,128)(2,1)S(1)}, u32[]{:S(2)}, u32[]{:S(2)}) collective-permute-start(bf16[3,48,768]{2,1,0:T(8,128)(2,1)S(1)} %get-tuple-element.151), channel_id=1, source_target_pairs={{0,8},{8,0},{16,24},{24,16},{1,9},{9,1},{17,25},{25,17},{2,10},{10... | collective-permute-start | bytes 663560 | tf_op jit(solution)/shard_map/ppermute | solution.py:354
  92.1 5.5 %collective-permute-start.31 = (bf16[3,48,768]{2,1,0:T(8,128)(2,1)S(1)}, bf16[3,48,768]{2,1,0:T(8,128)(2,1)S(1)}, u32[]{:S(2)}, u32[]{:S(2)}) collective-permute-start(bf16[3,48,768]{2,1,0:T(8,128)(2,1)S(1)} %get-tuple-element.150), channel_id=1, source_target_pairs={{0,8},{8,0},{16,24},{24,16},{1,9},{9,1},{17,25},{25,17},{2,10},{10... | collective-permute-start | bytes 663560 | tf_op jit(solution)/shard_map/ppermute | solution.py:354
  96.4 1.5 %collective-permute-start.37 = (bf16[3,48,768]{2,1,0:T(8,128)(2,1)S(1)}, bf16[3,48,768]{2,1,0:T(8,128)(2,1)S(1)}, u32[]{:S(2)}, u32[]{:S(2)}) collective-permute-start(bf16[3,48,768]{2,1,0:T(8,128)(2,1)S(1)} %collective-permute-done.36.refs_7_), channel_id=1, source_target_pairs={{0,8},{8,0},{16,24},{24,16},{1,9},{9,1},{17,25},{25,17},{2,10},{10... | collective-permute-start | bytes 663560 | tf_op jit(solution)/shard_map/ppermute | solution.py:354
  96.4 5.1 %collective-permute-start.33 = (bf16[3,96,768]{2,1,0:T(8,128)(2,1)S(1)}, bf16[3,96,768]{2,1,0:T(8,128)(2,1)S(1)}, u32[]{:S(2)}, u32[]{:S(2)}) collective-permute-start(bf16[3,96,768]{2,1,0:T(8,128)(2,1)S(1)} %get-tuple-element.152), channel_id=1, source_target_pairs={{0,8},{8,0},{16,24},{24,16},{1,9},{9,1},{17,25},{25,17},{2,10},{10... | collective-permute-start | bytes 1327112 | tf_op jit(solution)/shard_map/ppermute | solution.py:354
  97.6 10.8 %collective-permute-start.30 = (bf16[2,96,768]{2,1,0:T(8,128)(2,1)S(1)}, bf16[2,96,768]{2,1,0:T(8,128)(2,1)S(1)}, u32[]{:S(2)}, u32[]{:S(2)}) collective-permute-start(bf16[2,96,768]{2,1,0:T(8,128)(2,1)S(1)} %get-tuple-element.149), channel_id=1, source_target_pairs={{0,2},{2,4},{4,6},{6,0},{1,3},{3,5},{5,7},{7,1},{8,10},{10,12},{12... | collective-permute-start | bytes 884744 | tf_op jit(solution)/shard_map/ppermute | solution.py:363
  97.9 3.7 %collective-permute-start.35 = (bf16[3,48,768]{2,1,0:T(8,128)(2,1)S(1)}, bf16[3,48,768]{2,1,0:T(8,128)(2,1)S(1)}, u32[]{:S(2)}, u32[]{:S(2)}) collective-permute-start(bf16[3,48,768]{2,1,0:T(8,128)(2,1)S(1)} %collective-permute-done.34.refs_6_), channel_id=1, source_target_pairs={{0,8},{8,0},{16,24},{24,16},{1,9},{9,1},{17,25},{25,17},{2,10},{10... | collective-permute-start | bytes 663560 | tf_op jit(solution)/shard_map/ppermute | solution.py:354

commit v5 on v4

--- a/solution.py
+++ b/solution.py
@@ -19,7 +19,7 @@
 RING = True
 HOPS = 0
 HALVES = 2
-COSTS = {}
+COSTS = {('G', 4): 3000000000}
 PLANS = {
     3: (
         (
@@ -29,7 +29,6 @@
             ("S", 3), ("L", 0), ("L", 1), ("F", 0),
         ),
         {
-            ("H", 1): (("T", 0),),
             ("G", 0): (("O", 0),),
             ("U", 2): (("T", 1),),
             ("U", 3): (("T", 2),),

time: 110 us -> 106 us (0.964)
  waiting for transfers between devices: 32.3 us -> 27.3 us
  starting transfers between devices: 27.1 us -> 28.6 us
    ppermute x9, waiting for transfers between devices: 12.7 us -> 7.15 us  [to_depth(): lax.ppermute(value, 'depth', [(d, (d + k) % n_depth) for d in range(n_dep...]
    ppermute x5, starting transfers between devices: 4.31 us -> 8.05 us  [to_chip(): lax.ppermute(value, 'row', [(r, (r + 2 * k) % n_row) for r in range(n_row)])]
    ppermute x9, starting transfers between devices: 10.9 us -> 9.58 us  [to_depth(): lax.ppermute(value, 'depth', [(d, (d + k) % n_depth) for d in range(n_dep...]
    ppermute x6, starting transfers between devices: 7.84 us -> 6.55 us  [to_col(): lax.ppermute(value, 'col', [(c, (c + k) % n_col) for c in range(n_col)])]
  transfers between devices with their start and end apart: 40 -> 40, of which waited for: 15 -> 14; matrix products, arithmetic and copies ran while one was open for 0% -> 0% of each run, Pallas kernels for 41% -> 42%
where the time goes in v5:
time: 106 us
  Pallas kernels  49.3 us (47%)
  starting transfers between devices  28.6 us (27%)
  waiting for transfers between devices  27.3 us (26%)
    pallas_call x26, Pallas kernels, __call__(): pl.pallas_call(body, in_specs=[IN_SMEM] + (specs or [IN_VMEM] * n_in) + [...  49.3 us
    ppermute x6, waiting for transfers between devices, to_col(): lax.ppermute(value, 'col', [(c, (c + k) % n_col) for c in range(n_col)])  14.2 us
    ppermute x9, starting transfers between devices, to_depth(): lax.ppermute(value, 'depth', [(d, (d + k) % n_depth) for d in range(n_dep...  9.58 us
    ppermute x5, starting transfers between devices, to_chip(): lax.ppermute(value, 'row', [(r, (r + 2 * k) % n_row) for r in range(n_row)])  8.05 us
    ppermute x9, waiting for transfers between devices, to_depth(): lax.ppermute(value, 'depth', [(d, (d + k) % n_depth) for d in range(n_dep...  7.15 us
    ppermute x6, starting transfers between devices, to_col(): lax.ppermute(value, 'col', [(c, (c + k) % n_col) for c in range(n_col)])  6.55 us
    ppermute x20, starting transfers between devices, swap_cores(): return lax.ppermute(value, 'row', [(r, r ^ 1) for r in range(n_row)])  4.46 us
    ppermute x5, waiting for transfers between devices, to_chip(): lax.ppermute(value, 'row', [(r, (r + 2 * k) % n_row) for r in range(n_row)])  3.14 us
  transfers between devices with their start and end apart: 40, of which 14 were waited for; matrix products, arithmetic and copies ran while one was open for 0% of the time, Pallas kernels for 42%

profile of v5, /device:TPU:0, one launch (start us, length us, event | category | flops | bytes accessed | tf_op | source)
XLA Modules:
  0.0 106.3 jit_solution(399656989847862705)
XLA Ops:
  0.7 2.9 %shard_map.75 = (bf16[2,768,768]{2,1,0:T(8,128)(2,1)S(1)}, bf16[2,768,768]{2,1,0:T(8,128)(2,1)S(1)}, f32[8,128]{1,0:T(8,128)S(1)}) custom-call(s32[2]{0:T(128)S(1)} %pad_add_fusion.where, bf16[768,3072]{1,0:T(8,128)(2,1)} %refs_1_.5, bf16[3072,768]{1,0:T(8,128)(2,1)} %refs_2_.1, f32[8,128]{1,0:T(8,128)S(1)} %broadcast_in_dim.3.refs_2_), custom_call_target="tpu_custom_call" | custom-call | flops 1000 | bytes 1000 | tf_op jit(solution)/shard_map/pallas_call | solution.py:97
  4.3 1.7 %shard_map.76 = (bf16[2,96,768]{2,1,0:T(8,128)(2,1)S(1)}, bf16[2,96,768]{2,1,0:T(8,128)(2,1)S(1)}, bf16[96,1536]{1,0:T(8,128)(2,1)S(1)}, bf16[96,1152]{1,0:T(8,128)(2,1)S(1)}, f32[8,128]{1,0:T(8,128)S(1)}) custom-call(s32[2]{0:T(128)S(1)} %pad_add_fusion.where, bf16[96,768]{1,0:T(8,128)(2,1)S(1)} %copy-done, bf16[96,768]{1,0:T(8,128)(2,1)S(1)} %copy-done.1, ...), custom_call_target="tpu_custom_call" | custom-call | flops 1000 | bytes 1000 | tf_op jit(solution)/shard_map/pallas_call | solution.py:97
  6.6 3.0 %collective-permute-start.4 = (bf16[96,1536]{1,0:T(8,128)(2,1)S(1)}, bf16[96,1536]{1,0:T(8,128)(2,1)S(1)}, u32[]{:S(2)}, u32[]{:S(2)}) collective-permute-start(bf16[96,1536]{1,0:T(8,128)(2,1)S(1)} %get-tuple-element.89.refs_0_), channel_id=1, source_target_pairs={{0,2},{2,4},{4,6},{6,0},{1,3},{3,5},{5,7},{7,1},{8,10},{10,12},{12... | collective-permute-start | bytes 884744 | tf_op jit(solution)/shard_map/ppermute | solution.py:362
  9.6 3.8 %shard_map.77 = (bf16[2,768,768]{2,1,0:T(8,128)(2,1)S(1)}, bf16[2,768,768]{2,1,0:T(8,128)(2,1)S(1)}, bf16[2,96,768]{2,1,0:T(8,128)(2,1)S(1)}, bf16[2,96,768]{2,1,0:T(8,128)(2,1)S(1)}, f32[8,128]{1,0:T(8,128)S(1)}) custom-call(s32[2]{0:T(128)S(1)} %pad_add_fusion.where, bf16[96,1536]{1,0:T(8,128)(2,1)S(1)} %get-tuple-element.89.refs_0_, ...), custom_call_target="tpu_custom_call" | custom-call | flops 1000 | bytes 1000 | tf_op jit(solution)/shard_map/pallas_call | solution.py:97
  13.4 0.7 shard_map.78
  14.1 2.1 %collective-permute-start.2 = (bf16[2,2,96,768]{3,2,1,0:T(8,128)(2,1)S(1)}, bf16[2,2,96,768]{3,2,1,0:T(8,128)(2,1)S(1)}, u32[]{:S(2)}, u32[]{:S(2)}) collective-permute-start(bf16[2,2,96,768]{3,2,1,0:T(8,128)(2,1)S(1)} %get-tuple-element.96.refs_0_), channel_id=1, source_target_pairs={{0,16},{8,24},{16,0},{24,8},{1,17},{9,25},{17,1},{25,9},{2,18},{10... | collective-permute-start | bytes 1769480 | tf_op jit(solution)/shard_map/ppermute | solution.py:356
  16.2 2.7 %collective-permute-done.4.refs_0_.refs_1_ = bf16[96,1536]{1,0:T(8,128)(2,1)S(1)} collective-permute-done((bf16[96,1536]{1,0:T(8,128)(2,1)S(1)}, bf16[96,1536]{1,0:T(8,128)(2,1)S(1)}, u32[]{:S(2)}, u32[]{:S(2)}) %collective-permute-start.4) | collective-permute-done | bytes 294944 | tf_op jit(solution)/shard_map/ppermute | solution.py:362
  19.4 1.1 %collective-permute-done.5.refs_1_.refs_4_ = bf16[96,1536]{1,0:T(8,128)(2,1)S(1)} collective-permute-done((bf16[96,1536]{1,0:T(8,128)(2,1)S(1)}, bf16[96,1536]{1,0:T(8,128)(2,1)S(1)}, u32[]{:S(2)}, u32[]{:S(2)}) %collective-permute-start.5) | collective-permute-done | bytes 294944 | tf_op jit(solution)/shard_map/ppermute | solution.py:353
  20.4 1.5 %collective-permute-start.9 = (bf16[96,1152]{1,0:T(8,128)(2,1)S(1)}, bf16[96,1152]{1,0:T(8,128)(2,1)S(1)}, u32[]{:S(2)}, u32[]{:S(2)}) collective-permute-start(bf16[96,1152]{1,0:T(8,128)(2,1)S(1)} %get-tuple-element.104), channel_id=1, source_target_pairs={{0,1},{1,0},{2,3},{3,2},{4,5},{5,4},{6,7},{7,6},{8,9},{9,8},{10,11... | collective-permute-start | bytes 663560 | tf_op jit(solution)/shard_map/ppermute | solution.py:359
  22.0 3.1 %shard_map.79 = (bf16[2,2,96,768]{3,2,1,0:T(8,128)(2,1)S(1)}, bf16[96,1152]{1,0:T(8,128)(2,1)S(1)}, bf16[2,768,768]{2,1,0:T(8,128)(2,1)S(1)}, bf16[2,768,768]{2,1,0:T(8,128)(2,1)S(1)}, f32[8,128]{1,0:T(8,128)S(1)}) custom-call(s32[2]{0:T(128)S(1)} %pad_add_fusion.where, bf16[96,1536]{1,0:T(8,128)(2,1)S(1)} %collective-permute-done.4.refs_0_.refs_1_, ...), custom_call_target="tpu_custom_call" | custom-call | flops 1000 | bytes 1000 | tf_op jit(solution)/shard_map/pallas_call | solution.py:97
  25.1 0.6 collective-permute-start.10
  25.7 1.5 %collective-permute-start.15 = (bf16[2,2,96,768]{3,2,1,0:T(8,128)(2,1)S(1)}, bf16[2,2,96,768]{3,2,1,0:T(8,128)(2,1)S(1)}, u32[]{:S(2)}, u32[]{:S(2)}) collective-permute-start(bf16[2,2,96,768]{3,2,1,0:T(8,128)(2,1)S(1)} %get-tuple-element.113.refs_0_), channel_id=1, source_target_pairs={{0,16},{8,24},{16,0},{24,8},{1,17},{9,25},{17,1},{25,9},{2,18},{10... | collective-permute-start | bytes 1769480 | tf_op jit(solution)/shard_map/ppermute | solution.py:356
  27.1 3.1 %collective-permute-done.2.refs_1_ = bf16[2,2,96,768]{3,2,1,0:T(8,128)(2,1)S(1)} collective-permute-done((bf16[2,2,96,768]{3,2,1,0:T(8,128)(2,1)S(1)}, bf16[2,2,96,768]{3,2,1,0:T(8,128)(2,1)S(1)}, u32[]{:S(2)}, u32[]{:S(2)}) %collective-permute-start.2) | collective-permute-done | bytes 589856 | tf_op jit(solution)/shard_map/ppermute | solution.py:356
  30.3 1.1 %shard_map.80 = (bf16[2,2,96,768]{3,2,1,0:T(8,128)(2,1)S(1)}, bf16[3,96,768]{2,1,0:T(8,128)(2,1)S(1)}, f32[8,128]{1,0:T(8,128)S(1)}) custom-call(s32[2]{0:T(128)S(1)} %pad_add_fusion.where, bf16[2,2,96,768]{3,2,1,0:T(8,128)(2,1)S(1)} %get-tuple-element.96.refs_0_, bf16[2,2,96,768]{3,2,1,0:T(8,128)(2,1)S(1)} %collective-permute-done.2.refs_1_, ...), custom_call_target="tpu_custom_call" | custom-call | flops 1000 | bytes 1000 | tf_op jit(solution)/shard_map/pallas_call | solution.py:97
  31.4 2.2 %collective-permute-start.16 = (bf16[3,96,768]{2,1,0:T(8,128)(2,1)S(1)}, bf16[3,96,768]{2,1,0:T(8,128)(2,1)S(1)}, u32[]{:S(2)}, u32[]{:S(2)}) collective-permute-start(bf16[3,96,768]{2,1,0:T(8,128)(2,1)S(1)} %get-tuple-element.114), channel_id=1, source_target_pairs={{0,1},{1,0},{2,3},{3,2},{4,5},{5,4},{6,7},{7,6},{8,9},{9,8},{10,11... | collective-permute-start | bytes 1327112 | tf_op jit(solution)/shard_map/ppermute | solution.py:359
  33.6 0.6 shard_map.81
  34.3 2.8 %shard_map.82 = (bf16[2,96,768]{2,1,0:T(8,128)(2,1)S(1)}, bf16[2,96,768]{2,1,0:T(8,128)(2,1)S(1)}, f32[8,128]{1,0:T(8,128)S(1)}) custom-call(s32[2]{0:T(128)S(1)} %pad_add_fusion.where, bf16[2,2,96,768]{3,2,1,0:T(8,128)(2,1)S(1)} %get-tuple-element.101.refs_0_.refs_6_, bf16[2,768,768]{2,1,0:T(8,128)(2,1)S(1)} %get-tuple-element.97.refs_2_.refs_1_, ...), custom_call_target="tpu_custom_call" | custom-call | flops 1000 | bytes 1000 | tf_op jit(solution)/shard_map/pallas_call | solution.py:97
  37.6 1.6 %collective-permute-start.12 = (bf16[96,1536]{1,0:T(8,128)(2,1)S(1)}, bf16[96,1536]{1,0:T(8,128)(2,1)S(1)}, u32[]{:S(2)}, u32[]{:S(2)}) collective-permute-start(bf16[96,1536]{1,0:T(8,128)(2,1)S(1)} %collective-permute-done.8.refs_0_), channel_id=1, source_target_pairs={{0,2},{2,4},{4,6},{6,0},{1,3},{3,5},{5,7},{7,1},{8,10},{10,12},{12... | collective-permute-start | bytes 884744 | tf_op jit(solution)/shard_map/ppermute | solution.py:362
  39.2 2.8 %shard_map.83 = (bf16[2,2,96,768]{3,2,1,0:T(8,128)(2,1)S(1)}, bf16[96,1152]{1,0:T(8,128)(2,1)S(1)}, f32[8,128]{1,0:T(8,128)S(1)}) custom-call(s32[2]{0:T(128)S(1)} %pad_add_fusion.where, bf16[96,1536]{1,0:T(8,128)(2,1)S(1)} %get-tuple-element.110.refs_0_.refs_2_, bf16[96,1536]{1,0:T(8,128)(2,1)S(1)} %collective-permute-done.13.refs_1_.refs_5_, ...), custom_call_target="tpu_custom_call" | custom-call | flops 1000 | bytes 1000 | tf_op jit(solution)/shard_map/pallas_call | solution.py:97
  42.7 1.4 %collective-permute-start.20 = (bf16[2,2,96,768]{3,2,1,0:T(8,128)(2,1)S(1)}, bf16[2,2,96,768]{3,2,1,0:T(8,128)(2,1)S(1)}, u32[]{:S(2)}, u32[]{:S(2)}) collective-permute-start(bf16[2,2,96,768]{3,2,1,0:T(8,128)(2,1)S(1)} %get-tuple-element.123.refs_0_), channel_id=1, source_target_pairs={{0,16},{8,24},{16,0},{24,8},{1,17},{9,25},{17,1},{25,9},{2,18},{10... | collective-permute-start | bytes 1769480 | tf_op jit(solution)/shard_map/ppermute | solution.py:356
  44.1 1.1 %shard_map.84 = (bf16[2,2,96,768]{3,2,1,0:T(8,128)(2,1)S(1)}, bf16[3,96,768]{2,1,0:T(8,128)(2,1)S(1)}, f32[8,128]{1,0:T(8,128)S(1)}) custom-call(s32[2]{0:T(128)S(1)} %pad_add_fusion.where, bf16[2,2,96,768]{3,2,1,0:T(8,128)(2,1)S(1)} %get-tuple-element.113.refs_0_, bf16[2,2,96,768]{3,2,1,0:T(8,128)(2,1)S(1)} %collective-permute-done.15.refs_1_, ...), custom_call_target="tpu_custom_call" | custom-call | flops 1000 | bytes 1000 | tf_op jit(solution)/shard_map/pallas_call | solution.py:97
  45.3 1.6 %collective-permute-start.21 = (bf16[3,96,768]{2,1,0:T(8,128)(2,1)S(1)}, bf16[3,96,768]{2,1,0:T(8,128)(2,1)S(1)}, u32[]{:S(2)}, u32[]{:S(2)}) collective-permute-start(bf16[3,96,768]{2,1,0:T(8,128)(2,1)S(1)} %get-tuple-element.124), channel_id=1, source_target_pairs={{0,1},{1,0},{2,3},{3,2},{4,5},{5,4},{6,7},{7,6},{8,9},{9,8},{10,11... | collective-permute-start | bytes 1327112 | tf_op jit(solution)/shard_map/ppermute | solution.py:359
  46.9 1.8 %collective-permute-done.12.refs_0_ = bf16[96,1536]{1,0:T(8,128)(2,1)S(1)} collective-permute-done((bf16[96,1536]{1,0:T(8,128)(2,1)S(1)}, bf16[96,1536]{1,0:T(8,128)(2,1)S(1)}, u32[]{:S(2)}, u32[]{:S(2)}) %collective-permute-start.12) | collective-permute-done | bytes 294944 | tf_op jit(solution)/shard_map/ppermute | solution.py:362
  48.7 1.7 %collective-permute-done.14.refs_1_ = bf16[96,1152]{1,0:T(8,128)(2,1)S(1)} collective-permute-done((bf16[96,1152]{1,0:T(8,128)(2,1)S(1)}, bf16[96,1152]{1,0:T(8,128)(2,1)S(1)}, u32[]{:S(2)}, u32[]{:S(2)}) %collective-permute-start.14) | collective-permute-done | bytes 221216 | tf_op jit(solution)/shard_map/ppermute | solution.py:359
  51.5 2.8 %shard_map.86 = (bf16[2,96,768]{2,1,0:T(8,128)(2,1)S(1)}, bf16[2,96,768]{2,1,0:T(8,128)(2,1)S(1)}, f32[8,128]{1,0:T(8,128)S(1)}) custom-call(s32[2]{0:T(128)S(1)} %pad_add_fusion.where, bf16[2,2,96,768]{3,2,1,0:T(8,128)(2,1)S(1)} %get-tuple-element.118.refs_0_.refs_7_, bf16[2,768,768]{2,1,0:T(8,128)(2,1)S(1)} %get-tuple-element.97.refs_2_.refs_1_, ...), custom_call_target="tpu_custom_call" | custom-call | flops 1000 | bytes 1000 | tf_op jit(solution)/shard_map/pallas_call | solution.py:97
  54.5 2.8 %shard_map.87 = (bf16[2,2,48,768]{3,2,1,0:T(8,128)(2,1)S(1)}, bf16[2,2,48,768]{3,2,1,0:T(8,128)(2,1)S(1)}, bf16[96,1152]{1,0:T(8,128)(2,1)S(1)}, f32[8,128]{1,0:T(8,128)S(1)}) custom-call(s32[2]{0:T(128)S(1)} %pad_add_fusion.where, bf16[96,1536]{1,0:T(8,128)(2,1)S(1)} %get-tuple-element.117.refs_0_, bf16[96,1536]{1,0:T(8,128)(2,1)S(1)} %collective-permute-done.17.refs_1_, ...), custom_call_target="tpu_custom_call" | custom-call | flops 1000 | bytes 1000 | tf_op jit(solution)/shard_map/pallas_call | solution.py:97
  57.3 1.6 %collective-permute-start.18 = (bf16[2,2,48,768]{3,2,1,0:T(8,128)(2,1)S(1)}, bf16[2,2,48,768]{3,2,1,0:T(8,128)(2,1)S(1)}, u32[]{:S(2)}, u32[]{:S(2)}) collective-permute-start(bf16[2,2,48,768]{3,2,1,0:T(8,128)(2,1)S(1)} %get-tuple-element.121.refs_0_), channel_id=1, source_target_pairs={{0,16},{8,24},{16,0},{24,8},{1,17},{9,25},{17,1},{25,9},{2,18},{10... | collective-permute-start | bytes 884744 | tf_op jit(solution)/shard_map/ppermute | solution.py:356
  58.9 1.5 %collective-permute-start.24 = (bf16[2,2,48,768]{3,2,1,0:T(8,128)(2,1)S(1)}, bf16[2,2,48,768]{3,2,1,0:T(8,128)(2,1)S(1)}, u32[]{:S(2)}, u32[]{:S(2)}) collective-permute-start(bf16[2,2,48,768]{3,2,1,0:T(8,128)(2,1)S(1)} %get-tuple-element.135.refs_0_), channel_id=1, source_target_pairs={{0,16},{8,24},{16,0},{24,8},{1,17},{9,25},{17,1},{25,9},{2,18},{10... | collective-permute-start | bytes 884744 | tf_op jit(solution)/shard_map/ppermute | solution.py:356
  60.9 1.1 %shard_map.88 = (bf16[2,2,96,768]{3,2,1,0:T(8,128)(2,1)S(1)}, bf16[3,96,768]{2,1,0:T(8,128)(2,1)S(1)}, f32[8,128]{1,0:T(8,128)S(1)}) custom-call(s32[2]{0:T(128)S(1)} %pad_add_fusion.where, bf16[2,2,96,768]{3,2,1,0:T(8,128)(2,1)S(1)} %get-tuple-element.123.refs_0_, bf16[2,2,96,768]{3,2,1,0:T(8,128)(2,1)S(1)} %collective-permute-done.20.refs_1_, ...), custom_call_target="tpu_custom_call" | custom-call | flops 1000 | bytes 1000 | tf_op jit(solution)/shard_map/pallas_call | solution.py:97
  62.0 1.6 %collective-permute-start.25 = (bf16[3,96,768]{2,1,0:T(8,128)(2,1)S(1)}, bf16[3,96,768]{2,1,0:T(8,128)(2,1)S(1)}, u32[]{:S(2)}, u32[]{:S(2)}) collective-permute-start(bf16[3,96,768]{2,1,0:T(8,128)(2,1)S(1)} %get-tuple-element.138), channel_id=1, source_target_pairs={{0,1},{1,0},{2,3},{3,2},{4,5},{5,4},{6,7},{7,6},{8,9},{9,8},{10,11... | collective-permute-start | bytes 1327112 | tf_op jit(solution)/shard_map/ppermute | solution.py:359
  63.6 0.6 shard_map.89
  64.3 2.8 %shard_map.90 = (bf16[2,96,768]{2,1,0:T(8,128)(2,1)S(1)}, bf16[2,96,768]{2,1,0:T(8,128)(2,1)S(1)}, f32[8,128]{1,0:T(8,128)S(1)}) custom-call(s32[2]{0:T(128)S(1)} %pad_add_fusion.where, bf16[2,2,96,768]{3,2,1,0:T(8,128)(2,1)S(1)} %get-tuple-element.126.refs_0_.refs_8_, bf16[2,768,768]{2,1,0:T(8,128)(2,1)S(1)} %get-tuple-element.97.refs_2_.refs_1_, ...), custom_call_target="tpu_custom_call" | custom-call | flops 1000 | bytes 1000 | tf_op jit(solution)/shard_map/pallas_call | solution.py:97
  67.2 3.2 %shard_map.91 = (f32[2,384,768]{2,1,0:T(8,128)S(1)}, f32[768,768]{1,0:T(8,128)S(1)}, bf16[2,384,768]{2,1,0:T(8,128)(2,1)S(1)}, bf16[768,768]{1,0:T(8,128)(2,1)S(1)}, f32[8,128]{1,0:T(8,128)S(1)}) custom-call(s32[2]{0:T(128)S(1)} %pad_add_fusion.where, bf16[96,1536]{1,0:T(8,128)(2,1)S(1)} %get-tuple-element.89.refs_0_, ...), custom_call_target="tpu_custom_call" | custom-call | flops 1000 | bytes 1000 | tf_op jit(solution)/shard_map/pallas_call | solution.py:97
  70.4 1.9 %collective-permute-start.28 = (bf16[2,96,768]{2,1,0:T(8,128)(2,1)S(1)}, bf16[2,96,768]{2,1,0:T(8,128)(2,1)S(1)}, u32[]{:S(2)}, u32[]{:S(2)}) collective-permute-start(bf16[2,96,768]{2,1,0:T(8,128)(2,1)S(1)} %get-tuple-element.145), channel_id=1, source_target_pairs={{0,2},{2,4},{4,6},{6,0},{1,3},{3,5},{5,7},{7,1},{8,10},{10,12},{12... | collective-permute-start | bytes 884744 | tf_op jit(solution)/shard_map/ppermute | solution.py:362
  72.5 0.8 shard_map.92
  73.7 0.8 shard_map.93
  75.1 1.0 collective-permute-done.25.refs_0_.refs_5_
  77.2 2.8 %shard_map.95 = (bf16[2,96,768]{2,1,0:T(8,128)(2,1)S(1)}, bf16[2,96,768]{2,1,0:T(8,128)(2,1)S(1)}, f32[8,128]{1,0:T(8,128)S(1)}) custom-call(s32[2]{0:T(128)S(1)} %pad_add_fusion.where, bf16[2,2,48,768]{3,2,1,0:T(8,128)(2,1)S(1)} %get-tuple-element.134.refs_0_.refs_3_, bf16[2,2,48,768]{3,2,1,0:T(8,128)(2,1)S(1)} %get-tuple-element.137.refs_1_.refs_4_, ...), custom_call_target="tpu_custom_call" | custom-call | flops 1000 | bytes 1000 | tf_op jit(solution)/shard_map/pallas_call | solution.py:97
  80.0 1.9 %collective-permute-done.28.refs_2_ = bf16[2,96,768]{2,1,0:T(8,128)(2,1)S(1)} collective-permute-done((bf16[2,96,768]{2,1,0:T(8,128)(2,1)S(1)}, bf16[2,96,768]{2,1,0:T(8,128)(2,1)S(1)}, u32[]{:S(2)}, u32[]{:S(2)}) %collective-permute-start.28) | collective-permute-done | bytes 294944 | tf_op jit(solution)/shard_map/ppermute | solution.py:362
  81.9 0.7 shard_map.96
  82.8 4.0 %collective-permute-done.34.refs_6_ = bf16[3,48,768]{2,1,0:T(8,128)(2,1)S(1)} collective-permute-done((bf16[3,48,768]{2,1,0:T(8,128)(2,1)S(1)}, bf16[3,48,768]{2,1,0:T(8,128)(2,1)S(1)}, u32[]{:S(2)}, u32[]{:S(2)}) %collective-permute-start.34) | collective-permute-done | bytes 221216 | tf_op jit(solution)/shard_map/ppermute | solution.py:359
  86.8 1.5 %collective-permute-done.32.refs_4_ = bf16[3,48,768]{2,1,0:T(8,128)(2,1)S(1)} collective-permute-done((bf16[3,48,768]{2,1,0:T(8,128)(2,1)S(1)}, bf16[3,48,768]{2,1,0:T(8,128)(2,1)S(1)}, u32[]{:S(2)}, u32[]{:S(2)}) %collective-permute-start.32) | collective-permute-done | bytes 221216 | tf_op jit(solution)/shard_map/ppermute | solution.py:353
  88.4 4.6 %collective-permute-done.29.refs_2_ = bf16[2,96,768]{2,1,0:T(8,128)(2,1)S(1)} collective-permute-done((bf16[2,96,768]{2,1,0:T(8,128)(2,1)S(1)}, bf16[2,96,768]{2,1,0:T(8,128)(2,1)S(1)}, u32[]{:S(2)}, u32[]{:S(2)}) %collective-permute-start.29) | collective-permute-done | bytes 294944 | tf_op jit(solution)/shard_map/ppermute | solution.py:362
  93.5 0.6 shard_map.97
  94.6 3.5 %shard_map.98 = (f32[384,3072]{1,0:T(8,128)}, f32[1536,768]{1,0:T(8,128)}, f32[8,128]{1,0:T(8,128)S(1)}) custom-call(s32[2]{0:T(128)S(1)} %pad_add_fusion.where, bf16[96,1536]{1,0:T(8,128)(2,1)S(1)} %get-tuple-element.117.refs_0_, bf16[96,1152]{1,0:T(8,128)(2,1)S(1)} %collective-permute-done.14.refs_1_, ...), custom_call_target="tpu_custom_call" | custom-call | flops 1000 | bytes 1000 | tf_op jit(solution)/shard_map/pallas_call | solution.py:97
  98.2 3.5 %shard_map.99 = (f32[384,3072]{1,0:T(8,128)}, f32[1536,768]{1,0:T(8,128)}, f32[8,128]{1,0:T(8,128)S(1)}) custom-call(s32[2]{0:T(128)S(1)} %pad_add_fusion.where, bf16[96,1536]{1,0:T(8,128)(2,1)S(1)} %get-tuple-element.117.refs_0_, bf16[96,1152]{1,0:T(8,128)(2,1)S(1)} %collective-permute-done.14.refs_1_, ...), custom_call_target="tpu_custom_call", output_to_operand_aliasing={{0}: (11, {}), {1}: (12, {})} | custom-call | flops 1000 | bytes 1000 | tf_op jit(solution)/shard_map/pallas_call | solution.py:97
  101.7 3.3 %collective-permute-done.30.refs_2_ = bf16[2,96,768]{2,1,0:T(8,128)(2,1)S(1)} collective-permute-done((bf16[2,96,768]{2,1,0:T(8,128)(2,1)S(1)}, bf16[2,96,768]{2,1,0:T(8,128)(2,1)S(1)}, u32[]{:S(2)}, u32[]{:S(2)}) %collective-permute-start.30) | collective-permute-done | bytes 294944 | tf_op jit(solution)/shard_map/ppermute | solution.py:362
  105.0 1.3 %shard_map.100 = (bf16[96,768]{1,0:T(8,128)(2,1)}, bf16[96,768]{1,0:T(8,128)(2,1)}, f32[8,128]{1,0:T(8,128)}) custom-call(s32[2]{0:T(128)S(1)} %pad_add_fusion.where, bf16[2,96,768]{2,1,0:T(8,128)(2,1)S(1)} %get-tuple-element.108.refs_0_, bf16[2,96,768]{2,1,0:T(8,128)(2,1)S(1)} %collective-permute-done.11.refs_3_.refs_1_, ...), custom_call_target="tpu_custom_call" | custom-call | flops 1000 | bytes 1000 | tf_op jit(solution)/shard_map/pallas_call | solution.py:97
  (64 shorter events, 8.6 us)
Async XLA Ops:
  0.7 3.5 %copy-start = (bf16[96,768]{1,0:T(8,128)(2,1)S(1)}, bf16[96,768]{1,0:T(8,128)(2,1)}, u32[]{:S(2)}) copy-start(bf16[96,768]{1,0:T(8,128)(2,1)} %refs_0_.3) | copy-start | bytes 442372
  0.7 3.5 %copy-start.1 = (bf16[96,768]{1,0:T(8,128)(2,1)S(1)}, bf16[96,768]{1,0:T(8,128)(2,1)}, u32[]{:S(2)}) copy-start(bf16[96,768]{1,0:T(8,128)(2,1)} %refs_1_.4) | copy-start | bytes 442372
  3.7 16.8 %collective-permute-start.6 = (bf16[2,768,768]{2,1,0:T(8,128)(2,1)S(1)}, bf16[2,768,768]{2,1,0:T(8,128)(2,1)S(1)}, u32[]{:S(2)}, u32[]{:S(2)}) collective-permute-start(bf16[2,768,768]{2,1,0:T(8,128)(2,1)S(1)} %get-tuple-element.86.refs_2_), channel_id=1, source_target_pairs={{0,8},{8,0},{16,24},{24,16},{1,9},{9,1},{17,25},{25,17},{2,10},{10... | collective-permute-start | bytes 7077896 | tf_op jit(solution)/shard_map/ppermute | solution.py:353
  4.2 17.8 %collective-permute-start.7 = (bf16[2,768,768]{2,1,0:T(8,128)(2,1)S(1)}, bf16[2,768,768]{2,1,0:T(8,128)(2,1)S(1)}, u32[]{:S(2)}, u32[]{:S(2)}) collective-permute-start(bf16[2,768,768]{2,1,0:T(8,128)(2,1)S(1)} %get-tuple-element.87.refs_3_), channel_id=1, source_target_pairs={{0,8},{8,0},{16,24},{24,16},{1,9},{9,1},{17,25},{25,17},{2,10},{10... | collective-permute-start | bytes 7077896 | tf_op jit(solution)/shard_map/ppermute | solution.py:353
  6.0 7.4 %collective-permute-start = (bf16[2,96,768]{2,1,0:T(8,128)(2,1)S(1)}, bf16[2,96,768]{2,1,0:T(8,128)(2,1)S(1)}, u32[]{:S(2)}, u32[]{:S(2)}) collective-permute-start(bf16[2,96,768]{2,1,0:T(8,128)(2,1)S(1)} %get-tuple-element.93), channel_id=1, source_target_pairs={{0,8},{8,0},{16,24},{24,16},{1,9},{9,1},{17,25},{25,17},{2,10},{10... | collective-permute-start | bytes 884744 | tf_op jit(solution)/shard_map/ppermute | solution.py:353
  6.5 6.9 %collective-permute-start.1 = (bf16[2,96,768]{2,1,0:T(8,128)(2,1)S(1)}, bf16[2,96,768]{2,1,0:T(8,128)(2,1)S(1)}, u32[]{:S(2)}, u32[]{:S(2)}) collective-permute-start(bf16[2,96,768]{2,1,0:T(8,128)(2,1)S(1)} %get-tuple-element.94), channel_id=1, source_target_pairs={{0,8},{8,0},{16,24},{24,16},{1,9},{9,1},{17,25},{25,17},{2,10},{10... | collective-permute-start | bytes 884744 | tf_op jit(solution)/shard_map/ppermute | solution.py:353
  6.6 12.3 %collective-permute-start.4 = (bf16[96,1536]{1,0:T(8,128)(2,1)S(1)}, bf16[96,1536]{1,0:T(8,128)(2,1)S(1)}, u32[]{:S(2)}, u32[]{:S(2)}) collective-permute-start(bf16[96,1536]{1,0:T(8,128)(2,1)S(1)} %get-tuple-element.89.refs_0_), channel_id=1, source_target_pairs={{0,2},{2,4},{4,6},{6,0},{1,3},{3,5},{5,7},{7,1},{8,10},{10,12},{12... | collective-permute-start | bytes 884744 | tf_op jit(solution)/shard_map/ppermute | solution.py:362
  14.1 16.2 %collective-permute-start.2 = (bf16[2,2,96,768]{3,2,1,0:T(8,128)(2,1)S(1)}, bf16[2,2,96,768]{3,2,1,0:T(8,128)(2,1)S(1)}, u32[]{:S(2)}, u32[]{:S(2)}) collective-permute-start(bf16[2,2,96,768]{3,2,1,0:T(8,128)(2,1)S(1)} %get-tuple-element.96.refs_0_), channel_id=1, source_target_pairs={{0,16},{8,24},{16,0},{24,8},{1,17},{9,25},{17,1},{25,9},{2,18},{10... | collective-permute-start | bytes 1769480 | tf_op jit(solution)/shard_map/ppermute | solution.py:356
  18.8 1.6 %collective-permute-start.5 = (bf16[96,1536]{1,0:T(8,128)(2,1)S(1)}, bf16[96,1536]{1,0:T(8,128)(2,1)S(1)}, u32[]{:S(2)}, u32[]{:S(2)}) collective-permute-start(bf16[96,1536]{1,0:T(8,128)(2,1)S(1)} %collective-permute-done.4.refs_0_.refs_1_), channel_id=1, source_target_pairs={{0,8},{8,0},{16,24},{24,16},{1,9},{9,1},{17,25},{25,17},{2,10},{10... | collective-permute-start | bytes 884744 | tf_op jit(solution)/shard_map/ppermute | solution.py:353
  18.9 6.8 %collective-permute-start.3 = (bf16[96,1536]{1,0:T(8,128)(2,1)S(1)}, bf16[96,1536]{1,0:T(8,128)(2,1)S(1)}, u32[]{:S(2)}, u32[]{:S(2)}) collective-permute-start(bf16[96,1536]{1,0:T(8,128)(2,1)S(1)} %get-tuple-element.89.refs_0_), channel_id=1, source_target_pairs={{0,8},{8,0},{16,24},{24,16},{1,9},{9,1},{17,25},{25,17},{2,10},{10... | collective-permute-start | bytes 884744 | tf_op jit(solution)/shard_map/ppermute | solution.py:353
  20.4 13.2 %collective-permute-start.8 = (bf16[96,1536]{1,0:T(8,128)(2,1)S(1)}, bf16[96,1536]{1,0:T(8,128)(2,1)S(1)}, u32[]{:S(2)}, u32[]{:S(2)}) collective-permute-start(bf16[96,1536]{1,0:T(8,128)(2,1)S(1)} %collective-permute-done.4.refs_0_.refs_1_), channel_id=1, source_target_pairs={{0,2},{2,4},{4,6},{6,0},{1,3},{3,5},{5,7},{7,1},{8,10},{10,12},{12... | collective-permute-start | bytes 884744 | tf_op jit(solution)/shard_map/ppermute | solution.py:362
  20.4 13.1 %collective-permute-start.9 = (bf16[96,1152]{1,0:T(8,128)(2,1)S(1)}, bf16[96,1152]{1,0:T(8,128)(2,1)S(1)}, u32[]{:S(2)}, u32[]{:S(2)}) collective-permute-start(bf16[96,1152]{1,0:T(8,128)(2,1)S(1)} %get-tuple-element.104), channel_id=1, source_target_pairs={{0,1},{1,0},{2,3},{3,2},{4,5},{5,4},{6,7},{7,6},{8,9},{9,8},{10,11... | collective-permute-start | bytes 663560 | tf_op jit(solution)/shard_map/ppermute | solution.py:359
  25.1 8.5 %collective-permute-start.10 = (bf16[96,1152]{1,0:T(8,128)(2,1)S(1)}, bf16[96,1152]{1,0:T(8,128)(2,1)S(1)}, u32[]{:S(2)}, u32[]{:S(2)}) collective-permute-start(bf16[96,1152]{1,0:T(8,128)(2,1)S(1)} %get-tuple-element.105), channel_id=1, source_target_pairs={{0,1},{1,0},{2,3},{3,2},{4,5},{5,4},{6,7},{7,6},{8,9},{9,8},{10,11... | collective-permute-start | bytes 663560 | tf_op jit(solution)/shard_map/ppermute | solution.py:359
  25.7 18.5 %collective-permute-start.15 = (bf16[2,2,96,768]{3,2,1,0:T(8,128)(2,1)S(1)}, bf16[2,2,96,768]{3,2,1,0:T(8,128)(2,1)S(1)}, u32[]{:S(2)}, u32[]{:S(2)}) collective-permute-start(bf16[2,2,96,768]{3,2,1,0:T(8,128)(2,1)S(1)} %get-tuple-element.113.refs_0_), channel_id=1, source_target_pairs={{0,16},{8,24},{16,0},{24,8},{1,17},{9,25},{17,1},{25,9},{2,18},{10... | collective-permute-start | bytes 1769480 | tf_op jit(solution)/shard_map/ppermute | solution.py:356
  31.4 11.3 %collective-permute-start.16 = (bf16[3,96,768]{2,1,0:T(8,128)(2,1)S(1)}, bf16[3,96,768]{2,1,0:T(8,128)(2,1)S(1)}, u32[]{:S(2)}, u32[]{:S(2)}) collective-permute-start(bf16[3,96,768]{2,1,0:T(8,128)(2,1)S(1)} %get-tuple-element.114), channel_id=1, source_target_pairs={{0,1},{1,0},{2,3},{3,2},{4,5},{5,4},{6,7},{7,6},{8,9},{9,8},{10,11... | collective-permute-start | bytes 1327112 | tf_op jit(solution)/shard_map/ppermute | solution.py:359
  34.2 5.0 %collective-permute-start.13 = (bf16[96,1536]{1,0:T(8,128)(2,1)S(1)}, bf16[96,1536]{1,0:T(8,128)(2,1)S(1)}, u32[]{:S(2)}, u32[]{:S(2)}) collective-permute-start(bf16[96,1536]{1,0:T(8,128)(2,1)S(1)} %get-tuple-element.110.refs_0_.refs_2_), channel_id=1, source_target_pairs={{0,8},{8,0},{16,24},{24,16},{1,9},{9,1},{17,25},{25,17},{2,10},{10... | collective-permute-start | bytes 884744 | tf_op jit(solution)/shard_map/ppermute | solution.py:353
  37.1 7.1 %collective-permute-start.11 = (bf16[2,96,768]{2,1,0:T(8,128)(2,1)S(1)}, bf16[2,96,768]{2,1,0:T(8,128)(2,1)S(1)}, u32[]{:S(2)}, u32[]{:S(2)}) collective-permute-start(bf16[2,96,768]{2,1,0:T(8,128)(2,1)S(1)} %get-tuple-element.109), channel_id=1, source_target_pairs={{0,8},{8,0},{16,24},{24,16},{1,9},{9,1},{17,25},{25,17},{2,10},{10... | collective-permute-start | bytes 884744 | tf_op jit(solution)/shard_map/ppermute | solution.py:353
  37.6 11.0 %collective-permute-start.12 = (bf16[96,1536]{1,0:T(8,128)(2,1)S(1)}, bf16[96,1536]{1,0:T(8,128)(2,1)S(1)}, u32[]{:S(2)}, u32[]{:S(2)}) collective-permute-start(bf16[96,1536]{1,0:T(8,128)(2,1)S(1)} %collective-permute-done.8.refs_0_), channel_id=1, source_target_pairs={{0,2},{2,4},{4,6},{6,0},{1,3},{3,5},{5,7},{7,1},{8,10},{10,12},{12... | collective-permute-start | bytes 884744 | tf_op jit(solution)/shard_map/ppermute | solution.py:362
  42.0 8.4 %collective-permute-start.14 = (bf16[96,1152]{1,0:T(8,128)(2,1)S(1)}, bf16[96,1152]{1,0:T(8,128)(2,1)S(1)}, u32[]{:S(2)}, u32[]{:S(2)}) collective-permute-start(bf16[96,1152]{1,0:T(8,128)(2,1)S(1)} %get-tuple-element.112), channel_id=1, source_target_pairs={{0,1},{1,0},{2,3},{3,2},{4,5},{5,4},{6,7},{7,6},{8,9},{9,8},{10,11... | collective-permute-start | bytes 663560 | tf_op jit(solution)/shard_map/ppermute | solution.py:359
  42.7 17.7 %collective-permute-start.20 = (bf16[2,2,96,768]{3,2,1,0:T(8,128)(2,1)S(1)}, bf16[2,2,96,768]{3,2,1,0:T(8,128)(2,1)S(1)}, u32[]{:S(2)}, u32[]{:S(2)}) collective-permute-start(bf16[2,2,96,768]{3,2,1,0:T(8,128)(2,1)S(1)} %get-tuple-element.123.refs_0_), channel_id=1, source_target_pairs={{0,16},{8,24},{16,0},{24,8},{1,17},{9,25},{17,1},{25,9},{2,18},{10... | collective-permute-start | bytes 1769480 | tf_op jit(solution)/shard_map/ppermute | solution.py:356
  45.3 13.6 %collective-permute-start.21 = (bf16[3,96,768]{2,1,0:T(8,128)(2,1)S(1)}, bf16[3,96,768]{2,1,0:T(8,128)(2,1)S(1)}, u32[]{:S(2)}, u32[]{:S(2)}) collective-permute-start(bf16[3,96,768]{2,1,0:T(8,128)(2,1)S(1)} %get-tuple-element.124), channel_id=1, source_target_pairs={{0,1},{1,0},{2,3},{3,2},{4,5},{5,4},{6,7},{7,6},{8,9},{9,8},{10,11... | collective-permute-start | bytes 1327112 | tf_op jit(solution)/shard_map/ppermute | solution.py:359
  51.0 3.5 %collective-permute-start.17 = (bf16[96,1536]{1,0:T(8,128)(2,1)S(1)}, bf16[96,1536]{1,0:T(8,128)(2,1)S(1)}, u32[]{:S(2)}, u32[]{:S(2)}) collective-permute-start(bf16[96,1536]{1,0:T(8,128)(2,1)S(1)} %get-tuple-element.117.refs_0_), channel_id=1, source_target_pairs={{0,8},{8,0},{16,24},{24,16},{1,9},{9,1},{17,25},{25,17},{2,10},{10... | collective-permute-start | bytes 884744 | tf_op jit(solution)/shard_map/ppermute | solution.py:353
  51.0 16.0 %collective-permute-start.22 = (bf16[192,1152]{1,0:T(8,128)(2,1)S(1)}, bf16[192,1152]{1,0:T(8,128)(2,1)S(1)}, u32[]{:S(2)}, u32[]{:S(2)}) collective-permute-start(bf16[192,1152]{1,0:T(8,128)(2,1)S(1)} %get-tuple-element.127.refs_9_), channel_id=1, source_target_pairs={{0,8},{8,0},{16,24},{24,16},{1,9},{9,1},{17,25},{25,17},{2,10},{10... | collective-permute-start | bytes 1327112 | tf_op jit(solution)/shard_map/ppermute | solution.py:353
  54.3 7.7 %collective-permute-start.23 = (bf16[2,96,768]{2,1,0:T(8,128)(2,1)S(1)}, bf16[2,96,768]{2,1,0:T(8,128)(2,1)S(1)}, u32[]{:S(2)}, u32[]{:S(2)}) collective-permute-start(bf16[2,96,768]{2,1,0:T(8,128)(2,1)S(1)} %get-tuple-element.129), channel_id=1, source_target_pairs={{0,8},{8,0},{16,24},{24,16},{1,9},{9,1},{17,25},{25,17},{2,10},{10... | collective-permute-start | bytes 884744 | tf_op jit(solution)/shard_map/ppermute | solution.py:353
  57.3 15.0 %collective-permute-start.18 = (bf16[2,2,48,768]{3,2,1,0:T(8,128)(2,1)S(1)}, bf16[2,2,48,768]{3,2,1,0:T(8,128)(2,1)S(1)}, u32[]{:S(2)}, u32[]{:S(2)}) collective-permute-start(bf16[2,2,48,768]{3,2,1,0:T(8,128)(2,1)S(1)} %get-tuple-element.121.refs_0_), channel_id=1, source_target_pairs={{0,16},{8,24},{16,0},{24,8},{1,17},{9,25},{17,1},{25,9},{2,18},{10... | collective-permute-start | bytes 884744 | tf_op jit(solution)/shard_map/ppermute | solution.py:356
  58.9 14.4 %collective-permute-start.24 = (bf16[2,2,48,768]{3,2,1,0:T(8,128)(2,1)S(1)}, bf16[2,2,48,768]{3,2,1,0:T(8,128)(2,1)S(1)}, u32[]{:S(2)}, u32[]{:S(2)}) collective-permute-start(bf16[2,2,48,768]{3,2,1,0:T(8,128)(2,1)S(1)} %get-tuple-element.135.refs_0_), channel_id=1, source_target_pairs={{0,16},{8,24},{16,0},{24,8},{1,17},{9,25},{17,1},{25,9},{2,18},{10... | collective-permute-start | bytes 884744 | tf_op jit(solution)/shard_map/ppermute | solution.py:356
  60.4 10.0 %collective-permute-start.19 = (bf16[96,1152]{1,0:T(8,128)(2,1)S(1)}, bf16[96,1152]{1,0:T(8,128)(2,1)S(1)}, u32[]{:S(2)}, u32[]{:S(2)}) collective-permute-start(bf16[96,1152]{1,0:T(8,128)(2,1)S(1)} %get-tuple-element.122), channel_id=1, source_target_pairs={{0,1},{1,0},{2,3},{3,2},{4,5},{5,4},{6,7},{7,6},{8,9},{9,8},{10,11... | collective-permute-start | bytes 663560 | tf_op jit(solution)/shard_map/ppermute | solution.py:359
  62.0 14.1 %collective-permute-start.25 = (bf16[3,96,768]{2,1,0:T(8,128)(2,1)S(1)}, bf16[3,96,768]{2,1,0:T(8,128)(2,1)S(1)}, u32[]{:S(2)}, u32[]{:S(2)}) collective-permute-start(bf16[3,96,768]{2,1,0:T(8,128)(2,1)S(1)} %get-tuple-element.138), channel_id=1, source_target_pairs={{0,1},{1,0},{2,3},{3,2},{4,5},{5,4},{6,7},{7,6},{8,9},{9,8},{10,11... | collective-permute-start | bytes 1327112 | tf_op jit(solution)/shard_map/ppermute | solution.py:359
  67.1 7.4 %collective-permute-start.27 = (bf16[2,96,768]{2,1,0:T(8,128)(2,1)S(1)}, bf16[2,96,768]{2,1,0:T(8,128)(2,1)S(1)}, u32[]{:S(2)}, u32[]{:S(2)}) collective-permute-start(bf16[2,96,768]{2,1,0:T(8,128)(2,1)S(1)} %get-tuple-element.144), channel_id=1, source_target_pairs={{0,8},{8,0},{16,24},{24,16},{1,9},{9,1},{17,25},{25,17},{2,10},{10... | collective-permute-start | bytes 884744 | tf_op jit(solution)/shard_map/ppermute | solution.py:353
  70.4 11.5 %collective-permute-start.28 = (bf16[2,96,768]{2,1,0:T(8,128)(2,1)S(1)}, bf16[2,96,768]{2,1,0:T(8,128)(2,1)S(1)}, u32[]{:S(2)}, u32[]{:S(2)}) collective-permute-start(bf16[2,96,768]{2,1,0:T(8,128)(2,1)S(1)} %get-tuple-element.145), channel_id=1, source_target_pairs={{0,2},{2,4},{4,6},{6,0},{1,3},{3,5},{5,7},{7,1},{8,10},{10,12},{12... | collective-permute-start | bytes 884744 | tf_op jit(solution)/shard_map/ppermute | solution.py:362
  72.3 25.9 %collective-permute-start.38 = (bf16[2,384,768]{2,1,0:T(8,128)(2,1)S(1)}, bf16[2,384,768]{2,1,0:T(8,128)(2,1)S(1)}, u32[]{:S(2)}, u32[]{:S(2)}) collective-permute-start(bf16[2,384,768]{2,1,0:T(8,128)(2,1)S(1)} %get-tuple-element.155), channel_id=1, source_target_pairs={{0,8},{8,0},{16,24},{24,16},{1,9},{9,1},{17,25},{25,17},{2,10},{10... | collective-permute-start | bytes 3538952 | tf_op jit(solution)/shard_map/ppermute | solution.py:353
  73.3 24.9 %collective-permute-start.39 = (bf16[768,768]{1,0:T(8,128)(2,1)S(1)}, bf16[768,768]{1,0:T(8,128)(2,1)S(1)}, u32[]{:S(2)}, u32[]{:S(2)}) collective-permute-start(bf16[768,768]{1,0:T(8,128)(2,1)S(1)} %get-tuple-element.156), channel_id=1, source_target_pairs={{0,8},{8,0},{16,24},{24,16},{1,9},{9,1},{17,25},{25,17},{2,10},{10... | collective-permute-start | bytes 3538952 | tf_op jit(solution)/shard_map/ppermute | solution.py:353
  74.5 8.3 %collective-permute-start.36 = (bf16[3,48,768]{2,1,0:T(8,128)(2,1)S(1)}, bf16[3,48,768]{2,1,0:T(8,128)(2,1)S(1)}, u32[]{:S(2)}, u32[]{:S(2)}) collective-permute-start(bf16[3,48,768]{2,1,0:T(8,128)(2,1)S(1)} %get-tuple-element.154), channel_id=1, source_target_pairs={{0,1},{1,0},{2,3},{3,2},{4,5},{5,4},{6,7},{7,6},{8,9},{9,8},{10,11... | collective-permute-start | bytes 663560 | tf_op jit(solution)/shard_map/ppermute | solution.py:359
  76.1 10.7 %collective-permute-start.34 = (bf16[3,48,768]{2,1,0:T(8,128)(2,1)S(1)}, bf16[3,48,768]{2,1,0:T(8,128)(2,1)S(1)}, u32[]{:S(2)}, u32[]{:S(2)}) collective-permute-start(bf16[3,48,768]{2,1,0:T(8,128)(2,1)S(1)} %get-tuple-element.153), channel_id=1, source_target_pairs={{0,1},{1,0},{2,3},{3,2},{4,5},{5,4},{6,7},{7,6},{8,9},{9,8},{10,11... | collective-permute-start | bytes 663560 | tf_op jit(solution)/shard_map/ppermute | solution.py:359
  82.5 10.5 %collective-permute-start.29 = (bf16[2,96,768]{2,1,0:T(8,128)(2,1)S(1)}, bf16[2,96,768]{2,1,0:T(8,128)(2,1)S(1)}, u32[]{:S(2)}, u32[]{:S(2)}) collective-permute-start(bf16[2,96,768]{2,1,0:T(8,128)(2,1)S(1)} %get-tuple-element.147), channel_id=1, source_target_pairs={{0,2},{2,4},{4,6},{6,0},{1,3},{3,5},{5,7},{7,1},{8,10},{10,12},{12... | collective-permute-start | bytes 884744 | tf_op jit(solution)/shard_map/ppermute | solution.py:362
  82.8 10.2 %collective-permute-start.26 = (bf16[2,96,768]{2,1,0:T(8,128)(2,1)S(1)}, bf16[2,96,768]{2,1,0:T(8,128)(2,1)S(1)}, u32[]{:S(2)}, u32[]{:S(2)}) collective-permute-start(bf16[2,96,768]{2,1,0:T(8,128)(2,1)S(1)} %get-tuple-element.142), channel_id=1, source_target_pairs={{0,8},{8,0},{16,24},{24,16},{1,9},{9,1},{17,25},{25,17},{2,10},{10... | collective-permute-start | bytes 884744 | tf_op jit(solution)/shard_map/ppermute | solution.py:353
  86.8 1.5 %collective-permute-start.32 = (bf16[3,48,768]{2,1,0:T(8,128)(2,1)S(1)}, bf16[3,48,768]{2,1,0:T(8,128)(2,1)S(1)}, u32[]{:S(2)}, u32[]{:S(2)}) collective-permute-start(bf16[3,48,768]{2,1,0:T(8,128)(2,1)S(1)} %get-tuple-element.151), channel_id=1, source_target_pairs={{0,8},{8,0},{16,24},{24,16},{1,9},{9,1},{17,25},{25,17},{2,10},{10... | collective-permute-start | bytes 663560 | tf_op jit(solution)/shard_map/ppermute | solution.py:353
  88.3 5.9 %collective-permute-start.31 = (bf16[3,48,768]{2,1,0:T(8,128)(2,1)S(1)}, bf16[3,48,768]{2,1,0:T(8,128)(2,1)S(1)}, u32[]{:S(2)}, u32[]{:S(2)}) collective-permute-start(bf16[3,48,768]{2,1,0:T(8,128)(2,1)S(1)} %get-tuple-element.150), channel_id=1, source_target_pairs={{0,8},{8,0},{16,24},{24,16},{1,9},{9,1},{17,25},{25,17},{2,10},{10... | collective-permute-start | bytes 663560 | tf_op jit(solution)/shard_map/ppermute | solution.py:353
  93.0 1.5 %collective-permute-start.37 = (bf16[3,48,768]{2,1,0:T(8,128)(2,1)S(1)}, bf16[3,48,768]{2,1,0:T(8,128)(2,1)S(1)}, u32[]{:S(2)}, u32[]{:S(2)}) collective-permute-start(bf16[3,48,768]{2,1,0:T(8,128)(2,1)S(1)} %collective-permute-done.36.refs_7_), channel_id=1, source_target_pairs={{0,8},{8,0},{16,24},{24,16},{1,9},{9,1},{17,25},{25,17},{2,10},{10... | collective-permute-start | bytes 663560 | tf_op jit(solution)/shard_map/ppermute | solution.py:353
  93.0 5.1 %collective-permute-start.33 = (bf16[3,96,768]{2,1,0:T(8,128)(2,1)S(1)}, bf16[3,96,768]{2,1,0:T(8,128)(2,1)S(1)}, u32[]{:S(2)}, u32[]{:S(2)}) collective-permute-start(bf16[3,96,768]{2,1,0:T(8,128)(2,1)S(1)} %get-tuple-element.152), channel_id=1, source_target_pairs={{0,8},{8,0},{16,24},{24,16},{1,9},{9,1},{17,25},{25,17},{2,10},{10... | collective-permute-start | bytes 1327112 | tf_op jit(solution)/shard_map/ppermute | solution.py:353
  94.2 10.8 %collective-permute-start.30 = (bf16[2,96,768]{2,1,0:T(8,128)(2,1)S(1)}, bf16[2,96,768]{2,1,0:T(8,128)(2,1)S(1)}, u32[]{:S(2)}, u32[]{:S(2)}) collective-permute-start(bf16[2,96,768]{2,1,0:T(8,128)(2,1)S(1)} %get-tuple-element.149), channel_id=1, source_target_pairs={{0,2},{2,4},{4,6},{6,0},{1,3},{3,5},{5,7},{7,1},{8,10},{10,12},{12... | collective-permute-start | bytes 884744 | tf_op jit(solution)/shard_map/ppermute | solution.py:362
  94.5 3.7 %collective-permute-start.35 = (bf16[3,48,768]{2,1,0:T(8,128)(2,1)S(1)}, bf16[3,48,768]{2,1,0:T(8,128)(2,1)S(1)}, u32[]{:S(2)}, u32[]{:S(2)}) collective-permute-start(bf16[3,48,768]{2,1,0:T(8,128)(2,1)S(1)} %collective-permute-done.34.refs_6_), channel_id=1, source_target_pairs={{0,8},{8,0},{16,24},{24,16},{1,9},{9,1},{17,25},{25,17},{2,10},{10... | collective-permute-start | bytes 663560 | tf_op jit(solution)/shard_map/ppermute | solution.py:353

commit v6 on v5

--- a/solution.py
+++ b/solution.py
@@ -35,6 +35,7 @@
             ("G", 1): (("Y", 0), ("M", 0),),
             ("G", 2): (("Y", 1),),
             ("G", 3): (("T", 3),),
+            ("C", 0): (("S", 1),),
         },
     ),
 }
@@ -328,15 +329,15 @@
         copies[-1].start()
 
     core = where[0] if rel == 0 else 1 - where[0]
+    fill(blocks)
+    term = dot(all_values[...], all_cotangents[...], 0, 0) + early[1][...].astype(F32)
+    at = pl.ds(pl.multiple_of(core * width, 128), width)
+    put(held_out, outs[1].at[at, :], term)
     for index in range(blocks):
         fill(index)
         before = early[0][index].astype(F32)
         term = dot(all_tokens[...], all_values[...], 0, 0) + before
         put(held_in.at[index], outs[0].at[:, block_of(where, rel, index, width)], term)
-    fill(blocks)
-    term = dot(all_values[...], all_cotangents[...], 0, 0) + early[1][...].astype(F32)
-    at = pl.ds(pl.multiple_of(core * width, 128), width)
-    put(held_out, outs[1].at[at, :], term)
     for copy in copies:
         copy.wait()
 

time: 106 us -> 105 us (level)
  waiting for transfers between devices: 27.3 us -> 23.3 us
  starting transfers between devices: 28.6 us -> 30.3 us
    ppermute x6, waiting for transfers between devices: 14.2 us -> 9.69 us  [to_col(): lax.ppermute(value, 'col', [(c, (c + k) % n_col) for c in range(n_col)])]
    ppermute x6, starting transfers between devices: 6.55 us -> 8.12 us  [to_col(): lax.ppermute(value, 'col', [(c, (c + k) % n_col) for c in range(n_col)])]
  transfers between devices with their start and end apart: 40 -> 40, of which waited for: 14 -> 13; matrix products, arithmetic and copies ran while one was open for 0% -> 0% of each run, Pallas kernels for 42% -> 44%
where the time goes in v6:
time: 105 us
  Pallas kernels  49.9 us (48%)
  starting transfers between devices  30.3 us (29%)
  waiting for transfers between devices  23.3 us (22%)
    pallas_call x26, Pallas kernels, __call__(): pl.pallas_call(body, in_specs=[IN_SMEM] + (specs or [IN_VMEM] * n_in) + [...  49.9 us
    ppermute x6, waiting for transfers between devices, to_col(): lax.ppermute(value, 'col', [(c, (c + k) % n_col) for c in range(n_col)])  9.69 us
    ppermute x9, starting transfers between devices, to_depth(): lax.ppermute(value, 'depth', [(d, (d + k) % n_depth) for d in range(n_dep...  9.62 us
    ppermute x6, starting transfers between devices, to_col(): lax.ppermute(value, 'col', [(c, (c + k) % n_col) for c in range(n_col)])  8.12 us
    ppermute x5, starting transfers between devices, to_chip(): lax.ppermute(value, 'row', [(r, (r + 2 * k) % n_row) for r in range(n_row)])  8.05 us
    ppermute x9, waiting for transfers between devices, to_depth(): lax.ppermute(value, 'depth', [(d, (d + k) % n_depth) for d in range(n_dep...  7.66 us
    ppermute x20, starting transfers between devices, swap_cores(): return lax.ppermute(value, 'row', [(r, r ^ 1) for r in range(n_row)])  4.53 us
    ppermute x5, waiting for transfers between devices, to_chip(): lax.ppermute(value, 'row', [(r, (r + 2 * k) % n_row) for r in range(n_row)])  3.14 us
  transfers between devices with their start and end apart: 40, of which 13 were waited for; matrix products, arithmetic and copies ran while one was open for 0% of the time, Pallas kernels for 44%

profile of v6, /device:TPU:0, one launch (start us, length us, event | category | flops | bytes accessed | tf_op | source)
XLA Modules:
  0.0 104.6 jit_solution(18300021760513003291)
XLA Ops:
  0.7 2.9 %shard_map.75 = (bf16[2,768,768]{2,1,0:T(8,128)(2,1)S(1)}, bf16[2,768,768]{2,1,0:T(8,128)(2,1)S(1)}, f32[8,128]{1,0:T(8,128)S(1)}) custom-call(s32[2]{0:T(128)S(1)} %pad_add_fusion.where, bf16[768,3072]{1,0:T(8,128)(2,1)} %refs_1_.5, bf16[3072,768]{1,0:T(8,128)(2,1)} %refs_2_.1, f32[8,128]{1,0:T(8,128)S(1)} %broadcast_in_dim.3.refs_2_), custom_call_target="tpu_custom_call" | custom-call | flops 1000 | bytes 1000 | tf_op jit(solution)/shard_map/pallas_call | solution.py:98
  4.3 1.7 %shard_map.76 = (bf16[2,96,768]{2,1,0:T(8,128)(2,1)S(1)}, bf16[2,96,768]{2,1,0:T(8,128)(2,1)S(1)}, bf16[96,1536]{1,0:T(8,128)(2,1)S(1)}, bf16[96,1152]{1,0:T(8,128)(2,1)S(1)}, f32[8,128]{1,0:T(8,128)S(1)}) custom-call(s32[2]{0:T(128)S(1)} %pad_add_fusion.where, bf16[96,768]{1,0:T(8,128)(2,1)S(1)} %copy-done, bf16[96,768]{1,0:T(8,128)(2,1)S(1)} %copy-done.1, ...), custom_call_target="tpu_custom_call" | custom-call | flops 1000 | bytes 1000 | tf_op jit(solution)/shard_map/pallas_call | solution.py:98
  6.6 3.0 %collective-permute-start.4 = (bf16[96,1536]{1,0:T(8,128)(2,1)S(1)}, bf16[96,1536]{1,0:T(8,128)(2,1)S(1)}, u32[]{:S(2)}, u32[]{:S(2)}) collective-permute-start(bf16[96,1536]{1,0:T(8,128)(2,1)S(1)} %get-tuple-element.89.refs_0_), channel_id=1, source_target_pairs={{0,2},{2,4},{4,6},{6,0},{1,3},{3,5},{5,7},{7,1},{8,10},{10,12},{12... | collective-permute-start | bytes 884744 | tf_op jit(solution)/shard_map/ppermute | solution.py:363
  9.6 3.8 %shard_map.77 = (bf16[2,768,768]{2,1,0:T(8,128)(2,1)S(1)}, bf16[2,768,768]{2,1,0:T(8,128)(2,1)S(1)}, bf16[2,96,768]{2,1,0:T(8,128)(2,1)S(1)}, bf16[2,96,768]{2,1,0:T(8,128)(2,1)S(1)}, f32[8,128]{1,0:T(8,128)S(1)}) custom-call(s32[2]{0:T(128)S(1)} %pad_add_fusion.where, bf16[96,1536]{1,0:T(8,128)(2,1)S(1)} %get-tuple-element.89.refs_0_, ...), custom_call_target="tpu_custom_call" | custom-call | flops 1000 | bytes 1000 | tf_op jit(solution)/shard_map/pallas_call | solution.py:98
  13.4 0.7 shard_map.78
  14.1 2.1 %collective-permute-start.2 = (bf16[2,2,96,768]{3,2,1,0:T(8,128)(2,1)S(1)}, bf16[2,2,96,768]{3,2,1,0:T(8,128)(2,1)S(1)}, u32[]{:S(2)}, u32[]{:S(2)}) collective-permute-start(bf16[2,2,96,768]{3,2,1,0:T(8,128)(2,1)S(1)} %get-tuple-element.96.refs_0_), channel_id=1, source_target_pairs={{0,16},{8,24},{16,0},{24,8},{1,17},{9,25},{17,1},{25,9},{2,18},{10... | collective-permute-start | bytes 1769480 | tf_op jit(solution)/shard_map/ppermute | solution.py:357
  16.2 2.7 %collective-permute-done.4.refs_0_.refs_1_ = bf16[96,1536]{1,0:T(8,128)(2,1)S(1)} collective-permute-done((bf16[96,1536]{1,0:T(8,128)(2,1)S(1)}, bf16[96,1536]{1,0:T(8,128)(2,1)S(1)}, u32[]{:S(2)}, u32[]{:S(2)}) %collective-permute-start.4) | collective-permute-done | bytes 294944 | tf_op jit(solution)/shard_map/ppermute | solution.py:363
  19.4 1.1 %collective-permute-done.5.refs_1_.refs_4_ = bf16[96,1536]{1,0:T(8,128)(2,1)S(1)} collective-permute-done((bf16[96,1536]{1,0:T(8,128)(2,1)S(1)}, bf16[96,1536]{1,0:T(8,128)(2,1)S(1)}, u32[]{:S(2)}, u32[]{:S(2)}) %collective-permute-start.5) | collective-permute-done | bytes 294944 | tf_op jit(solution)/shard_map/ppermute | solution.py:354
  20.4 1.5 %collective-permute-start.9 = (bf16[96,1152]{1,0:T(8,128)(2,1)S(1)}, bf16[96,1152]{1,0:T(8,128)(2,1)S(1)}, u32[]{:S(2)}, u32[]{:S(2)}) collective-permute-start(bf16[96,1152]{1,0:T(8,128)(2,1)S(1)} %get-tuple-element.104), channel_id=1, source_target_pairs={{0,1},{1,0},{2,3},{3,2},{4,5},{5,4},{6,7},{7,6},{8,9},{9,8},{10,11... | collective-permute-start | bytes 663560 | tf_op jit(solution)/shard_map/ppermute | solution.py:360
  22.0 3.1 %shard_map.79 = (bf16[2,2,96,768]{3,2,1,0:T(8,128)(2,1)S(1)}, bf16[96,1152]{1,0:T(8,128)(2,1)S(1)}, bf16[2,768,768]{2,1,0:T(8,128)(2,1)S(1)}, bf16[2,768,768]{2,1,0:T(8,128)(2,1)S(1)}, f32[8,128]{1,0:T(8,128)S(1)}) custom-call(s32[2]{0:T(128)S(1)} %pad_add_fusion.where, bf16[96,1536]{1,0:T(8,128)(2,1)S(1)} %collective-permute-done.4.refs_0_.refs_1_, ...), custom_call_target="tpu_custom_call" | custom-call | flops 1000 | bytes 1000 | tf_op jit(solution)/shard_map/pallas_call | solution.py:98
  25.1 0.6 collective-permute-start.10
  25.7 1.5 %collective-permute-start.15 = (bf16[2,2,96,768]{3,2,1,0:T(8,128)(2,1)S(1)}, bf16[2,2,96,768]{3,2,1,0:T(8,128)(2,1)S(1)}, u32[]{:S(2)}, u32[]{:S(2)}) collective-permute-start(bf16[2,2,96,768]{3,2,1,0:T(8,128)(2,1)S(1)} %get-tuple-element.113.refs_0_), channel_id=1, source_target_pairs={{0,16},{8,24},{16,0},{24,8},{1,17},{9,25},{17,1},{25,9},{2,18},{10... | collective-permute-start | bytes 1769480 | tf_op jit(solution)/shard_map/ppermute | solution.py:357
  27.1 3.1 %collective-permute-done.2.refs_1_ = bf16[2,2,96,768]{3,2,1,0:T(8,128)(2,1)S(1)} collective-permute-done((bf16[2,2,96,768]{3,2,1,0:T(8,128)(2,1)S(1)}, bf16[2,2,96,768]{3,2,1,0:T(8,128)(2,1)S(1)}, u32[]{:S(2)}, u32[]{:S(2)}) %collective-permute-start.2) | collective-permute-done | bytes 589856 | tf_op jit(solution)/shard_map/ppermute | solution.py:357
  30.3 1.1 %shard_map.80 = (bf16[2,2,96,768]{3,2,1,0:T(8,128)(2,1)S(1)}, bf16[3,96,768]{2,1,0:T(8,128)(2,1)S(1)}, f32[8,128]{1,0:T(8,128)S(1)}) custom-call(s32[2]{0:T(128)S(1)} %pad_add_fusion.where, bf16[2,2,96,768]{3,2,1,0:T(8,128)(2,1)S(1)} %get-tuple-element.96.refs_0_, bf16[2,2,96,768]{3,2,1,0:T(8,128)(2,1)S(1)} %collective-permute-done.2.refs_1_, ...), custom_call_target="tpu_custom_call" | custom-call | flops 1000 | bytes 1000 | tf_op jit(solution)/shard_map/pallas_call | solution.py:98
  31.4 2.2 %collective-permute-start.16 = (bf16[3,96,768]{2,1,0:T(8,128)(2,1)S(1)}, bf16[3,96,768]{2,1,0:T(8,128)(2,1)S(1)}, u32[]{:S(2)}, u32[]{:S(2)}) collective-permute-start(bf16[3,96,768]{2,1,0:T(8,128)(2,1)S(1)} %get-tuple-element.114), channel_id=1, source_target_pairs={{0,1},{1,0},{2,3},{3,2},{4,5},{5,4},{6,7},{7,6},{8,9},{9,8},{10,11... | collective-permute-start | bytes 1327112 | tf_op jit(solution)/shard_map/ppermute | solution.py:360
  33.6 0.6 shard_map.81
  34.3 2.8 %shard_map.82 = (bf16[2,96,768]{2,1,0:T(8,128)(2,1)S(1)}, bf16[2,96,768]{2,1,0:T(8,128)(2,1)S(1)}, f32[8,128]{1,0:T(8,128)S(1)}) custom-call(s32[2]{0:T(128)S(1)} %pad_add_fusion.where, bf16[2,2,96,768]{3,2,1,0:T(8,128)(2,1)S(1)} %get-tuple-element.101.refs_0_.refs_6_, bf16[2,768,768]{2,1,0:T(8,128)(2,1)S(1)} %get-tuple-element.97.refs_2_.refs_1_, ...), custom_call_target="tpu_custom_call" | custom-call | flops 1000 | bytes 1000 | tf_op jit(solution)/shard_map/pallas_call | solution.py:98
  37.6 1.6 %collective-permute-start.12 = (bf16[96,1536]{1,0:T(8,128)(2,1)S(1)}, bf16[96,1536]{1,0:T(8,128)(2,1)S(1)}, u32[]{:S(2)}, u32[]{:S(2)}) collective-permute-start(bf16[96,1536]{1,0:T(8,128)(2,1)S(1)} %collective-permute-done.8.refs_0_), channel_id=1, source_target_pairs={{0,2},{2,4},{4,6},{6,0},{1,3},{3,5},{5,7},{7,1},{8,10},{10,12},{12... | collective-permute-start | bytes 884744 | tf_op jit(solution)/shard_map/ppermute | solution.py:363
  39.2 2.8 %shard_map.83 = (bf16[2,2,96,768]{3,2,1,0:T(8,128)(2,1)S(1)}, bf16[96,1152]{1,0:T(8,128)(2,1)S(1)}, f32[8,128]{1,0:T(8,128)S(1)}) custom-call(s32[2]{0:T(128)S(1)} %pad_add_fusion.where, bf16[96,1536]{1,0:T(8,128)(2,1)S(1)} %get-tuple-element.110.refs_0_.refs_2_, bf16[96,1536]{1,0:T(8,128)(2,1)S(1)} %collective-permute-done.13.refs_1_.refs_5_, ...), custom_call_target="tpu_custom_call" | custom-call | flops 1000 | bytes 1000 | tf_op jit(solution)/shard_map/pallas_call | solution.py:98
  42.7 1.4 %collective-permute-start.20 = (bf16[2,2,96,768]{3,2,1,0:T(8,128)(2,1)S(1)}, bf16[2,2,96,768]{3,2,1,0:T(8,128)(2,1)S(1)}, u32[]{:S(2)}, u32[]{:S(2)}) collective-permute-start(bf16[2,2,96,768]{3,2,1,0:T(8,128)(2,1)S(1)} %get-tuple-element.123.refs_0_), channel_id=1, source_target_pairs={{0,16},{8,24},{16,0},{24,8},{1,17},{9,25},{17,1},{25,9},{2,18},{10... | collective-permute-start | bytes 1769480 | tf_op jit(solution)/shard_map/ppermute | solution.py:357
  44.1 1.1 %shard_map.84 = (bf16[2,2,96,768]{3,2,1,0:T(8,128)(2,1)S(1)}, bf16[3,96,768]{2,1,0:T(8,128)(2,1)S(1)}, f32[8,128]{1,0:T(8,128)S(1)}) custom-call(s32[2]{0:T(128)S(1)} %pad_add_fusion.where, bf16[2,2,96,768]{3,2,1,0:T(8,128)(2,1)S(1)} %get-tuple-element.113.refs_0_, bf16[2,2,96,768]{3,2,1,0:T(8,128)(2,1)S(1)} %collective-permute-done.15.refs_1_, ...), custom_call_target="tpu_custom_call" | custom-call | flops 1000 | bytes 1000 | tf_op jit(solution)/shard_map/pallas_call | solution.py:98
  45.3 1.6 %collective-permute-start.21 = (bf16[3,96,768]{2,1,0:T(8,128)(2,1)S(1)}, bf16[3,96,768]{2,1,0:T(8,128)(2,1)S(1)}, u32[]{:S(2)}, u32[]{:S(2)}) collective-permute-start(bf16[3,96,768]{2,1,0:T(8,128)(2,1)S(1)} %get-tuple-element.124), channel_id=1, source_target_pairs={{0,1},{1,0},{2,3},{3,2},{4,5},{5,4},{6,7},{7,6},{8,9},{9,8},{10,11... | collective-permute-start | bytes 1327112 | tf_op jit(solution)/shard_map/ppermute | solution.py:360
  46.9 1.8 %collective-permute-done.12.refs_0_ = bf16[96,1536]{1,0:T(8,128)(2,1)S(1)} collective-permute-done((bf16[96,1536]{1,0:T(8,128)(2,1)S(1)}, bf16[96,1536]{1,0:T(8,128)(2,1)S(1)}, u32[]{:S(2)}, u32[]{:S(2)}) %collective-permute-start.12) | collective-permute-done | bytes 294944 | tf_op jit(solution)/shard_map/ppermute | solution.py:363
  48.7 1.7 %collective-permute-done.14.refs_1_ = bf16[96,1152]{1,0:T(8,128)(2,1)S(1)} collective-permute-done((bf16[96,1152]{1,0:T(8,128)(2,1)S(1)}, bf16[96,1152]{1,0:T(8,128)(2,1)S(1)}, u32[]{:S(2)}, u32[]{:S(2)}) %collective-permute-start.14) | collective-permute-done | bytes 221216 | tf_op jit(solution)/shard_map/ppermute | solution.py:360
  51.5 2.8 %shard_map.86 = (bf16[2,96,768]{2,1,0:T(8,128)(2,1)S(1)}, bf16[2,96,768]{2,1,0:T(8,128)(2,1)S(1)}, f32[8,128]{1,0:T(8,128)S(1)}) custom-call(s32[2]{0:T(128)S(1)} %pad_add_fusion.where, bf16[2,2,96,768]{3,2,1,0:T(8,128)(2,1)S(1)} %get-tuple-element.118.refs_0_.refs_7_, bf16[2,768,768]{2,1,0:T(8,128)(2,1)S(1)} %get-tuple-element.97.refs_2_.refs_1_, ...), custom_call_target="tpu_custom_call" | custom-call | flops 1000 | bytes 1000 | tf_op jit(solution)/shard_map/pallas_call | solution.py:98
  54.5 2.8 %shard_map.87 = (bf16[2,2,48,768]{3,2,1,0:T(8,128)(2,1)S(1)}, bf16[2,2,48,768]{3,2,1,0:T(8,128)(2,1)S(1)}, bf16[96,1152]{1,0:T(8,128)(2,1)S(1)}, f32[8,128]{1,0:T(8,128)S(1)}) custom-call(s32[2]{0:T(128)S(1)} %pad_add_fusion.where, bf16[96,1536]{1,0:T(8,128)(2,1)S(1)} %get-tuple-element.117.refs_0_, bf16[96,1536]{1,0:T(8,128)(2,1)S(1)} %collective-permute-done.17.refs_1_, ...), custom_call_target="tpu_custom_call" | custom-call | flops 1000 | bytes 1000 | tf_op jit(solution)/shard_map/pallas_call | solution.py:98
  57.3 1.6 %collective-permute-start.18 = (bf16[2,2,48,768]{3,2,1,0:T(8,128)(2,1)S(1)}, bf16[2,2,48,768]{3,2,1,0:T(8,128)(2,1)S(1)}, u32[]{:S(2)}, u32[]{:S(2)}) collective-permute-start(bf16[2,2,48,768]{3,2,1,0:T(8,128)(2,1)S(1)} %get-tuple-element.121.refs_0_), channel_id=1, source_target_pairs={{0,16},{8,24},{16,0},{24,8},{1,17},{9,25},{17,1},{25,9},{2,18},{10... | collective-permute-start | bytes 884744 | tf_op jit(solution)/shard_map/ppermute | solution.py:357
  58.9 1.5 %collective-permute-start.24 = (bf16[2,2,48,768]{3,2,1,0:T(8,128)(2,1)S(1)}, bf16[2,2,48,768]{3,2,1,0:T(8,128)(2,1)S(1)}, u32[]{:S(2)}, u32[]{:S(2)}) collective-permute-start(bf16[2,2,48,768]{3,2,1,0:T(8,128)(2,1)S(1)} %get-tuple-element.135.refs_0_), channel_id=1, source_target_pairs={{0,16},{8,24},{16,0},{24,8},{1,17},{9,25},{17,1},{25,9},{2,18},{10... | collective-permute-start | bytes 884744 | tf_op jit(solution)/shard_map/ppermute | solution.py:357
  60.9 1.1 %shard_map.88 = (bf16[2,2,96,768]{3,2,1,0:T(8,128)(2,1)S(1)}, bf16[3,96,768]{2,1,0:T(8,128)(2,1)S(1)}, f32[8,128]{1,0:T(8,128)S(1)}) custom-call(s32[2]{0:T(128)S(1)} %pad_add_fusion.where, bf16[2,2,96,768]{3,2,1,0:T(8,128)(2,1)S(1)} %get-tuple-element.123.refs_0_, bf16[2,2,96,768]{3,2,1,0:T(8,128)(2,1)S(1)} %collective-permute-done.20.refs_1_, ...), custom_call_target="tpu_custom_call" | custom-call | flops 1000 | bytes 1000 | tf_op jit(solution)/shard_map/pallas_call | solution.py:98
  62.0 1.6 %collective-permute-start.25 = (bf16[3,96,768]{2,1,0:T(8,128)(2,1)S(1)}, bf16[3,96,768]{2,1,0:T(8,128)(2,1)S(1)}, u32[]{:S(2)}, u32[]{:S(2)}) collective-permute-start(bf16[3,96,768]{2,1,0:T(8,128)(2,1)S(1)} %get-tuple-element.138), channel_id=1, source_target_pairs={{0,1},{1,0},{2,3},{3,2},{4,5},{5,4},{6,7},{7,6},{8,9},{9,8},{10,11... | collective-permute-start | bytes 1327112 | tf_op jit(solution)/shard_map/ppermute | solution.py:360
  63.6 0.6 shard_map.89
  64.3 1.9 %collective-permute-start.26 = (bf16[2,96,768]{2,1,0:T(8,128)(2,1)S(1)}, bf16[2,96,768]{2,1,0:T(8,128)(2,1)S(1)}, u32[]{:S(2)}, u32[]{:S(2)}) collective-permute-start(bf16[2,96,768]{2,1,0:T(8,128)(2,1)S(1)} %get-tuple-element.139), channel_id=1, source_target_pairs={{0,2},{2,4},{4,6},{6,0},{1,3},{3,5},{5,7},{7,1},{8,10},{10,12},{12... | collective-permute-start | bytes 884744 | tf_op jit(solution)/shard_map/ppermute | solution.py:363
  66.1 2.8 %shard_map.90 = (bf16[2,96,768]{2,1,0:T(8,128)(2,1)S(1)}, bf16[2,96,768]{2,1,0:T(8,128)(2,1)S(1)}, f32[8,128]{1,0:T(8,128)S(1)}) custom-call(s32[2]{0:T(128)S(1)} %pad_add_fusion.where, bf16[2,2,96,768]{3,2,1,0:T(8,128)(2,1)S(1)} %get-tuple-element.126.refs_0_.refs_8_, bf16[2,768,768]{2,1,0:T(8,128)(2,1)S(1)} %get-tuple-element.97.refs_2_.refs_1_, ...), custom_call_target="tpu_custom_call" | custom-call | flops 1000 | bytes 1000 | tf_op jit(solution)/shard_map/pallas_call | solution.py:98
  68.9 3.2 %shard_map.91 = (f32[2,384,768]{2,1,0:T(8,128)S(1)}, f32[768,768]{1,0:T(8,128)S(1)}, bf16[2,384,768]{2,1,0:T(8,128)(2,1)S(1)}, bf16[768,768]{1,0:T(8,128)(2,1)S(1)}, f32[8,128]{1,0:T(8,128)S(1)}) custom-call(s32[2]{0:T(128)S(1)} %pad_add_fusion.where, bf16[96,1536]{1,0:T(8,128)(2,1)S(1)} %get-tuple-element.89.refs_0_, ...), custom_call_target="tpu_custom_call" | custom-call | flops 1000 | bytes 1000 | tf_op jit(solution)/shard_map/pallas_call | solution.py:98
  72.8 0.8 shard_map.92
  73.7 0.8 shard_map.93
  75.1 1.0 collective-permute-done.25.refs_0_.refs_5_
  77.2 2.8 %shard_map.95 = (bf16[2,96,768]{2,1,0:T(8,128)(2,1)S(1)}, bf16[2,96,768]{2,1,0:T(8,128)(2,1)S(1)}, f32[8,128]{1,0:T(8,128)S(1)}) custom-call(s32[2]{0:T(128)S(1)} %pad_add_fusion.where, bf16[2,2,48,768]{3,2,1,0:T(8,128)(2,1)S(1)} %get-tuple-element.134.refs_0_.refs_3_, bf16[2,2,48,768]{3,2,1,0:T(8,128)(2,1)S(1)} %get-tuple-element.137.refs_1_.refs_4_, ...), custom_call_target="tpu_custom_call" | custom-call | flops 1000 | bytes 1000 | tf_op jit(solution)/shard_map/pallas_call | solution.py:98
  80.0 0.7 shard_map.96
  80.7 1.6 %collective-permute-start.29 = (bf16[2,96,768]{2,1,0:T(8,128)(2,1)S(1)}, bf16[2,96,768]{2,1,0:T(8,128)(2,1)S(1)}, u32[]{:S(2)}, u32[]{:S(2)}) collective-permute-start(bf16[2,96,768]{2,1,0:T(8,128)(2,1)S(1)} %get-tuple-element.147), channel_id=1, source_target_pairs={{0,2},{2,4},{4,6},{6,0},{1,3},{3,5},{5,7},{7,1},{8,10},{10,12},{12... | collective-permute-start | bytes 884744 | tf_op jit(solution)/shard_map/ppermute | solution.py:363
  82.9 4.3 %collective-permute-done.34.refs_6_ = bf16[3,48,768]{2,1,0:T(8,128)(2,1)S(1)} collective-permute-done((bf16[3,48,768]{2,1,0:T(8,128)(2,1)S(1)}, bf16[3,48,768]{2,1,0:T(8,128)(2,1)S(1)}, u32[]{:S(2)}, u32[]{:S(2)}) %collective-permute-start.34) | collective-permute-done | bytes 221216 | tf_op jit(solution)/shard_map/ppermute | solution.py:360
  87.1 1.5 %collective-permute-done.32.refs_4_ = bf16[3,48,768]{2,1,0:T(8,128)(2,1)S(1)} collective-permute-done((bf16[3,48,768]{2,1,0:T(8,128)(2,1)S(1)}, bf16[3,48,768]{2,1,0:T(8,128)(2,1)S(1)}, u32[]{:S(2)}, u32[]{:S(2)}) %collective-permute-start.32) | collective-permute-done | bytes 221216 | tf_op jit(solution)/shard_map/ppermute | solution.py:354
  88.8 2.6 %collective-permute-done.29.refs_2_ = bf16[2,96,768]{2,1,0:T(8,128)(2,1)S(1)} collective-permute-done((bf16[2,96,768]{2,1,0:T(8,128)(2,1)S(1)}, bf16[2,96,768]{2,1,0:T(8,128)(2,1)S(1)}, u32[]{:S(2)}, u32[]{:S(2)}) %collective-permute-start.29) | collective-permute-done | bytes 294944 | tf_op jit(solution)/shard_map/ppermute | solution.py:363
  91.9 0.6 shard_map.97
  93.0 3.8 %shard_map.98 = (f32[384,3072]{1,0:T(8,128)}, f32[1536,768]{1,0:T(8,128)}, f32[8,128]{1,0:T(8,128)S(1)}) custom-call(s32[2]{0:T(128)S(1)} %pad_add_fusion.where, bf16[96,1536]{1,0:T(8,128)(2,1)S(1)} %get-tuple-element.117.refs_0_, bf16[96,1152]{1,0:T(8,128)(2,1)S(1)} %collective-permute-done.14.refs_1_, ...), custom_call_target="tpu_custom_call" | custom-call | flops 1000 | bytes 1000 | tf_op jit(solution)/shard_map/pallas_call | solution.py:98
  96.8 3.8 %shard_map.99 = (f32[384,3072]{1,0:T(8,128)}, f32[1536,768]{1,0:T(8,128)}, f32[8,128]{1,0:T(8,128)S(1)}) custom-call(s32[2]{0:T(128)S(1)} %pad_add_fusion.where, bf16[96,1536]{1,0:T(8,128)(2,1)S(1)} %get-tuple-element.117.refs_0_, bf16[96,1152]{1,0:T(8,128)(2,1)S(1)} %collective-permute-done.14.refs_1_, ...), custom_call_target="tpu_custom_call", output_to_operand_aliasing={{0}: (11, {}), {1}: (12, {})} | custom-call | flops 1000 | bytes 1000 | tf_op jit(solution)/shard_map/pallas_call | solution.py:98
  100.7 2.6 %collective-permute-done.30.refs_2_ = bf16[2,96,768]{2,1,0:T(8,128)(2,1)S(1)} collective-permute-done((bf16[2,96,768]{2,1,0:T(8,128)(2,1)S(1)}, bf16[2,96,768]{2,1,0:T(8,128)(2,1)S(1)}, u32[]{:S(2)}, u32[]{:S(2)}) %collective-permute-start.30) | collective-permute-done | bytes 294944 | tf_op jit(solution)/shard_map/ppermute | solution.py:363
  103.3 1.3 %shard_map.100 = (bf16[96,768]{1,0:T(8,128)(2,1)}, bf16[96,768]{1,0:T(8,128)(2,1)}, f32[8,128]{1,0:T(8,128)}) custom-call(s32[2]{0:T(128)S(1)} %pad_add_fusion.where, bf16[2,96,768]{2,1,0:T(8,128)(2,1)S(1)} %get-tuple-element.108.refs_0_, bf16[2,96,768]{2,1,0:T(8,128)(2,1)S(1)} %collective-permute-done.11.refs_3_.refs_1_, ...), custom_call_target="tpu_custom_call" | custom-call | flops 1000 | bytes 1000 | tf_op jit(solution)/shard_map/pallas_call | solution.py:98
  (64 shorter events, 9.0 us)
Async XLA Ops:
  0.7 3.5 %copy-start = (bf16[96,768]{1,0:T(8,128)(2,1)S(1)}, bf16[96,768]{1,0:T(8,128)(2,1)}, u32[]{:S(2)}) copy-start(bf16[96,768]{1,0:T(8,128)(2,1)} %refs_0_.3) | copy-start | bytes 442372
  0.7 3.5 %copy-start.1 = (bf16[96,768]{1,0:T(8,128)(2,1)S(1)}, bf16[96,768]{1,0:T(8,128)(2,1)}, u32[]{:S(2)}) copy-start(bf16[96,768]{1,0:T(8,128)(2,1)} %refs_1_.4) | copy-start | bytes 442372
  3.7 16.8 %collective-permute-start.6 = (bf16[2,768,768]{2,1,0:T(8,128)(2,1)S(1)}, bf16[2,768,768]{2,1,0:T(8,128)(2,1)S(1)}, u32[]{:S(2)}, u32[]{:S(2)}) collective-permute-start(bf16[2,768,768]{2,1,0:T(8,128)(2,1)S(1)} %get-tuple-element.86.refs_2_), channel_id=1, source_target_pairs={{0,8},{8,0},{16,24},{24,16},{1,9},{9,1},{17,25},{25,17},{2,10},{10... | collective-permute-start | bytes 7077896 | tf_op jit(solution)/shard_map/ppermute | solution.py:354
  4.2 17.8 %collective-permute-start.7 = (bf16[2,768,768]{2,1,0:T(8,128)(2,1)S(1)}, bf16[2,768,768]{2,1,0:T(8,128)(2,1)S(1)}, u32[]{:S(2)}, u32[]{:S(2)}) collective-permute-start(bf16[2,768,768]{2,1,0:T(8,128)(2,1)S(1)} %get-tuple-element.87.refs_3_), channel_id=1, source_target_pairs={{0,8},{8,0},{16,24},{24,16},{1,9},{9,1},{17,25},{25,17},{2,10},{10... | collective-permute-start | bytes 7077896 | tf_op jit(solution)/shard_map/ppermute | solution.py:354
  6.0 7.4 %collective-permute-start = (bf16[2,96,768]{2,1,0:T(8,128)(2,1)S(1)}, bf16[2,96,768]{2,1,0:T(8,128)(2,1)S(1)}, u32[]{:S(2)}, u32[]{:S(2)}) collective-permute-start(bf16[2,96,768]{2,1,0:T(8,128)(2,1)S(1)} %get-tuple-element.93), channel_id=1, source_target_pairs={{0,8},{8,0},{16,24},{24,16},{1,9},{9,1},{17,25},{25,17},{2,10},{10... | collective-permute-start | bytes 884744 | tf_op jit(solution)/shard_map/ppermute | solution.py:354
  6.5 6.9 %collective-permute-start.1 = (bf16[2,96,768]{2,1,0:T(8,128)(2,1)S(1)}, bf16[2,96,768]{2,1,0:T(8,128)(2,1)S(1)}, u32[]{:S(2)}, u32[]{:S(2)}) collective-permute-start(bf16[2,96,768]{2,1,0:T(8,128)(2,1)S(1)} %get-tuple-element.94), channel_id=1, source_target_pairs={{0,8},{8,0},{16,24},{24,16},{1,9},{9,1},{17,25},{25,17},{2,10},{10... | collective-permute-start | bytes 884744 | tf_op jit(solution)/shard_map/ppermute | solution.py:354
  6.6 12.3 %collective-permute-start.4 = (bf16[96,1536]{1,0:T(8,128)(2,1)S(1)}, bf16[96,1536]{1,0:T(8,128)(2,1)S(1)}, u32[]{:S(2)}, u32[]{:S(2)}) collective-permute-start(bf16[96,1536]{1,0:T(8,128)(2,1)S(1)} %get-tuple-element.89.refs_0_), channel_id=1, source_target_pairs={{0,2},{2,4},{4,6},{6,0},{1,3},{3,5},{5,7},{7,1},{8,10},{10,12},{12... | collective-permute-start | bytes 884744 | tf_op jit(solution)/shard_map/ppermute | solution.py:363
  14.1 16.2 %collective-permute-start.2 = (bf16[2,2,96,768]{3,2,1,0:T(8,128)(2,1)S(1)}, bf16[2,2,96,768]{3,2,1,0:T(8,128)(2,1)S(1)}, u32[]{:S(2)}, u32[]{:S(2)}) collective-permute-start(bf16[2,2,96,768]{3,2,1,0:T(8,128)(2,1)S(1)} %get-tuple-element.96.refs_0_), channel_id=1, source_target_pairs={{0,16},{8,24},{16,0},{24,8},{1,17},{9,25},{17,1},{25,9},{2,18},{10... | collective-permute-start | bytes 1769480 | tf_op jit(solution)/shard_map/ppermute | solution.py:357
  18.8 1.6 %collective-permute-start.5 = (bf16[96,1536]{1,0:T(8,128)(2,1)S(1)}, bf16[96,1536]{1,0:T(8,128)(2,1)S(1)}, u32[]{:S(2)}, u32[]{:S(2)}) collective-permute-start(bf16[96,1536]{1,0:T(8,128)(2,1)S(1)} %collective-permute-done.4.refs_0_.refs_1_), channel_id=1, source_target_pairs={{0,8},{8,0},{16,24},{24,16},{1,9},{9,1},{17,25},{25,17},{2,10},{10... | collective-permute-start | bytes 884744 | tf_op jit(solution)/shard_map/ppermute | solution.py:354
  18.9 6.8 %collective-permute-start.3 = (bf16[96,1536]{1,0:T(8,128)(2,1)S(1)}, bf16[96,1536]{1,0:T(8,128)(2,1)S(1)}, u32[]{:S(2)}, u32[]{:S(2)}) collective-permute-start(bf16[96,1536]{1,0:T(8,128)(2,1)S(1)} %get-tuple-element.89.refs_0_), channel_id=1, source_target_pairs={{0,8},{8,0},{16,24},{24,16},{1,9},{9,1},{17,25},{25,17},{2,10},{10... | collective-permute-start | bytes 884744 | tf_op jit(solution)/shard_map/ppermute | solution.py:354
  20.4 13.2 %collective-permute-start.8 = (bf16[96,1536]{1,0:T(8,128)(2,1)S(1)}, bf16[96,1536]{1,0:T(8,128)(2,1)S(1)}, u32[]{:S(2)}, u32[]{:S(2)}) collective-permute-start(bf16[96,1536]{1,0:T(8,128)(2,1)S(1)} %collective-permute-done.4.refs_0_.refs_1_), channel_id=1, source_target_pairs={{0,2},{2,4},{4,6},{6,0},{1,3},{3,5},{5,7},{7,1},{8,10},{10,12},{12... | collective-permute-start | bytes 884744 | tf_op jit(solution)/shard_map/ppermute | solution.py:363
  20.4 13.1 %collective-permute-start.9 = (bf16[96,1152]{1,0:T(8,128)(2,1)S(1)}, bf16[96,1152]{1,0:T(8,128)(2,1)S(1)}, u32[]{:S(2)}, u32[]{:S(2)}) collective-permute-start(bf16[96,1152]{1,0:T(8,128)(2,1)S(1)} %get-tuple-element.104), channel_id=1, source_target_pairs={{0,1},{1,0},{2,3},{3,2},{4,5},{5,4},{6,7},{7,6},{8,9},{9,8},{10,11... | collective-permute-start | bytes 663560 | tf_op jit(solution)/shard_map/ppermute | solution.py:360
  25.1 8.5 %collective-permute-start.10 = (bf16[96,1152]{1,0:T(8,128)(2,1)S(1)}, bf16[96,1152]{1,0:T(8,128)(2,1)S(1)}, u32[]{:S(2)}, u32[]{:S(2)}) collective-permute-start(bf16[96,1152]{1,0:T(8,128)(2,1)S(1)} %get-tuple-element.105), channel_id=1, source_target_pairs={{0,1},{1,0},{2,3},{3,2},{4,5},{5,4},{6,7},{7,6},{8,9},{9,8},{10,11... | collective-permute-start | bytes 663560 | tf_op jit(solution)/shard_map/ppermute | solution.py:360
  25.7 18.5 %collective-permute-start.15 = (bf16[2,2,96,768]{3,2,1,0:T(8,128)(2,1)S(1)}, bf16[2,2,96,768]{3,2,1,0:T(8,128)(2,1)S(1)}, u32[]{:S(2)}, u32[]{:S(2)}) collective-permute-start(bf16[2,2,96,768]{3,2,1,0:T(8,128)(2,1)S(1)} %get-tuple-element.113.refs_0_), channel_id=1, source_target_pairs={{0,16},{8,24},{16,0},{24,8},{1,17},{9,25},{17,1},{25,9},{2,18},{10... | collective-permute-start | bytes 1769480 | tf_op jit(solution)/shard_map/ppermute | solution.py:357
  31.4 11.3 %collective-permute-start.16 = (bf16[3,96,768]{2,1,0:T(8,128)(2,1)S(1)}, bf16[3,96,768]{2,1,0:T(8,128)(2,1)S(1)}, u32[]{:S(2)}, u32[]{:S(2)}) collective-permute-start(bf16[3,96,768]{2,1,0:T(8,128)(2,1)S(1)} %get-tuple-element.114), channel_id=1, source_target_pairs={{0,1},{1,0},{2,3},{3,2},{4,5},{5,4},{6,7},{7,6},{8,9},{9,8},{10,11... | collective-permute-start | bytes 1327112 | tf_op jit(solution)/shard_map/ppermute | solution.py:360
  34.2 5.0 %collective-permute-start.13 = (bf16[96,1536]{1,0:T(8,128)(2,1)S(1)}, bf16[96,1536]{1,0:T(8,128)(2,1)S(1)}, u32[]{:S(2)}, u32[]{:S(2)}) collective-permute-start(bf16[96,1536]{1,0:T(8,128)(2,1)S(1)} %get-tuple-element.110.refs_0_.refs_2_), channel_id=1, source_target_pairs={{0,8},{8,0},{16,24},{24,16},{1,9},{9,1},{17,25},{25,17},{2,10},{10... | collective-permute-start | bytes 884744 | tf_op jit(solution)/shard_map/ppermute | solution.py:354
  37.1 7.1 %collective-permute-start.11 = (bf16[2,96,768]{2,1,0:T(8,128)(2,1)S(1)}, bf16[2,96,768]{2,1,0:T(8,128)(2,1)S(1)}, u32[]{:S(2)}, u32[]{:S(2)}) collective-permute-start(bf16[2,96,768]{2,1,0:T(8,128)(2,1)S(1)} %get-tuple-element.109), channel_id=1, source_target_pairs={{0,8},{8,0},{16,24},{24,16},{1,9},{9,1},{17,25},{25,17},{2,10},{10... | collective-permute-start | bytes 884744 | tf_op jit(solution)/shard_map/ppermute | solution.py:354
  37.6 11.0 %collective-permute-start.12 = (bf16[96,1536]{1,0:T(8,128)(2,1)S(1)}, bf16[96,1536]{1,0:T(8,128)(2,1)S(1)}, u32[]{:S(2)}, u32[]{:S(2)}) collective-permute-start(bf16[96,1536]{1,0:T(8,128)(2,1)S(1)} %collective-permute-done.8.refs_0_), channel_id=1, source_target_pairs={{0,2},{2,4},{4,6},{6,0},{1,3},{3,5},{5,7},{7,1},{8,10},{10,12},{12... | collective-permute-start | bytes 884744 | tf_op jit(solution)/shard_map/ppermute | solution.py:363
  42.0 8.4 %collective-permute-start.14 = (bf16[96,1152]{1,0:T(8,128)(2,1)S(1)}, bf16[96,1152]{1,0:T(8,128)(2,1)S(1)}, u32[]{:S(2)}, u32[]{:S(2)}) collective-permute-start(bf16[96,1152]{1,0:T(8,128)(2,1)S(1)} %get-tuple-element.112), channel_id=1, source_target_pairs={{0,1},{1,0},{2,3},{3,2},{4,5},{5,4},{6,7},{7,6},{8,9},{9,8},{10,11... | collective-permute-start | bytes 663560 | tf_op jit(solution)/shard_map/ppermute | solution.py:360
  42.7 17.7 %collective-permute-start.20 = (bf16[2,2,96,768]{3,2,1,0:T(8,128)(2,1)S(1)}, bf16[2,2,96,768]{3,2,1,0:T(8,128)(2,1)S(1)}, u32[]{:S(2)}, u32[]{:S(2)}) collective-permute-start(bf16[2,2,96,768]{3,2,1,0:T(8,128)(2,1)S(1)} %get-tuple-element.123.refs_0_), channel_id=1, source_target_pairs={{0,16},{8,24},{16,0},{24,8},{1,17},{9,25},{17,1},{25,9},{2,18},{10... | collective-permute-start | bytes 1769480 | tf_op jit(solution)/shard_map/ppermute | solution.py:357
  45.3 13.6 %collective-permute-start.21 = (bf16[3,96,768]{2,1,0:T(8,128)(2,1)S(1)}, bf16[3,96,768]{2,1,0:T(8,128)(2,1)S(1)}, u32[]{:S(2)}, u32[]{:S(2)}) collective-permute-start(bf16[3,96,768]{2,1,0:T(8,128)(2,1)S(1)} %get-tuple-element.124), channel_id=1, source_target_pairs={{0,1},{1,0},{2,3},{3,2},{4,5},{5,4},{6,7},{7,6},{8,9},{9,8},{10,11... | collective-permute-start | bytes 1327112 | tf_op jit(solution)/shard_map/ppermute | solution.py:360
  51.0 3.5 %collective-permute-start.17 = (bf16[96,1536]{1,0:T(8,128)(2,1)S(1)}, bf16[96,1536]{1,0:T(8,128)(2,1)S(1)}, u32[]{:S(2)}, u32[]{:S(2)}) collective-permute-start(bf16[96,1536]{1,0:T(8,128)(2,1)S(1)} %get-tuple-element.117.refs_0_), channel_id=1, source_target_pairs={{0,8},{8,0},{16,24},{24,16},{1,9},{9,1},{17,25},{25,17},{2,10},{10... | collective-permute-start | bytes 884744 | tf_op jit(solution)/shard_map/ppermute | solution.py:354
  51.0 13.2 %collective-permute-start.22 = (bf16[192,1152]{1,0:T(8,128)(2,1)S(1)}, bf16[192,1152]{1,0:T(8,128)(2,1)S(1)}, u32[]{:S(2)}, u32[]{:S(2)}) collective-permute-start(bf16[192,1152]{1,0:T(8,128)(2,1)S(1)} %get-tuple-element.127.refs_9_), channel_id=1, source_target_pairs={{0,8},{8,0},{16,24},{24,16},{1,9},{9,1},{17,25},{25,17},{2,10},{10... | collective-permute-start | bytes 1327112 | tf_op jit(solution)/shard_map/ppermute | solution.py:354
  54.3 7.7 %collective-permute-start.23 = (bf16[2,96,768]{2,1,0:T(8,128)(2,1)S(1)}, bf16[2,96,768]{2,1,0:T(8,128)(2,1)S(1)}, u32[]{:S(2)}, u32[]{:S(2)}) collective-permute-start(bf16[2,96,768]{2,1,0:T(8,128)(2,1)S(1)} %get-tuple-element.129), channel_id=1, source_target_pairs={{0,8},{8,0},{16,24},{24,16},{1,9},{9,1},{17,25},{25,17},{2,10},{10... | collective-permute-start | bytes 884744 | tf_op jit(solution)/shard_map/ppermute | solution.py:354
  57.3 15.0 %collective-permute-start.18 = (bf16[2,2,48,768]{3,2,1,0:T(8,128)(2,1)S(1)}, bf16[2,2,48,768]{3,2,1,0:T(8,128)(2,1)S(1)}, u32[]{:S(2)}, u32[]{:S(2)}) collective-permute-start(bf16[2,2,48,768]{3,2,1,0:T(8,128)(2,1)S(1)} %get-tuple-element.121.refs_0_), channel_id=1, source_target_pairs={{0,16},{8,24},{16,0},{24,8},{1,17},{9,25},{17,1},{25,9},{2,18},{10... | collective-permute-start | bytes 884744 | tf_op jit(solution)/shard_map/ppermute | solution.py:357
  58.9 14.7 %collective-permute-start.24 = (bf16[2,2,48,768]{3,2,1,0:T(8,128)(2,1)S(1)}, bf16[2,2,48,768]{3,2,1,0:T(8,128)(2,1)S(1)}, u32[]{:S(2)}, u32[]{:S(2)}) collective-permute-start(bf16[2,2,48,768]{3,2,1,0:T(8,128)(2,1)S(1)} %get-tuple-element.135.refs_0_), channel_id=1, source_target_pairs={{0,16},{8,24},{16,0},{24,8},{1,17},{9,25},{17,1},{25,9},{2,18},{10... | collective-permute-start | bytes 884744 | tf_op jit(solution)/shard_map/ppermute | solution.py:357
  60.4 11.8 %collective-permute-start.19 = (bf16[96,1152]{1,0:T(8,128)(2,1)S(1)}, bf16[96,1152]{1,0:T(8,128)(2,1)S(1)}, u32[]{:S(2)}, u32[]{:S(2)}) collective-permute-start(bf16[96,1152]{1,0:T(8,128)(2,1)S(1)} %get-tuple-element.122), channel_id=1, source_target_pairs={{0,1},{1,0},{2,3},{3,2},{4,5},{5,4},{6,7},{7,6},{8,9},{9,8},{10,11... | collective-permute-start | bytes 663560 | tf_op jit(solution)/shard_map/ppermute | solution.py:360
  62.0 14.1 %collective-permute-start.25 = (bf16[3,96,768]{2,1,0:T(8,128)(2,1)S(1)}, bf16[3,96,768]{2,1,0:T(8,128)(2,1)S(1)}, u32[]{:S(2)}, u32[]{:S(2)}) collective-permute-start(bf16[3,96,768]{2,1,0:T(8,128)(2,1)S(1)} %get-tuple-element.138), channel_id=1, source_target_pairs={{0,1},{1,0},{2,3},{3,2},{4,5},{5,4},{6,7},{7,6},{8,9},{9,8},{10,11... | collective-permute-start | bytes 1327112 | tf_op jit(solution)/shard_map/ppermute | solution.py:360
  64.3 10.3 %collective-permute-start.26 = (bf16[2,96,768]{2,1,0:T(8,128)(2,1)S(1)}, bf16[2,96,768]{2,1,0:T(8,128)(2,1)S(1)}, u32[]{:S(2)}, u32[]{:S(2)}) collective-permute-start(bf16[2,96,768]{2,1,0:T(8,128)(2,1)S(1)} %get-tuple-element.139), channel_id=1, source_target_pairs={{0,2},{2,4},{4,6},{6,0},{1,3},{3,5},{5,7},{7,1},{8,10},{10,12},{12... | collective-permute-start | bytes 884744 | tf_op jit(solution)/shard_map/ppermute | solution.py:363
  72.2 7.9 %collective-permute-start.28 = (bf16[2,96,768]{2,1,0:T(8,128)(2,1)S(1)}, bf16[2,96,768]{2,1,0:T(8,128)(2,1)S(1)}, u32[]{:S(2)}, u32[]{:S(2)}) collective-permute-start(bf16[2,96,768]{2,1,0:T(8,128)(2,1)S(1)} %get-tuple-element.145), channel_id=1, source_target_pairs={{0,8},{8,0},{16,24},{24,16},{1,9},{9,1},{17,25},{25,17},{2,10},{10... | collective-permute-start | bytes 884744 | tf_op jit(solution)/shard_map/ppermute | solution.py:354
  72.3 24.5 %collective-permute-start.38 = (bf16[2,384,768]{2,1,0:T(8,128)(2,1)S(1)}, bf16[2,384,768]{2,1,0:T(8,128)(2,1)S(1)}, u32[]{:S(2)}, u32[]{:S(2)}) collective-permute-start(bf16[2,384,768]{2,1,0:T(8,128)(2,1)S(1)} %get-tuple-element.155), channel_id=1, source_target_pairs={{0,8},{8,0},{16,24},{24,16},{1,9},{9,1},{17,25},{25,17},{2,10},{10... | collective-permute-start | bytes 3538952 | tf_op jit(solution)/shard_map/ppermute | solution.py:354
  73.6 23.2 %collective-permute-start.39 = (bf16[768,768]{1,0:T(8,128)(2,1)S(1)}, bf16[768,768]{1,0:T(8,128)(2,1)S(1)}, u32[]{:S(2)}, u32[]{:S(2)}) collective-permute-start(bf16[768,768]{1,0:T(8,128)(2,1)S(1)} %get-tuple-element.156), channel_id=1, source_target_pairs={{0,8},{8,0},{16,24},{24,16},{1,9},{9,1},{17,25},{25,17},{2,10},{10... | collective-permute-start | bytes 3538952 | tf_op jit(solution)/shard_map/ppermute | solution.py:354
  74.6 8.3 %collective-permute-start.36 = (bf16[3,48,768]{2,1,0:T(8,128)(2,1)S(1)}, bf16[3,48,768]{2,1,0:T(8,128)(2,1)S(1)}, u32[]{:S(2)}, u32[]{:S(2)}) collective-permute-start(bf16[3,48,768]{2,1,0:T(8,128)(2,1)S(1)} %get-tuple-element.154), channel_id=1, source_target_pairs={{0,1},{1,0},{2,3},{3,2},{4,5},{5,4},{6,7},{7,6},{8,9},{9,8},{10,11... | collective-permute-start | bytes 663560 | tf_op jit(solution)/shard_map/ppermute | solution.py:360
  76.1 11.0 %collective-permute-start.34 = (bf16[3,48,768]{2,1,0:T(8,128)(2,1)S(1)}, bf16[3,48,768]{2,1,0:T(8,128)(2,1)S(1)}, u32[]{:S(2)}, u32[]{:S(2)}) collective-permute-start(bf16[3,48,768]{2,1,0:T(8,128)(2,1)S(1)} %get-tuple-element.153), channel_id=1, source_target_pairs={{0,1},{1,0},{2,3},{3,2},{4,5},{5,4},{6,7},{7,6},{8,9},{9,8},{10,11... | collective-permute-start | bytes 663560 | tf_op jit(solution)/shard_map/ppermute | solution.py:360
  80.7 10.6 %collective-permute-start.29 = (bf16[2,96,768]{2,1,0:T(8,128)(2,1)S(1)}, bf16[2,96,768]{2,1,0:T(8,128)(2,1)S(1)}, u32[]{:S(2)}, u32[]{:S(2)}) collective-permute-start(bf16[2,96,768]{2,1,0:T(8,128)(2,1)S(1)} %get-tuple-element.147), channel_id=1, source_target_pairs={{0,2},{2,4},{4,6},{6,0},{1,3},{3,5},{5,7},{7,1},{8,10},{10,12},{12... | collective-permute-start | bytes 884744 | tf_op jit(solution)/shard_map/ppermute | solution.py:363
  82.9 8.5 %collective-permute-start.27 = (bf16[2,96,768]{2,1,0:T(8,128)(2,1)S(1)}, bf16[2,96,768]{2,1,0:T(8,128)(2,1)S(1)}, u32[]{:S(2)}, u32[]{:S(2)}) collective-permute-start(bf16[2,96,768]{2,1,0:T(8,128)(2,1)S(1)} %get-tuple-element.143), channel_id=1, source_target_pairs={{0,8},{8,0},{16,24},{24,16},{1,9},{9,1},{17,25},{25,17},{2,10},{10... | collective-permute-start | bytes 884744 | tf_op jit(solution)/shard_map/ppermute | solution.py:354
  87.1 1.5 %collective-permute-start.32 = (bf16[3,48,768]{2,1,0:T(8,128)(2,1)S(1)}, bf16[3,48,768]{2,1,0:T(8,128)(2,1)S(1)}, u32[]{:S(2)}, u32[]{:S(2)}) collective-permute-start(bf16[3,48,768]{2,1,0:T(8,128)(2,1)S(1)} %get-tuple-element.151), channel_id=1, source_target_pairs={{0,8},{8,0},{16,24},{24,16},{1,9},{9,1},{17,25},{25,17},{2,10},{10... | collective-permute-start | bytes 663560 | tf_op jit(solution)/shard_map/ppermute | solution.py:354
  88.6 3.9 %collective-permute-start.31 = (bf16[3,48,768]{2,1,0:T(8,128)(2,1)S(1)}, bf16[3,48,768]{2,1,0:T(8,128)(2,1)S(1)}, u32[]{:S(2)}, u32[]{:S(2)}) collective-permute-start(bf16[3,48,768]{2,1,0:T(8,128)(2,1)S(1)} %get-tuple-element.150), channel_id=1, source_target_pairs={{0,8},{8,0},{16,24},{24,16},{1,9},{9,1},{17,25},{25,17},{2,10},{10... | collective-permute-start | bytes 663560 | tf_op jit(solution)/shard_map/ppermute | solution.py:354
  91.3 1.5 %collective-permute-start.37 = (bf16[3,48,768]{2,1,0:T(8,128)(2,1)S(1)}, bf16[3,48,768]{2,1,0:T(8,128)(2,1)S(1)}, u32[]{:S(2)}, u32[]{:S(2)}) collective-permute-start(bf16[3,48,768]{2,1,0:T(8,128)(2,1)S(1)} %collective-permute-done.36.refs_7_), channel_id=1, source_target_pairs={{0,8},{8,0},{16,24},{24,16},{1,9},{9,1},{17,25},{25,17},{2,10},{10... | collective-permute-start | bytes 663560 | tf_op jit(solution)/shard_map/ppermute | solution.py:354
  91.4 5.5 %collective-permute-start.33 = (bf16[3,96,768]{2,1,0:T(8,128)(2,1)S(1)}, bf16[3,96,768]{2,1,0:T(8,128)(2,1)S(1)}, u32[]{:S(2)}, u32[]{:S(2)}) collective-permute-start(bf16[3,96,768]{2,1,0:T(8,128)(2,1)S(1)} %get-tuple-element.152), channel_id=1, source_target_pairs={{0,8},{8,0},{16,24},{24,16},{1,9},{9,1},{17,25},{25,17},{2,10},{10... | collective-permute-start | bytes 1327112 | tf_op jit(solution)/shard_map/ppermute | solution.py:354
  92.5 10.8 %collective-permute-start.30 = (bf16[2,96,768]{2,1,0:T(8,128)(2,1)S(1)}, bf16[2,96,768]{2,1,0:T(8,128)(2,1)S(1)}, u32[]{:S(2)}, u32[]{:S(2)}) collective-permute-start(bf16[2,96,768]{2,1,0:T(8,128)(2,1)S(1)} %get-tuple-element.149), channel_id=1, source_target_pairs={{0,2},{2,4},{4,6},{6,0},{1,3},{3,5},{5,7},{7,1},{8,10},{10,12},{12... | collective-permute-start | bytes 884744 | tf_op jit(solution)/shard_map/ppermute | solution.py:363
  92.8 4.0 %collective-permute-start.35 = (bf16[3,48,768]{2,1,0:T(8,128)(2,1)S(1)}, bf16[3,48,768]{2,1,0:T(8,128)(2,1)S(1)}, u32[]{:S(2)}, u32[]{:S(2)}) collective-permute-start(bf16[3,48,768]{2,1,0:T(8,128)(2,1)S(1)} %collective-permute-done.34.refs_6_), channel_id=1, source_target_pairs={{0,8},{8,0},{16,24},{24,16},{1,9},{9,1},{17,25},{25,17},{2,10},{10... | collective-permute-start | bytes 663560 | tf_op jit(solution)/shard_map/ppermute | solution.py:354
